TPU v7x, 128 devices: a whole 4x4x4 slice. The times are simulated.
128 devices in a mesh: row: 8 (over x, y_lo), col: 16 (over z, y_hi, core).
Axes of the slice: x: 4, y: 4 (y_hi: 2, y_lo: 2; y = y_hi * 2 + y_lo), z: 4, core: 2. Of those that a mesh axis runs over, the one named last changes fastest.
Arguments:
- x_slab: bfloat16 [16, 32, 64, 128], P('row', 'col'), may hold values from -220 to 220
- h_blocks: bfloat16 [16, 32, 25, 4096], P('row', 'col'), may hold values from -0.21875 to 0.21875
- h_cols: int32 [16, 32, 25], P('row', 'col'), may hold values from 0 to 511, as said below
- h_count: int32 [16, 32], P('row', 'col'), may hold values from 1 to 25, as said below
- z_blocks: bfloat16 [16, 32, 25, 4096], P('row', 'col'), may hold values from -0.15625 to 0.15625
- z_cols: int32 [16, 32, 25], P('row', 'col'), may hold values from 0 to 511, as said below
- z_count: int32 [16, 32], P('row', 'col'), may hold values from 1 to 25, as said below
Outputs:
- cheb_one: bfloat16 [16, 32, 64, 128], P('row', 'col')
- cheb_two: bfloat16 [16, 32, 64, 128], P('row', 'col')
Inputs may be any that keep to these rules, and one draw needn't show every extreme that they name: `h_cols`: the 25 entries of a block cell name the 25 distinct cells within 2 cells of it along each lattice dimension, the lattice being periodic; only the first h_count entries of a cell are live, the others are padding. `h_count`: some cell has 25 live entries and some cell has 1. `z_cols`: the 25 entries of a block cell name the 25 distinct cells within 2 cells of it along each lattice dimension, the lattice being periodic; only the first z_count entries of a cell are live, the others are padding. `z_count`: some cell has 25 live entries and some cell has 1.
All inputs are finite; a program needn't handle non-finite values.
Results may differ from a plain program's by a relative error of at most 0.0085.
Values may be sent and summed in bfloat16 or wider, within the bound.
No kernel may reach another device: no remote copies, remote signals or barrier semaphores. Data moves between devices by JAX's collectives and lax.ppermute only.
A program may use at most 64 MiB of HBM per device.

v0:
```python
import jax
import jax.numpy as jnp
from jax import lax
from jax.sharding import PartitionSpec as P

REACH = 2


def extended(cells, sides, width):
    for axis, dim in sides:
        count = lax.axis_size(axis)
        head = lax.slice_in_dim(cells, 0, width, axis=dim)
        tail = lax.slice_in_dim(cells, cells.shape[dim] - width, cells.shape[dim], axis=dim)
        cells = jnp.concatenate(
            [
                lax.ppermute(tail, axis, [(i, (i + 1) % count) for i in range(count)]),
                cells,
                lax.ppermute(head, axis, [((i + 1) % count, i) for i in range(count)]),
            ],
            axis=dim,
        )
    return cells


def surround(slab_field):
    rim_depth = REACH
    wide_grid = extended(slab_field, (("row", 0), ("col", 1)), REACH)
    return (wide_grid, rim_depth)


def offset_blocks(blocks, col_ids, live_count):
    side_cells = col_ids.shape[0]
    max_entries = col_ids.shape[2]
    block_area = blocks.shape[3]
    span = 2 * REACH + 1
    grid_rows = lax.axis_size("row") * side_cells
    grid_cols = lax.axis_size("col") * side_cells
    cell_y = lax.axis_index("row") * side_cells + lax.broadcasted_iota(jnp.int32, col_ids.shape, 0)
    cell_x = lax.axis_index("col") * side_cells + lax.broadcasted_iota(jnp.int32, col_ids.shape, 1)
    delta_y = (col_ids // grid_cols - cell_y + REACH) % grid_rows
    delta_x = (col_ids % grid_cols - cell_x + REACH) % grid_cols
    offset_id = delta_y * span + delta_x
    is_live = lax.broadcasted_iota(jnp.int32, col_ids.shape, 2) < live_count[:, :, None]
    offsets = jnp.arange(span * span, dtype=jnp.int32)
    selector = ((offset_id[:, :, :, None] == offsets) & is_live[:, :, :, None]).astype(jnp.bfloat16)
    selector = selector.reshape(side_cells * side_cells, max_entries, span * span)
    flat_blocks = blocks.reshape(side_cells * side_cells, max_entries, block_area)
    arranged = jnp.einsum("cko,ckm->ocm", selector, flat_blocks, preferred_element_type=jnp.float32)
    used = jnp.sum(selector.astype(jnp.float32), axis=(0, 1)) > 0.0
    return (arranged.astype(jnp.bfloat16), used)


def apply_sparse(slab_field, arranged):
    wide_grid, rim_depth = surround(slab_field)
    side_cells = slab_field.shape[0]
    block_size = slab_field.shape[2]
    slab_cols = slab_field.shape[3]
    cell_count = side_cells * side_cells
    span = 2 * REACH + 1
    mats = arranged.reshape(span * span, cell_count, block_size, block_size)
    start_base = rim_depth - REACH
    product = jnp.zeros((cell_count, block_size, slab_cols), jnp.float32)
    for offset_index in range(span * span):
        start_y = start_base + offset_index // span
        start_x = start_base + offset_index % span
        window = lax.dynamic_slice(
            wide_grid, (start_y, start_x, 0, 0), (side_cells, side_cells, block_size, slab_cols)
        )
        mats_now = lax.dynamic_index_in_dim(mats, offset_index, 0, keepdims=False)
        product = product + jnp.einsum(
            "cij,cjs->cis",
            mats_now,
            window.reshape(cell_count, block_size, slab_cols),
            preferred_element_type=jnp.float32,
        )
    return product.reshape(side_cells, side_cells, block_size, slab_cols)


def body(x_slab, h_blocks, h_cols, h_count, z_blocks, z_cols, z_count):
    z_arranged, z_used = offset_blocks(z_blocks, z_cols, z_count)
    h_arranged, h_used = offset_blocks(h_blocks, h_cols, h_count)

    def apply_root(slab_field):
        return slab_field.astype(jnp.float32) + apply_sparse(slab_field, z_arranged)

    def apply_hamilton(slab_field):
        return apply_sparse(slab_field, h_arranged).astype(jnp.bfloat16)

    u_one = apply_root(x_slab).astype(jnp.bfloat16)
    u_two = apply_hamilton(u_one)
    power_image = apply_root(u_two)
    slab_float = x_slab.astype(jnp.float32)
    image_square, slab_square = lax.psum(
        (jnp.sum(power_image * power_image), jnp.sum(slab_float * slab_float)), ("row", "col")
    )
    scale_ratio = jnp.sqrt(image_square / (slab_square + 1e-06))
    cheb_one = (power_image / scale_ratio).astype(jnp.bfloat16)
    v_one = apply_root(cheb_one).astype(jnp.bfloat16)
    v_two = apply_hamilton(v_one)
    v_three = apply_root(v_two)
    cheb_two = (2.0 * v_three / scale_ratio - slab_float).astype(jnp.bfloat16)
    return (cheb_one, cheb_two)


def solution(mesh):
    in_specs = (
        P("row", "col", None, None),
        P("row", "col", None, None),
        P("row", "col", None),
        P("row", "col"),
        P("row", "col", None, None),
        P("row", "col", None),
        P("row", "col"),
    )
    out_specs = (P("row", "col", None, None), P("row", "col", None, None))
    return jax.shard_map(body, mesh=mesh, in_specs=in_specs, out_specs=out_specs, check_vma=False)
```

profile of v0, /device:TPU:0, one launch (start us, length us, event | category | flops | bytes accessed | tf_op | source)
XLA Modules:
  0.0 206.8 jit_solution(9348688201349915139)
XLA Ops:
  0.7 3.9 %collective-permute-start.1 = (bf16[2,2,64,128]{3,2,1,0:T(8,128)(2,1)}, bf16[2,2,64,128]{3,2,1,0:T(8,128)(2,1)}, u32[]{:S(2)}, u32[]{:S(2)}) collective-permute-start(bf16[2,2,64,128]{3,2,1,0:T(8,128)(2,1)} %param.7), channel_id=1, source_target_pairs={{16,0},{32,16},{48,32},{64,48},{80,64},{96,80},{112,96},{0,112},{1... | collective-permute-start | bytes 196616 | tf_op jit(solution)/shard_map/ppermute | solution.py:18
  6.9 2.9 %slice_reduce_fusion.35 = (bf16[4,4096]{1,0:T(4,128)(2,1)S(1)}, bf16[4,4096]{1,0:T(4,128)(2,1)S(1)}, bf16[4,4096]{1,0:T(4,128)(2,1)S(1)}, bf16[4,4096]{1,0:T(4,1...) fusion(bf16[25,4,4096]{2,0,1:T(8,128)(2,1)S(1)} %fusion.1), kind=kLoop, calls=%fused_computation.289 | loop fusion | bytes 1245184 | tf_op jit(solution)/shard_map/jit(dynamic_index_in_dim)/dynamic_slice | solution.py:69
  12.0 2.9 %slice_reduce_fusion.11 = (bf16[4,4096]{1,0:T(4,128)(2,1)S(1)}, bf16[4,4096]{1,0:T(4,128)(2,1)S(1)}, bf16[4,4096]{1,0:T(4,128)(2,1)S(1)}, bf16[4,4096]{1,0:T(4,1...) fusion(bf16[25,4,4096]{2,0,1:T(8,128)(2,1)S(1)} %fusion), kind=kLoop, calls=%fused_computation.253 | loop fusion | bytes 1245184 | tf_op jit(solution)/shard_map/jit(dynamic_index_in_dim)/dynamic_slice | solution.py:69
  24.1 5.6 %collective-permute-start.3 = (bf16[6,2,64,128]{3,2,1,0:T(8,128)(2,1)S(1)}, bf16[6,2,64,128]{3,2,1,0:T(8,128)(2,1)S(1)}, u32[]{:S(2)}, u32[]{:S(2)}) collective-permute-start(bf16[6,2,64,128]{3,2,1,0:T(8,128)(2,1)S(1)} %constant_dynamic-update-slice_fusion), channel_id=1, source_target_pairs={{1,0},{2,1},{3,2},{4,3},{5,4},{6,5},{7,6},{8,7},{9,8},{10,9},{11,1... | collective-permute-start | bytes 589832 | tf_op jit(solution)/shard_map/ppermute | solution.py:18
  37.3 3.6 %collective-permute-start.5 = (bf16[2,2,64,128]{3,2,1,0:T(8,128)(2,1)S(1)}, bf16[2,2,64,128]{3,2,1,0:T(8,128)(2,1)S(1)}, u32[]{:S(2)}, u32[]{:S(2)}) collective-permute-start(bf16[2,2,64,128]{3,2,1,0:T(8,128)(2,1)S(1)} %get-tuple-element.185), channel_id=1, source_target_pairs={{16,0},{32,16},{48,32},{64,48},{80,64},{96,80},{112,96},{0,112},{1... | collective-permute-start | bytes 196616 | tf_op jit(solution)/shard_map/ppermute | solution.py:18
  41.0 2.7 %collective-permute-done.4 = bf16[2,2,64,128]{3,2,1,0:T(8,128)(2,1)S(1)} collective-permute-done((bf16[2,2,64,128]{3,2,1,0:T(8,128)(2,1)S(1)}, bf16[2,2,64,128]{3,2,1,0:T(8,128)(2,1)S(1)}, u32[]{:S(2)}, u32[]{:S(2)}) %collective-permute-start.4) | collective-permute-done | bytes 65568 | tf_op jit(solution)/shard_map/ppermute | solution.py:16
  43.9 5.2 %collective-permute-start.7 = (bf16[6,2,64,128]{3,2,1,0:T(8,128)(2,1)S(1)}, bf16[6,2,64,128]{3,2,1,0:T(8,128)(2,1)S(1)}, u32[]{:S(2)}, u32[]{:S(2)}) collective-permute-start(bf16[6,2,64,128]{3,2,1,0:T(8,128)(2,1)S(1)} %pad_maximum_fusion), channel_id=1, source_target_pairs={{1,0},{2,1},{3,2},{4,3},{5,4},{6,5},{7,6},{8,7},{9,8},{10,9},{11,1... | collective-permute-start | bytes 589832 | tf_op jit(solution)/shard_map/ppermute | solution.py:18
  49.4 3.2 %collective-permute-done.6 = bf16[6,2,64,128]{3,2,1,0:T(8,128)(2,1)S(1)} collective-permute-done((bf16[6,2,64,128]{3,2,1,0:T(8,128)(2,1)S(1)}, bf16[6,2,64,128]{3,2,1,0:T(8,128)(2,1)S(1)}, u32[]{:S(2)}, u32[]{:S(2)}) %collective-permute-start.6) | collective-permute-done | bytes 196640 | tf_op jit(solution)/shard_map/ppermute | solution.py:16
  56.3 4.6 %collective-permute-start.9 = (bf16[2,2,64,128]{3,2,1,0:T(8,128)(2,1)S(1)}, bf16[2,2,64,128]{3,2,1,0:T(8,128)(2,1)S(1)}, u32[]{:S(2)}, u32[]{:S(2)}) collective-permute-start(bf16[2,2,64,128]{3,2,1,0:T(8,128)(2,1)S(1)} %bitcast.467), channel_id=1, source_target_pairs={{16,0},{32,16},{48,32},{64,48},{80,64},{96,80},{112,96},{0,112},{1... | collective-permute-start | bytes 196616 | tf_op jit(solution)/shard_map/ppermute | solution.py:18
  63.1 5.3 %collective-permute-start.11 = (bf16[6,2,64,128]{3,2,1,0:T(8,128)(2,1)S(1)}, bf16[6,2,64,128]{3,2,1,0:T(8,128)(2,1)S(1)}, u32[]{:S(2)}, u32[]{:S(2)}) collective-permute-start(bf16[6,2,64,128]{3,2,1,0:T(8,128)(2,1)S(1)} %pad_maximum_fusion.1), channel_id=1, source_target_pairs={{1,0},{2,1},{3,2},{4,3},{5,4},{6,5},{7,6},{8,7},{9,8},{10,9},{11,1... | collective-permute-start | bytes 589832 | tf_op jit(solution)/shard_map/ppermute | solution.py:18
  68.8 4.6 %collective-permute-done.10 = bf16[6,2,64,128]{3,2,1,0:T(8,128)(2,1)S(1)} collective-permute-done((bf16[6,2,64,128]{3,2,1,0:T(8,128)(2,1)S(1)}, bf16[6,2,64,128]{3,2,1,0:T(8,128)(2,1)S(1)}, u32[]{:S(2)}, u32[]{:S(2)}) %collective-permute-start.10) | collective-permute-done | bytes 196640 | tf_op jit(solution)/shard_map/ppermute | solution.py:16
  77.6 66.6 %all-reduce = (f32[]{:T(128)}, f32[]{:T(128)}) all-reduce(f32[]{:T(128)} %get-tuple-element.191, f32[]{:T(128)} %get-tuple-element.184), channel_id=1, replica_groups=mesh['row'=8,'col'=16] {'row','col'}, use_global_device_ids=true, to_apply=%region_1.2 | all-reduce | flops 2 | bytes 16 | tf_op jit(solution)/shard_map/psum | solution.py:93
  145.7 4.1 %collective-permute-start.13 = (bf16[2,2,64,128]{3,2,1,0:T(8,128)(2,1)S(1)}, bf16[2,2,64,128]{3,2,1,0:T(8,128)(2,1)S(1)}, u32[]{:S(2)}, u32[]{:S(2)}) collective-permute-start(bf16[2,2,64,128]{3,2,1,0:T(8,128)(2,1)S(1)} %divide_convert_fusion.1), channel_id=1, source_target_pairs={{16,0},{32,16},{48,32},{64,48},{80,64},{96,80},{112,96},{0,112},{1... | collective-permute-start | bytes 196616 | tf_op jit(solution)/shard_map/ppermute | solution.py:18
  150.0 2.1 %collective-permute-done.12 = bf16[2,2,64,128]{3,2,1,0:T(8,128)(2,1)S(1)} collective-permute-done((bf16[2,2,64,128]{3,2,1,0:T(8,128)(2,1)S(1)}, bf16[2,2,64,128]{3,2,1,0:T(8,128)(2,1)S(1)}, u32[]{:S(2)}, u32[]{:S(2)}) %collective-permute-start.12) | collective-permute-done | bytes 65568 | tf_op jit(solution)/shard_map/ppermute | solution.py:16
  152.2 5.3 %collective-permute-start.15 = (bf16[6,2,64,128]{3,2,1,0:T(8,128)(2,1)S(1)}, bf16[6,2,64,128]{3,2,1,0:T(8,128)(2,1)S(1)}, u32[]{:S(2)}, u32[]{:S(2)}) collective-permute-start(bf16[6,2,64,128]{3,2,1,0:T(8,128)(2,1)S(1)} %pad_maximum_fusion.2), channel_id=1, source_target_pairs={{1,0},{2,1},{3,2},{4,3},{5,4},{6,5},{7,6},{8,7},{9,8},{10,9},{11,1... | collective-permute-start | bytes 589832 | tf_op jit(solution)/shard_map/ppermute | solution.py:18
  157.8 4.5 %collective-permute-done.14 = bf16[6,2,64,128]{3,2,1,0:T(8,128)(2,1)S(1)} collective-permute-done((bf16[6,2,64,128]{3,2,1,0:T(8,128)(2,1)S(1)}, bf16[6,2,64,128]{3,2,1,0:T(8,128)(2,1)S(1)}, u32[]{:S(2)}, u32[]{:S(2)}) %collective-permute-start.14) | collective-permute-done | bytes 196640 | tf_op jit(solution)/shard_map/ppermute | solution.py:16
  166.0 4.4 %collective-permute-start.17 = (bf16[2,2,64,128]{3,2,1,0:T(8,128)(2,1)S(1)}, bf16[2,2,64,128]{3,2,1,0:T(8,128)(2,1)S(1)}, u32[]{:S(2)}, u32[]{:S(2)}) collective-permute-start(bf16[2,2,64,128]{3,2,1,0:T(8,128)(2,1)S(1)} %add_convert_fusion.1), channel_id=1, source_target_pairs={{16,0},{32,16},{48,32},{64,48},{80,64},{96,80},{112,96},{0,112},{1... | collective-permute-start | bytes 196616 | tf_op jit(solution)/shard_map/ppermute | solution.py:18
  170.6 2.1 %collective-permute-done.16 = bf16[2,2,64,128]{3,2,1,0:T(8,128)(2,1)S(1)} collective-permute-done((bf16[2,2,64,128]{3,2,1,0:T(8,128)(2,1)S(1)}, bf16[2,2,64,128]{3,2,1,0:T(8,128)(2,1)S(1)}, u32[]{:S(2)}, u32[]{:S(2)}) %collective-permute-start.16) | collective-permute-done | bytes 65568 | tf_op jit(solution)/shard_map/ppermute | solution.py:16
  172.8 5.3 %collective-permute-start.19 = (bf16[6,2,64,128]{3,2,1,0:T(8,128)(2,1)S(1)}, bf16[6,2,64,128]{3,2,1,0:T(8,128)(2,1)S(1)}, u32[]{:S(2)}, u32[]{:S(2)}) collective-permute-start(bf16[6,2,64,128]{3,2,1,0:T(8,128)(2,1)S(1)} %pad_maximum_fusion.3), channel_id=1, source_target_pairs={{1,0},{2,1},{3,2},{4,3},{5,4},{6,5},{7,6},{8,7},{9,8},{10,9},{11,1... | collective-permute-start | bytes 589832 | tf_op jit(solution)/shard_map/ppermute | solution.py:18
  178.4 3.3 %collective-permute-done.18 = bf16[6,2,64,128]{3,2,1,0:T(8,128)(2,1)S(1)} collective-permute-done((bf16[6,2,64,128]{3,2,1,0:T(8,128)(2,1)S(1)}, bf16[6,2,64,128]{3,2,1,0:T(8,128)(2,1)S(1)}, u32[]{:S(2)}, u32[]{:S(2)}) %collective-permute-start.18) | collective-permute-done | bytes 196640 | tf_op jit(solution)/shard_map/ppermute | solution.py:16
  185.5 4.1 %collective-permute-start.21 = (bf16[2,2,64,128]{3,2,1,0:T(8,128)(2,1)S(1)}, bf16[2,2,64,128]{3,2,1,0:T(8,128)(2,1)S(1)}, u32[]{:S(2)}, u32[]{:S(2)}) collective-permute-start(bf16[2,2,64,128]{3,2,1,0:T(8,128)(2,1)S(1)} %bitcast.476), channel_id=1, source_target_pairs={{16,0},{32,16},{48,32},{64,48},{80,64},{96,80},{112,96},{0,112},{1... | collective-permute-start | bytes 196616 | tf_op jit(solution)/shard_map/ppermute | solution.py:18
  189.7 2.2 %collective-permute-done.20 = bf16[2,2,64,128]{3,2,1,0:T(8,128)(2,1)S(1)} collective-permute-done((bf16[2,2,64,128]{3,2,1,0:T(8,128)(2,1)S(1)}, bf16[2,2,64,128]{3,2,1,0:T(8,128)(2,1)S(1)}, u32[]{:S(2)}, u32[]{:S(2)}) %collective-permute-start.20) | collective-permute-done | bytes 65568 | tf_op jit(solution)/shard_map/ppermute | solution.py:16
  192.0 5.3 %collective-permute-start.23 = (bf16[6,2,64,128]{3,2,1,0:T(8,128)(2,1)S(1)}, bf16[6,2,64,128]{3,2,1,0:T(8,128)(2,1)S(1)}, u32[]{:S(2)}, u32[]{:S(2)}) collective-permute-start(bf16[6,2,64,128]{3,2,1,0:T(8,128)(2,1)S(1)} %pad_maximum_fusion.4), channel_id=1, source_target_pairs={{1,0},{2,1},{3,2},{4,3},{5,4},{6,5},{7,6},{8,7},{9,8},{10,9},{11,1... | collective-permute-start | bytes 589832 | tf_op jit(solution)/shard_map/ppermute | solution.py:18
  197.7 4.8 %collective-permute-done.22 = bf16[6,2,64,128]{3,2,1,0:T(8,128)(2,1)S(1)} collective-permute-done((bf16[6,2,64,128]{3,2,1,0:T(8,128)(2,1)S(1)}, bf16[6,2,64,128]{3,2,1,0:T(8,128)(2,1)S(1)}, u32[]{:S(2)}, u32[]{:S(2)}) %collective-permute-start.22) | collective-permute-done | bytes 196640 | tf_op jit(solution)/shard_map/ppermute | solution.py:16
  (282 shorter events, 45.0 us)
Async XLA Ops:
  0.7 21.5 %collective-permute-start.1 = (bf16[2,2,64,128]{3,2,1,0:T(8,128)(2,1)}, bf16[2,2,64,128]{3,2,1,0:T(8,128)(2,1)}, u32[]{:S(2)}, u32[]{:S(2)}) collective-permute-start(bf16[2,2,64,128]{3,2,1,0:T(8,128)(2,1)} %param.7), channel_id=1, source_target_pairs={{16,0},{32,16},{48,32},{64,48},{80,64},{96,80},{112,96},{0,112},{1... | collective-permute-start | bytes 196616 | tf_op jit(solution)/shard_map/ppermute | solution.py:18
  4.6 17.6 %collective-permute-start = (bf16[2,2,64,128]{3,2,1,0:T(8,128)(2,1)}, bf16[2,2,64,128]{3,2,1,0:T(8,128)(2,1)}, u32[]{:S(2)}, u32[]{:S(2)}) collective-permute-start(bf16[2,2,64,128]{3,2,1,0:T(8,128)(2,1)} %param.7), channel_id=1, source_target_pairs={{0,16},{16,32},{32,48},{48,64},{64,80},{80,96},{96,112},{112,0},{1... | collective-permute-start | bytes 196616 | tf_op jit(solution)/shard_map/ppermute | solution.py:16
  24.0 8.9 %collective-permute-start.2 = (bf16[6,2,64,128]{3,2,1,0:T(8,128)(2,1)S(1)}, bf16[6,2,64,128]{3,2,1,0:T(8,128)(2,1)S(1)}, u32[]{:S(2)}, u32[]{:S(2)}) collective-permute-start(bf16[6,2,64,128]{3,2,1,0:T(8,128)(2,1)S(1)} %constant_dynamic-update-slice_fusion), channel_id=1, source_target_pairs={{0,1},{1,2},{2,3},{3,4},{4,5},{5,6},{6,7},{7,8},{8,9},{9,10},{10,1... | collective-permute-start | bytes 589832 | tf_op jit(solution)/shard_map/ppermute | solution.py:16
  24.1 9.1 %collective-permute-start.3 = (bf16[6,2,64,128]{3,2,1,0:T(8,128)(2,1)S(1)}, bf16[6,2,64,128]{3,2,1,0:T(8,128)(2,1)S(1)}, u32[]{:S(2)}, u32[]{:S(2)}) collective-permute-start(bf16[6,2,64,128]{3,2,1,0:T(8,128)(2,1)S(1)} %constant_dynamic-update-slice_fusion), channel_id=1, source_target_pairs={{1,0},{2,1},{3,2},{4,3},{5,4},{6,5},{7,6},{8,7},{9,8},{10,9},{11,1... | collective-permute-start | bytes 589832 | tf_op jit(solution)/shard_map/ppermute | solution.py:18
  36.7 7.0 %collective-permute-start.4 = (bf16[2,2,64,128]{3,2,1,0:T(8,128)(2,1)S(1)}, bf16[2,2,64,128]{3,2,1,0:T(8,128)(2,1)S(1)}, u32[]{:S(2)}, u32[]{:S(2)}) collective-permute-start(bf16[2,2,64,128]{3,2,1,0:T(8,128)(2,1)S(1)} %get-tuple-element.185), channel_id=1, source_target_pairs={{0,16},{16,32},{32,48},{48,64},{64,80},{80,96},{96,112},{112,0},{1... | collective-permute-start | bytes 196616 | tf_op jit(solution)/shard_map/ppermute | solution.py:16
  37.3 6.4 %collective-permute-start.5 = (bf16[2,2,64,128]{3,2,1,0:T(8,128)(2,1)S(1)}, bf16[2,2,64,128]{3,2,1,0:T(8,128)(2,1)S(1)}, u32[]{:S(2)}, u32[]{:S(2)}) collective-permute-start(bf16[2,2,64,128]{3,2,1,0:T(8,128)(2,1)S(1)} %get-tuple-element.185), channel_id=1, source_target_pairs={{16,0},{32,16},{48,32},{64,48},{80,64},{96,80},{112,96},{0,112},{1... | collective-permute-start | bytes 196616 | tf_op jit(solution)/shard_map/ppermute | solution.py:18
  43.7 8.9 %collective-permute-start.6 = (bf16[6,2,64,128]{3,2,1,0:T(8,128)(2,1)S(1)}, bf16[6,2,64,128]{3,2,1,0:T(8,128)(2,1)S(1)}, u32[]{:S(2)}, u32[]{:S(2)}) collective-permute-start(bf16[6,2,64,128]{3,2,1,0:T(8,128)(2,1)S(1)} %pad_maximum_fusion), channel_id=1, source_target_pairs={{0,1},{1,2},{2,3},{3,4},{4,5},{5,6},{6,7},{7,8},{8,9},{9,10},{10,1... | collective-permute-start | bytes 589832 | tf_op jit(solution)/shard_map/ppermute | solution.py:16
  43.9 9.2 %collective-permute-start.7 = (bf16[6,2,64,128]{3,2,1,0:T(8,128)(2,1)S(1)}, bf16[6,2,64,128]{3,2,1,0:T(8,128)(2,1)S(1)}, u32[]{:S(2)}, u32[]{:S(2)}) collective-permute-start(bf16[6,2,64,128]{3,2,1,0:T(8,128)(2,1)S(1)} %pad_maximum_fusion), channel_id=1, source_target_pairs={{1,0},{2,1},{3,2},{4,3},{5,4},{6,5},{7,6},{8,7},{9,8},{10,9},{11,1... | collective-permute-start | bytes 589832 | tf_op jit(solution)/shard_map/ppermute | solution.py:18
  56.2 6.8 %collective-permute-start.8 = (bf16[2,2,64,128]{3,2,1,0:T(8,128)(2,1)S(1)}, bf16[2,2,64,128]{3,2,1,0:T(8,128)(2,1)S(1)}, u32[]{:S(2)}, u32[]{:S(2)}) collective-permute-start(bf16[2,2,64,128]{3,2,1,0:T(8,128)(2,1)S(1)} %bitcast.466), channel_id=1, source_target_pairs={{0,16},{16,32},{32,48},{48,64},{64,80},{80,96},{96,112},{112,0},{1... | collective-permute-start | bytes 196616 | tf_op jit(solution)/shard_map/ppermute | solution.py:16
  56.3 6.7 %collective-permute-start.9 = (bf16[2,2,64,128]{3,2,1,0:T(8,128)(2,1)S(1)}, bf16[2,2,64,128]{3,2,1,0:T(8,128)(2,1)S(1)}, u32[]{:S(2)}, u32[]{:S(2)}) collective-permute-start(bf16[2,2,64,128]{3,2,1,0:T(8,128)(2,1)S(1)} %bitcast.467), channel_id=1, source_target_pairs={{16,0},{32,16},{48,32},{64,48},{80,64},{96,80},{112,96},{0,112},{1... | collective-permute-start | bytes 196616 | tf_op jit(solution)/shard_map/ppermute | solution.py:18
  63.1 10.3 %collective-permute-start.10 = (bf16[6,2,64,128]{3,2,1,0:T(8,128)(2,1)S(1)}, bf16[6,2,64,128]{3,2,1,0:T(8,128)(2,1)S(1)}, u32[]{:S(2)}, u32[]{:S(2)}) collective-permute-start(bf16[6,2,64,128]{3,2,1,0:T(8,128)(2,1)S(1)} %pad_maximum_fusion.1), channel_id=1, source_target_pairs={{0,1},{1,2},{2,3},{3,4},{4,5},{5,6},{6,7},{7,8},{8,9},{9,10},{10,1... | collective-permute-start | bytes 589832 | tf_op jit(solution)/shard_map/ppermute | solution.py:16
  63.1 10.7 %collective-permute-start.11 = (bf16[6,2,64,128]{3,2,1,0:T(8,128)(2,1)S(1)}, bf16[6,2,64,128]{3,2,1,0:T(8,128)(2,1)S(1)}, u32[]{:S(2)}, u32[]{:S(2)}) collective-permute-start(bf16[6,2,64,128]{3,2,1,0:T(8,128)(2,1)S(1)} %pad_maximum_fusion.1), channel_id=1, source_target_pairs={{1,0},{2,1},{3,2},{4,3},{5,4},{6,5},{7,6},{8,7},{9,8},{10,9},{11,1... | collective-permute-start | bytes 589832 | tf_op jit(solution)/shard_map/ppermute | solution.py:18
  145.6 6.4 %collective-permute-start.12 = (bf16[2,2,64,128]{3,2,1,0:T(8,128)(2,1)S(1)}, bf16[2,2,64,128]{3,2,1,0:T(8,128)(2,1)S(1)}, u32[]{:S(2)}, u32[]{:S(2)}) collective-permute-start(bf16[2,2,64,128]{3,2,1,0:T(8,128)(2,1)S(1)} %divide_convert_fusion.1), channel_id=1, source_target_pairs={{0,16},{16,32},{32,48},{48,64},{64,80},{80,96},{96,112},{112,0},{1... | collective-permute-start | bytes 196616 | tf_op jit(solution)/shard_map/ppermute | solution.py:16
  145.7 6.4 %collective-permute-start.13 = (bf16[2,2,64,128]{3,2,1,0:T(8,128)(2,1)S(1)}, bf16[2,2,64,128]{3,2,1,0:T(8,128)(2,1)S(1)}, u32[]{:S(2)}, u32[]{:S(2)}) collective-permute-start(bf16[2,2,64,128]{3,2,1,0:T(8,128)(2,1)S(1)} %divide_convert_fusion.1), channel_id=1, source_target_pairs={{16,0},{32,16},{48,32},{64,48},{80,64},{96,80},{112,96},{0,112},{1... | collective-permute-start | bytes 196616 | tf_op jit(solution)/shard_map/ppermute | solution.py:18
  152.1 10.2 %collective-permute-start.14 = (bf16[6,2,64,128]{3,2,1,0:T(8,128)(2,1)S(1)}, bf16[6,2,64,128]{3,2,1,0:T(8,128)(2,1)S(1)}, u32[]{:S(2)}, u32[]{:S(2)}) collective-permute-start(bf16[6,2,64,128]{3,2,1,0:T(8,128)(2,1)S(1)} %pad_maximum_fusion.2), channel_id=1, source_target_pairs={{0,1},{1,2},{2,3},{3,4},{4,5},{5,6},{6,7},{7,8},{8,9},{9,10},{10,1... | collective-permute-start | bytes 589832 | tf_op jit(solution)/shard_map/ppermute | solution.py:16
  152.2 10.6 %collective-permute-start.15 = (bf16[6,2,64,128]{3,2,1,0:T(8,128)(2,1)S(1)}, bf16[6,2,64,128]{3,2,1,0:T(8,128)(2,1)S(1)}, u32[]{:S(2)}, u32[]{:S(2)}) collective-permute-start(bf16[6,2,64,128]{3,2,1,0:T(8,128)(2,1)S(1)} %pad_maximum_fusion.2), channel_id=1, source_target_pairs={{1,0},{2,1},{3,2},{4,3},{5,4},{6,5},{7,6},{8,7},{9,8},{10,9},{11,1... | collective-permute-start | bytes 589832 | tf_op jit(solution)/shard_map/ppermute | solution.py:18
  166.0 6.7 %collective-permute-start.16 = (bf16[2,2,64,128]{3,2,1,0:T(8,128)(2,1)S(1)}, bf16[2,2,64,128]{3,2,1,0:T(8,128)(2,1)S(1)}, u32[]{:S(2)}, u32[]{:S(2)}) collective-permute-start(bf16[2,2,64,128]{3,2,1,0:T(8,128)(2,1)S(1)} %add_convert_fusion.1), channel_id=1, source_target_pairs={{0,16},{16,32},{32,48},{48,64},{64,80},{80,96},{96,112},{112,0},{1... | collective-permute-start | bytes 196616 | tf_op jit(solution)/shard_map/ppermute | solution.py:16
  166.0 6.6 %collective-permute-start.17 = (bf16[2,2,64,128]{3,2,1,0:T(8,128)(2,1)S(1)}, bf16[2,2,64,128]{3,2,1,0:T(8,128)(2,1)S(1)}, u32[]{:S(2)}, u32[]{:S(2)}) collective-permute-start(bf16[2,2,64,128]{3,2,1,0:T(8,128)(2,1)S(1)} %add_convert_fusion.1), channel_id=1, source_target_pairs={{16,0},{32,16},{48,32},{64,48},{80,64},{96,80},{112,96},{0,112},{1... | collective-permute-start | bytes 196616 | tf_op jit(solution)/shard_map/ppermute | solution.py:18
  172.7 9.1 %collective-permute-start.18 = (bf16[6,2,64,128]{3,2,1,0:T(8,128)(2,1)S(1)}, bf16[6,2,64,128]{3,2,1,0:T(8,128)(2,1)S(1)}, u32[]{:S(2)}, u32[]{:S(2)}) collective-permute-start(bf16[6,2,64,128]{3,2,1,0:T(8,128)(2,1)S(1)} %pad_maximum_fusion.3), channel_id=1, source_target_pairs={{0,1},{1,2},{2,3},{3,4},{4,5},{5,6},{6,7},{7,8},{8,9},{9,10},{10,1... | collective-permute-start | bytes 589832 | tf_op jit(solution)/shard_map/ppermute | solution.py:16
  172.8 9.5 %collective-permute-start.19 = (bf16[6,2,64,128]{3,2,1,0:T(8,128)(2,1)S(1)}, bf16[6,2,64,128]{3,2,1,0:T(8,128)(2,1)S(1)}, u32[]{:S(2)}, u32[]{:S(2)}) collective-permute-start(bf16[6,2,64,128]{3,2,1,0:T(8,128)(2,1)S(1)} %pad_maximum_fusion.3), channel_id=1, source_target_pairs={{1,0},{2,1},{3,2},{4,3},{5,4},{6,5},{7,6},{8,7},{9,8},{10,9},{11,1... | collective-permute-start | bytes 589832 | tf_op jit(solution)/shard_map/ppermute | solution.py:18
  185.4 6.5 %collective-permute-start.20 = (bf16[2,2,64,128]{3,2,1,0:T(8,128)(2,1)S(1)}, bf16[2,2,64,128]{3,2,1,0:T(8,128)(2,1)S(1)}, u32[]{:S(2)}, u32[]{:S(2)}) collective-permute-start(bf16[2,2,64,128]{3,2,1,0:T(8,128)(2,1)S(1)} %bitcast.475), channel_id=1, source_target_pairs={{0,16},{16,32},{32,48},{48,64},{64,80},{80,96},{96,112},{112,0},{1... | collective-permute-start | bytes 196616 | tf_op jit(solution)/shard_map/ppermute | solution.py:16
  185.5 6.5 %collective-permute-start.21 = (bf16[2,2,64,128]{3,2,1,0:T(8,128)(2,1)S(1)}, bf16[2,2,64,128]{3,2,1,0:T(8,128)(2,1)S(1)}, u32[]{:S(2)}, u32[]{:S(2)}) collective-permute-start(bf16[2,2,64,128]{3,2,1,0:T(8,128)(2,1)S(1)} %bitcast.476), channel_id=1, source_target_pairs={{16,0},{32,16},{48,32},{64,48},{80,64},{96,80},{112,96},{0,112},{1... | collective-permute-start | bytes 196616 | tf_op jit(solution)/shard_map/ppermute | solution.py:18
  192.0 10.5 %collective-permute-start.22 = (bf16[6,2,64,128]{3,2,1,0:T(8,128)(2,1)S(1)}, bf16[6,2,64,128]{3,2,1,0:T(8,128)(2,1)S(1)}, u32[]{:S(2)}, u32[]{:S(2)}) collective-permute-start(bf16[6,2,64,128]{3,2,1,0:T(8,128)(2,1)S(1)} %pad_maximum_fusion.4), channel_id=1, source_target_pairs={{0,1},{1,2},{2,3},{3,4},{4,5},{5,6},{6,7},{7,8},{8,9},{9,10},{10,1... | collective-permute-start | bytes 589832 | tf_op jit(solution)/shard_map/ppermute | solution.py:16
  192.0 10.9 %collective-permute-start.23 = (bf16[6,2,64,128]{3,2,1,0:T(8,128)(2,1)S(1)}, bf16[6,2,64,128]{3,2,1,0:T(8,128)(2,1)S(1)}, u32[]{:S(2)}, u32[]{:S(2)}) collective-permute-start(bf16[6,2,64,128]{3,2,1,0:T(8,128)(2,1)S(1)} %pad_maximum_fusion.4), channel_id=1, source_target_pairs={{1,0},{2,1},{3,2},{4,3},{5,4},{6,5},{7,6},{8,7},{9,8},{10,9},{11,1... | collective-permute-start | bytes 589832 | tf_op jit(solution)/shard_map/ppermute | solution.py:18
  (7 other events, 44.9 us)
where the time goes:
time: 207 us
  blocking collectives  66.6 us (32%)
  starting transfers between devices  58.3 us (28%)
  waiting for transfers between devices  32.6 us (16%)
  matrix products  26.5 us (13%)
  local copies, waits for them, and re-layouts  16.9 us (8%)
  between operations  2.95 us (1%)
  other arithmetic  2.77 us (1%)
    psum x1, blocking collectives, body(): lax.psum((jnp.sum(power_image * power_image), jnp.sum(slab_float * slab_f...  66.6 us
    ppermute x12, starting transfers between devices, extended(): lax.ppermute(head, axis, [((i + 1) % count, i) for i in range(count)])  56.9 us
    ppermute x12, waiting for transfers between devices, extended(): lax.ppermute(tail, axis, [(i, (i + 1) % count) for i in range(count)])  32.5 us
    dot_general x150, matrix products, apply_sparse(): jnp.einsum('cij,cjs->cis', mats_now, window.reshape(cell_count, block_siz...  25.7 us
    dynamic_slice x4, local copies, waits for them, and re-layouts, apply_sparse(): mats_now = lax.dynamic_index_in_dim(mats, offset_index, 0, keepdims=False)  7.57 us
    squeeze x50, local copies, waits for them, and re-layouts, apply_sparse(): mats_now = lax.dynamic_index_in_dim(mats, offset_index, 0, keepdims=False)  6.17 us
  transfers between devices with their start and end apart: 24, of which 11 were waited for; matrix products, arithmetic and copies ran while one was open for 12% of the time, Pallas kernels for 0%

commit v1 on v0

v1 whole, which is shorter than its diff:
```python
import functools

import jax
import jax.numpy as jnp
from jax import lax
from jax.experimental import pallas as pl
from jax.experimental.pallas import tpu as pltpu
from jax.sharding import PartitionSpec as P

REACH = 2
SIDE = 2
BLOCK = 64
SLAB = 128
ENTRIES = 25
LAT_Y = 16
LAT_X = 32
CELLS = SIDE * SIDE
HALF = BLOCK // 2
WIDE = SIDE + 2 * REACH
THIRD = WIDE * SIDE * BLOCK
DEPTH = 3 * THIRD
ROWS = CELLS * BLOCK


def vmem():
    return pl.BlockSpec(memory_space=pltpu.VMEM)


def smem():
    return pl.BlockSpec(memory_space=pltpu.SMEM)


def build_kernel(origin_ref, cols_ref, count_ref, blocks_ref, out_ref, wide_ref):
    out_ref[...] = jnp.zeros_like(out_ref)
    wide_ref[...] = blocks_ref[...].astype(jnp.float32)
    lane_half = lax.broadcasted_iota(jnp.int32, (HALF, 2 * BLOCK), 1) // BLOCK
    for cell_y in range(SIDE):
        for cell_x in range(SIDE):
            cell = cell_y * SIDE + cell_x

            def place(entry, carry, cell_y=cell_y, cell_x=cell_x, cell=cell):
                col_id = cols_ref[cell_y, cell_x, entry]
                step_y = lax.rem(lax.div(col_id, LAT_X) - origin_ref[0] - cell_y + REACH + LAT_Y, LAT_Y)
                step_x = lax.rem(lax.rem(col_id, LAT_X) - origin_ref[1] - cell_x + REACH + LAT_X, LAT_X)
                win_y = step_y + cell_y
                win_x = step_x + cell_x
                tile = lax.div(win_x, 2) * WIDE + win_y
                side = lax.rem(win_x, 2)
                base = pl.multiple_of((cell_y * ENTRIES + entry) * BLOCK, BLOCK)
                pair = wide_ref[pl.ds(base + cell_x, HALF, stride=2), :]
                turned = pltpu.roll(pair, BLOCK, 1)
                here = lane_half == side
                lanes = pl.ds(pl.multiple_of(tile * 2 * BLOCK, 2 * BLOCK), 2 * BLOCK)
                for parity in range(2):
                    first = parity * CELLS * HALF + cell * HALF
                    rows = pl.ds(first, HALF)
                    new = jnp.where(side == parity, pair, turned)
                    old = out_ref[rows, lanes].astype(jnp.float32)
                    out_ref[rows, lanes] = jnp.where(here, new, old).astype(jnp.bfloat16)
                return carry

            lax.fori_loop(0, count_ref[cell_y, cell_x], place, 0)


def build(origin, blocks, cols, count):
    rows = blocks.reshape(SIDE, SIDE, ENTRIES, HALF, 2 * BLOCK).transpose(0, 2, 3, 1, 4)
    rows = rows.reshape(SIDE * ENTRIES * HALF * SIDE, 2 * BLOCK)
    return pl.pallas_call(
        build_kernel,
        out_shape=jax.ShapeDtypeStruct((ROWS, DEPTH), jnp.bfloat16),
        in_specs=[smem(), smem(), smem(), vmem()],
        out_specs=vmem(),
        scratch_shapes=[pltpu.VMEM(rows.shape, jnp.float32)],
        compiler_params=pltpu.CompilerParams(vmem_limit_bytes=24 * 2**20),
        cost_estimate=pl.CostEstimate(flops=10_000_000, bytes_accessed=4_000_000, transcendentals=0),
    )(origin, cols, count, rows)


def product(mat_ref, left_ref, mid_ref, right_ref, turn_ref):
    total = jnp.dot(mat_ref[:, :THIRD], left_ref[...], preferred_element_type=jnp.float32)
    total += jnp.dot(mat_ref[:, THIRD : 2 * THIRD], mid_ref[...], preferred_element_type=jnp.float32)
    total += jnp.dot(mat_ref[:, 2 * THIRD :], right_ref[...], preferred_element_type=jnp.float32)
    for cell in range(CELLS):
        for parity in range(2):
            first = parity * CELLS * HALF + cell * HALF
            turn_ref[pl.ds(cell * BLOCK + parity, HALF, stride=2), :] = total[first : first + HALF]
    return turn_ref[...]


def root_kernel(mat_ref, left_ref, mid_ref, right_ref, own_ref, out_ref, turn_ref):
    image = product(mat_ref, left_ref, mid_ref, right_ref, turn_ref)
    out_ref[...] = (own_ref[...].astype(jnp.float32) + image).astype(jnp.bfloat16)


def hamilton_kernel(mat_ref, left_ref, mid_ref, right_ref, out_ref, turn_ref):
    out_ref[...] = product(mat_ref, left_ref, mid_ref, right_ref, turn_ref).astype(jnp.bfloat16)


def power_kernel(mat_ref, left_ref, mid_ref, right_ref, own_ref, slab_ref, out_ref, power_ref, sums_ref, turn_ref):
    power = own_ref[...].astype(jnp.float32) + product(mat_ref, left_ref, mid_ref, right_ref, turn_ref)
    slab = slab_ref[...].astype(jnp.float32)
    power_ref[...] = power
    out_ref[...] = power.astype(jnp.bfloat16)
    image_square = jnp.sum(power * power)
    slab_square = jnp.sum(slab * slab)
    row = lax.broadcasted_iota(jnp.int32, sums_ref.shape, 0)
    sums_ref[...] = jnp.where(row == 0, image_square, slab_square)


def last_kernel(mat_ref, left_ref, mid_ref, right_ref, own_ref, slab_ref, power_ref, sums_ref, one_ref, two_ref, turn_ref):
    sums = sums_ref[...]
    ratio = jnp.sqrt(sums[0:1] / (sums[1:2] + 1e-06))
    image = own_ref[...].astype(jnp.float32) + product(mat_ref, left_ref, mid_ref, right_ref, turn_ref)
    one_ref[...] = (power_ref[...] / ratio).astype(jnp.bfloat16)
    two_ref[...] = (2.0 * (image / ratio) / ratio - slab_ref[...].astype(jnp.float32)).astype(jnp.bfloat16)


def apply(kernel, outs, *operands):
    return pl.pallas_call(
        kernel,
        out_shape=outs,
        in_specs=[vmem()] * len(operands),
        out_specs=jax.tree.map(lambda _: vmem(), outs),
        scratch_shapes=[pltpu.VMEM((ROWS, SLAB), jnp.float32)],
        compiler_params=pltpu.CompilerParams(vmem_limit_bytes=16 * 2**20),
        cost_estimate=pl.CostEstimate(flops=2 * ROWS * DEPTH * SLAB, bytes_accessed=2_000_000, transcendentals=0),
    )(*operands)


def around(value, axis):
    count = lax.axis_size(axis)
    before = lax.ppermute(value, axis, [(i, (i + 1) % count) for i in range(count)])
    after = lax.ppermute(value, axis, [((i + 1) % count, i) for i in range(count)])
    return before, after


def surround(field):
    above, below = around(field, "row")
    mid = jnp.concatenate([above, field, below], axis=0)
    left, right = around(mid, "col")
    return left, mid, right


def total_of(sums):
    for axis in ("row", "col"):
        count = lax.axis_size(axis)
        bit = 1
        while bit < count:
            sums = sums + lax.ppermute(sums, axis, [(i, i ^ bit) for i in range(count)])
            bit *= 2
    return sums


def body(x_slab, h_blocks, h_cols, h_count, z_blocks, z_cols, z_count):
    origin = jnp.stack([lax.axis_index("row") * SIDE, lax.axis_index("col") * SIDE]).astype(jnp.int32)
    z_mat = build(origin, z_blocks, z_cols, z_count)
    h_mat = build(origin, h_blocks, h_cols, h_count)
    flat = jax.ShapeDtypeStruct((ROWS, SLAB), jnp.bfloat16)
    wide = jax.ShapeDtypeStruct((ROWS, SLAB), jnp.float32)
    sums_shape = jax.ShapeDtypeStruct((8, SLAB), jnp.float32)
    slab = x_slab.reshape(ROWS, SLAB)

    u_one = apply(root_kernel, flat, z_mat, *surround(slab), slab)
    u_two = apply(hamilton_kernel, flat, h_mat, *surround(u_one))
    power, power_full, sums = apply(power_kernel, (flat, wide, sums_shape), z_mat, *surround(u_two), u_two, slab)
    v_one = apply(root_kernel, flat, z_mat, *surround(power), power)
    v_two = apply(hamilton_kernel, flat, h_mat, *surround(v_one))
    sums = total_of(sums)
    one, two = apply(last_kernel, (flat, flat), z_mat, *surround(v_two), v_two, slab, power_full, sums)
    return one.reshape(x_slab.shape), two.reshape(x_slab.shape)


def solution(mesh):
    in_specs = (
        P("row", "col", None, None),
        P("row", "col", None, None),
        P("row", "col", None),
        P("row", "col"),
        P("row", "col", None, None),
        P("row", "col", None),
        P("row", "col"),
    )
    out_specs = (P("row", "col", None, None), P("row", "col", None, None))
    return jax.shard_map(body, mesh=mesh, in_specs=in_specs, out_specs=out_specs, check_vma=False)
```

time: 207 us -> 138 us (0.67)
  blocking collectives: 66.6 us -> 0 us
  waiting for transfers between devices: 32.6 us -> 90.8 us
  starting transfers between devices: 58.3 us -> 30.3 us
  matrix products: 26.5 us -> 0 us
  local copies, waits for them, and re-layouts: 16.9 us -> 2.56 us
  Pallas kernels: 0 us -> 11.5 us
  between operations: 2.95 us -> 0.81 us
    psum x1 -> x0, blocking collectives: 66.6 us -> none  [body(): lax.psum((jnp.sum(power_image * power_image), jnp.sum(slab_float * slab_f...]
    ppermute x24 -> x31, waiting for transfers between devices: 32.6 us -> 90.8 us  [the longest x12 38.3 us: around(): lax.ppermute(value, axis, [(i, (i + 1) % count) for i in range(count)])]
    ppermute x24 -> x31, starting transfers between devices: 58.3 us -> 30.3 us  [the longest x12 23.2 us: around(): lax.ppermute(value, axis, [((i + 1) % count, i) for i in range(count)])]
    dot_general x152 -> x0, matrix products: 26.5 us -> none  [the longest x150 25.7 us: apply_sparse(): jnp.einsum('cij,cjs->cis', mats_now, window.reshape(cell_count, block_siz...]
    pallas_call x0 -> x8, Pallas kernels: none -> 11.5 us  [the longest x2 7.9 us: build(): pl.pallas_call(build_kernel, out_shape=jax.ShapeDtypeStruct((ROWS, DEPTH)...]
    dynamic_slice x4 -> x0, local copies, waits for them, and re-layouts: 7.57 us -> none  [apply_sparse(): mats_now = lax.dynamic_index_in_dim(mats, offset_index, 0, keepdims=False)]
    squeeze x50 -> x0, local copies, waits for them, and re-layouts: 6.17 us -> none  [apply_sparse(): mats_now = lax.dynamic_index_in_dim(mats, offset_index, 0, keepdims=False)]
    unnamed x15 -> x16, local copies, waits for them, and re-layouts: 0.12 us -> 2.54 us
  transfers between devices with their start and end apart: 24 -> 31, of which waited for: 11 -> 26; matrix products, arithmetic and copies ran while one was open for 12% -> 0% of each run, Pallas kernels for 0% -> 6%
where the time goes in v1:
time: 138 us; the launch traced here: 137 us
  waiting for transfers between devices  90.8 us (66%)
  starting transfers between devices  30.3 us (22%)
  Pallas kernels  11.5 us (8%)
  local copies, waits for them, and re-layouts  2.56 us (2%)
    ppermute x12, waiting for transfers between devices, around(): lax.ppermute(value, axis, [(i, (i + 1) % count) for i in range(count)])  38.3 us
    ppermute x7, waiting for transfers between devices, total_of(): sums = sums + lax.ppermute(sums, axis, [(i, i ^ bit) for i in range(count)])  27.9 us
    ppermute x12, waiting for transfers between devices, around(): lax.ppermute(value, axis, [((i + 1) % count, i) for i in range(count)])  24.7 us
    ppermute x12, starting transfers between devices, around(): lax.ppermute(value, axis, [((i + 1) % count, i) for i in range(count)])  23.2 us
    pallas_call x2, Pallas kernels, build(): pl.pallas_call(build_kernel, out_shape=jax.ShapeDtypeStruct((ROWS, DEPTH)...  7.9 us
    ppermute x12, starting transfers between devices, around(): lax.ppermute(value, axis, [(i, (i + 1) % count) for i in range(count)])  6.55 us
    pallas_call x6, Pallas kernels, apply(): pl.pallas_call(kernel, out_shape=outs, in_specs=[vmem()] * len(operands),...  3.64 us
  transfers between devices with their start and end apart: 31, of which 26 were waited for; matrix products, arithmetic and copies ran while one was open for 0% of the time, Pallas kernels for 6%

profile of v1, /device:TPU:0, one launch (start us, length us, event | category | flops | bytes accessed | tf_op | source)
XLA Modules:
  0.0 137.0 jit_solution(1215877042427214239)
XLA Ops:
  0.6 3.9 %collective-permute-start.1 = (bf16[256,128]{1,0:T(8,128)(2,1)}, bf16[256,128]{1,0:T(8,128)(2,1)S(1)}, u32[]{:S(2)}, u32[]{:S(2)}) collective-permute-start(bf16[256,128]{1,0:T(8,128)(2,1)} %bitcast.15), channel_id=1, source_target_pairs={{16,0},{32,16},{48,32},{64,48},{80,64},{96,80},{112,96},{0,112},{1... | collective-permute-start | bytes 196616 | tf_op jit(solution)/shard_map/ppermute | solution.py:133
  6.8 4.4 %collective-permute-done = bf16[256,128]{1,0:T(8,128)(2,1)S(1)} collective-permute-done((bf16[256,128]{1,0:T(8,128)(2,1)}, bf16[256,128]{1,0:T(8,128)(2,1)S(1)}, u32[]{:S(2)}, u32[]{:S(2)}) %collective-permute-start) | collective-permute-done | bytes 65568 | tf_op jit(solution)/shard_map/ppermute | solution.py:132
  12.0 4.5 %collective-permute-start.3 = (bf16[768,128]{1,0:T(8,128)(2,1)S(1)}, bf16[768,128]{1,0:T(8,128)(2,1)S(1)}, u32[]{:S(2)}, u32[]{:S(2)}) collective-permute-start(bf16[768,128]{1,0:T(8,128)(2,1)S(1)} %pad_maximum_fusion.mid_ref), channel_id=1, source_target_pairs={{1,0},{2,1},{3,2},{4,3},{5,4},{6,5},{7,6},{8,7},{9,8},{10,9},{11,1... | collective-permute-start | bytes 589832 | tf_op jit(solution)/shard_map/ppermute | solution.py:133
  19.0 2.8 %shard_map.86.mat_ref = bf16[256,2304]{1,0:T(8,128)(2,1)S(1)} custom-call(s32[2]{0:T(128)S(1)} %pad_add_fusion.origin_ref, s32[2,2,25]{2,1,0:T(2,128)S(1)} %copy-done.3, s32[2,2]{1,0:T(2,128)S(1)} %copy-done.5, bf16[3200,128]{1,0:T(8,128)(2,1)S(1)} %bitcast.21), custom_call_target="tpu_custom_call" | custom-call | flops 10000000 | bytes 4000000 | tf_op jit(solution)/shard_map/pallas_call | solution.py:68
  21.9 3.3 %collective-permute-done.2.left_ref = bf16[768,128]{1,0:T(8,128)(2,1)S(1)} collective-permute-done((bf16[768,128]{1,0:T(8,128)(2,1)S(1)}, bf16[768,128]{1,0:T(8,128)(2,1)S(1)}, u32[]{:S(2)}, u32[]{:S(2)}) %collective-permute-start.2) | collective-permute-done | bytes 196640 | tf_op jit(solution)/shard_map/ppermute | solution.py:132
  32.2 3.9 %collective-permute-start.7 = (bf16[768,128]{1,0:T(8,128)(2,1)S(1)}, bf16[768,128]{1,0:T(8,128)(2,1)S(1)}, u32[]{:S(2)}, u32[]{:S(2)}) collective-permute-start(bf16[768,128]{1,0:T(8,128)(2,1)S(1)} %pad_maximum_fusion.1.mid_ref), channel_id=1, source_target_pairs={{1,0},{2,1},{3,2},{4,3},{5,4},{6,5},{7,6},{8,7},{9,8},{10,9},{11,1... | collective-permute-start | bytes 589832 | tf_op jit(solution)/shard_map/ppermute | solution.py:133
  36.1 5.1 %shard_map.87.mat_ref = bf16[256,2304]{1,0:T(8,128)(2,1)S(1)} custom-call(s32[2]{0:T(128)S(1)} %pad_add_fusion.origin_ref, s32[2,2,25]{2,1,0:T(2,128)S(1)} %copy-done.4, s32[2,2]{1,0:T(2,128)S(1)} %copy-done.6, bf16[3200,128]{1,0:T(8,128)(2,1)S(1)} %bitcast.22), custom_call_target="tpu_custom_call" | custom-call | flops 10000000 | bytes 4000000 | tf_op jit(solution)/shard_map/pallas_call | solution.py:68
  41.2 4.3 %collective-permute-done.6.left_ref = bf16[768,128]{1,0:T(8,128)(2,1)S(1)} collective-permute-done((bf16[768,128]{1,0:T(8,128)(2,1)S(1)}, bf16[768,128]{1,0:T(8,128)(2,1)S(1)}, u32[]{:S(2)}, u32[]{:S(2)}) %collective-permute-start.6) | collective-permute-done | bytes 196640 | tf_op jit(solution)/shard_map/ppermute | solution.py:132
  53.1 4.6 %collective-permute-done.11.right_ref = bf16[768,128]{1,0:T(8,128)(2,1)S(1)} collective-permute-done((bf16[768,128]{1,0:T(8,128)(2,1)S(1)}, bf16[768,128]{1,0:T(8,128)(2,1)S(1)}, u32[]{:S(2)}, u32[]{:S(2)}) %collective-permute-start.11) | collective-permute-done | bytes 196640 | tf_op jit(solution)/shard_map/ppermute | solution.py:133
  57.7 4.0 %collective-permute-done.10.left_ref = bf16[768,128]{1,0:T(8,128)(2,1)S(1)} collective-permute-done((bf16[768,128]{1,0:T(8,128)(2,1)S(1)}, bf16[768,128]{1,0:T(8,128)(2,1)S(1)}, u32[]{:S(2)}, u32[]{:S(2)}) %collective-permute-start.10) | collective-permute-done | bytes 196640 | tf_op jit(solution)/shard_map/ppermute | solution.py:132
  62.4 4.1 %collective-permute-start.13 = (bf16[256,128]{1,0:T(8,128)(2,1)S(1)}, bf16[256,128]{1,0:T(8,128)(2,1)S(1)}, u32[]{:S(2)}, u32[]{:S(2)}) collective-permute-start(bf16[256,128]{1,0:T(8,128)(2,1)S(1)} %get-tuple-element.7.own_ref), channel_id=1, source_target_pairs={{16,0},{32,16},{48,32},{64,48},{80,64},{96,80},{112,96},{0,112},{1... | collective-permute-start | bytes 196616 | tf_op jit(solution)/shard_map/ppermute | solution.py:133
  69.4 4.6 %collective-permute-done.15.right_ref = bf16[768,128]{1,0:T(8,128)(2,1)S(1)} collective-permute-done((bf16[768,128]{1,0:T(8,128)(2,1)S(1)}, bf16[768,128]{1,0:T(8,128)(2,1)S(1)}, u32[]{:S(2)}, u32[]{:S(2)}) %collective-permute-start.15) | collective-permute-done | bytes 196640 | tf_op jit(solution)/shard_map/ppermute | solution.py:133
  74.0 4.0 %collective-permute-done.14.left_ref = bf16[768,128]{1,0:T(8,128)(2,1)S(1)} collective-permute-done((bf16[768,128]{1,0:T(8,128)(2,1)S(1)}, bf16[768,128]{1,0:T(8,128)(2,1)S(1)}, u32[]{:S(2)}, u32[]{:S(2)}) %collective-permute-start.14) | collective-permute-done | bytes 196640 | tf_op jit(solution)/shard_map/ppermute | solution.py:132
  78.5 4.7 %collective-permute-start.17 = (bf16[256,128]{1,0:T(8,128)(2,1)S(1)}, bf16[256,128]{1,0:T(8,128)(2,1)S(1)}, u32[]{:S(2)}, u32[]{:S(2)}) collective-permute-start(bf16[256,128]{1,0:T(8,128)(2,1)S(1)} %shard_map.91), channel_id=1, source_target_pairs={{16,0},{32,16},{48,32},{64,48},{80,64},{96,80},{112,96},{0,112},{1... | collective-permute-start | bytes 196616 | tf_op jit(solution)/shard_map/ppermute | solution.py:133
  85.1 4.5 %collective-permute-done.16 = bf16[256,128]{1,0:T(8,128)(2,1)S(1)} collective-permute-done((bf16[256,128]{1,0:T(8,128)(2,1)S(1)}, bf16[256,128]{1,0:T(8,128)(2,1)S(1)}, u32[]{:S(2)}, u32[]{:S(2)}) %collective-permute-start.16) | collective-permute-done | bytes 65568 | tf_op jit(solution)/shard_map/ppermute | solution.py:132
  90.2 4.6 %collective-permute-done.19.right_ref = bf16[768,128]{1,0:T(8,128)(2,1)S(1)} collective-permute-done((bf16[768,128]{1,0:T(8,128)(2,1)S(1)}, bf16[768,128]{1,0:T(8,128)(2,1)S(1)}, u32[]{:S(2)}, u32[]{:S(2)}) %collective-permute-start.19) | collective-permute-done | bytes 196640 | tf_op jit(solution)/shard_map/ppermute | solution.py:133
  94.8 4.6 %collective-permute-done.18.left_ref = bf16[768,128]{1,0:T(8,128)(2,1)S(1)} collective-permute-done((bf16[768,128]{1,0:T(8,128)(2,1)S(1)}, bf16[768,128]{1,0:T(8,128)(2,1)S(1)}, u32[]{:S(2)}, u32[]{:S(2)}) %collective-permute-start.18) | collective-permute-done | bytes 196640 | tf_op jit(solution)/shard_map/ppermute | solution.py:132
  104.2 2.6 %collective-permute-done.20 = bf16[256,128]{1,0:T(8,128)(2,1)S(1)} collective-permute-done((bf16[256,128]{1,0:T(8,128)(2,1)S(1)}, bf16[256,128]{1,0:T(8,128)(2,1)S(1)}, u32[]{:S(2)}, u32[]{:S(2)}) %collective-permute-start.20) | collective-permute-done | bytes 65568 | tf_op jit(solution)/shard_map/ppermute | solution.py:132
  107.4 4.7 %collective-permute-done.24 = f32[8,128]{1,0:T(8,128)S(1)} collective-permute-done((f32[8,128]{1,0:T(8,128)S(1)}, f32[8,128]{1,0:T(8,128)S(1)}, u32[]{:S(2)}, u32[]{:S(2)}) %collective-permute-start.24) | collective-permute-done | bytes 4128 | tf_op jit(solution)/shard_map/ppermute | solution.py:149
  112.1 3.6 %collective-permute-done.25 = f32[8,128]{1,0:T(8,128)S(1)} collective-permute-done((f32[8,128]{1,0:T(8,128)S(1)}, f32[8,128]{1,0:T(8,128)S(1)}, u32[]{:S(2)}, u32[]{:S(2)}) %collective-permute-start.25) | collective-permute-done | bytes 4128 | tf_op jit(solution)/shard_map/ppermute | solution.py:149
  116.3 4.6 %collective-permute-done.26 = f32[8,128]{1,0:T(8,128)S(1)} collective-permute-done((f32[8,128]{1,0:T(8,128)S(1)}, f32[8,128]{1,0:T(8,128)S(1)}, u32[]{:S(2)}, u32[]{:S(2)}) %collective-permute-start.26) | collective-permute-done | bytes 4128 | tf_op jit(solution)/shard_map/ppermute | solution.py:149
  122.0 5.1 %collective-permute-done.28 = f32[8,128]{1,0:T(8,128)S(1)} collective-permute-done((f32[8,128]{1,0:T(8,128)S(1)}, f32[8,128]{1,0:T(8,128)S(1)}, u32[]{:S(2)}, u32[]{:S(2)}) %collective-permute-start.28) | collective-permute-done | bytes 4128 | tf_op jit(solution)/shard_map/ppermute | solution.py:149
  127.2 3.6 %collective-permute-done.29 = f32[8,128]{1,0:T(8,128)S(1)} collective-permute-done((f32[8,128]{1,0:T(8,128)S(1)}, f32[8,128]{1,0:T(8,128)S(1)}, u32[]{:S(2)}, u32[]{:S(2)}) %collective-permute-start.29) | collective-permute-done | bytes 4128 | tf_op jit(solution)/shard_map/ppermute | solution.py:149
  130.8 5.1 %collective-permute-done.30 = f32[8,128]{1,0:T(8,128)S(1)} collective-permute-done((f32[8,128]{1,0:T(8,128)S(1)}, f32[8,128]{1,0:T(8,128)S(1)}, u32[]{:S(2)}, u32[]{:S(2)}) %collective-permute-start.30) | collective-permute-done | bytes 4128 | tf_op jit(solution)/shard_map/ppermute | solution.py:149
  (76 shorter events, 35.0 us)
Async XLA Ops:
  0.6 6.1 %collective-permute-start.1 = (bf16[256,128]{1,0:T(8,128)(2,1)}, bf16[256,128]{1,0:T(8,128)(2,1)S(1)}, u32[]{:S(2)}, u32[]{:S(2)}) collective-permute-start(bf16[256,128]{1,0:T(8,128)(2,1)} %bitcast.15), channel_id=1, source_target_pairs={{16,0},{32,16},{48,32},{64,48},{80,64},{96,80},{112,96},{0,112},{1... | collective-permute-start | bytes 196616 | tf_op jit(solution)/shard_map/ppermute | solution.py:133
  4.6 6.6 %collective-permute-start = (bf16[256,128]{1,0:T(8,128)(2,1)}, bf16[256,128]{1,0:T(8,128)(2,1)S(1)}, u32[]{:S(2)}, u32[]{:S(2)}) collective-permute-start(bf16[256,128]{1,0:T(8,128)(2,1)} %bitcast.16), channel_id=1, source_target_pairs={{0,16},{16,32},{32,48},{48,64},{64,80},{80,96},{96,112},{112,0},{1... | collective-permute-start | bytes 196616 | tf_op jit(solution)/shard_map/ppermute | solution.py:132
  12.0 9.9 %collective-permute-start.3 = (bf16[768,128]{1,0:T(8,128)(2,1)S(1)}, bf16[768,128]{1,0:T(8,128)(2,1)S(1)}, u32[]{:S(2)}, u32[]{:S(2)}) collective-permute-start(bf16[768,128]{1,0:T(8,128)(2,1)S(1)} %pad_maximum_fusion.mid_ref), channel_id=1, source_target_pairs={{1,0},{2,1},{3,2},{4,3},{5,4},{6,5},{7,6},{8,7},{9,8},{10,9},{11,1... | collective-permute-start | bytes 589832 | tf_op jit(solution)/shard_map/ppermute | solution.py:133
  16.5 8.7 %collective-permute-start.2 = (bf16[768,128]{1,0:T(8,128)(2,1)S(1)}, bf16[768,128]{1,0:T(8,128)(2,1)S(1)}, u32[]{:S(2)}, u32[]{:S(2)}) collective-permute-start(bf16[768,128]{1,0:T(8,128)(2,1)S(1)} %pad_maximum_fusion.mid_ref), channel_id=1, source_target_pairs={{0,1},{1,2},{2,3},{3,4},{4,5},{5,6},{6,7},{7,8},{8,9},{9,10},{10,1... | collective-permute-start | bytes 589832 | tf_op jit(solution)/shard_map/ppermute | solution.py:132
  25.7 6.4 %collective-permute-start.4 = (bf16[256,128]{1,0:T(8,128)(2,1)S(1)}, bf16[256,128]{1,0:T(8,128)(2,1)S(1)}, u32[]{:S(2)}, u32[]{:S(2)}) collective-permute-start(bf16[256,128]{1,0:T(8,128)(2,1)S(1)} %shard_map.88), channel_id=1, source_target_pairs={{0,16},{16,32},{32,48},{48,64},{64,80},{80,96},{96,112},{112,0},{1... | collective-permute-start | bytes 196616 | tf_op jit(solution)/shard_map/ppermute | solution.py:132
  32.2 9.0 %collective-permute-start.7 = (bf16[768,128]{1,0:T(8,128)(2,1)S(1)}, bf16[768,128]{1,0:T(8,128)(2,1)S(1)}, u32[]{:S(2)}, u32[]{:S(2)}) collective-permute-start(bf16[768,128]{1,0:T(8,128)(2,1)S(1)} %pad_maximum_fusion.1.mid_ref), channel_id=1, source_target_pairs={{1,0},{2,1},{3,2},{4,3},{5,4},{6,5},{7,6},{8,7},{9,8},{10,9},{11,1... | collective-permute-start | bytes 589832 | tf_op jit(solution)/shard_map/ppermute | solution.py:133
  36.1 9.4 %collective-permute-start.6 = (bf16[768,128]{1,0:T(8,128)(2,1)S(1)}, bf16[768,128]{1,0:T(8,128)(2,1)S(1)}, u32[]{:S(2)}, u32[]{:S(2)}) collective-permute-start(bf16[768,128]{1,0:T(8,128)(2,1)S(1)} %pad_maximum_fusion.1.mid_ref), channel_id=1, source_target_pairs={{0,1},{1,2},{2,3},{3,4},{4,5},{5,6},{6,7},{7,8},{8,9},{9,10},{10,1... | collective-permute-start | bytes 589832 | tf_op jit(solution)/shard_map/ppermute | solution.py:132
  46.1 6.4 %collective-permute-start.8 = (bf16[256,128]{1,0:T(8,128)(2,1)S(1)}, bf16[256,128]{1,0:T(8,128)(2,1)S(1)}, u32[]{:S(2)}, u32[]{:S(2)}) collective-permute-start(bf16[256,128]{1,0:T(8,128)(2,1)S(1)} %shard_map.89.own_ref), channel_id=1, source_target_pairs={{0,16},{16,32},{32,48},{48,64},{64,80},{80,96},{96,112},{112,0},{1... | collective-permute-start | bytes 196616 | tf_op jit(solution)/shard_map/ppermute | solution.py:132
  52.5 5.2 %collective-permute-start.11 = (bf16[768,128]{1,0:T(8,128)(2,1)S(1)}, bf16[768,128]{1,0:T(8,128)(2,1)S(1)}, u32[]{:S(2)}, u32[]{:S(2)}) collective-permute-start(bf16[768,128]{1,0:T(8,128)(2,1)S(1)} %pad_maximum_fusion.2.mid_ref), channel_id=1, source_target_pairs={{1,0},{2,1},{3,2},{4,3},{5,4},{6,5},{7,6},{8,7},{9,8},{10,9},{11,1... | collective-permute-start | bytes 589832 | tf_op jit(solution)/shard_map/ppermute | solution.py:133
  53.0 8.7 %collective-permute-start.10 = (bf16[768,128]{1,0:T(8,128)(2,1)S(1)}, bf16[768,128]{1,0:T(8,128)(2,1)S(1)}, u32[]{:S(2)}, u32[]{:S(2)}) collective-permute-start(bf16[768,128]{1,0:T(8,128)(2,1)S(1)} %pad_maximum_fusion.2.mid_ref), channel_id=1, source_target_pairs={{0,1},{1,2},{2,3},{3,4},{4,5},{5,6},{6,7},{7,8},{8,9},{9,10},{10,1... | collective-permute-start | bytes 589832 | tf_op jit(solution)/shard_map/ppermute | solution.py:132
  62.3 6.4 %collective-permute-start.12 = (bf16[256,128]{1,0:T(8,128)(2,1)S(1)}, bf16[256,128]{1,0:T(8,128)(2,1)S(1)}, u32[]{:S(2)}, u32[]{:S(2)}) collective-permute-start(bf16[256,128]{1,0:T(8,128)(2,1)S(1)} %get-tuple-element.7.own_ref), channel_id=1, source_target_pairs={{0,16},{16,32},{32,48},{48,64},{64,80},{80,96},{96,112},{112,0},{1... | collective-permute-start | bytes 196616 | tf_op jit(solution)/shard_map/ppermute | solution.py:132
  62.4 6.4 %collective-permute-start.13 = (bf16[256,128]{1,0:T(8,128)(2,1)S(1)}, bf16[256,128]{1,0:T(8,128)(2,1)S(1)}, u32[]{:S(2)}, u32[]{:S(2)}) collective-permute-start(bf16[256,128]{1,0:T(8,128)(2,1)S(1)} %get-tuple-element.7.own_ref), channel_id=1, source_target_pairs={{16,0},{32,16},{48,32},{64,48},{80,64},{96,80},{112,96},{0,112},{1... | collective-permute-start | bytes 196616 | tf_op jit(solution)/shard_map/ppermute | solution.py:133
  68.8 5.2 %collective-permute-start.15 = (bf16[768,128]{1,0:T(8,128)(2,1)S(1)}, bf16[768,128]{1,0:T(8,128)(2,1)S(1)}, u32[]{:S(2)}, u32[]{:S(2)}) collective-permute-start(bf16[768,128]{1,0:T(8,128)(2,1)S(1)} %constant_dynamic-update-slice_fusion.mid_ref), channel_id=1, source_target_pairs={{1,0},{2,1},{3,2},{4,3},{5,4},{6,5},{7,6},{8,7},{9,8},{10,9},{11,1... | collective-permute-start | bytes 589832 | tf_op jit(solution)/shard_map/ppermute | solution.py:133
  69.3 8.7 %collective-permute-start.14 = (bf16[768,128]{1,0:T(8,128)(2,1)S(1)}, bf16[768,128]{1,0:T(8,128)(2,1)S(1)}, u32[]{:S(2)}, u32[]{:S(2)}) collective-permute-start(bf16[768,128]{1,0:T(8,128)(2,1)S(1)} %constant_dynamic-update-slice_fusion.mid_ref), channel_id=1, source_target_pairs={{0,1},{1,2},{2,3},{3,4},{4,5},{5,6},{6,7},{7,8},{8,9},{9,10},{10,1... | collective-permute-start | bytes 589832 | tf_op jit(solution)/shard_map/ppermute | solution.py:132
  78.5 6.6 %collective-permute-start.17 = (bf16[256,128]{1,0:T(8,128)(2,1)S(1)}, bf16[256,128]{1,0:T(8,128)(2,1)S(1)}, u32[]{:S(2)}, u32[]{:S(2)}) collective-permute-start(bf16[256,128]{1,0:T(8,128)(2,1)S(1)} %shard_map.91), channel_id=1, source_target_pairs={{16,0},{32,16},{48,32},{64,48},{80,64},{96,80},{112,96},{0,112},{1... | collective-permute-start | bytes 196616 | tf_op jit(solution)/shard_map/ppermute | solution.py:133
  83.2 6.4 %collective-permute-start.16 = (bf16[256,128]{1,0:T(8,128)(2,1)S(1)}, bf16[256,128]{1,0:T(8,128)(2,1)S(1)}, u32[]{:S(2)}, u32[]{:S(2)}) collective-permute-start(bf16[256,128]{1,0:T(8,128)(2,1)S(1)} %shard_map.91), channel_id=1, source_target_pairs={{0,16},{16,32},{32,48},{48,64},{64,80},{80,96},{96,112},{112,0},{1... | collective-permute-start | bytes 196616 | tf_op jit(solution)/shard_map/ppermute | solution.py:132
  89.7 5.2 %collective-permute-start.19 = (bf16[768,128]{1,0:T(8,128)(2,1)S(1)}, bf16[768,128]{1,0:T(8,128)(2,1)S(1)}, u32[]{:S(2)}, u32[]{:S(2)}) collective-permute-start(bf16[768,128]{1,0:T(8,128)(2,1)S(1)} %pad_maximum_fusion.3.mid_ref), channel_id=1, source_target_pairs={{1,0},{2,1},{3,2},{4,3},{5,4},{6,5},{7,6},{8,7},{9,8},{10,9},{11,1... | collective-permute-start | bytes 589832 | tf_op jit(solution)/shard_map/ppermute | solution.py:133
  90.0 9.4 %collective-permute-start.18 = (bf16[768,128]{1,0:T(8,128)(2,1)S(1)}, bf16[768,128]{1,0:T(8,128)(2,1)S(1)}, u32[]{:S(2)}, u32[]{:S(2)}) collective-permute-start(bf16[768,128]{1,0:T(8,128)(2,1)S(1)} %pad_maximum_fusion.3.mid_ref), channel_id=1, source_target_pairs={{0,1},{1,2},{2,3},{3,4},{4,5},{5,6},{6,7},{7,8},{8,9},{9,10},{10,1... | collective-permute-start | bytes 589832 | tf_op jit(solution)/shard_map/ppermute | solution.py:132
  100.5 6.4 %collective-permute-start.20 = (bf16[256,128]{1,0:T(8,128)(2,1)S(1)}, bf16[256,128]{1,0:T(8,128)(2,1)S(1)}, u32[]{:S(2)}, u32[]{:S(2)}) collective-permute-start(bf16[256,128]{1,0:T(8,128)(2,1)S(1)} %shard_map.92.own_ref), channel_id=1, source_target_pairs={{0,16},{16,32},{32,48},{48,64},{64,80},{80,96},{96,112},{112,0},{1... | collective-permute-start | bytes 196616 | tf_op jit(solution)/shard_map/ppermute | solution.py:132
  106.9 29.0 %collective-permute-start.23 = (bf16[768,128]{1,0:T(8,128)(2,1)S(1)}, bf16[768,128]{1,0:T(8,128)(2,1)S(1)}, u32[]{:S(2)}, u32[]{:S(2)}) collective-permute-start(bf16[768,128]{1,0:T(8,128)(2,1)S(1)} %pad_maximum_fusion.4.mid_ref), channel_id=1, source_target_pairs={{1,0},{2,1},{3,2},{4,3},{5,4},{6,5},{7,6},{8,7},{9,8},{10,9},{11,1... | collective-permute-start | bytes 589832 | tf_op jit(solution)/shard_map/ppermute | solution.py:133
  106.9 28.9 %collective-permute-start.22 = (bf16[768,128]{1,0:T(8,128)(2,1)S(1)}, bf16[768,128]{1,0:T(8,128)(2,1)S(1)}, u32[]{:S(2)}, u32[]{:S(2)}) collective-permute-start(bf16[768,128]{1,0:T(8,128)(2,1)S(1)} %pad_maximum_fusion.4.mid_ref), channel_id=1, source_target_pairs={{0,1},{1,2},{2,3},{3,4},{4,5},{5,6},{6,7},{7,8},{8,9},{9,10},{10,1... | collective-permute-start | bytes 589832 | tf_op jit(solution)/shard_map/ppermute | solution.py:132
  115.7 5.1 %collective-permute-start.26 = (f32[8,128]{1,0:T(8,128)S(1)}, f32[8,128]{1,0:T(8,128)S(1)}, u32[]{:S(2)}, u32[]{:S(2)}) collective-permute-start(f32[8,128]{1,0:T(8,128)S(1)} %add.22), channel_id=1, source_target_pairs={{0,64},{16,80},{32,96},{48,112},{64,0},{80,16},{96,32},{112,48},{1... | collective-permute-start | bytes 12296 | tf_op jit(solution)/shard_map/ppermute | solution.py:149
  122.0 5.1 %collective-permute-start.28 = (f32[8,128]{1,0:T(8,128)S(1)}, f32[8,128]{1,0:T(8,128)S(1)}, u32[]{:S(2)}, u32[]{:S(2)}) collective-permute-start(f32[8,128]{1,0:T(8,128)S(1)} %add.24), channel_id=1, source_target_pairs={{0,2},{1,3},{2,0},{3,1},{4,6},{5,7},{6,4},{7,5},{8,10},{9,11},{10,... | collective-permute-start | bytes 12296 | tf_op jit(solution)/shard_map/ppermute | solution.py:149
  130.8 5.1 %collective-permute-start.30 = (f32[8,128]{1,0:T(8,128)S(1)}, f32[8,128]{1,0:T(8,128)S(1)}, u32[]{:S(2)}, u32[]{:S(2)}) collective-permute-start(f32[8,128]{1,0:T(8,128)S(1)} %add.26), channel_id=1, source_target_pairs={{0,8},{1,9},{2,10},{3,11},{4,12},{5,13},{6,14},{7,15},{8,0},{9,1},... | collective-permute-start | bytes 12296 | tf_op jit(solution)/shard_map/ppermute | solution.py:149
  (14 other events, 95.8 us)

commit v2 on v1

v2 whole, which is shorter than its diff:
```python
import jax
import jax.numpy as jnp
from jax import lax
from jax.experimental import pallas as pl
from jax.experimental.pallas import tpu as pltpu
from jax.sharding import PartitionSpec as P

REACH = 2
SIDE = 2
BLOCK = 64
SLAB = 128
ENTRIES = 25
LAT_Y = 16
LAT_X = 32
CELLS = SIDE * SIDE
HALF = BLOCK // 2
LANES = 2 * BLOCK
ROWS = CELLS * BLOCK
PARTS = 9
DEPTH = PARTS * ROWS
BLOCK_ROWS = CELLS * ENTRIES * HALF


def vmem():
    return pl.BlockSpec(memory_space=pltpu.VMEM)


def smem():
    return pl.BlockSpec(memory_space=pltpu.SMEM)


def role(step, is_odd):
    return jnp.where(step == 1, 0, jnp.where((step == 2) == (is_odd == 0), 1, 2))


def build_kernel(origin_ref, cols_any, count_any, blocks_any, out_ref, blocks_ref, wide_ref, cols_ref, count_ref, sems):
    copies = [
        pltpu.make_async_copy(blocks_any, blocks_ref, sems.at[0]),
        pltpu.make_async_copy(cols_any, cols_ref, sems.at[1]),
        pltpu.make_async_copy(count_any, count_ref, sems.at[2]),
    ]
    for copy in copies:
        copy.start()
    out_ref[...] = jnp.zeros_like(out_ref)
    for copy in copies:
        copy.wait()
    wide_ref[...] = blocks_ref[...].astype(jnp.float32)
    lane_half = lax.broadcasted_iota(jnp.int32, (HALF, LANES), 1) // BLOCK
    odd_y = origin_ref[0] % 2
    odd_x = origin_ref[1] % 2

    def place(entry, carry):
        loaded = []
        for cell in range(CELLS):
            cell_y, cell_x = divmod(cell, SIDE)
            col_id = cols_ref[cell_y, cell_x, entry]
            step_y = (lax.div(col_id, LAT_X) - origin_ref[0] * SIDE - cell_y + REACH) & (LAT_Y - 1)
            step_x = (lax.rem(col_id, LAT_X) - origin_ref[1] * SIDE - cell_x + REACH) & (LAT_X - 1)
            win_y = step_y + cell_y
            win_x = step_x + cell_x
            part = role(win_x >> 1, odd_x) * 3 + role(win_y >> 1, odd_y)
            tile = jnp.where(entry < count_ref[cell_y, cell_x], part * 2 + (win_y & 1), 2 * PARTS)
            side = win_x & 1
            base = pl.multiple_of((cell_y * ENTRIES + entry) * BLOCK, BLOCK)
            pair = wide_ref[pl.ds(base + cell_x, HALF, stride=2), :]
            lanes = pl.ds(pl.multiple_of(tile * LANES, LANES), LANES)
            spots = [(pl.ds(parity * CELLS * HALF + cell * HALF, HALF), lanes) for parity in range(2)]
            olds = [out_ref[spot].astype(jnp.float32) for spot in spots]
            loaded.append((side, pair, spots, olds))
        stores = []
        for side, pair, spots, olds in loaded:
            turned = pltpu.roll(pair, BLOCK, 1)
            here = lane_half == side
            for parity in range(2):
                new = jnp.where(side == parity, pair, turned)
                stores.append((spots[parity], jnp.where(here, new, olds[parity]).astype(jnp.bfloat16)))
        for spot, value in stores:
            out_ref[spot] = value
        return carry

    counts = [count_ref[divmod(cell, SIDE)] for cell in range(CELLS)]
    most = jnp.maximum(jnp.maximum(counts[0], counts[1]), jnp.maximum(counts[2], counts[3]))
    lax.fori_loop(0, most, place, 0)


def build(origin, blocks, cols, count):
    rows = blocks.reshape(SIDE, SIDE, ENTRIES, HALF, LANES).transpose(0, 2, 3, 1, 4).reshape(BLOCK_ROWS, LANES)
    any_space = pl.BlockSpec(memory_space=pl.ANY)
    return pl.pallas_call(
        build_kernel,
        out_shape=jax.ShapeDtypeStruct((ROWS, DEPTH + LANES), jnp.bfloat16),
        in_specs=[smem(), any_space, any_space, any_space],
        out_specs=vmem(),
        scratch_shapes=[
            pltpu.VMEM(rows.shape, jnp.bfloat16),
            pltpu.VMEM(rows.shape, jnp.float32),
            pltpu.SMEM(cols.shape, jnp.int32),
            pltpu.SMEM(count.shape, jnp.int32),
            pltpu.SemaphoreType.DMA((3,)),
        ],
        compiler_params=pltpu.CompilerParams(vmem_limit_bytes=16 * 2**20),
        cost_estimate=pl.CostEstimate(flops=10_000_000, bytes_accessed=4_000_000, transcendentals=0),
    )(origin, cols, count, rows)


def product(mat_ref, part_refs, turn_ref):
    total = None
    for index, part_ref in enumerate(part_refs):
        term = jnp.dot(mat_ref[:, index * ROWS : (index + 1) * ROWS], part_ref[...], preferred_element_type=jnp.float32)
        total = term if total is None else total + term
    for cell in range(CELLS):
        for parity in range(2):
            first = parity * CELLS * HALF + cell * HALF
            turn_ref[pl.ds(cell * BLOCK + parity, HALF, stride=2), :] = total[first : first + HALF]
    return turn_ref[...]


def root_kernel(mat_ref, *refs):
    *part_refs, out_ref, turn_ref = refs
    own = part_refs[0][...].astype(jnp.float32)
    out_ref[...] = (own + product(mat_ref, part_refs, turn_ref)).astype(jnp.bfloat16)


def hamilton_kernel(mat_ref, *refs):
    *part_refs, out_ref, turn_ref = refs
    out_ref[...] = product(mat_ref, part_refs, turn_ref).astype(jnp.bfloat16)


def power_kernel(mat_ref, slab_ref, *refs):
    *part_refs, out_ref, power_ref, sums_ref, turn_ref = refs
    power = part_refs[0][...].astype(jnp.float32) + product(mat_ref, part_refs, turn_ref)
    slab = slab_ref[...].astype(jnp.float32)
    power_ref[...] = power
    out_ref[...] = power.astype(jnp.bfloat16)
    image_square = jnp.sum(power * power)
    slab_square = jnp.sum(slab * slab)
    row = lax.broadcasted_iota(jnp.int32, sums_ref.shape, 0)
    sums_ref[...] = jnp.where(row == 0, image_square, slab_square)


def last_kernel(mat_ref, slab_ref, power_ref, sums_ref, *refs):
    *part_refs, one_ref, two_ref, turn_ref = refs
    sums = sums_ref[...]
    ratio = jnp.sqrt(sums[0:1] / (sums[1:2] + 1e-06))
    image = part_refs[0][...].astype(jnp.float32) + product(mat_ref, part_refs, turn_ref)
    one_ref[...] = (power_ref[...] / ratio).astype(jnp.bfloat16)
    two_ref[...] = (2.0 * (image / ratio) / ratio - slab_ref[...].astype(jnp.float32)).astype(jnp.bfloat16)


def apply(kernel, outs, *operands):
    return pl.pallas_call(
        kernel,
        out_shape=outs,
        in_specs=[vmem()] * len(operands),
        out_specs=jax.tree.map(lambda _: vmem(), outs),
        scratch_shapes=[pltpu.VMEM((ROWS, SLAB), jnp.float32)],
        compiler_params=pltpu.CompilerParams(vmem_limit_bytes=16 * 2**20),
        cost_estimate=pl.CostEstimate(flops=2 * ROWS * DEPTH * SLAB, bytes_accessed=2_000_000, transcendentals=0),
    )(*operands)


def same(index, count):
    return index


def near(index, count):
    return index ^ 1


def cross(index, count):
    return (index + 1 if index % 2 else index - 1) % count


def swap(value, row_map, col_map):
    rows, cols = lax.axis_size("row"), lax.axis_size("col")
    pairs = [(r * cols + c, row_map(r, rows) * cols + col_map(c, cols)) for r in range(rows) for c in range(cols)]
    return lax.ppermute(value, ("row", "col"), pairs)


def surround(field):
    near_y = swap(field, near, same)
    far_y = swap(field, cross, same)
    across = [swap(field, row_map, cross) for row_map in (same, near, cross)]
    beside = swap(field, same, near)
    near_y, far_y, *across = lax.optimization_barrier((near_y, far_y, *across))
    beside_near = swap(near_y, same, near)
    beside_far = swap(far_y, same, near)
    return [field, near_y, far_y, beside, beside_near, beside_far, *across]


def total_of(sums, axis, bits):
    count = lax.axis_size(axis)
    for bit in bits:
        sums = sums + lax.ppermute(sums, axis, [(i, i ^ bit) for i in range(count)])
    return sums


def body(x_slab, h_blocks, h_cols, h_count, z_blocks, z_cols, z_count):
    origin = jnp.stack([lax.axis_index("row"), lax.axis_index("col")]).astype(jnp.int32)
    z_mat = build(origin, z_blocks, z_cols, z_count)
    h_mat = build(origin, h_blocks, h_cols, h_count)
    flat = jax.ShapeDtypeStruct((ROWS, SLAB), jnp.bfloat16)
    wide = jax.ShapeDtypeStruct((ROWS, SLAB), jnp.float32)
    sums_shape = jax.ShapeDtypeStruct((8, SLAB), jnp.float32)
    slab = x_slab.reshape(ROWS, SLAB)

    u_one = apply(root_kernel, flat, z_mat, *surround(slab))
    u_two = apply(hamilton_kernel, flat, h_mat, *surround(u_one))
    power, power_full, sums = apply(power_kernel, (flat, wide, sums_shape), z_mat, slab, *surround(u_two))

    parts = surround(power)
    sums = total_of(sums, "col", (1,))
    sums = total_of(sums, "row", (1, 2))
    sums, *parts = lax.optimization_barrier((sums, *parts))
    v_one = apply(root_kernel, flat, z_mat, *parts)

    parts = surround(v_one)
    sums = total_of(sums, "col", (4, 2))
    sums, *parts = lax.optimization_barrier((sums, *parts))
    v_two = apply(hamilton_kernel, flat, h_mat, *parts)

    parts = surround(v_two)
    sums = total_of(sums, "row", (4,))
    sums = total_of(sums, "col", (8,))
    one, two = apply(last_kernel, (flat, flat), z_mat, slab, power_full, sums, *parts)
    return one.reshape(x_slab.shape), two.reshape(x_slab.shape)


def solution(mesh):
    in_specs = (
        P("row", "col", None, None),
        P("row", "col", None, None),
        P("row", "col", None),
        P("row", "col"),
        P("row", "col", None, None),
        P("row", "col", None),
        P("row", "col"),
    )
    out_specs = (P("row", "col", None, None), P("row", "col", None, None))
    return jax.shard_map(body, mesh=mesh, in_specs=in_specs, out_specs=out_specs, check_vma=False)
```

time: 138 us -> 131 us (0.949)
  waiting for transfers between devices: 90.8 us -> 51.2 us
  starting transfers between devices: 30.3 us -> 66.7 us
  Pallas kernels: 11.5 us -> 8.94 us
    ppermute x24 -> x48, waiting for transfers between devices: 63 us -> 27.8 us  [swap(): return lax.ppermute(value, ('row', 'col'), pairs)]
    ppermute x24 -> x48, starting transfers between devices: 29.7 us -> 62.7 us  [swap(): return lax.ppermute(value, ('row', 'col'), pairs)]
    ppermute x7, waiting for transfers between devices: 27.9 us -> 23.3 us  [total_of(): sums = sums + lax.ppermute(sums, axis, [(i, i ^ bit) for i in range(count)])]
    ppermute x7, starting transfers between devices: 0.54 us -> 3.99 us  [total_of(): sums = sums + lax.ppermute(sums, axis, [(i, i ^ bit) for i in range(count)])]
    pallas_call x2, Pallas kernels: 7.9 us -> 5.25 us  [build(): pl.pallas_call(build_kernel, out_shape=jax.ShapeDtypeStruct((ROWS, DEPTH...]
  transfers between devices with their start and end apart: 31 -> 55, of which waited for: 26 -> 31; matrix products, arithmetic and copies ran while one was open for 0% -> 0% of each run, Pallas kernels for 6% -> 4%
where the time goes in v2:
time: 131 us; the launch traced here: 130 us
  starting transfers between devices  66.7 us (51%)
  waiting for transfers between devices  51.2 us (39%)
  Pallas kernels  8.94 us (7%)
  local copies, waits for them, and re-layouts  2.53 us (2%)
    ppermute x48, starting transfers between devices, swap(): return lax.ppermute(value, ('row', 'col'), pairs)  62.7 us
    ppermute x48, waiting for transfers between devices, swap(): return lax.ppermute(value, ('row', 'col'), pairs)  27.8 us
    ppermute x7, waiting for transfers between devices, total_of(): sums = sums + lax.ppermute(sums, axis, [(i, i ^ bit) for i in range(count)])  23.3 us
    pallas_call x2, Pallas kernels, build(): pl.pallas_call(build_kernel, out_shape=jax.ShapeDtypeStruct((ROWS, DEPTH...  5.25 us
    ppermute x7, starting transfers between devices, total_of(): sums = sums + lax.ppermute(sums, axis, [(i, i ^ bit) for i in range(count)])  3.99 us
    pallas_call x6, Pallas kernels, apply(): pl.pallas_call(kernel, out_shape=outs, in_specs=[vmem()] * len(operands),...  3.69 us
  transfers between devices with their start and end apart: 55, of which 31 were waited for; matrix products, arithmetic and copies ran while one was open for 0% of the time, Pallas kernels for 4%

profile of v2, /device:TPU:0, one launch (start us, length us, event | category | flops | bytes accessed | tf_op | source)
XLA Modules:
  0.0 130.3 jit_solution(15567096348296374350)
XLA Ops:
  0.6 8.3 %collective-permute-start.4 = (bf16[256,128]{1,0:T(8,128)(2,1)}, bf16[256,128]{1,0:T(8,128)(2,1)S(1)}, u32[]{:S(2)}, u32[]{:S(2)}) collective-permute-start(bf16[256,128]{1,0:T(8,128)(2,1)} %bitcast.17), channel_id=1, source_target_pairs={{0,127},{1,114},{2,113},{3,116},{4,115},{5,118},{6,117},{7,120},{8... | collective-permute-start | bytes 196616 | tf_op jit(solution)/shard_map/ppermute | solution.py:177
  8.9 2.8 %collective-permute-start.2 = (bf16[256,128]{1,0:T(8,128)(2,1)}, bf16[256,128]{1,0:T(8,128)(2,1)S(1)}, u32[]{:S(2)}, u32[]{:S(2)}) collective-permute-start(bf16[256,128]{1,0:T(8,128)(2,1)} %bitcast.19), channel_id=1, source_target_pairs={{0,15},{1,2},{2,1},{3,4},{4,3},{5,6},{6,5},{7,8},{8,7},{9,10},{10,... | collective-permute-start | bytes 196616 | tf_op jit(solution)/shard_map/ppermute | solution.py:177
  11.7 3.4 %collective-permute-start.1 = (bf16[256,128]{1,0:T(8,128)(2,1)}, bf16[256,128]{1,0:T(8,128)(2,1)S(1)}, u32[]{:S(2)}, u32[]{:S(2)}) collective-permute-start(bf16[256,128]{1,0:T(8,128)(2,1)} %bitcast.20), channel_id=1, source_target_pairs={{0,112},{1,113},{2,114},{3,115},{4,116},{5,117},{6,118},{7,119},{8... | collective-permute-start | bytes 196616 | tf_op jit(solution)/shard_map/ppermute | solution.py:177
  22.7 2.8 %shard_map.86.mat_ref = bf16[256,2432]{1,0:T(8,128)(2,1)S(1)} custom-call(s32[2]{0:T(128)S(1)} %pad_add_fusion.origin_ref, s32[2,2,25]{2,1,0:T(2,128)S(1)} %copy-done.3, s32[2,2]{1,0:T(2,128)S(1)} %copy-done.5, bf16[3200,128]{1,0:T(8,128)(2,1)S(1)} %bitcast.15), custom_call_target="tpu_custom_call" | custom-call | flops 10000000 | bytes 4000000 | tf_op jit(solution)/shard_map/pallas_call | solution.py:89
  26.1 2.8 %collective-permute-start.12 = (bf16[256,128]{1,0:T(8,128)(2,1)S(1)}, bf16[256,128]{1,0:T(8,128)(2,1)S(1)}, u32[]{:S(2)}, u32[]{:S(2)}) collective-permute-start(bf16[256,128]{1,0:T(8,128)(2,1)S(1)} %shard_map.88.refs_0_), channel_id=1, source_target_pairs={{0,127},{1,114},{2,113},{3,116},{4,115},{5,118},{6,117},{7,120},{8... | collective-permute-start | bytes 196616 | tf_op jit(solution)/shard_map/ppermute | solution.py:177
  28.9 2.5 %collective-permute-start.11 = (bf16[256,128]{1,0:T(8,128)(2,1)S(1)}, bf16[256,128]{1,0:T(8,128)(2,1)S(1)}, u32[]{:S(2)}, u32[]{:S(2)}) collective-permute-start(bf16[256,128]{1,0:T(8,128)(2,1)S(1)} %shard_map.88.refs_0_), channel_id=1, source_target_pairs={{0,31},{1,18},{2,17},{3,20},{4,19},{5,22},{6,21},{7,24},{8,23},{9,... | collective-permute-start | bytes 196616 | tf_op jit(solution)/shard_map/ppermute | solution.py:177
  31.7 2.7 %collective-permute-start.9 = (bf16[256,128]{1,0:T(8,128)(2,1)S(1)}, bf16[256,128]{1,0:T(8,128)(2,1)S(1)}, u32[]{:S(2)}, u32[]{:S(2)}) collective-permute-start(bf16[256,128]{1,0:T(8,128)(2,1)S(1)} %shard_map.88.refs_0_), channel_id=1, source_target_pairs={{0,112},{1,113},{2,114},{3,115},{4,116},{5,117},{6,118},{7,119},{8... | collective-permute-start | bytes 196616 | tf_op jit(solution)/shard_map/ppermute | solution.py:177
  36.0 2.7 %collective-permute-done.10.refs_6_ = bf16[256,128]{1,0:T(8,128)(2,1)S(1)} collective-permute-done((bf16[256,128]{1,0:T(8,128)(2,1)S(1)}, bf16[256,128]{1,0:T(8,128)(2,1)S(1)}, u32[]{:S(2)}, u32[]{:S(2)}) %collective-permute-start.10) | collective-permute-done | bytes 65568 | tf_op jit(solution)/shard_map/ppermute | solution.py:177
  39.3 2.4 %shard_map.87.mat_ref = bf16[256,2432]{1,0:T(8,128)(2,1)S(1)} custom-call(s32[2]{0:T(128)S(1)} %pad_add_fusion.origin_ref, s32[2,2,25]{2,1,0:T(2,128)S(1)} %copy-done.4, s32[2,2]{1,0:T(2,128)S(1)} %copy-done.6, bf16[3200,128]{1,0:T(8,128)(2,1)S(1)} %bitcast.16), custom_call_target="tpu_custom_call" | custom-call | flops 10000000 | bytes 4000000 | tf_op jit(solution)/shard_map/pallas_call | solution.py:89
  42.3 3.4 %collective-permute-start.20 = (bf16[256,128]{1,0:T(8,128)(2,1)S(1)}, bf16[256,128]{1,0:T(8,128)(2,1)S(1)}, u32[]{:S(2)}, u32[]{:S(2)}) collective-permute-start(bf16[256,128]{1,0:T(8,128)(2,1)S(1)} %shard_map.89.refs_0_), channel_id=1, source_target_pairs={{0,127},{1,114},{2,113},{3,116},{4,115},{5,118},{6,117},{7,120},{8... | collective-permute-start | bytes 196616 | tf_op jit(solution)/shard_map/ppermute | solution.py:177
  45.6 3.3 %collective-permute-start.19 = (bf16[256,128]{1,0:T(8,128)(2,1)S(1)}, bf16[256,128]{1,0:T(8,128)(2,1)S(1)}, u32[]{:S(2)}, u32[]{:S(2)}) collective-permute-start(bf16[256,128]{1,0:T(8,128)(2,1)S(1)} %shard_map.89.refs_0_), channel_id=1, source_target_pairs={{0,31},{1,18},{2,17},{3,20},{4,19},{5,22},{6,21},{7,24},{8,23},{9,... | collective-permute-start | bytes 196616 | tf_op jit(solution)/shard_map/ppermute | solution.py:177
  49.8 2.4 %collective-permute-start.17 = (bf16[256,128]{1,0:T(8,128)(2,1)S(1)}, bf16[256,128]{1,0:T(8,128)(2,1)S(1)}, u32[]{:S(2)}, u32[]{:S(2)}) collective-permute-start(bf16[256,128]{1,0:T(8,128)(2,1)S(1)} %shard_map.89.refs_0_), channel_id=1, source_target_pairs={{0,112},{1,113},{2,114},{3,115},{4,116},{5,117},{6,118},{7,119},{8... | collective-permute-start | bytes 196616 | tf_op jit(solution)/shard_map/ppermute | solution.py:177
  53.0 3.2 %collective-permute-done.18.refs_6_ = bf16[256,128]{1,0:T(8,128)(2,1)S(1)} collective-permute-done((bf16[256,128]{1,0:T(8,128)(2,1)S(1)}, bf16[256,128]{1,0:T(8,128)(2,1)S(1)}, u32[]{:S(2)}, u32[]{:S(2)}) %collective-permute-start.18) | collective-permute-done | bytes 65568 | tf_op jit(solution)/shard_map/ppermute | solution.py:177
  58.9 2.9 %collective-permute-start.31 = (bf16[256,128]{1,0:T(8,128)(2,1)S(1)}, bf16[256,128]{1,0:T(8,128)(2,1)S(1)}, u32[]{:S(2)}, u32[]{:S(2)}) collective-permute-start(bf16[256,128]{1,0:T(8,128)(2,1)S(1)} %get-tuple-element.81.refs_0_), channel_id=1, source_target_pairs={{0,127},{1,114},{2,113},{3,116},{4,115},{5,118},{6,117},{7,120},{8... | collective-permute-start | bytes 196616 | tf_op jit(solution)/shard_map/ppermute | solution.py:177
  61.9 2.6 %collective-permute-start.30 = (bf16[256,128]{1,0:T(8,128)(2,1)S(1)}, bf16[256,128]{1,0:T(8,128)(2,1)S(1)}, u32[]{:S(2)}, u32[]{:S(2)}) collective-permute-start(bf16[256,128]{1,0:T(8,128)(2,1)S(1)} %get-tuple-element.81.refs_0_), channel_id=1, source_target_pairs={{0,31},{1,18},{2,17},{3,20},{4,19},{5,22},{6,21},{7,24},{8,23},{9,... | collective-permute-start | bytes 196616 | tf_op jit(solution)/shard_map/ppermute | solution.py:177
  75.4 3.0 %collective-permute-done.25 = f32[8,128]{1,0:T(8,128)S(1)} collective-permute-done((f32[8,128]{1,0:T(8,128)S(1)}, f32[8,128]{1,0:T(8,128)S(1)}, u32[]{:S(2)}, u32[]{:S(2)}) %collective-permute-start.25) | collective-permute-done | bytes 4128 | tf_op jit(solution)/shard_map/ppermute | solution.py:194
  79.4 2.6 %collective-permute-done.26 = f32[8,128]{1,0:T(8,128)S(1)} collective-permute-done((f32[8,128]{1,0:T(8,128)S(1)}, f32[8,128]{1,0:T(8,128)S(1)}, u32[]{:S(2)}, u32[]{:S(2)}) %collective-permute-start.26) | collective-permute-done | bytes 4128 | tf_op jit(solution)/shard_map/ppermute | solution.py:194
  82.8 5.3 %collective-permute-start.40 = (bf16[256,128]{1,0:T(8,128)(2,1)S(1)}, bf16[256,128]{1,0:T(8,128)(2,1)S(1)}, u32[]{:S(2)}, u32[]{:S(2)}) collective-permute-start(bf16[256,128]{1,0:T(8,128)(2,1)S(1)} %shard_map.91.refs_0_), channel_id=1, source_target_pairs={{0,31},{1,18},{2,17},{3,20},{4,19},{5,22},{6,21},{7,24},{8,23},{9,... | collective-permute-start | bytes 196616 | tf_op jit(solution)/shard_map/ppermute | solution.py:177
  91.9 3.5 %collective-permute-done.39.refs_6_ = bf16[256,128]{1,0:T(8,128)(2,1)S(1)} collective-permute-done((bf16[256,128]{1,0:T(8,128)(2,1)S(1)}, bf16[256,128]{1,0:T(8,128)(2,1)S(1)}, u32[]{:S(2)}, u32[]{:S(2)}) %collective-permute-start.39) | collective-permute-done | bytes 65568 | tf_op jit(solution)/shard_map/ppermute | solution.py:177
  96.1 3.6 %collective-permute-done.35 = f32[8,128]{1,0:T(8,128)S(1)} collective-permute-done((f32[8,128]{1,0:T(8,128)S(1)}, f32[8,128]{1,0:T(8,128)S(1)}, u32[]{:S(2)}, u32[]{:S(2)}) %collective-permute-start.35) | collective-permute-done | bytes 4128 | tf_op jit(solution)/shard_map/ppermute | solution.py:194
  99.7 5.1 %collective-permute-done.36 = f32[8,128]{1,0:T(8,128)S(1)} collective-permute-done((f32[8,128]{1,0:T(8,128)S(1)}, f32[8,128]{1,0:T(8,128)S(1)}, u32[]{:S(2)}, u32[]{:S(2)}) %collective-permute-start.36) | collective-permute-done | bytes 4128 | tf_op jit(solution)/shard_map/ppermute | solution.py:194
  106.8 2.9 %collective-permute-start.50 = (bf16[256,128]{1,0:T(8,128)(2,1)S(1)}, bf16[256,128]{1,0:T(8,128)(2,1)S(1)}, u32[]{:S(2)}, u32[]{:S(2)}) collective-permute-start(bf16[256,128]{1,0:T(8,128)(2,1)S(1)} %shard_map.92.refs_0_), channel_id=1, source_target_pairs={{0,31},{1,18},{2,17},{3,20},{4,19},{5,22},{6,21},{7,24},{8,23},{9,... | collective-permute-start | bytes 196616 | tf_op jit(solution)/shard_map/ppermute | solution.py:177
  121.2 2.8 %collective-permute-done.45 = f32[8,128]{1,0:T(8,128)S(1)} collective-permute-done((f32[8,128]{1,0:T(8,128)S(1)}, f32[8,128]{1,0:T(8,128)S(1)}, u32[]{:S(2)}, u32[]{:S(2)}) %collective-permute-start.45) | collective-permute-done | bytes 4128 | tf_op jit(solution)/shard_map/ppermute | solution.py:194
  124.0 5.1 %collective-permute-done.46 = f32[8,128]{1,0:T(8,128)S(1)} collective-permute-done((f32[8,128]{1,0:T(8,128)S(1)}, f32[8,128]{1,0:T(8,128)S(1)}, u32[]{:S(2)}, u32[]{:S(2)}) %collective-permute-start.46) | collective-permute-done | bytes 4128 | tf_op jit(solution)/shard_map/ppermute | solution.py:194
  (116 shorter events, 47.4 us)
Async XLA Ops:
  0.6 14.5 %collective-permute-start.4 = (bf16[256,128]{1,0:T(8,128)(2,1)}, bf16[256,128]{1,0:T(8,128)(2,1)S(1)}, u32[]{:S(2)}, u32[]{:S(2)}) collective-permute-start(bf16[256,128]{1,0:T(8,128)(2,1)} %bitcast.17), channel_id=1, source_target_pairs={{0,127},{1,114},{2,113},{3,116},{4,115},{5,118},{6,117},{7,120},{8... | collective-permute-start | bytes 196616 | tf_op jit(solution)/shard_map/ppermute | solution.py:177
  8.9 7.9 %collective-permute-start.3 = (bf16[256,128]{1,0:T(8,128)(2,1)}, bf16[256,128]{1,0:T(8,128)(2,1)S(1)}, u32[]{:S(2)}, u32[]{:S(2)}) collective-permute-start(bf16[256,128]{1,0:T(8,128)(2,1)} %bitcast.18), channel_id=1, source_target_pairs={{0,31},{1,18},{2,17},{3,20},{4,19},{5,22},{6,21},{7,24},{8,23},{9,... | collective-permute-start | bytes 196616 | tf_op jit(solution)/shard_map/ppermute | solution.py:177
  8.9 9.4 %collective-permute-start.2 = (bf16[256,128]{1,0:T(8,128)(2,1)}, bf16[256,128]{1,0:T(8,128)(2,1)S(1)}, u32[]{:S(2)}, u32[]{:S(2)}) collective-permute-start(bf16[256,128]{1,0:T(8,128)(2,1)} %bitcast.19), channel_id=1, source_target_pairs={{0,15},{1,2},{2,1},{3,4},{4,3},{5,6},{6,5},{7,8},{8,7},{9,10},{10,... | collective-permute-start | bytes 196616 | tf_op jit(solution)/shard_map/ppermute | solution.py:177
  15.1 10.4 %collective-permute-start.5 = (bf16[256,128]{1,0:T(8,128)(2,1)}, bf16[256,128]{1,0:T(8,128)(2,1)S(1)}, u32[]{:S(2)}, u32[]{:S(2)}) collective-permute-start(bf16[256,128]{1,0:T(8,128)(2,1)} %bitcast.22), channel_id=1, source_target_pairs={{0,1},{1,0},{2,3},{3,2},{4,5},{5,4},{6,7},{7,6},{8,9},{9,8},{10,11... | collective-permute-start | bytes 196616 | tf_op jit(solution)/shard_map/ppermute | solution.py:177
  26.1 9.2 %collective-permute-start.12 = (bf16[256,128]{1,0:T(8,128)(2,1)S(1)}, bf16[256,128]{1,0:T(8,128)(2,1)S(1)}, u32[]{:S(2)}, u32[]{:S(2)}) collective-permute-start(bf16[256,128]{1,0:T(8,128)(2,1)S(1)} %shard_map.88.refs_0_), channel_id=1, source_target_pairs={{0,127},{1,114},{2,113},{3,116},{4,115},{5,118},{6,117},{7,120},{8... | collective-permute-start | bytes 196616 | tf_op jit(solution)/shard_map/ppermute | solution.py:177
  31.4 7.3 %collective-permute-start.10 = (bf16[256,128]{1,0:T(8,128)(2,1)S(1)}, bf16[256,128]{1,0:T(8,128)(2,1)S(1)}, u32[]{:S(2)}, u32[]{:S(2)}) collective-permute-start(bf16[256,128]{1,0:T(8,128)(2,1)S(1)} %shard_map.88.refs_0_), channel_id=1, source_target_pairs={{0,15},{1,2},{2,1},{3,4},{4,3},{5,6},{6,5},{7,8},{8,7},{9,10},{10,... | collective-permute-start | bytes 196616 | tf_op jit(solution)/shard_map/ppermute | solution.py:177
  42.3 10.3 %collective-permute-start.20 = (bf16[256,128]{1,0:T(8,128)(2,1)S(1)}, bf16[256,128]{1,0:T(8,128)(2,1)S(1)}, u32[]{:S(2)}, u32[]{:S(2)}) collective-permute-start(bf16[256,128]{1,0:T(8,128)(2,1)S(1)} %shard_map.89.refs_0_), channel_id=1, source_target_pairs={{0,127},{1,114},{2,113},{3,116},{4,115},{5,118},{6,117},{7,120},{8... | collective-permute-start | bytes 196616 | tf_op jit(solution)/shard_map/ppermute | solution.py:177
  45.6 7.4 %collective-permute-start.19 = (bf16[256,128]{1,0:T(8,128)(2,1)S(1)}, bf16[256,128]{1,0:T(8,128)(2,1)S(1)}, u32[]{:S(2)}, u32[]{:S(2)}) collective-permute-start(bf16[256,128]{1,0:T(8,128)(2,1)S(1)} %shard_map.89.refs_0_), channel_id=1, source_target_pairs={{0,31},{1,18},{2,17},{3,20},{4,19},{5,22},{6,21},{7,24},{8,23},{9,... | collective-permute-start | bytes 196616 | tf_op jit(solution)/shard_map/ppermute | solution.py:177
  58.9 9.9 %collective-permute-start.31 = (bf16[256,128]{1,0:T(8,128)(2,1)S(1)}, bf16[256,128]{1,0:T(8,128)(2,1)S(1)}, u32[]{:S(2)}, u32[]{:S(2)}) collective-permute-start(bf16[256,128]{1,0:T(8,128)(2,1)S(1)} %get-tuple-element.81.refs_0_), channel_id=1, source_target_pairs={{0,127},{1,114},{2,113},{3,116},{4,115},{5,118},{6,117},{7,120},{8... | collective-permute-start | bytes 196616 | tf_op jit(solution)/shard_map/ppermute | solution.py:177
  61.9 7.5 %collective-permute-start.30 = (bf16[256,128]{1,0:T(8,128)(2,1)S(1)}, bf16[256,128]{1,0:T(8,128)(2,1)S(1)}, u32[]{:S(2)}, u32[]{:S(2)}) collective-permute-start(bf16[256,128]{1,0:T(8,128)(2,1)S(1)} %get-tuple-element.81.refs_0_), channel_id=1, source_target_pairs={{0,31},{1,18},{2,17},{3,20},{4,19},{5,22},{6,21},{7,24},{8,23},{9,... | collective-permute-start | bytes 196616 | tf_op jit(solution)/shard_map/ppermute | solution.py:177
  68.8 13.1 %collective-permute-start.32 = (bf16[256,128]{1,0:T(8,128)(2,1)S(1)}, bf16[256,128]{1,0:T(8,128)(2,1)S(1)}, u32[]{:S(2)}, u32[]{:S(2)}) collective-permute-start(bf16[256,128]{1,0:T(8,128)(2,1)S(1)} %get-tuple-element.81.refs_0_), channel_id=1, source_target_pairs={{0,1},{1,0},{2,3},{3,2},{4,5},{5,4},{6,7},{7,6},{8,9},{9,8},{10,11... | collective-permute-start | bytes 196616 | tf_op jit(solution)/shard_map/ppermute | solution.py:177
  73.1 8.9 %collective-permute-start.33 = (bf16[256,128]{1,0:T(8,128)(2,1)S(1)}, bf16[256,128]{1,0:T(8,128)(2,1)S(1)}, u32[]{:S(2)}, u32[]{:S(2)}) collective-permute-start(bf16[256,128]{1,0:T(8,128)(2,1)S(1)} %collective-permute-done.27.refs_1_), channel_id=1, source_target_pairs={{0,1},{1,0},{2,3},{3,2},{4,5},{5,4},{6,7},{7,6},{8,9},{9,8},{10,11... | collective-permute-start | bytes 196616 | tf_op jit(solution)/shard_map/ppermute | solution.py:177
  73.1 8.9 %collective-permute-start.34 = (bf16[256,128]{1,0:T(8,128)(2,1)S(1)}, bf16[256,128]{1,0:T(8,128)(2,1)S(1)}, u32[]{:S(2)}, u32[]{:S(2)}) collective-permute-start(bf16[256,128]{1,0:T(8,128)(2,1)S(1)} %collective-permute-done.28.refs_2_), channel_id=1, source_target_pairs={{0,1},{1,0},{2,3},{3,2},{4,5},{5,4},{6,7},{7,6},{8,9},{9,8},{10,11... | collective-permute-start | bytes 196616 | tf_op jit(solution)/shard_map/ppermute | solution.py:177
  82.5 9.2 %collective-permute-start.41 = (bf16[256,128]{1,0:T(8,128)(2,1)S(1)}, bf16[256,128]{1,0:T(8,128)(2,1)S(1)}, u32[]{:S(2)}, u32[]{:S(2)}) collective-permute-start(bf16[256,128]{1,0:T(8,128)(2,1)S(1)} %shard_map.91.refs_0_), channel_id=1, source_target_pairs={{0,127},{1,114},{2,113},{3,116},{4,115},{5,118},{6,117},{7,120},{8... | collective-permute-start | bytes 196616 | tf_op jit(solution)/shard_map/ppermute | solution.py:177
  82.8 9.1 %collective-permute-start.40 = (bf16[256,128]{1,0:T(8,128)(2,1)S(1)}, bf16[256,128]{1,0:T(8,128)(2,1)S(1)}, u32[]{:S(2)}, u32[]{:S(2)}) collective-permute-start(bf16[256,128]{1,0:T(8,128)(2,1)S(1)} %shard_map.91.refs_0_), channel_id=1, source_target_pairs={{0,31},{1,18},{2,17},{3,20},{4,19},{5,22},{6,21},{7,24},{8,23},{9,... | collective-permute-start | bytes 196616 | tf_op jit(solution)/shard_map/ppermute | solution.py:177
  91.7 13.1 %collective-permute-start.42 = (bf16[256,128]{1,0:T(8,128)(2,1)S(1)}, bf16[256,128]{1,0:T(8,128)(2,1)S(1)}, u32[]{:S(2)}, u32[]{:S(2)}) collective-permute-start(bf16[256,128]{1,0:T(8,128)(2,1)S(1)} %shard_map.91.refs_0_), channel_id=1, source_target_pairs={{0,1},{1,0},{2,3},{3,2},{4,5},{5,4},{6,7},{7,6},{8,9},{9,8},{10,11... | collective-permute-start | bytes 196616 | tf_op jit(solution)/shard_map/ppermute | solution.py:177
  95.6 9.2 %collective-permute-start.43 = (bf16[256,128]{1,0:T(8,128)(2,1)S(1)}, bf16[256,128]{1,0:T(8,128)(2,1)S(1)}, u32[]{:S(2)}, u32[]{:S(2)}) collective-permute-start(bf16[256,128]{1,0:T(8,128)(2,1)S(1)} %collective-permute-done.37.refs_1_), channel_id=1, source_target_pairs={{0,1},{1,0},{2,3},{3,2},{4,5},{5,4},{6,7},{7,6},{8,9},{9,8},{10,11... | collective-permute-start | bytes 196616 | tf_op jit(solution)/shard_map/ppermute | solution.py:177
  95.6 9.2 %collective-permute-start.44 = (bf16[256,128]{1,0:T(8,128)(2,1)S(1)}, bf16[256,128]{1,0:T(8,128)(2,1)S(1)}, u32[]{:S(2)}, u32[]{:S(2)}) collective-permute-start(bf16[256,128]{1,0:T(8,128)(2,1)S(1)} %collective-permute-done.38.refs_2_), channel_id=1, source_target_pairs={{0,1},{1,0},{2,3},{3,2},{4,5},{5,4},{6,7},{7,6},{8,9},{9,8},{10,11... | collective-permute-start | bytes 196616 | tf_op jit(solution)/shard_map/ppermute | solution.py:177
  105.3 9.9 %collective-permute-start.51 = (bf16[256,128]{1,0:T(8,128)(2,1)S(1)}, bf16[256,128]{1,0:T(8,128)(2,1)S(1)}, u32[]{:S(2)}, u32[]{:S(2)}) collective-permute-start(bf16[256,128]{1,0:T(8,128)(2,1)S(1)} %shard_map.92.refs_0_), channel_id=1, source_target_pairs={{0,127},{1,114},{2,113},{3,116},{4,115},{5,118},{6,117},{7,120},{8... | collective-permute-start | bytes 196616 | tf_op jit(solution)/shard_map/ppermute | solution.py:177
  106.8 8.8 %collective-permute-start.50 = (bf16[256,128]{1,0:T(8,128)(2,1)S(1)}, bf16[256,128]{1,0:T(8,128)(2,1)S(1)}, u32[]{:S(2)}, u32[]{:S(2)}) collective-permute-start(bf16[256,128]{1,0:T(8,128)(2,1)S(1)} %shard_map.92.refs_0_), channel_id=1, source_target_pairs={{0,31},{1,18},{2,17},{3,20},{4,19},{5,22},{6,21},{7,24},{8,23},{9,... | collective-permute-start | bytes 196616 | tf_op jit(solution)/shard_map/ppermute | solution.py:177
  109.6 8.3 %collective-permute-start.49 = (bf16[256,128]{1,0:T(8,128)(2,1)S(1)}, bf16[256,128]{1,0:T(8,128)(2,1)S(1)}, u32[]{:S(2)}, u32[]{:S(2)}) collective-permute-start(bf16[256,128]{1,0:T(8,128)(2,1)S(1)} %shard_map.92.refs_0_), channel_id=1, source_target_pairs={{0,15},{1,2},{2,1},{3,4},{4,3},{5,6},{6,5},{7,8},{8,7},{9,10},{10,... | collective-permute-start | bytes 196616 | tf_op jit(solution)/shard_map/ppermute | solution.py:177
  115.3 13.9 %collective-permute-start.52 = (bf16[256,128]{1,0:T(8,128)(2,1)S(1)}, bf16[256,128]{1,0:T(8,128)(2,1)S(1)}, u32[]{:S(2)}, u32[]{:S(2)}) collective-permute-start(bf16[256,128]{1,0:T(8,128)(2,1)S(1)} %shard_map.92.refs_0_), channel_id=1, source_target_pairs={{0,1},{1,0},{2,3},{3,2},{4,5},{5,4},{6,7},{7,6},{8,9},{9,8},{10,11... | collective-permute-start | bytes 196616 | tf_op jit(solution)/shard_map/ppermute | solution.py:177
  118.4 10.7 %collective-permute-start.53 = (bf16[256,128]{1,0:T(8,128)(2,1)S(1)}, bf16[256,128]{1,0:T(8,128)(2,1)S(1)}, u32[]{:S(2)}, u32[]{:S(2)}) collective-permute-start(bf16[256,128]{1,0:T(8,128)(2,1)S(1)} %collective-permute-done.47.refs_1_), channel_id=1, source_target_pairs={{0,1},{1,0},{2,3},{3,2},{4,5},{5,4},{6,7},{7,6},{8,9},{9,8},{10,11... | collective-permute-start | bytes 196616 | tf_op jit(solution)/shard_map/ppermute | solution.py:177
  118.4 10.8 %collective-permute-start.54 = (bf16[256,128]{1,0:T(8,128)(2,1)S(1)}, bf16[256,128]{1,0:T(8,128)(2,1)S(1)}, u32[]{:S(2)}, u32[]{:S(2)}) collective-permute-start(bf16[256,128]{1,0:T(8,128)(2,1)S(1)} %collective-permute-done.48.refs_2_), channel_id=1, source_target_pairs={{0,1},{1,0},{2,3},{3,2},{4,5},{5,4},{6,7},{7,6},{8,9},{9,8},{10,11... | collective-permute-start | bytes 196616 | tf_op jit(solution)/shard_map/ppermute | solution.py:177
  (38 other events, 203.5 us)

commit v3 on v2

--- a/solution.py
+++ b/solution.py
@@ -85,7 +85,7 @@
 
 def build(origin, blocks, cols, count):
     rows = blocks.reshape(SIDE, SIDE, ENTRIES, HALF, LANES).transpose(0, 2, 3, 1, 4).reshape(BLOCK_ROWS, LANES)
-    any_space = pl.BlockSpec(memory_space=pl.ANY)
+    any_space = pl.BlockSpec(memory_space=pltpu.HBM)
     return pl.pallas_call(
         build_kernel,
         out_shape=jax.ShapeDtypeStruct((ROWS, DEPTH + LANES), jnp.bfloat16),
@@ -177,22 +177,24 @@
     return lax.ppermute(value, ("row", "col"), pairs)
 
 
-def surround(field):
+def surround(field, early=(), late=()):
     near_y = swap(field, near, same)
     far_y = swap(field, cross, same)
-    across = [swap(field, row_map, cross) for row_map in (same, near, cross)]
+    across_far = swap(field, cross, cross)
+    across_same = swap(field, same, cross)
+    across_near = swap(field, near, cross)
     beside = swap(field, same, near)
-    near_y, far_y, *across = lax.optimization_barrier((near_y, far_y, *across))
+    *late, across_near, across_same, across_far, far_y, near_y = lax.optimization_barrier(
+        (*late, across_near, across_same, across_far, far_y, near_y, *early)
+    )[: len(late) + 5]
     beside_near = swap(near_y, same, near)
     beside_far = swap(far_y, same, near)
-    return [field, near_y, far_y, beside, beside_near, beside_far, *across]
-
-
-def total_of(sums, axis, bits):
+    return [field, near_y, far_y, beside, beside_near, beside_far, across_same, across_near, across_far], late
+
+
+def total_of(sums, axis, bit):
     count = lax.axis_size(axis)
-    for bit in bits:
-        sums = sums + lax.ppermute(sums, axis, [(i, i ^ bit) for i in range(count)])
-    return sums
+    return sums + lax.ppermute(sums, axis, [(i, i ^ bit) for i in range(count)])
 
 
 def body(x_slab, h_blocks, h_cols, h_count, z_blocks, z_cols, z_count):
@@ -204,24 +206,24 @@
     sums_shape = jax.ShapeDtypeStruct((8, SLAB), jnp.float32)
     slab = x_slab.reshape(ROWS, SLAB)
 
-    u_one = apply(root_kernel, flat, z_mat, *surround(slab))
-    u_two = apply(hamilton_kernel, flat, h_mat, *surround(u_one))
-    power, power_full, sums = apply(power_kernel, (flat, wide, sums_shape), z_mat, slab, *surround(u_two))
-
-    parts = surround(power)
-    sums = total_of(sums, "col", (1,))
-    sums = total_of(sums, "row", (1, 2))
-    sums, *parts = lax.optimization_barrier((sums, *parts))
+    parts, (z_mat,) = surround(slab, late=(z_mat,))
+    u_one = apply(root_kernel, flat, z_mat, *parts)
+    parts, (h_mat,) = surround(u_one, late=(h_mat,))
+    u_two = apply(hamilton_kernel, flat, h_mat, *parts)
+    parts, _ = surround(u_two)
+    power, power_full, sums = apply(power_kernel, (flat, wide, sums_shape), z_mat, slab, *parts)
+
+    first = total_of(sums, "row", 1)
+    parts, (sums,) = surround(power, early=(first,), late=(total_of(first, "row", 4),))
     v_one = apply(root_kernel, flat, z_mat, *parts)
 
-    parts = surround(v_one)
-    sums = total_of(sums, "col", (4, 2))
-    sums, *parts = lax.optimization_barrier((sums, *parts))
+    first = total_of(sums, "row", 2)
+    parts, (sums,) = surround(v_one, early=(first,), late=(total_of(first, "col", 2),))
     v_two = apply(hamilton_kernel, flat, h_mat, *parts)
 
-    parts = surround(v_two)
-    sums = total_of(sums, "row", (4,))
-    sums = total_of(sums, "col", (8,))
+    first = total_of(sums, "col", 4)
+    parts, (sums,) = surround(v_two, early=(first,), late=(total_of(first, "col", 8),))
+    sums = total_of(sums, "col", 1)
     one, two = apply(last_kernel, (flat, flat), z_mat, slab, power_full, sums, *parts)
     return one.reshape(x_slab.shape), two.reshape(x_slab.shape)
 

time: 131 us -> 115 us (0.88)
  waiting for transfers between devices: 51.2 us -> 36.8 us
  starting transfers between devices: 66.7 us -> 64.1 us
    ppermute x7, waiting for transfers between devices: 23.3 us -> 10.8 us  [total_of(): return sums + lax.ppermute(sums, axis, [(i, i ^ bit) for i in range(count)])]
    ppermute x48, waiting for transfers between devices: 27.8 us -> 26 us  [swap(): return lax.ppermute(value, ('row', 'col'), pairs)]
    ppermute x7, starting transfers between devices: 3.99 us -> 2.3 us  [total_of(): return sums + lax.ppermute(sums, axis, [(i, i ^ bit) for i in range(count)])]
  transfers between devices with their start and end apart: 55 -> 55, of which waited for: 31 -> 19; matrix products, arithmetic and copies ran while one was open for 0% -> 0% of each run, Pallas kernels for 4% -> 6%
where the time goes in v3:
time: 115 us; the launch traced here: 114 us
  starting transfers between devices  64.1 us (56%)
  waiting for transfers between devices  36.8 us (32%)
  Pallas kernels  9.48 us (8%)
  local copies, waits for them, and re-layouts  2.53 us (2%)
    ppermute x48, starting transfers between devices, swap(): return lax.ppermute(value, ('row', 'col'), pairs)  61.8 us
    ppermute x48, waiting for transfers between devices, swap(): return lax.ppermute(value, ('row', 'col'), pairs)  26 us
    ppermute x7, waiting for transfers between devices, total_of(): return sums + lax.ppermute(sums, axis, [(i, i ^ bit) for i in range(count)])  10.8 us
    pallas_call x2, Pallas kernels, build(): pl.pallas_call(build_kernel, out_shape=jax.ShapeDtypeStruct((ROWS, DEPTH...  5.8 us
    pallas_call x6, Pallas kernels, apply(): pl.pallas_call(kernel, out_shape=outs, in_specs=[vmem()] * len(operands),...  3.67 us
    unnamed x14, local copies, waits for them, and re-layouts  2.53 us
    ppermute x7, starting transfers between devices, total_of(): return sums + lax.ppermute(sums, axis, [(i, i ^ bit) for i in range(count)])  2.3 us
  transfers between devices with their start and end apart: 55, of which 19 were waited for; matrix products, arithmetic and copies ran while one was open for 0% of the time, Pallas kernels for 6%

profile of v3, /device:TPU:0, one launch (start us, length us, event | category | flops | bytes accessed | tf_op | source)
XLA Modules:
  0.0 114.0 jit_solution(11655166189236989961)
XLA Ops:
  0.6 6.1 %collective-permute-start = (bf16[256,128]{1,0:T(8,128)(2,1)}, bf16[256,128]{1,0:T(8,128)(2,1)S(1)}, u32[]{:S(2)}, u32[]{:S(2)}) collective-permute-start(bf16[256,128]{1,0:T(8,128)(2,1)} %bitcast.17), channel_id=1, source_target_pairs={{0,31},{1,18},{2,17},{3,20},{4,19},{5,22},{6,21},{7,24},{8,23},{9,... | collective-permute-start | bytes 196616 | tf_op jit(solution)/shard_map/ppermute | solution.py:177
  7.0 6.6 %collective-permute-start.2 = (bf16[256,128]{1,0:T(8,128)(2,1)}, bf16[256,128]{1,0:T(8,128)(2,1)S(1)}, u32[]{:S(2)}, u32[]{:S(2)}) collective-permute-start(bf16[256,128]{1,0:T(8,128)(2,1)} %bitcast.19), channel_id=1, source_target_pairs={{0,127},{1,114},{2,113},{3,116},{4,115},{5,118},{6,117},{7,120},{8... | collective-permute-start | bytes 196616 | tf_op jit(solution)/shard_map/ppermute | solution.py:177
  16.9 3.6 %shard_map.86.mat_ref = bf16[256,2432]{1,0:T(8,128)(2,1)S(1)} custom-call(s32[2]{0:T(128)S(1)} %pad_add_fusion.origin_ref, s32[2,2,25]{2,1,0:T(2,128)S(1)} %copy-done.3, s32[2,2]{1,0:T(2,128)S(1)} %copy-done.5, bf16[3200,128]{1,0:T(8,128)(2,1)S(1)} %bitcast.15), custom_call_target="tpu_custom_call" | custom-call | flops 10000000 | bytes 4000000 | tf_op jit(solution)/shard_map/pallas_call | solution.py:89
  23.0 1.9 %collective-permute-start.10 = (bf16[256,128]{1,0:T(8,128)(2,1)S(1)}, bf16[256,128]{1,0:T(8,128)(2,1)S(1)}, u32[]{:S(2)}, u32[]{:S(2)}) collective-permute-start(bf16[256,128]{1,0:T(8,128)(2,1)S(1)} %shard_map.88.refs_0_), channel_id=1, source_target_pairs={{0,127},{1,114},{2,113},{3,116},{4,115},{5,118},{6,117},{7,120},{8... | collective-permute-start | bytes 196616 | tf_op jit(solution)/shard_map/ppermute | solution.py:177
  26.1 5.6 %collective-permute-start.8 = (bf16[256,128]{1,0:T(8,128)(2,1)S(1)}, bf16[256,128]{1,0:T(8,128)(2,1)S(1)}, u32[]{:S(2)}, u32[]{:S(2)}) collective-permute-start(bf16[256,128]{1,0:T(8,128)(2,1)S(1)} %shard_map.88.refs_0_), channel_id=1, source_target_pairs={{0,31},{1,18},{2,17},{3,20},{4,19},{5,22},{6,21},{7,24},{8,23},{9,... | collective-permute-start | bytes 196616 | tf_op jit(solution)/shard_map/ppermute | solution.py:177
  32.1 2.2 %shard_map.87.mat_ref = bf16[256,2432]{1,0:T(8,128)(2,1)S(1)} custom-call(s32[2]{0:T(128)S(1)} %pad_add_fusion.origin_ref, s32[2,2,25]{2,1,0:T(2,128)S(1)} %copy-done.4, s32[2,2]{1,0:T(2,128)S(1)} %copy-done.6, bf16[3200,128]{1,0:T(8,128)(2,1)S(1)} %bitcast.16), custom_call_target="tpu_custom_call" | custom-call | flops 10000000 | bytes 4000000 | tf_op jit(solution)/shard_map/pallas_call | solution.py:89
  34.4 4.7 %collective-permute-done.9.refs_6_ = bf16[256,128]{1,0:T(8,128)(2,1)S(1)} collective-permute-done((bf16[256,128]{1,0:T(8,128)(2,1)S(1)}, bf16[256,128]{1,0:T(8,128)(2,1)S(1)}, u32[]{:S(2)}, u32[]{:S(2)}) %collective-permute-start.9) | collective-permute-done | bytes 65568 | tf_op jit(solution)/shard_map/ppermute | solution.py:177
  41.4 3.2 %collective-permute-start.17 = (bf16[256,128]{1,0:T(8,128)(2,1)S(1)}, bf16[256,128]{1,0:T(8,128)(2,1)S(1)}, u32[]{:S(2)}, u32[]{:S(2)}) collective-permute-start(bf16[256,128]{1,0:T(8,128)(2,1)S(1)} %shard_map.89.refs_0_), channel_id=1, source_target_pairs={{0,15},{1,2},{2,1},{3,4},{4,3},{5,6},{6,5},{7,8},{8,7},{9,10},{10,... | collective-permute-start | bytes 196616 | tf_op jit(solution)/shard_map/ppermute | solution.py:177
  44.6 3.7 %collective-permute-start.18 = (bf16[256,128]{1,0:T(8,128)(2,1)S(1)}, bf16[256,128]{1,0:T(8,128)(2,1)S(1)}, u32[]{:S(2)}, u32[]{:S(2)}) collective-permute-start(bf16[256,128]{1,0:T(8,128)(2,1)S(1)} %shard_map.89.refs_0_), channel_id=1, source_target_pairs={{0,127},{1,114},{2,113},{3,116},{4,115},{5,118},{6,117},{7,120},{8... | collective-permute-start | bytes 196616 | tf_op jit(solution)/shard_map/ppermute | solution.py:177
  50.3 3.4 %collective-permute-done.18.refs_8_ = bf16[256,128]{1,0:T(8,128)(2,1)S(1)} collective-permute-done((bf16[256,128]{1,0:T(8,128)(2,1)S(1)}, bf16[256,128]{1,0:T(8,128)(2,1)S(1)}, u32[]{:S(2)}, u32[]{:S(2)}) %collective-permute-start.18) | collective-permute-done | bytes 65568 | tf_op jit(solution)/shard_map/ppermute | solution.py:177
  56.8 3.6 %collective-permute-done.24 = f32[8,128]{1,0:T(8,128)S(1)} collective-permute-done((f32[8,128]{1,0:T(8,128)S(1)}, f32[8,128]{1,0:T(8,128)S(1)}, u32[]{:S(2)}, u32[]{:S(2)}) %collective-permute-start.24) | collective-permute-done | bytes 4128 | tf_op jit(solution)/shard_map/ppermute | solution.py:197
  61.5 3.8 %collective-permute-start.27 = (bf16[256,128]{1,0:T(8,128)(2,1)S(1)}, bf16[256,128]{1,0:T(8,128)(2,1)S(1)}, u32[]{:S(2)}, u32[]{:S(2)}) collective-permute-start(bf16[256,128]{1,0:T(8,128)(2,1)S(1)} %get-tuple-element.61.refs_0_), channel_id=1, source_target_pairs={{0,15},{1,2},{2,1},{3,4},{4,3},{5,6},{6,5},{7,8},{8,7},{9,10},{10,... | collective-permute-start | bytes 196616 | tf_op jit(solution)/shard_map/ppermute | solution.py:177
  65.3 1.9 %collective-permute-start.28 = (bf16[256,128]{1,0:T(8,128)(2,1)S(1)}, bf16[256,128]{1,0:T(8,128)(2,1)S(1)}, u32[]{:S(2)}, u32[]{:S(2)}) collective-permute-start(bf16[256,128]{1,0:T(8,128)(2,1)S(1)} %get-tuple-element.61.refs_0_), channel_id=1, source_target_pairs={{0,127},{1,114},{2,113},{3,116},{4,115},{5,118},{6,117},{7,120},{8... | collective-permute-start | bytes 196616 | tf_op jit(solution)/shard_map/ppermute | solution.py:177
  67.2 1.7 %collective-permute-start.29 = (bf16[256,128]{1,0:T(8,128)(2,1)S(1)}, bf16[256,128]{1,0:T(8,128)(2,1)S(1)}, u32[]{:S(2)}, u32[]{:S(2)}) collective-permute-start(bf16[256,128]{1,0:T(8,128)(2,1)S(1)} %get-tuple-element.61.refs_0_), channel_id=1, source_target_pairs={{0,112},{1,113},{2,114},{3,115},{4,116},{5,117},{6,118},{7,119},{8... | collective-permute-start | bytes 196616 | tf_op jit(solution)/shard_map/ppermute | solution.py:177
  69.4 5.1 %collective-permute-done.28.refs_8_ = bf16[256,128]{1,0:T(8,128)(2,1)S(1)} collective-permute-done((bf16[256,128]{1,0:T(8,128)(2,1)S(1)}, bf16[256,128]{1,0:T(8,128)(2,1)S(1)}, u32[]{:S(2)}, u32[]{:S(2)}) %collective-permute-start.28) | collective-permute-done | bytes 65568 | tf_op jit(solution)/shard_map/ppermute | solution.py:177
  76.2 2.4 %collective-permute-done.31 = f32[8,128]{1,0:T(8,128)S(1)} collective-permute-done((f32[8,128]{1,0:T(8,128)S(1)}, f32[8,128]{1,0:T(8,128)S(1)}, u32[]{:S(2)}, u32[]{:S(2)}) %collective-permute-start.31) | collective-permute-done | bytes 4128 | tf_op jit(solution)/shard_map/ppermute | solution.py:197
  79.9 2.7 %collective-permute-start.37 = (bf16[256,128]{1,0:T(8,128)(2,1)S(1)}, bf16[256,128]{1,0:T(8,128)(2,1)S(1)}, u32[]{:S(2)}, u32[]{:S(2)}) collective-permute-start(bf16[256,128]{1,0:T(8,128)(2,1)S(1)} %shard_map.91.refs_0_), channel_id=1, source_target_pairs={{0,15},{1,2},{2,1},{3,4},{4,3},{5,6},{6,5},{7,8},{8,7},{9,10},{10,... | collective-permute-start | bytes 196616 | tf_op jit(solution)/shard_map/ppermute | solution.py:177
  82.7 3.0 %collective-permute-start.38 = (bf16[256,128]{1,0:T(8,128)(2,1)S(1)}, bf16[256,128]{1,0:T(8,128)(2,1)S(1)}, u32[]{:S(2)}, u32[]{:S(2)}) collective-permute-start(bf16[256,128]{1,0:T(8,128)(2,1)S(1)} %shard_map.91.refs_0_), channel_id=1, source_target_pairs={{0,127},{1,114},{2,113},{3,116},{4,115},{5,118},{6,117},{7,120},{8... | collective-permute-start | bytes 196616 | tf_op jit(solution)/shard_map/ppermute | solution.py:177
  85.6 1.7 %collective-permute-start.39 = (bf16[256,128]{1,0:T(8,128)(2,1)S(1)}, bf16[256,128]{1,0:T(8,128)(2,1)S(1)}, u32[]{:S(2)}, u32[]{:S(2)}) collective-permute-start(bf16[256,128]{1,0:T(8,128)(2,1)S(1)} %shard_map.91.refs_0_), channel_id=1, source_target_pairs={{0,112},{1,113},{2,114},{3,115},{4,116},{5,117},{6,118},{7,119},{8... | collective-permute-start | bytes 196616 | tf_op jit(solution)/shard_map/ppermute | solution.py:177
  88.5 3.9 %collective-permute-done.38.refs_8_ = bf16[256,128]{1,0:T(8,128)(2,1)S(1)} collective-permute-done((bf16[256,128]{1,0:T(8,128)(2,1)S(1)}, bf16[256,128]{1,0:T(8,128)(2,1)S(1)}, u32[]{:S(2)}, u32[]{:S(2)}) %collective-permute-start.38) | collective-permute-done | bytes 65568 | tf_op jit(solution)/shard_map/ppermute | solution.py:177
  92.9 3.6 %collective-permute-done.41 = f32[8,128]{1,0:T(8,128)S(1)} collective-permute-done((f32[8,128]{1,0:T(8,128)S(1)}, f32[8,128]{1,0:T(8,128)S(1)}, u32[]{:S(2)}, u32[]{:S(2)}) %collective-permute-start.41) | collective-permute-done | bytes 4128 | tf_op jit(solution)/shard_map/ppermute | solution.py:197
  98.1 3.7 %collective-permute-start.47 = (bf16[256,128]{1,0:T(8,128)(2,1)S(1)}, bf16[256,128]{1,0:T(8,128)(2,1)S(1)}, u32[]{:S(2)}, u32[]{:S(2)}) collective-permute-start(bf16[256,128]{1,0:T(8,128)(2,1)S(1)} %shard_map.92.refs_0_), channel_id=1, source_target_pairs={{0,15},{1,2},{2,1},{3,4},{4,3},{5,6},{6,5},{7,8},{8,7},{9,10},{10,... | collective-permute-start | bytes 196616 | tf_op jit(solution)/shard_map/ppermute | solution.py:177
  101.8 3.0 %collective-permute-start.48 = (bf16[256,128]{1,0:T(8,128)(2,1)S(1)}, bf16[256,128]{1,0:T(8,128)(2,1)S(1)}, u32[]{:S(2)}, u32[]{:S(2)}) collective-permute-start(bf16[256,128]{1,0:T(8,128)(2,1)S(1)} %shard_map.92.refs_0_), channel_id=1, source_target_pairs={{0,127},{1,114},{2,113},{3,116},{4,115},{5,118},{6,117},{7,120},{8... | collective-permute-start | bytes 196616 | tf_op jit(solution)/shard_map/ppermute | solution.py:177
  106.3 4.6 %collective-permute-done.48.refs_8_ = bf16[256,128]{1,0:T(8,128)(2,1)S(1)} collective-permute-done((bf16[256,128]{1,0:T(8,128)(2,1)S(1)}, bf16[256,128]{1,0:T(8,128)(2,1)S(1)}, u32[]{:S(2)}, u32[]{:S(2)}) %collective-permute-start.48) | collective-permute-done | bytes 65568 | tf_op jit(solution)/shard_map/ppermute | solution.py:177
  (116 shorter events, 27.5 us)
Async XLA Ops:
  0.6 19.9 %collective-permute-start = (bf16[256,128]{1,0:T(8,128)(2,1)}, bf16[256,128]{1,0:T(8,128)(2,1)S(1)}, u32[]{:S(2)}, u32[]{:S(2)}) collective-permute-start(bf16[256,128]{1,0:T(8,128)(2,1)} %bitcast.17), channel_id=1, source_target_pairs={{0,31},{1,18},{2,17},{3,20},{4,19},{5,22},{6,21},{7,24},{8,23},{9,... | collective-permute-start | bytes 196616 | tf_op jit(solution)/shard_map/ppermute | solution.py:177
  6.7 13.9 %collective-permute-start.1 = (bf16[256,128]{1,0:T(8,128)(2,1)}, bf16[256,128]{1,0:T(8,128)(2,1)S(1)}, u32[]{:S(2)}, u32[]{:S(2)}) collective-permute-start(bf16[256,128]{1,0:T(8,128)(2,1)} %bitcast.18), channel_id=1, source_target_pairs={{0,15},{1,2},{2,1},{3,4},{4,3},{5,6},{6,5},{7,8},{8,7},{9,10},{10,... | collective-permute-start | bytes 196616 | tf_op jit(solution)/shard_map/ppermute | solution.py:177
  7.0 13.7 %collective-permute-start.2 = (bf16[256,128]{1,0:T(8,128)(2,1)}, bf16[256,128]{1,0:T(8,128)(2,1)S(1)}, u32[]{:S(2)}, u32[]{:S(2)}) collective-permute-start(bf16[256,128]{1,0:T(8,128)(2,1)} %bitcast.19), channel_id=1, source_target_pairs={{0,127},{1,114},{2,113},{3,116},{4,115},{5,118},{6,117},{7,120},{8... | collective-permute-start | bytes 196616 | tf_op jit(solution)/shard_map/ppermute | solution.py:177
  23.0 11.2 %collective-permute-start.10 = (bf16[256,128]{1,0:T(8,128)(2,1)S(1)}, bf16[256,128]{1,0:T(8,128)(2,1)S(1)}, u32[]{:S(2)}, u32[]{:S(2)}) collective-permute-start(bf16[256,128]{1,0:T(8,128)(2,1)S(1)} %shard_map.88.refs_0_), channel_id=1, source_target_pairs={{0,127},{1,114},{2,113},{3,116},{4,115},{5,118},{6,117},{7,120},{8... | collective-permute-start | bytes 196616 | tf_op jit(solution)/shard_map/ppermute | solution.py:177
  24.9 9.5 %collective-permute-start.11 = (bf16[256,128]{1,0:T(8,128)(2,1)S(1)}, bf16[256,128]{1,0:T(8,128)(2,1)S(1)}, u32[]{:S(2)}, u32[]{:S(2)}) collective-permute-start(bf16[256,128]{1,0:T(8,128)(2,1)S(1)} %shard_map.88.refs_0_), channel_id=1, source_target_pairs={{0,112},{1,113},{2,114},{3,115},{4,116},{5,117},{6,118},{7,119},{8... | collective-permute-start | bytes 196616 | tf_op jit(solution)/shard_map/ppermute | solution.py:177
  26.1 8.2 %collective-permute-start.12 = (bf16[256,128]{1,0:T(8,128)(2,1)S(1)}, bf16[256,128]{1,0:T(8,128)(2,1)S(1)}, u32[]{:S(2)}, u32[]{:S(2)}) collective-permute-start(bf16[256,128]{1,0:T(8,128)(2,1)S(1)} %shard_map.88.refs_0_), channel_id=1, source_target_pairs={{0,16},{1,17},{2,18},{3,19},{4,20},{5,21},{6,22},{7,23},{8,24},{9,... | collective-permute-start | bytes 196616 | tf_op jit(solution)/shard_map/ppermute | solution.py:177
  26.1 8.2 %collective-permute-start.8 = (bf16[256,128]{1,0:T(8,128)(2,1)S(1)}, bf16[256,128]{1,0:T(8,128)(2,1)S(1)}, u32[]{:S(2)}, u32[]{:S(2)}) collective-permute-start(bf16[256,128]{1,0:T(8,128)(2,1)S(1)} %shard_map.88.refs_0_), channel_id=1, source_target_pairs={{0,31},{1,18},{2,17},{3,20},{4,19},{5,22},{6,21},{7,24},{8,23},{9,... | collective-permute-start | bytes 196616 | tf_op jit(solution)/shard_map/ppermute | solution.py:177
  40.9 9.4 %collective-permute-start.16 = (bf16[256,128]{1,0:T(8,128)(2,1)S(1)}, bf16[256,128]{1,0:T(8,128)(2,1)S(1)}, u32[]{:S(2)}, u32[]{:S(2)}) collective-permute-start(bf16[256,128]{1,0:T(8,128)(2,1)S(1)} %shard_map.89.refs_0_), channel_id=1, source_target_pairs={{0,31},{1,18},{2,17},{3,20},{4,19},{5,22},{6,21},{7,24},{8,23},{9,... | collective-permute-start | bytes 196616 | tf_op jit(solution)/shard_map/ppermute | solution.py:177
  41.4 8.9 %collective-permute-start.17 = (bf16[256,128]{1,0:T(8,128)(2,1)S(1)}, bf16[256,128]{1,0:T(8,128)(2,1)S(1)}, u32[]{:S(2)}, u32[]{:S(2)}) collective-permute-start(bf16[256,128]{1,0:T(8,128)(2,1)S(1)} %shard_map.89.refs_0_), channel_id=1, source_target_pairs={{0,15},{1,2},{2,1},{3,4},{4,3},{5,6},{6,5},{7,8},{8,7},{9,10},{10,... | collective-permute-start | bytes 196616 | tf_op jit(solution)/shard_map/ppermute | solution.py:177
  44.6 9.1 %collective-permute-start.18 = (bf16[256,128]{1,0:T(8,128)(2,1)S(1)}, bf16[256,128]{1,0:T(8,128)(2,1)S(1)}, u32[]{:S(2)}, u32[]{:S(2)}) collective-permute-start(bf16[256,128]{1,0:T(8,128)(2,1)S(1)} %shard_map.89.refs_0_), channel_id=1, source_target_pairs={{0,127},{1,114},{2,113},{3,116},{4,115},{5,118},{6,117},{7,120},{8... | collective-permute-start | bytes 196616 | tf_op jit(solution)/shard_map/ppermute | solution.py:177
  60.4 8.6 %collective-permute-start.25 = (f32[8,128]{1,0:T(8,128)S(1)}, f32[8,128]{1,0:T(8,128)S(1)}, u32[]{:S(2)}, u32[]{:S(2)}) collective-permute-start(f32[8,128]{1,0:T(8,128)S(1)} %add.21), channel_id=1, source_target_pairs={{0,64},{16,80},{32,96},{48,112},{64,0},{80,16},{96,32},{112,48},{1... | collective-permute-start | bytes 12296 | tf_op jit(solution)/shard_map/ppermute | solution.py:197
  60.4 8.8 %collective-permute-start.26 = (bf16[256,128]{1,0:T(8,128)(2,1)S(1)}, bf16[256,128]{1,0:T(8,128)(2,1)S(1)}, u32[]{:S(2)}, u32[]{:S(2)}) collective-permute-start(bf16[256,128]{1,0:T(8,128)(2,1)S(1)} %get-tuple-element.61.refs_0_), channel_id=1, source_target_pairs={{0,31},{1,18},{2,17},{3,20},{4,19},{5,22},{6,21},{7,24},{8,23},{9,... | collective-permute-start | bytes 196616 | tf_op jit(solution)/shard_map/ppermute | solution.py:177
  61.5 7.9 %collective-permute-start.27 = (bf16[256,128]{1,0:T(8,128)(2,1)S(1)}, bf16[256,128]{1,0:T(8,128)(2,1)S(1)}, u32[]{:S(2)}, u32[]{:S(2)}) collective-permute-start(bf16[256,128]{1,0:T(8,128)(2,1)S(1)} %get-tuple-element.61.refs_0_), channel_id=1, source_target_pairs={{0,15},{1,2},{2,1},{3,4},{4,3},{5,6},{6,5},{7,8},{8,7},{9,10},{10,... | collective-permute-start | bytes 196616 | tf_op jit(solution)/shard_map/ppermute | solution.py:177
  65.3 9.1 %collective-permute-start.28 = (bf16[256,128]{1,0:T(8,128)(2,1)S(1)}, bf16[256,128]{1,0:T(8,128)(2,1)S(1)}, u32[]{:S(2)}, u32[]{:S(2)}) collective-permute-start(bf16[256,128]{1,0:T(8,128)(2,1)S(1)} %get-tuple-element.61.refs_0_), channel_id=1, source_target_pairs={{0,127},{1,114},{2,113},{3,116},{4,115},{5,118},{6,117},{7,120},{8... | collective-permute-start | bytes 196616 | tf_op jit(solution)/shard_map/ppermute | solution.py:177
  69.2 9.4 %collective-permute-start.33 = (bf16[256,128]{1,0:T(8,128)(2,1)S(1)}, bf16[256,128]{1,0:T(8,128)(2,1)S(1)}, u32[]{:S(2)}, u32[]{:S(2)}) collective-permute-start(bf16[256,128]{1,0:T(8,128)(2,1)S(1)} %get-tuple-element.61.refs_0_), channel_id=1, source_target_pairs={{0,1},{1,0},{2,3},{3,2},{4,5},{5,4},{6,7},{7,6},{8,9},{9,8},{10,11... | collective-permute-start | bytes 196616 | tf_op jit(solution)/shard_map/ppermute | solution.py:177
  78.6 8.8 %collective-permute-start.32 = (f32[8,128]{1,0:T(8,128)S(1)}, f32[8,128]{1,0:T(8,128)S(1)}, u32[]{:S(2)}, u32[]{:S(2)}) collective-permute-start(f32[8,128]{1,0:T(8,128)S(1)} %add.23), channel_id=1, source_target_pairs={{0,2},{1,3},{2,0},{3,1},{4,6},{5,7},{6,4},{7,5},{8,10},{9,11},{10,... | collective-permute-start | bytes 12296 | tf_op jit(solution)/shard_map/ppermute | solution.py:197
  79.1 9.4 %collective-permute-start.36 = (bf16[256,128]{1,0:T(8,128)(2,1)S(1)}, bf16[256,128]{1,0:T(8,128)(2,1)S(1)}, u32[]{:S(2)}, u32[]{:S(2)}) collective-permute-start(bf16[256,128]{1,0:T(8,128)(2,1)S(1)} %shard_map.91.refs_0_), channel_id=1, source_target_pairs={{0,31},{1,18},{2,17},{3,20},{4,19},{5,22},{6,21},{7,24},{8,23},{9,... | collective-permute-start | bytes 196616 | tf_op jit(solution)/shard_map/ppermute | solution.py:177
  79.9 8.6 %collective-permute-start.37 = (bf16[256,128]{1,0:T(8,128)(2,1)S(1)}, bf16[256,128]{1,0:T(8,128)(2,1)S(1)}, u32[]{:S(2)}, u32[]{:S(2)}) collective-permute-start(bf16[256,128]{1,0:T(8,128)(2,1)S(1)} %shard_map.91.refs_0_), channel_id=1, source_target_pairs={{0,15},{1,2},{2,1},{3,4},{4,3},{5,6},{6,5},{7,8},{8,7},{9,10},{10,... | collective-permute-start | bytes 196616 | tf_op jit(solution)/shard_map/ppermute | solution.py:177
  82.7 9.7 %collective-permute-start.38 = (bf16[256,128]{1,0:T(8,128)(2,1)S(1)}, bf16[256,128]{1,0:T(8,128)(2,1)S(1)}, u32[]{:S(2)}, u32[]{:S(2)}) collective-permute-start(bf16[256,128]{1,0:T(8,128)(2,1)S(1)} %shard_map.91.refs_0_), channel_id=1, source_target_pairs={{0,127},{1,114},{2,113},{3,116},{4,115},{5,118},{6,117},{7,120},{8... | collective-permute-start | bytes 196616 | tf_op jit(solution)/shard_map/ppermute | solution.py:177
  88.5 9.0 %collective-permute-start.43 = (bf16[256,128]{1,0:T(8,128)(2,1)S(1)}, bf16[256,128]{1,0:T(8,128)(2,1)S(1)}, u32[]{:S(2)}, u32[]{:S(2)}) collective-permute-start(bf16[256,128]{1,0:T(8,128)(2,1)S(1)} %shard_map.91.refs_0_), channel_id=1, source_target_pairs={{0,1},{1,0},{2,3},{3,2},{4,5},{5,4},{6,7},{7,6},{8,9},{9,8},{10,11... | collective-permute-start | bytes 196616 | tf_op jit(solution)/shard_map/ppermute | solution.py:177
  96.5 9.1 %collective-permute-start.42 = (f32[8,128]{1,0:T(8,128)S(1)}, f32[8,128]{1,0:T(8,128)S(1)}, u32[]{:S(2)}, u32[]{:S(2)}) collective-permute-start(f32[8,128]{1,0:T(8,128)S(1)} %add.25), channel_id=1, source_target_pairs={{0,8},{1,9},{2,10},{3,11},{4,12},{5,13},{6,14},{7,15},{8,0},{9,1},... | collective-permute-start | bytes 12296 | tf_op jit(solution)/shard_map/ppermute | solution.py:197
  98.0 8.2 %collective-permute-start.46 = (bf16[256,128]{1,0:T(8,128)(2,1)S(1)}, bf16[256,128]{1,0:T(8,128)(2,1)S(1)}, u32[]{:S(2)}, u32[]{:S(2)}) collective-permute-start(bf16[256,128]{1,0:T(8,128)(2,1)S(1)} %shard_map.92.refs_0_), channel_id=1, source_target_pairs={{0,31},{1,18},{2,17},{3,20},{4,19},{5,22},{6,21},{7,24},{8,23},{9,... | collective-permute-start | bytes 196616 | tf_op jit(solution)/shard_map/ppermute | solution.py:177
  98.1 8.2 %collective-permute-start.47 = (bf16[256,128]{1,0:T(8,128)(2,1)S(1)}, bf16[256,128]{1,0:T(8,128)(2,1)S(1)}, u32[]{:S(2)}, u32[]{:S(2)}) collective-permute-start(bf16[256,128]{1,0:T(8,128)(2,1)S(1)} %shard_map.92.refs_0_), channel_id=1, source_target_pairs={{0,15},{1,2},{2,1},{3,4},{4,3},{5,6},{6,5},{7,8},{8,7},{9,10},{10,... | collective-permute-start | bytes 196616 | tf_op jit(solution)/shard_map/ppermute | solution.py:177
  101.8 9.1 %collective-permute-start.48 = (bf16[256,128]{1,0:T(8,128)(2,1)S(1)}, bf16[256,128]{1,0:T(8,128)(2,1)S(1)}, u32[]{:S(2)}, u32[]{:S(2)}) collective-permute-start(bf16[256,128]{1,0:T(8,128)(2,1)S(1)} %shard_map.92.refs_0_), channel_id=1, source_target_pairs={{0,127},{1,114},{2,113},{3,116},{4,115},{5,118},{6,117},{7,120},{8... | collective-permute-start | bytes 196616 | tf_op jit(solution)/shard_map/ppermute | solution.py:177
  (38 other events, 170.6 us)

commit v4 on v3

--- a/solution.py
+++ b/solution.py
@@ -126,6 +126,18 @@
     out_ref[...] = product(mat_ref, part_refs, turn_ref).astype(jnp.bfloat16)
 
 
+def root_sums_kernel(mat_ref, term_ref, other_ref, *refs):
+    *part_refs, out_ref, sums_ref, turn_ref = refs
+    sums_ref[...] = term_ref[...] + other_ref[...]
+    root_kernel(mat_ref, *part_refs, out_ref, turn_ref)
+
+
+def hamilton_sums_kernel(mat_ref, term_ref, other_ref, *refs):
+    *part_refs, out_ref, sums_ref, turn_ref = refs
+    sums_ref[...] = term_ref[...] + other_ref[...]
+    hamilton_kernel(mat_ref, *part_refs, out_ref, turn_ref)
+
+
 def power_kernel(mat_ref, slab_ref, *refs):
     *part_refs, out_ref, power_ref, sums_ref, turn_ref = refs
     power = part_refs[0][...].astype(jnp.float32) + product(mat_ref, part_refs, turn_ref)
@@ -177,24 +189,27 @@
     return lax.ppermute(value, ("row", "col"), pairs)
 
 
-def surround(field, early=(), late=()):
+def surround(field, late=(), whole=True):
     near_y = swap(field, near, same)
     far_y = swap(field, cross, same)
     across_far = swap(field, cross, cross)
     across_same = swap(field, same, cross)
     across_near = swap(field, near, cross)
     beside = swap(field, same, near)
-    *late, across_near, across_same, across_far, far_y, near_y = lax.optimization_barrier(
-        (*late, across_near, across_same, across_far, far_y, near_y, *early)
-    )[: len(late) + 5]
+    if whole:
+        *late, across_near, across_same, across_far, far_y, near_y = lax.optimization_barrier(
+            (*late, across_near, across_same, across_far, far_y, near_y)
+        )
+    else:
+        across_near, far_y, near_y = lax.optimization_barrier((across_near, far_y, near_y))
     beside_near = swap(near_y, same, near)
     beside_far = swap(far_y, same, near)
     return [field, near_y, far_y, beside, beside_near, beside_far, across_same, across_near, across_far], late
 
 
-def total_of(sums, axis, bit):
+def flipped(sums, axis, bit):
     count = lax.axis_size(axis)
-    return sums + lax.ppermute(sums, axis, [(i, i ^ bit) for i in range(count)])
+    return lax.ppermute(sums, axis, [(i, i ^ bit) for i in range(count)])
 
 
 def body(x_slab, h_blocks, h_cols, h_count, z_blocks, z_cols, z_count):
@@ -210,20 +225,24 @@
     u_one = apply(root_kernel, flat, z_mat, *parts)
     parts, (h_mat,) = surround(u_one, late=(h_mat,))
     u_two = apply(hamilton_kernel, flat, h_mat, *parts)
-    parts, _ = surround(u_two)
+    parts, _ = surround(u_two, whole=False)
     power, power_full, sums = apply(power_kernel, (flat, wide, sums_shape), z_mat, slab, *parts)
 
-    first = total_of(sums, "row", 1)
-    parts, (sums,) = surround(power, early=(first,), late=(total_of(first, "row", 4),))
-    v_one = apply(root_kernel, flat, z_mat, *parts)
-
-    first = total_of(sums, "row", 2)
-    parts, (sums,) = surround(v_one, early=(first,), late=(total_of(first, "col", 2),))
-    v_two = apply(hamilton_kernel, flat, h_mat, *parts)
-
-    first = total_of(sums, "col", 4)
-    parts, (sums,) = surround(v_two, early=(first,), late=(total_of(first, "col", 8),))
-    sums = total_of(sums, "col", 1)
+    pair = sums + flipped(sums, "row", 4)
+    other = flipped(pair, "row", 1)
+    parts, (pair,) = surround(power, late=(pair,))
+    v_one, sums = apply(root_sums_kernel, (flat, sums_shape), z_mat, pair, other, *parts)
+
+    pair = sums + flipped(sums, "col", 2)
+    other = flipped(pair, "row", 2)
+    parts, (pair,) = surround(v_one, late=(pair,))
+    v_two, sums = apply(hamilton_sums_kernel, (flat, sums_shape), h_mat, pair, other, *parts)
+
+    pair = sums + flipped(sums, "col", 8)
+    other = flipped(pair, "col", 4)
+    parts, (pair,) = surround(v_two, late=(pair,))
+    sums = pair + other
+    sums = sums + flipped(sums, "col", 1)
     one, two = apply(last_kernel, (flat, flat), z_mat, slab, power_full, sums, *parts)
     return one.reshape(x_slab.shape), two.reshape(x_slab.shape)
 

time: 115 us -> 121 us (1.052)
  waiting for transfers between devices: 36.8 us -> 44.8 us
  starting transfers between devices: 64.1 us -> 62.7 us
    ppermute x48, waiting for transfers between devices: 26 us -> 32.8 us  [swap(): return lax.ppermute(value, ('row', 'col'), pairs)]
    ppermute x48, starting transfers between devices: 61.8 us -> 60.2 us  [swap(): return lax.ppermute(value, ('row', 'col'), pairs)]
  transfers between devices with their start and end apart: 55 -> 55, of which waited for: 19 -> 22; matrix products, arithmetic and copies ran while one was open for 0% -> 0% of each run, Pallas kernels for 6% -> 5%
where the time goes in v4:
time: 121 us; the launch traced here: 120 us
  starting transfers between devices  62.7 us (52%)
  waiting for transfers between devices  44.8 us (37%)
  Pallas kernels  9.12 us (8%)
  local copies, waits for them, and re-layouts  2.53 us (2%)
    ppermute x48, starting transfers between devices, swap(): return lax.ppermute(value, ('row', 'col'), pairs)  60.2 us
    ppermute x48, waiting for transfers between devices, swap(): return lax.ppermute(value, ('row', 'col'), pairs)  32.8 us
    ppermute x7, waiting for transfers between devices, flipped(): return lax.ppermute(sums, axis, [(i, i ^ bit) for i in range(count)])  12 us
    pallas_call x2, Pallas kernels, build(): pl.pallas_call(build_kernel, out_shape=jax.ShapeDtypeStruct((ROWS, DEPTH...  5.44 us
    pallas_call x6, Pallas kernels, apply(): pl.pallas_call(kernel, out_shape=outs, in_specs=[vmem()] * len(operands),...  3.68 us
    unnamed x14, local copies, waits for them, and re-layouts  2.53 us
    ppermute x7, starting transfers between devices, flipped(): return lax.ppermute(sums, axis, [(i, i ^ bit) for i in range(count)])  2.46 us
  transfers between devices with their start and end apart: 55, of which 22 were waited for; matrix products, arithmetic and copies ran while one was open for 0% of the time, Pallas kernels for 5%

profile of v4, /device:TPU:0, one launch (start us, length us, event | category | flops | bytes accessed | tf_op | source)
XLA Modules:
  0.0 120.2 jit_solution(16627969899260858355)
XLA Ops:
  2.4 2.6 %collective-permute-start.3 = (bf16[256,128]{1,0:T(8,128)(2,1)}, bf16[256,128]{1,0:T(8,128)(2,1)S(1)}, u32[]{:S(2)}, u32[]{:S(2)}) collective-permute-start(bf16[256,128]{1,0:T(8,128)(2,1)} %bitcast.18), channel_id=1, source_target_pairs={{0,112},{1,113},{2,114},{3,115},{4,116},{5,117},{6,118},{7,119},{8... | collective-permute-start | bytes 196616 | tf_op jit(solution)/shard_map/ppermute | solution.py:189
  5.0 5.3 %collective-permute-start.2 = (bf16[256,128]{1,0:T(8,128)(2,1)}, bf16[256,128]{1,0:T(8,128)(2,1)S(1)}, u32[]{:S(2)}, u32[]{:S(2)}) collective-permute-start(bf16[256,128]{1,0:T(8,128)(2,1)} %bitcast.19), channel_id=1, source_target_pairs={{0,127},{1,114},{2,113},{3,116},{4,115},{5,118},{6,117},{7,120},{8... | collective-permute-start | bytes 196616 | tf_op jit(solution)/shard_map/ppermute | solution.py:189
  10.6 3.2 %collective-permute-start = (bf16[256,128]{1,0:T(8,128)(2,1)}, bf16[256,128]{1,0:T(8,128)(2,1)S(1)}, u32[]{:S(2)}, u32[]{:S(2)}) collective-permute-start(bf16[256,128]{1,0:T(8,128)(2,1)} %bitcast.21), channel_id=1, source_target_pairs={{0,31},{1,18},{2,17},{3,20},{4,19},{5,22},{6,21},{7,24},{8,23},{9,... | collective-permute-start | bytes 196616 | tf_op jit(solution)/shard_map/ppermute | solution.py:189
  16.3 3.1 %shard_map.86.mat_ref = bf16[256,2432]{1,0:T(8,128)(2,1)S(1)} custom-call(s32[2]{0:T(128)S(1)} %pad_add_fusion.origin_ref, s32[2,2,25]{2,1,0:T(2,128)S(1)} %copy-done.3, s32[2,2]{1,0:T(2,128)S(1)} %copy-done.5, bf16[3200,128]{1,0:T(8,128)(2,1)S(1)} %bitcast.15), custom_call_target="tpu_custom_call" | custom-call | flops 10000000 | bytes 4000000 | tf_op jit(solution)/shard_map/pallas_call | solution.py:89
  23.5 3.3 %collective-permute-start.11 = (bf16[256,128]{1,0:T(8,128)(2,1)S(1)}, bf16[256,128]{1,0:T(8,128)(2,1)S(1)}, u32[]{:S(2)}, u32[]{:S(2)}) collective-permute-start(bf16[256,128]{1,0:T(8,128)(2,1)S(1)} %shard_map.88.refs_0_), channel_id=1, source_target_pairs={{0,112},{1,113},{2,114},{3,115},{4,116},{5,117},{6,118},{7,119},{8... | collective-permute-start | bytes 196616 | tf_op jit(solution)/shard_map/ppermute | solution.py:189
  27.5 4.1 %collective-permute-start.9 = (bf16[256,128]{1,0:T(8,128)(2,1)S(1)}, bf16[256,128]{1,0:T(8,128)(2,1)S(1)}, u32[]{:S(2)}, u32[]{:S(2)}) collective-permute-start(bf16[256,128]{1,0:T(8,128)(2,1)S(1)} %shard_map.88.refs_0_), channel_id=1, source_target_pairs={{0,15},{1,2},{2,1},{3,4},{4,3},{5,6},{6,5},{7,8},{8,7},{9,10},{10,... | collective-permute-start | bytes 196616 | tf_op jit(solution)/shard_map/ppermute | solution.py:189
  35.9 2.7 %collective-permute-done.8.refs_7_ = bf16[256,128]{1,0:T(8,128)(2,1)S(1)} collective-permute-done((bf16[256,128]{1,0:T(8,128)(2,1)S(1)}, bf16[256,128]{1,0:T(8,128)(2,1)S(1)}, u32[]{:S(2)}, u32[]{:S(2)}) %collective-permute-start.8) | collective-permute-done | bytes 65568 | tf_op jit(solution)/shard_map/ppermute | solution.py:189
  40.5 2.4 %collective-permute-start.17 = (bf16[256,128]{1,0:T(8,128)(2,1)S(1)}, bf16[256,128]{1,0:T(8,128)(2,1)S(1)}, u32[]{:S(2)}, u32[]{:S(2)}) collective-permute-start(bf16[256,128]{1,0:T(8,128)(2,1)S(1)} %shard_map.89.refs_0_), channel_id=1, source_target_pairs={{0,112},{1,113},{2,114},{3,115},{4,116},{5,117},{6,118},{7,119},{8... | collective-permute-start | bytes 196616 | tf_op jit(solution)/shard_map/ppermute | solution.py:189
  43.0 5.6 %collective-permute-start.23 = (bf16[256,128]{1,0:T(8,128)(2,1)S(1)}, bf16[256,128]{1,0:T(8,128)(2,1)S(1)}, u32[]{:S(2)}, u32[]{:S(2)}) collective-permute-start(bf16[256,128]{1,0:T(8,128)(2,1)S(1)} %shard_map.89.refs_0_), channel_id=1, source_target_pairs={{0,127},{1,114},{2,113},{3,116},{4,115},{5,118},{6,117},{7,120},{8... | collective-permute-start | bytes 196616 | tf_op jit(solution)/shard_map/ppermute | solution.py:189
  52.5 3.4 %collective-permute-done.22.refs_6_ = bf16[256,128]{1,0:T(8,128)(2,1)S(1)} collective-permute-done((bf16[256,128]{1,0:T(8,128)(2,1)S(1)}, bf16[256,128]{1,0:T(8,128)(2,1)S(1)}, u32[]{:S(2)}, u32[]{:S(2)}) %collective-permute-start.22) | collective-permute-done | bytes 65568 | tf_op jit(solution)/shard_map/ppermute | solution.py:189
  58.6 3.0 %collective-permute-start.28 = (bf16[256,128]{1,0:T(8,128)(2,1)S(1)}, bf16[256,128]{1,0:T(8,128)(2,1)S(1)}, u32[]{:S(2)}, u32[]{:S(2)}) collective-permute-start(bf16[256,128]{1,0:T(8,128)(2,1)S(1)} %get-tuple-element.61.refs_0_), channel_id=1, source_target_pairs={{0,112},{1,113},{2,114},{3,115},{4,116},{5,117},{6,118},{7,119},{8... | collective-permute-start | bytes 196616 | tf_op jit(solution)/shard_map/ppermute | solution.py:189
  61.6 2.5 %collective-permute-start.27 = (bf16[256,128]{1,0:T(8,128)(2,1)S(1)}, bf16[256,128]{1,0:T(8,128)(2,1)S(1)}, u32[]{:S(2)}, u32[]{:S(2)}) collective-permute-start(bf16[256,128]{1,0:T(8,128)(2,1)S(1)} %get-tuple-element.61.refs_0_), channel_id=1, source_target_pairs={{0,127},{1,114},{2,113},{3,116},{4,115},{5,118},{6,117},{7,120},{8... | collective-permute-start | bytes 196616 | tf_op jit(solution)/shard_map/ppermute | solution.py:189
  64.1 2.5 %collective-permute-start.26 = (bf16[256,128]{1,0:T(8,128)(2,1)S(1)}, bf16[256,128]{1,0:T(8,128)(2,1)S(1)}, u32[]{:S(2)}, u32[]{:S(2)}) collective-permute-start(bf16[256,128]{1,0:T(8,128)(2,1)S(1)} %get-tuple-element.61.refs_0_), channel_id=1, source_target_pairs={{0,15},{1,2},{2,1},{3,4},{4,3},{5,6},{6,5},{7,8},{8,7},{9,10},{10,... | collective-permute-start | bytes 196616 | tf_op jit(solution)/shard_map/ppermute | solution.py:189
  67.1 3.7 %collective-permute-done.27.refs_8_ = bf16[256,128]{1,0:T(8,128)(2,1)S(1)} collective-permute-done((bf16[256,128]{1,0:T(8,128)(2,1)S(1)}, bf16[256,128]{1,0:T(8,128)(2,1)S(1)}, u32[]{:S(2)}, u32[]{:S(2)}) %collective-permute-start.27) | collective-permute-done | bytes 65568 | tf_op jit(solution)/shard_map/ppermute | solution.py:189
  74.2 3.6 %collective-permute-done.30.other_ref = f32[8,128]{1,0:T(8,128)S(1)} collective-permute-done((f32[8,128]{1,0:T(8,128)S(1)}, f32[8,128]{1,0:T(8,128)S(1)}, u32[]{:S(2)}, u32[]{:S(2)}) %collective-permute-start.30) | collective-permute-done | bytes 4128 | tf_op jit(solution)/shard_map/ppermute | solution.py:212
  82.0 4.8 %collective-permute-start.36 = (bf16[256,128]{1,0:T(8,128)(2,1)S(1)}, bf16[256,128]{1,0:T(8,128)(2,1)S(1)}, u32[]{:S(2)}, u32[]{:S(2)}) collective-permute-start(bf16[256,128]{1,0:T(8,128)(2,1)S(1)} %get-tuple-element.69.refs_0_), channel_id=1, source_target_pairs={{0,15},{1,2},{2,1},{3,4},{4,3},{5,6},{6,5},{7,8},{8,7},{9,10},{10,... | collective-permute-start | bytes 196616 | tf_op jit(solution)/shard_map/ppermute | solution.py:189
  87.5 3.6 %collective-permute-done.37.refs_8_ = bf16[256,128]{1,0:T(8,128)(2,1)S(1)} collective-permute-done((bf16[256,128]{1,0:T(8,128)(2,1)S(1)}, bf16[256,128]{1,0:T(8,128)(2,1)S(1)}, u32[]{:S(2)}, u32[]{:S(2)}) %collective-permute-start.37) | collective-permute-done | bytes 65568 | tf_op jit(solution)/shard_map/ppermute | solution.py:189
  91.3 2.5 %collective-permute-done.35.refs_7_ = bf16[256,128]{1,0:T(8,128)(2,1)S(1)} collective-permute-done((bf16[256,128]{1,0:T(8,128)(2,1)S(1)}, bf16[256,128]{1,0:T(8,128)(2,1)S(1)}, u32[]{:S(2)}, u32[]{:S(2)}) %collective-permute-start.35) | collective-permute-done | bytes 65568 | tf_op jit(solution)/shard_map/ppermute | solution.py:189
  94.3 3.6 %collective-permute-done.40.other_ref = f32[8,128]{1,0:T(8,128)S(1)} collective-permute-done((f32[8,128]{1,0:T(8,128)S(1)}, f32[8,128]{1,0:T(8,128)S(1)}, u32[]{:S(2)}, u32[]{:S(2)}) %collective-permute-start.40) | collective-permute-done | bytes 4128 | tf_op jit(solution)/shard_map/ppermute | solution.py:212
  98.6 2.5 %collective-permute-start.48 = (bf16[256,128]{1,0:T(8,128)(2,1)S(1)}, bf16[256,128]{1,0:T(8,128)(2,1)S(1)}, u32[]{:S(2)}, u32[]{:S(2)}) collective-permute-start(bf16[256,128]{1,0:T(8,128)(2,1)S(1)} %get-tuple-element.77.refs_0_), channel_id=1, source_target_pairs={{0,112},{1,113},{2,114},{3,115},{4,116},{5,117},{6,118},{7,119},{8... | collective-permute-start | bytes 196616 | tf_op jit(solution)/shard_map/ppermute | solution.py:189
  102.4 4.3 %collective-permute-start.46 = (bf16[256,128]{1,0:T(8,128)(2,1)S(1)}, bf16[256,128]{1,0:T(8,128)(2,1)S(1)}, u32[]{:S(2)}, u32[]{:S(2)}) collective-permute-start(bf16[256,128]{1,0:T(8,128)(2,1)S(1)} %get-tuple-element.77.refs_0_), channel_id=1, source_target_pairs={{0,15},{1,2},{2,1},{3,4},{4,3},{5,6},{6,5},{7,8},{8,7},{9,10},{10,... | collective-permute-start | bytes 196616 | tf_op jit(solution)/shard_map/ppermute | solution.py:189
  106.8 4.2 %collective-permute-done.47.refs_8_ = bf16[256,128]{1,0:T(8,128)(2,1)S(1)} collective-permute-done((bf16[256,128]{1,0:T(8,128)(2,1)S(1)}, bf16[256,128]{1,0:T(8,128)(2,1)S(1)}, u32[]{:S(2)}, u32[]{:S(2)}) %collective-permute-start.47) | collective-permute-done | bytes 65568 | tf_op jit(solution)/shard_map/ppermute | solution.py:189
  111.0 2.7 %collective-permute-done.45.refs_7_ = bf16[256,128]{1,0:T(8,128)(2,1)S(1)} collective-permute-done((bf16[256,128]{1,0:T(8,128)(2,1)S(1)}, bf16[256,128]{1,0:T(8,128)(2,1)S(1)}, u32[]{:S(2)}, u32[]{:S(2)}) %collective-permute-start.45) | collective-permute-done | bytes 65568 | tf_op jit(solution)/shard_map/ppermute | solution.py:189
  114.2 3.6 %collective-permute-done.50 = f32[8,128]{1,0:T(8,128)S(1)} collective-permute-done((f32[8,128]{1,0:T(8,128)S(1)}, f32[8,128]{1,0:T(8,128)S(1)}, u32[]{:S(2)}, u32[]{:S(2)}) %collective-permute-start.50) | collective-permute-done | bytes 4128 | tf_op jit(solution)/shard_map/ppermute | solution.py:212
  (114 shorter events, 36.6 us)
Async XLA Ops:
  0.6 18.8 %collective-permute-start.4 = (bf16[256,128]{1,0:T(8,128)(2,1)}, bf16[256,128]{1,0:T(8,128)(2,1)S(1)}, u32[]{:S(2)}, u32[]{:S(2)}) collective-permute-start(bf16[256,128]{1,0:T(8,128)(2,1)} %bitcast.17), channel_id=1, source_target_pairs={{0,16},{1,17},{2,18},{3,19},{4,20},{5,21},{6,22},{7,23},{8,24},{9,... | collective-permute-start | bytes 196616 | tf_op jit(solution)/shard_map/ppermute | solution.py:189
  2.4 17.2 %collective-permute-start.3 = (bf16[256,128]{1,0:T(8,128)(2,1)}, bf16[256,128]{1,0:T(8,128)(2,1)S(1)}, u32[]{:S(2)}, u32[]{:S(2)}) collective-permute-start(bf16[256,128]{1,0:T(8,128)(2,1)} %bitcast.18), channel_id=1, source_target_pairs={{0,112},{1,113},{2,114},{3,115},{4,116},{5,117},{6,118},{7,119},{8... | collective-permute-start | bytes 196616 | tf_op jit(solution)/shard_map/ppermute | solution.py:189
  5.0 14.6 %collective-permute-start.2 = (bf16[256,128]{1,0:T(8,128)(2,1)}, bf16[256,128]{1,0:T(8,128)(2,1)S(1)}, u32[]{:S(2)}, u32[]{:S(2)}) collective-permute-start(bf16[256,128]{1,0:T(8,128)(2,1)} %bitcast.19), channel_id=1, source_target_pairs={{0,127},{1,114},{2,113},{3,116},{4,115},{5,118},{6,117},{7,120},{8... | collective-permute-start | bytes 196616 | tf_op jit(solution)/shard_map/ppermute | solution.py:189
  10.3 9.3 %collective-permute-start.1 = (bf16[256,128]{1,0:T(8,128)(2,1)}, bf16[256,128]{1,0:T(8,128)(2,1)S(1)}, u32[]{:S(2)}, u32[]{:S(2)}) collective-permute-start(bf16[256,128]{1,0:T(8,128)(2,1)} %bitcast.20), channel_id=1, source_target_pairs={{0,15},{1,2},{2,1},{3,4},{4,3},{5,6},{6,5},{7,8},{8,7},{9,10},{10,... | collective-permute-start | bytes 196616 | tf_op jit(solution)/shard_map/ppermute | solution.py:189
  10.6 9.0 %collective-permute-start = (bf16[256,128]{1,0:T(8,128)(2,1)}, bf16[256,128]{1,0:T(8,128)(2,1)S(1)}, u32[]{:S(2)}, u32[]{:S(2)}) collective-permute-start(bf16[256,128]{1,0:T(8,128)(2,1)} %bitcast.21), channel_id=1, source_target_pairs={{0,31},{1,18},{2,17},{3,20},{4,19},{5,22},{6,21},{7,24},{8,23},{9,... | collective-permute-start | bytes 196616 | tf_op jit(solution)/shard_map/ppermute | solution.py:189
  21.9 12.0 %collective-permute-start.12 = (bf16[256,128]{1,0:T(8,128)(2,1)S(1)}, bf16[256,128]{1,0:T(8,128)(2,1)S(1)}, u32[]{:S(2)}, u32[]{:S(2)}) collective-permute-start(bf16[256,128]{1,0:T(8,128)(2,1)S(1)} %shard_map.88.refs_0_), channel_id=1, source_target_pairs={{0,16},{1,17},{2,18},{3,19},{4,20},{5,21},{6,22},{7,23},{8,24},{9,... | collective-permute-start | bytes 196616 | tf_op jit(solution)/shard_map/ppermute | solution.py:189
  23.5 10.5 %collective-permute-start.11 = (bf16[256,128]{1,0:T(8,128)(2,1)S(1)}, bf16[256,128]{1,0:T(8,128)(2,1)S(1)}, u32[]{:S(2)}, u32[]{:S(2)}) collective-permute-start(bf16[256,128]{1,0:T(8,128)(2,1)S(1)} %shard_map.88.refs_0_), channel_id=1, source_target_pairs={{0,112},{1,113},{2,114},{3,115},{4,116},{5,117},{6,118},{7,119},{8... | collective-permute-start | bytes 196616 | tf_op jit(solution)/shard_map/ppermute | solution.py:189
  26.8 9.1 %collective-permute-start.10 = (bf16[256,128]{1,0:T(8,128)(2,1)S(1)}, bf16[256,128]{1,0:T(8,128)(2,1)S(1)}, u32[]{:S(2)}, u32[]{:S(2)}) collective-permute-start(bf16[256,128]{1,0:T(8,128)(2,1)S(1)} %shard_map.88.refs_0_), channel_id=1, source_target_pairs={{0,127},{1,114},{2,113},{3,116},{4,115},{5,118},{6,117},{7,120},{8... | collective-permute-start | bytes 196616 | tf_op jit(solution)/shard_map/ppermute | solution.py:189
  27.5 8.4 %collective-permute-start.9 = (bf16[256,128]{1,0:T(8,128)(2,1)S(1)}, bf16[256,128]{1,0:T(8,128)(2,1)S(1)}, u32[]{:S(2)}, u32[]{:S(2)}) collective-permute-start(bf16[256,128]{1,0:T(8,128)(2,1)S(1)} %shard_map.88.refs_0_), channel_id=1, source_target_pairs={{0,15},{1,2},{2,1},{3,4},{4,3},{5,6},{6,5},{7,8},{8,7},{9,10},{10,... | collective-permute-start | bytes 196616 | tf_op jit(solution)/shard_map/ppermute | solution.py:189
  40.4 8.5 %collective-permute-start.18 = (bf16[256,128]{1,0:T(8,128)(2,1)S(1)}, bf16[256,128]{1,0:T(8,128)(2,1)S(1)}, u32[]{:S(2)}, u32[]{:S(2)}) collective-permute-start(bf16[256,128]{1,0:T(8,128)(2,1)S(1)} %shard_map.89.refs_0_), channel_id=1, source_target_pairs={{0,16},{1,17},{2,18},{3,19},{4,20},{5,21},{6,22},{7,23},{8,24},{9,... | collective-permute-start | bytes 196616 | tf_op jit(solution)/shard_map/ppermute | solution.py:189
  43.0 9.5 %collective-permute-start.23 = (bf16[256,128]{1,0:T(8,128)(2,1)S(1)}, bf16[256,128]{1,0:T(8,128)(2,1)S(1)}, u32[]{:S(2)}, u32[]{:S(2)}) collective-permute-start(bf16[256,128]{1,0:T(8,128)(2,1)S(1)} %shard_map.89.refs_0_), channel_id=1, source_target_pairs={{0,127},{1,114},{2,113},{3,116},{4,115},{5,118},{6,117},{7,120},{8... | collective-permute-start | bytes 196616 | tf_op jit(solution)/shard_map/ppermute | solution.py:189
  56.5 10.1 %collective-permute-start.24 = (f32[8,128]{1,0:T(8,128)S(1)}, f32[8,128]{1,0:T(8,128)S(1)}, u32[]{:S(2)}, u32[]{:S(2)}) collective-permute-start(f32[8,128]{1,0:T(8,128)S(1)} %get-tuple-element.60), channel_id=1, source_target_pairs={{0,64},{16,80},{32,96},{48,112},{64,0},{80,16},{96,32},{112,48},{1... | collective-permute-start | bytes 12296 | tf_op jit(solution)/shard_map/ppermute | solution.py:212
  58.6 8.5 %collective-permute-start.29 = (bf16[256,128]{1,0:T(8,128)(2,1)S(1)}, bf16[256,128]{1,0:T(8,128)(2,1)S(1)}, u32[]{:S(2)}, u32[]{:S(2)}) collective-permute-start(bf16[256,128]{1,0:T(8,128)(2,1)S(1)} %get-tuple-element.61.refs_0_), channel_id=1, source_target_pairs={{0,16},{1,17},{2,18},{3,19},{4,20},{5,21},{6,22},{7,23},{8,24},{9,... | collective-permute-start | bytes 196616 | tf_op jit(solution)/shard_map/ppermute | solution.py:189
  58.6 8.5 %collective-permute-start.28 = (bf16[256,128]{1,0:T(8,128)(2,1)S(1)}, bf16[256,128]{1,0:T(8,128)(2,1)S(1)}, u32[]{:S(2)}, u32[]{:S(2)}) collective-permute-start(bf16[256,128]{1,0:T(8,128)(2,1)S(1)} %get-tuple-element.61.refs_0_), channel_id=1, source_target_pairs={{0,112},{1,113},{2,114},{3,115},{4,116},{5,117},{6,118},{7,119},{8... | collective-permute-start | bytes 196616 | tf_op jit(solution)/shard_map/ppermute | solution.py:189
  61.6 9.2 %collective-permute-start.27 = (bf16[256,128]{1,0:T(8,128)(2,1)S(1)}, bf16[256,128]{1,0:T(8,128)(2,1)S(1)}, u32[]{:S(2)}, u32[]{:S(2)}) collective-permute-start(bf16[256,128]{1,0:T(8,128)(2,1)S(1)} %get-tuple-element.61.refs_0_), channel_id=1, source_target_pairs={{0,127},{1,114},{2,113},{3,116},{4,115},{5,118},{6,117},{7,120},{8... | collective-permute-start | bytes 196616 | tf_op jit(solution)/shard_map/ppermute | solution.py:189
  67.1 10.7 %collective-permute-start.31 = (bf16[256,128]{1,0:T(8,128)(2,1)S(1)}, bf16[256,128]{1,0:T(8,128)(2,1)S(1)}, u32[]{:S(2)}, u32[]{:S(2)}) collective-permute-start(bf16[256,128]{1,0:T(8,128)(2,1)S(1)} %get-tuple-element.61.refs_0_), channel_id=1, source_target_pairs={{0,1},{1,0},{2,3},{3,2},{4,5},{5,4},{6,7},{7,6},{8,9},{9,8},{10,11... | collective-permute-start | bytes 196616 | tf_op jit(solution)/shard_map/ppermute | solution.py:189
  78.3 8.5 %collective-permute-start.34 = (f32[8,128]{1,0:T(8,128)S(1)}, f32[8,128]{1,0:T(8,128)S(1)}, u32[]{:S(2)}, u32[]{:S(2)}) collective-permute-start(f32[8,128]{1,0:T(8,128)S(1)} %get-tuple-element.68), channel_id=1, source_target_pairs={{0,2},{1,3},{2,0},{3,1},{4,6},{5,7},{6,4},{7,5},{8,10},{9,11},{10,... | collective-permute-start | bytes 12296 | tf_op jit(solution)/shard_map/ppermute | solution.py:212
  78.7 8.8 %collective-permute-start.38 = (bf16[256,128]{1,0:T(8,128)(2,1)S(1)}, bf16[256,128]{1,0:T(8,128)(2,1)S(1)}, u32[]{:S(2)}, u32[]{:S(2)}) collective-permute-start(bf16[256,128]{1,0:T(8,128)(2,1)S(1)} %get-tuple-element.69.refs_0_), channel_id=1, source_target_pairs={{0,112},{1,113},{2,114},{3,115},{4,116},{5,117},{6,118},{7,119},{8... | collective-permute-start | bytes 196616 | tf_op jit(solution)/shard_map/ppermute | solution.py:189
  80.6 10.5 %collective-permute-start.37 = (bf16[256,128]{1,0:T(8,128)(2,1)S(1)}, bf16[256,128]{1,0:T(8,128)(2,1)S(1)}, u32[]{:S(2)}, u32[]{:S(2)}) collective-permute-start(bf16[256,128]{1,0:T(8,128)(2,1)S(1)} %get-tuple-element.69.refs_0_), channel_id=1, source_target_pairs={{0,127},{1,114},{2,113},{3,116},{4,115},{5,118},{6,117},{7,120},{8... | collective-permute-start | bytes 196616 | tf_op jit(solution)/shard_map/ppermute | solution.py:189
  82.0 9.3 %collective-permute-start.36 = (bf16[256,128]{1,0:T(8,128)(2,1)S(1)}, bf16[256,128]{1,0:T(8,128)(2,1)S(1)}, u32[]{:S(2)}, u32[]{:S(2)}) collective-permute-start(bf16[256,128]{1,0:T(8,128)(2,1)S(1)} %get-tuple-element.69.refs_0_), channel_id=1, source_target_pairs={{0,15},{1,2},{2,1},{3,4},{4,3},{5,6},{6,5},{7,8},{8,7},{9,10},{10,... | collective-permute-start | bytes 196616 | tf_op jit(solution)/shard_map/ppermute | solution.py:189
  86.8 11.1 %collective-permute-start.41 = (bf16[256,128]{1,0:T(8,128)(2,1)S(1)}, bf16[256,128]{1,0:T(8,128)(2,1)S(1)}, u32[]{:S(2)}, u32[]{:S(2)}) collective-permute-start(bf16[256,128]{1,0:T(8,128)(2,1)S(1)} %get-tuple-element.69.refs_0_), channel_id=1, source_target_pairs={{0,1},{1,0},{2,3},{3,2},{4,5},{5,4},{6,7},{7,6},{8,9},{9,8},{10,11... | collective-permute-start | bytes 196616 | tf_op jit(solution)/shard_map/ppermute | solution.py:189
  101.1 9.9 %collective-permute-start.47 = (bf16[256,128]{1,0:T(8,128)(2,1)S(1)}, bf16[256,128]{1,0:T(8,128)(2,1)S(1)}, u32[]{:S(2)}, u32[]{:S(2)}) collective-permute-start(bf16[256,128]{1,0:T(8,128)(2,1)S(1)} %get-tuple-element.77.refs_0_), channel_id=1, source_target_pairs={{0,127},{1,114},{2,113},{3,116},{4,115},{5,118},{6,117},{7,120},{8... | collective-permute-start | bytes 196616 | tf_op jit(solution)/shard_map/ppermute | solution.py:189
  102.4 8.6 %collective-permute-start.46 = (bf16[256,128]{1,0:T(8,128)(2,1)S(1)}, bf16[256,128]{1,0:T(8,128)(2,1)S(1)}, u32[]{:S(2)}, u32[]{:S(2)}) collective-permute-start(bf16[256,128]{1,0:T(8,128)(2,1)S(1)} %get-tuple-element.77.refs_0_), channel_id=1, source_target_pairs={{0,15},{1,2},{2,1},{3,4},{4,3},{5,6},{6,5},{7,8},{8,7},{9,10},{10,... | collective-permute-start | bytes 196616 | tf_op jit(solution)/shard_map/ppermute | solution.py:189
  106.7 12.3 %collective-permute-start.52 = (bf16[256,128]{1,0:T(8,128)(2,1)S(1)}, bf16[256,128]{1,0:T(8,128)(2,1)S(1)}, u32[]{:S(2)}, u32[]{:S(2)}) collective-permute-start(bf16[256,128]{1,0:T(8,128)(2,1)S(1)} %get-tuple-element.77.refs_0_), channel_id=1, source_target_pairs={{0,1},{1,0},{2,3},{3,2},{4,5},{5,4},{6,7},{7,6},{8,9},{9,8},{10,11... | collective-permute-start | bytes 196616 | tf_op jit(solution)/shard_map/ppermute | solution.py:189
  (38 other events, 202.8 us)

commit v5 on v3

--- a/solution.py
+++ b/solution.py
@@ -18,6 +18,7 @@
 ROWS = CELLS * BLOCK
 PARTS = 9
 DEPTH = PARTS * ROWS
+NOTE = 16
 BLOCK_ROWS = CELLS * ENTRIES * HALF
 
 
@@ -106,7 +107,7 @@
 def product(mat_ref, part_refs, turn_ref):
     total = None
     for index, part_ref in enumerate(part_refs):
-        term = jnp.dot(mat_ref[:, index * ROWS : (index + 1) * ROWS], part_ref[...], preferred_element_type=jnp.float32)
+        term = jnp.dot(mat_ref[:, index * ROWS : (index + 1) * ROWS], part_ref[:ROWS], preferred_element_type=jnp.float32)
         total = term if total is None else total + term
     for cell in range(CELLS):
         for parity in range(2):
@@ -115,9 +116,25 @@
     return turn_ref[...]
 
 
+def write_note(note, sums):
+    row = lax.broadcasted_iota(jnp.int32, (NOTE, SLAB), 0)
+    rest = jnp.broadcast_to(sums, (NOTE, SLAB))
+    rows = jnp.zeros((NOTE, SLAB), jnp.float32)
+    for index in range(3):
+        term = rest.astype(jnp.bfloat16).astype(jnp.float32)
+        rows = jnp.where(row == index, term, rows)
+        rest = rest - term
+    note[ROWS:, :] = rows.astype(jnp.bfloat16)
+
+
+def read_notes(part_refs):
+    notes = [jnp.sum(ref[ROWS:, :].astype(jnp.float32), axis=0, keepdims=True) for ref in part_refs]
+    return notes[0] + notes[1] + notes[2] + notes[3]
+
+
 def root_kernel(mat_ref, *refs):
     *part_refs, out_ref, turn_ref = refs
-    own = part_refs[0][...].astype(jnp.float32)
+    own = part_refs[0][:ROWS].astype(jnp.float32)
     out_ref[...] = (own + product(mat_ref, part_refs, turn_ref)).astype(jnp.bfloat16)
 
 
@@ -127,22 +144,32 @@
 
 
 def power_kernel(mat_ref, slab_ref, *refs):
-    *part_refs, out_ref, power_ref, sums_ref, turn_ref = refs
+    *part_refs, out_ref, power_ref, turn_ref = refs
     power = part_refs[0][...].astype(jnp.float32) + product(mat_ref, part_refs, turn_ref)
     slab = slab_ref[...].astype(jnp.float32)
     power_ref[...] = power
-    out_ref[...] = power.astype(jnp.bfloat16)
-    image_square = jnp.sum(power * power)
-    slab_square = jnp.sum(slab * slab)
-    row = lax.broadcasted_iota(jnp.int32, sums_ref.shape, 0)
-    sums_ref[...] = jnp.where(row == 0, image_square, slab_square)
-
-
-def last_kernel(mat_ref, slab_ref, power_ref, sums_ref, *refs):
+    out_ref[:ROWS] = power.astype(jnp.bfloat16)
+    lane = lax.broadcasted_iota(jnp.int32, (1, SLAB), 1)
+    write_note(out_ref, jnp.where(lane < SLAB // 2, jnp.sum(power * power), jnp.sum(slab * slab)))
+
+
+def root_sums_kernel(mat_ref, *refs):
+    *part_refs, out_ref, sums_ref, turn_ref = refs
+    sums_ref[...] = jnp.broadcast_to(read_notes([part_refs[part] for part in (0, 1, 3, 4)]), sums_ref.shape)
+    root_kernel(mat_ref, *part_refs, out_ref, turn_ref)
+
+
+def hamilton_sums_kernel(mat_ref, term_ref, other_ref, *refs):
+    *part_refs, out_ref, turn_ref = refs
+    out_ref[:ROWS] = product(mat_ref, part_refs, turn_ref).astype(jnp.bfloat16)
+    write_note(out_ref, term_ref[:1] + other_ref[:1])
+
+
+def last_kernel(mat_ref, slab_ref, power_ref, *refs):
     *part_refs, one_ref, two_ref, turn_ref = refs
-    sums = sums_ref[...]
-    ratio = jnp.sqrt(sums[0:1] / (sums[1:2] + 1e-06))
-    image = part_refs[0][...].astype(jnp.float32) + product(mat_ref, part_refs, turn_ref)
+    sums = read_notes([part_refs[part] for part in (0, 2, 6, 8)])
+    ratio = jnp.sqrt(sums[:, :1] / (sums[:, SLAB // 2 : SLAB // 2 + 1] + 1e-06))
+    image = part_refs[0][:ROWS].astype(jnp.float32) + product(mat_ref, part_refs, turn_ref)
     one_ref[...] = (power_ref[...] / ratio).astype(jnp.bfloat16)
     two_ref[...] = (2.0 * (image / ratio) / ratio - slab_ref[...].astype(jnp.float32)).astype(jnp.bfloat16)
 
@@ -177,24 +204,27 @@
     return lax.ppermute(value, ("row", "col"), pairs)
 
 
-def surround(field, early=(), late=()):
+def surround(field, late=(), whole=True):
     near_y = swap(field, near, same)
     far_y = swap(field, cross, same)
     across_far = swap(field, cross, cross)
     across_same = swap(field, same, cross)
     across_near = swap(field, near, cross)
     beside = swap(field, same, near)
-    *late, across_near, across_same, across_far, far_y, near_y = lax.optimization_barrier(
-        (*late, across_near, across_same, across_far, far_y, near_y, *early)
-    )[: len(late) + 5]
+    if whole:
+        *late, across_near, across_same, across_far, far_y, near_y = lax.optimization_barrier(
+            (*late, across_near, across_same, across_far, far_y, near_y)
+        )
+    else:
+        across_near, far_y, near_y = lax.optimization_barrier((across_near, far_y, near_y))
     beside_near = swap(near_y, same, near)
     beside_far = swap(far_y, same, near)
     return [field, near_y, far_y, beside, beside_near, beside_far, across_same, across_near, across_far], late
 
 
-def total_of(sums, axis, bit):
+def shifted(sums, axis, step):
     count = lax.axis_size(axis)
-    return sums + lax.ppermute(sums, axis, [(i, i ^ bit) for i in range(count)])
+    return lax.ppermute(sums, axis, [(i, (i + step) % count) for i in range(count)])
 
 
 def body(x_slab, h_blocks, h_cols, h_count, z_blocks, z_cols, z_count):
@@ -204,27 +234,24 @@
     flat = jax.ShapeDtypeStruct((ROWS, SLAB), jnp.bfloat16)
     wide = jax.ShapeDtypeStruct((ROWS, SLAB), jnp.float32)
     sums_shape = jax.ShapeDtypeStruct((8, SLAB), jnp.float32)
+    noted = jax.ShapeDtypeStruct((ROWS + NOTE, SLAB), jnp.bfloat16)
     slab = x_slab.reshape(ROWS, SLAB)
 
     parts, (z_mat,) = surround(slab, late=(z_mat,))
     u_one = apply(root_kernel, flat, z_mat, *parts)
     parts, (h_mat,) = surround(u_one, late=(h_mat,))
     u_two = apply(hamilton_kernel, flat, h_mat, *parts)
-    parts, _ = surround(u_two)
-    power, power_full, sums = apply(power_kernel, (flat, wide, sums_shape), z_mat, slab, *parts)
-
-    first = total_of(sums, "row", 1)
-    parts, (sums,) = surround(power, early=(first,), late=(total_of(first, "row", 4),))
-    v_one = apply(root_kernel, flat, z_mat, *parts)
-
-    first = total_of(sums, "row", 2)
-    parts, (sums,) = surround(v_one, early=(first,), late=(total_of(first, "col", 2),))
-    v_two = apply(hamilton_kernel, flat, h_mat, *parts)
-
-    first = total_of(sums, "col", 4)
-    parts, (sums,) = surround(v_two, early=(first,), late=(total_of(first, "col", 8),))
-    sums = total_of(sums, "col", 1)
-    one, two = apply(last_kernel, (flat, flat), z_mat, slab, power_full, sums, *parts)
+    parts, _ = surround(u_two, whole=False)
+    power, power_full = apply(power_kernel, (noted, wide), z_mat, slab, *parts)
+
+    parts, _ = surround(power, whole=False)
+    v_one, sums = apply(root_sums_kernel, (flat, sums_shape), z_mat, *parts)
+    ring = sums + shifted(sums, "col", 4) + shifted(sums, "col", 8) + shifted(sums, "col", 12)
+    other = shifted(ring, "row", 4)
+    parts, (ring,) = surround(v_one, late=(ring,))
+    v_two = apply(hamilton_sums_kernel, noted, h_mat, ring, other, *parts)
+    parts, _ = surround(v_two, whole=False)
+    one, two = apply(last_kernel, (flat, flat), z_mat, slab, power_full, *parts)
     return one.reshape(x_slab.shape), two.reshape(x_slab.shape)
 
 

time: 115 us -> 113 us (0.983)
    ppermute x7 -> x4, waiting for transfers between devices: 10.8 us -> 5.12 us  [shifted(): lax.ppermute(sums, axis, [(i, (i + step) % count) for i in range(count)])]
    ppermute x48, waiting for transfers between devices: 26 us -> 30.8 us  [swap(): return lax.ppermute(value, ('row', 'col'), pairs)]
    ppermute x7 -> x4, starting transfers between devices: 2.3 us -> 2.09 us  [shifted(): lax.ppermute(sums, axis, [(i, (i + step) % count) for i in range(count)])]
  transfers between devices with their start and end apart: 55 -> 52, of which waited for: 19 -> 20; matrix products, arithmetic and copies ran while one was open for 0% -> 0% of each run, Pallas kernels for 6% -> 5%
where the time goes in v5:
time: 113 us; the launch traced here: 112 us
  starting transfers between devices  63.4 us (56%)
  waiting for transfers between devices  36 us (32%)
  Pallas kernels  8.88 us (8%)
  local copies, waits for them, and re-layouts  2.53 us (2%)
    ppermute x48, starting transfers between devices, swap(): return lax.ppermute(value, ('row', 'col'), pairs)  61.4 us
    ppermute x48, waiting for transfers between devices, swap(): return lax.ppermute(value, ('row', 'col'), pairs)  30.8 us
    pallas_call x2, Pallas kernels, build(): pl.pallas_call(build_kernel, out_shape=jax.ShapeDtypeStruct((ROWS, DEPTH...  5.16 us
    ppermute x4, waiting for transfers between devices, shifted(): lax.ppermute(sums, axis, [(i, (i + step) % count) for i in range(count)])  5.12 us
    pallas_call x6, Pallas kernels, apply(): pl.pallas_call(kernel, out_shape=outs, in_specs=[vmem()] * len(operands),...  3.72 us
    unnamed x14, local copies, waits for them, and re-layouts  2.53 us
  transfers between devices with their start and end apart: 52, of which 20 were waited for; matrix products, arithmetic and copies ran while one was open for 0% of the time, Pallas kernels for 5%

profile of v5, /device:TPU:0, one launch (start us, length us, event | category | flops | bytes accessed | tf_op | source)
XLA Modules:
  0.0 111.8 jit_solution(9705457420496909444)
XLA Ops:
  2.4 2.6 %collective-permute-start.3 = (bf16[256,128]{1,0:T(8,128)(2,1)}, bf16[256,128]{1,0:T(8,128)(2,1)S(1)}, u32[]{:S(2)}, u32[]{:S(2)}) collective-permute-start(bf16[256,128]{1,0:T(8,128)(2,1)} %bitcast.18), channel_id=1, source_target_pairs={{0,112},{1,113},{2,114},{3,115},{4,116},{5,117},{6,118},{7,119},{8... | collective-permute-start | bytes 196616 | tf_op jit(solution)/shard_map/ppermute | solution.py:204
  5.0 5.3 %collective-permute-start.2 = (bf16[256,128]{1,0:T(8,128)(2,1)}, bf16[256,128]{1,0:T(8,128)(2,1)S(1)}, u32[]{:S(2)}, u32[]{:S(2)}) collective-permute-start(bf16[256,128]{1,0:T(8,128)(2,1)} %bitcast.19), channel_id=1, source_target_pairs={{0,127},{1,114},{2,113},{3,116},{4,115},{5,118},{6,117},{7,120},{8... | collective-permute-start | bytes 196616 | tf_op jit(solution)/shard_map/ppermute | solution.py:204
  10.6 3.2 %collective-permute-start = (bf16[256,128]{1,0:T(8,128)(2,1)}, bf16[256,128]{1,0:T(8,128)(2,1)S(1)}, u32[]{:S(2)}, u32[]{:S(2)}) collective-permute-start(bf16[256,128]{1,0:T(8,128)(2,1)} %bitcast.21), channel_id=1, source_target_pairs={{0,31},{1,18},{2,17},{3,20},{4,19},{5,22},{6,21},{7,24},{8,23},{9,... | collective-permute-start | bytes 196616 | tf_op jit(solution)/shard_map/ppermute | solution.py:204
  16.3 2.2 %shard_map.86.mat_ref = bf16[256,2432]{1,0:T(8,128)(2,1)S(1)} custom-call(s32[2]{0:T(128)S(1)} %pad_add_fusion.origin_ref, s32[2,2,25]{2,1,0:T(2,128)S(1)} %copy-done.3, s32[2,2]{1,0:T(2,128)S(1)} %copy-done.5, bf16[3200,128]{1,0:T(8,128)(2,1)S(1)} %bitcast.15), custom_call_target="tpu_custom_call" | custom-call | flops 10000000 | bytes 4000000 | tf_op jit(solution)/shard_map/pallas_call | solution.py:90
  21.1 2.8 %collective-permute-start.12 = (bf16[256,128]{1,0:T(8,128)(2,1)S(1)}, bf16[256,128]{1,0:T(8,128)(2,1)S(1)}, u32[]{:S(2)}, u32[]{:S(2)}) collective-permute-start(bf16[256,128]{1,0:T(8,128)(2,1)S(1)} %shard_map.88.refs_0_), channel_id=1, source_target_pairs={{0,16},{1,17},{2,18},{3,19},{4,20},{5,21},{6,22},{7,23},{8,24},{9,... | collective-permute-start | bytes 196616 | tf_op jit(solution)/shard_map/ppermute | solution.py:204
  23.9 2.7 %collective-permute-start.11 = (bf16[256,128]{1,0:T(8,128)(2,1)S(1)}, bf16[256,128]{1,0:T(8,128)(2,1)S(1)}, u32[]{:S(2)}, u32[]{:S(2)}) collective-permute-start(bf16[256,128]{1,0:T(8,128)(2,1)S(1)} %shard_map.88.refs_0_), channel_id=1, source_target_pairs={{0,112},{1,113},{2,114},{3,115},{4,116},{5,117},{6,118},{7,119},{8... | collective-permute-start | bytes 196616 | tf_op jit(solution)/shard_map/ppermute | solution.py:204
  26.6 5.3 %collective-permute-start.9 = (bf16[256,128]{1,0:T(8,128)(2,1)S(1)}, bf16[256,128]{1,0:T(8,128)(2,1)S(1)}, u32[]{:S(2)}, u32[]{:S(2)}) collective-permute-start(bf16[256,128]{1,0:T(8,128)(2,1)S(1)} %shard_map.88.refs_0_), channel_id=1, source_target_pairs={{0,15},{1,2},{2,1},{3,4},{4,3},{5,6},{6,5},{7,8},{8,7},{9,10},{10,... | collective-permute-start | bytes 196616 | tf_op jit(solution)/shard_map/ppermute | solution.py:204
  31.9 3.0 %shard_map.87.mat_ref = bf16[256,2432]{1,0:T(8,128)(2,1)S(1)} custom-call(s32[2]{0:T(128)S(1)} %pad_add_fusion.origin_ref, s32[2,2,25]{2,1,0:T(2,128)S(1)} %copy-done.4, s32[2,2]{1,0:T(2,128)S(1)} %copy-done.6, bf16[3200,128]{1,0:T(8,128)(2,1)S(1)} %bitcast.16), custom_call_target="tpu_custom_call" | custom-call | flops 10000000 | bytes 4000000 | tf_op jit(solution)/shard_map/pallas_call | solution.py:90
  35.7 3.2 %collective-permute-done.8.refs_7_ = bf16[256,128]{1,0:T(8,128)(2,1)S(1)} collective-permute-done((bf16[256,128]{1,0:T(8,128)(2,1)S(1)}, bf16[256,128]{1,0:T(8,128)(2,1)S(1)}, u32[]{:S(2)}, u32[]{:S(2)}) %collective-permute-start.8) | collective-permute-done | bytes 65568 | tf_op jit(solution)/shard_map/ppermute | solution.py:204
  42.6 5.4 %collective-permute-start.23 = (bf16[256,128]{1,0:T(8,128)(2,1)S(1)}, bf16[256,128]{1,0:T(8,128)(2,1)S(1)}, u32[]{:S(2)}, u32[]{:S(2)}) collective-permute-start(bf16[256,128]{1,0:T(8,128)(2,1)S(1)} %shard_map.89.refs_0_), channel_id=1, source_target_pairs={{0,127},{1,114},{2,113},{3,116},{4,115},{5,118},{6,117},{7,120},{8... | collective-permute-start | bytes 196616 | tf_op jit(solution)/shard_map/ppermute | solution.py:204
  52.0 3.2 %collective-permute-done.22.refs_6_ = bf16[256,128]{1,0:T(8,128)(2,1)S(1)} collective-permute-done((bf16[256,128]{1,0:T(8,128)(2,1)S(1)}, bf16[256,128]{1,0:T(8,128)(2,1)S(1)}, u32[]{:S(2)}, u32[]{:S(2)}) %collective-permute-start.22) | collective-permute-done | bytes 65568 | tf_op jit(solution)/shard_map/ppermute | solution.py:204
  57.8 2.3 %collective-permute-start.24 = (bf16[272,128]{1,0:T(8,128)(2,1)S(1)}, bf16[272,128]{1,0:T(8,128)(2,1)S(1)}, u32[]{:S(2)}, u32[]{:S(2)}) collective-permute-start(bf16[272,128]{1,0:T(8,128)(2,1)S(1)} %get-tuple-element.51.refs_0_), channel_id=1, source_target_pairs={{0,31},{1,18},{2,17},{3,20},{4,19},{5,22},{6,21},{7,24},{8,23},{9,... | collective-permute-start | bytes 208904 | tf_op jit(solution)/shard_map/ppermute | solution.py:204
  60.1 5.4 %collective-permute-start.31 = (bf16[272,128]{1,0:T(8,128)(2,1)S(1)}, bf16[272,128]{1,0:T(8,128)(2,1)S(1)}, u32[]{:S(2)}, u32[]{:S(2)}) collective-permute-start(bf16[272,128]{1,0:T(8,128)(2,1)S(1)} %get-tuple-element.51.refs_0_), channel_id=1, source_target_pairs={{0,127},{1,114},{2,113},{3,116},{4,115},{5,118},{6,117},{7,120},{8... | collective-permute-start | bytes 208904 | tf_op jit(solution)/shard_map/ppermute | solution.py:204
  66.3 2.9 %collective-permute-done.31.refs_8_ = bf16[272,128]{1,0:T(8,128)(2,1)S(1)} collective-permute-done((bf16[272,128]{1,0:T(8,128)(2,1)S(1)}, bf16[272,128]{1,0:T(8,128)(2,1)S(1)}, u32[]{:S(2)}, u32[]{:S(2)}) %collective-permute-start.31) | collective-permute-done | bytes 69664 | tf_op jit(solution)/shard_map/ppermute | solution.py:204
  69.2 3.7 %collective-permute-done.30.refs_6_ = bf16[272,128]{1,0:T(8,128)(2,1)S(1)} collective-permute-done((bf16[272,128]{1,0:T(8,128)(2,1)S(1)}, bf16[272,128]{1,0:T(8,128)(2,1)S(1)}, u32[]{:S(2)}, u32[]{:S(2)}) %collective-permute-start.30) | collective-permute-done | bytes 69664 | tf_op jit(solution)/shard_map/ppermute | solution.py:204
  73.6 1.9 %collective-permute-start.32 = (f32[8,128]{1,0:T(8,128)S(1)}, f32[8,128]{1,0:T(8,128)S(1)}, u32[]{:S(2)}, u32[]{:S(2)}) collective-permute-start(f32[8,128]{1,0:T(8,128)S(1)} %get-tuple-element.55), channel_id=1, source_target_pairs={{0,4},{1,5},{2,6},{3,7},{4,8},{5,9},{6,10},{7,11},{8,12},{9,13},{1... | collective-permute-start | bytes 12296 | tf_op jit(solution)/shard_map/ppermute | solution.py:227
  77.2 2.4 %collective-permute-start.37 = (bf16[256,128]{1,0:T(8,128)(2,1)S(1)}, bf16[256,128]{1,0:T(8,128)(2,1)S(1)}, u32[]{:S(2)}, u32[]{:S(2)}) collective-permute-start(bf16[256,128]{1,0:T(8,128)(2,1)S(1)} %get-tuple-element.56.refs_0_), channel_id=1, source_target_pairs={{0,127},{1,114},{2,113},{3,116},{4,115},{5,118},{6,117},{7,120},{8... | collective-permute-start | bytes 196616 | tf_op jit(solution)/shard_map/ppermute | solution.py:204
  79.6 4.0 %collective-permute-start.36 = (bf16[256,128]{1,0:T(8,128)(2,1)S(1)}, bf16[256,128]{1,0:T(8,128)(2,1)S(1)}, u32[]{:S(2)}, u32[]{:S(2)}) collective-permute-start(bf16[256,128]{1,0:T(8,128)(2,1)S(1)} %get-tuple-element.56.refs_0_), channel_id=1, source_target_pairs={{0,15},{1,2},{2,1},{3,4},{4,3},{5,6},{6,5},{7,8},{8,7},{9,10},{10,... | collective-permute-start | bytes 196616 | tf_op jit(solution)/shard_map/ppermute | solution.py:204
  83.7 2.7 %collective-permute-done.37.refs_8_ = bf16[256,128]{1,0:T(8,128)(2,1)S(1)} collective-permute-done((bf16[256,128]{1,0:T(8,128)(2,1)S(1)}, bf16[256,128]{1,0:T(8,128)(2,1)S(1)}, u32[]{:S(2)}, u32[]{:S(2)}) %collective-permute-start.37) | collective-permute-done | bytes 65568 | tf_op jit(solution)/shard_map/ppermute | solution.py:204
  87.0 3.6 %collective-permute-done.35.refs_7_ = bf16[256,128]{1,0:T(8,128)(2,1)S(1)} collective-permute-done((bf16[256,128]{1,0:T(8,128)(2,1)S(1)}, bf16[256,128]{1,0:T(8,128)(2,1)S(1)}, u32[]{:S(2)}, u32[]{:S(2)}) %collective-permute-start.35) | collective-permute-done | bytes 65568 | tf_op jit(solution)/shard_map/ppermute | solution.py:204
  91.1 5.1 %collective-permute-done.40.other_ref = f32[8,128]{1,0:T(8,128)S(1)} collective-permute-done((f32[8,128]{1,0:T(8,128)S(1)}, f32[8,128]{1,0:T(8,128)S(1)}, u32[]{:S(2)}, u32[]{:S(2)}) %collective-permute-start.40) | collective-permute-done | bytes 4128 | tf_op jit(solution)/shard_map/ppermute | solution.py:227
  97.5 5.8 %collective-permute-start.51 = (bf16[272,128]{1,0:T(8,128)(2,1)S(1)}, bf16[272,128]{1,0:T(8,128)(2,1)S(1)}, u32[]{:S(2)}, u32[]{:S(2)}) collective-permute-start(bf16[272,128]{1,0:T(8,128)(2,1)S(1)} %shard_map.92.refs_0_), channel_id=1, source_target_pairs={{0,127},{1,114},{2,113},{3,116},{4,115},{5,118},{6,117},{7,120},{8... | collective-permute-start | bytes 208904 | tf_op jit(solution)/shard_map/ppermute | solution.py:204
  105.5 2.0 %collective-permute-done.51.refs_8_ = bf16[272,128]{1,0:T(8,128)(2,1)S(1)} collective-permute-done((bf16[272,128]{1,0:T(8,128)(2,1)S(1)}, bf16[272,128]{1,0:T(8,128)(2,1)S(1)}, u32[]{:S(2)}, u32[]{:S(2)}) %collective-permute-start.51) | collective-permute-done | bytes 69664 | tf_op jit(solution)/shard_map/ppermute | solution.py:204
  107.5 3.1 %collective-permute-done.50.refs_6_ = bf16[272,128]{1,0:T(8,128)(2,1)S(1)} collective-permute-done((bf16[272,128]{1,0:T(8,128)(2,1)S(1)}, bf16[272,128]{1,0:T(8,128)(2,1)S(1)}, u32[]{:S(2)}, u32[]{:S(2)}) %collective-permute-start.50) | collective-permute-done | bytes 69664 | tf_op jit(solution)/shard_map/ppermute | solution.py:204
  (104 shorter events, 27.2 us)
Async XLA Ops:
  0.6 17.9 %collective-permute-start.4 = (bf16[256,128]{1,0:T(8,128)(2,1)}, bf16[256,128]{1,0:T(8,128)(2,1)S(1)}, u32[]{:S(2)}, u32[]{:S(2)}) collective-permute-start(bf16[256,128]{1,0:T(8,128)(2,1)} %bitcast.17), channel_id=1, source_target_pairs={{0,16},{1,17},{2,18},{3,19},{4,20},{5,21},{6,22},{7,23},{8,24},{9,... | collective-permute-start | bytes 196616 | tf_op jit(solution)/shard_map/ppermute | solution.py:204
  2.4 16.3 %collective-permute-start.3 = (bf16[256,128]{1,0:T(8,128)(2,1)}, bf16[256,128]{1,0:T(8,128)(2,1)S(1)}, u32[]{:S(2)}, u32[]{:S(2)}) collective-permute-start(bf16[256,128]{1,0:T(8,128)(2,1)} %bitcast.18), channel_id=1, source_target_pairs={{0,112},{1,113},{2,114},{3,115},{4,116},{5,117},{6,118},{7,119},{8... | collective-permute-start | bytes 196616 | tf_op jit(solution)/shard_map/ppermute | solution.py:204
  5.0 13.6 %collective-permute-start.2 = (bf16[256,128]{1,0:T(8,128)(2,1)}, bf16[256,128]{1,0:T(8,128)(2,1)S(1)}, u32[]{:S(2)}, u32[]{:S(2)}) collective-permute-start(bf16[256,128]{1,0:T(8,128)(2,1)} %bitcast.19), channel_id=1, source_target_pairs={{0,127},{1,114},{2,113},{3,116},{4,115},{5,118},{6,117},{7,120},{8... | collective-permute-start | bytes 196616 | tf_op jit(solution)/shard_map/ppermute | solution.py:204
  10.3 8.4 %collective-permute-start.1 = (bf16[256,128]{1,0:T(8,128)(2,1)}, bf16[256,128]{1,0:T(8,128)(2,1)S(1)}, u32[]{:S(2)}, u32[]{:S(2)}) collective-permute-start(bf16[256,128]{1,0:T(8,128)(2,1)} %bitcast.20), channel_id=1, source_target_pairs={{0,15},{1,2},{2,1},{3,4},{4,3},{5,6},{6,5},{7,8},{8,7},{9,10},{10,... | collective-permute-start | bytes 196616 | tf_op jit(solution)/shard_map/ppermute | solution.py:204
  10.6 8.6 %collective-permute-start = (bf16[256,128]{1,0:T(8,128)(2,1)}, bf16[256,128]{1,0:T(8,128)(2,1)S(1)}, u32[]{:S(2)}, u32[]{:S(2)}) collective-permute-start(bf16[256,128]{1,0:T(8,128)(2,1)} %bitcast.21), channel_id=1, source_target_pairs={{0,31},{1,18},{2,17},{3,20},{4,19},{5,22},{6,21},{7,24},{8,23},{9,... | collective-permute-start | bytes 196616 | tf_op jit(solution)/shard_map/ppermute | solution.py:204
  21.1 13.8 %collective-permute-start.12 = (bf16[256,128]{1,0:T(8,128)(2,1)S(1)}, bf16[256,128]{1,0:T(8,128)(2,1)S(1)}, u32[]{:S(2)}, u32[]{:S(2)}) collective-permute-start(bf16[256,128]{1,0:T(8,128)(2,1)S(1)} %shard_map.88.refs_0_), channel_id=1, source_target_pairs={{0,16},{1,17},{2,18},{3,19},{4,20},{5,21},{6,22},{7,23},{8,24},{9,... | collective-permute-start | bytes 196616 | tf_op jit(solution)/shard_map/ppermute | solution.py:204
  23.9 11.2 %collective-permute-start.11 = (bf16[256,128]{1,0:T(8,128)(2,1)S(1)}, bf16[256,128]{1,0:T(8,128)(2,1)S(1)}, u32[]{:S(2)}, u32[]{:S(2)}) collective-permute-start(bf16[256,128]{1,0:T(8,128)(2,1)S(1)} %shard_map.88.refs_0_), channel_id=1, source_target_pairs={{0,112},{1,113},{2,114},{3,115},{4,116},{5,117},{6,118},{7,119},{8... | collective-permute-start | bytes 196616 | tf_op jit(solution)/shard_map/ppermute | solution.py:204
  26.6 9.1 %collective-permute-start.10 = (bf16[256,128]{1,0:T(8,128)(2,1)S(1)}, bf16[256,128]{1,0:T(8,128)(2,1)S(1)}, u32[]{:S(2)}, u32[]{:S(2)}) collective-permute-start(bf16[256,128]{1,0:T(8,128)(2,1)S(1)} %shard_map.88.refs_0_), channel_id=1, source_target_pairs={{0,127},{1,114},{2,113},{3,116},{4,115},{5,118},{6,117},{7,120},{8... | collective-permute-start | bytes 196616 | tf_op jit(solution)/shard_map/ppermute | solution.py:204
  26.6 9.1 %collective-permute-start.9 = (bf16[256,128]{1,0:T(8,128)(2,1)S(1)}, bf16[256,128]{1,0:T(8,128)(2,1)S(1)}, u32[]{:S(2)}, u32[]{:S(2)}) collective-permute-start(bf16[256,128]{1,0:T(8,128)(2,1)S(1)} %shard_map.88.refs_0_), channel_id=1, source_target_pairs={{0,15},{1,2},{2,1},{3,4},{4,3},{5,6},{6,5},{7,8},{8,7},{9,10},{10,... | collective-permute-start | bytes 196616 | tf_op jit(solution)/shard_map/ppermute | solution.py:204
  40.8 8.2 %collective-permute-start.18 = (bf16[256,128]{1,0:T(8,128)(2,1)S(1)}, bf16[256,128]{1,0:T(8,128)(2,1)S(1)}, u32[]{:S(2)}, u32[]{:S(2)}) collective-permute-start(bf16[256,128]{1,0:T(8,128)(2,1)S(1)} %shard_map.89.refs_0_), channel_id=1, source_target_pairs={{0,16},{1,17},{2,18},{3,19},{4,20},{5,21},{6,22},{7,23},{8,24},{9,... | collective-permute-start | bytes 196616 | tf_op jit(solution)/shard_map/ppermute | solution.py:204
  40.9 8.2 %collective-permute-start.17 = (bf16[256,128]{1,0:T(8,128)(2,1)S(1)}, bf16[256,128]{1,0:T(8,128)(2,1)S(1)}, u32[]{:S(2)}, u32[]{:S(2)}) collective-permute-start(bf16[256,128]{1,0:T(8,128)(2,1)S(1)} %shard_map.89.refs_0_), channel_id=1, source_target_pairs={{0,112},{1,113},{2,114},{3,115},{4,116},{5,117},{6,118},{7,119},{8... | collective-permute-start | bytes 196616 | tf_op jit(solution)/shard_map/ppermute | solution.py:204
  42.6 9.4 %collective-permute-start.23 = (bf16[256,128]{1,0:T(8,128)(2,1)S(1)}, bf16[256,128]{1,0:T(8,128)(2,1)S(1)}, u32[]{:S(2)}, u32[]{:S(2)}) collective-permute-start(bf16[256,128]{1,0:T(8,128)(2,1)S(1)} %shard_map.89.refs_0_), channel_id=1, source_target_pairs={{0,127},{1,114},{2,113},{3,116},{4,115},{5,118},{6,117},{7,120},{8... | collective-permute-start | bytes 196616 | tf_op jit(solution)/shard_map/ppermute | solution.py:204
  55.9 9.6 %collective-permute-start.26 = (bf16[272,128]{1,0:T(8,128)(2,1)S(1)}, bf16[272,128]{1,0:T(8,128)(2,1)S(1)}, u32[]{:S(2)}, u32[]{:S(2)}) collective-permute-start(bf16[272,128]{1,0:T(8,128)(2,1)S(1)} %get-tuple-element.51.refs_0_), channel_id=1, source_target_pairs={{0,16},{1,17},{2,18},{3,19},{4,20},{5,21},{6,22},{7,23},{8,24},{9,... | collective-permute-start | bytes 208904 | tf_op jit(solution)/shard_map/ppermute | solution.py:204
  56.0 9.5 %collective-permute-start.25 = (bf16[272,128]{1,0:T(8,128)(2,1)S(1)}, bf16[272,128]{1,0:T(8,128)(2,1)S(1)}, u32[]{:S(2)}, u32[]{:S(2)}) collective-permute-start(bf16[272,128]{1,0:T(8,128)(2,1)S(1)} %get-tuple-element.51.refs_0_), channel_id=1, source_target_pairs={{0,112},{1,113},{2,114},{3,115},{4,116},{5,117},{6,118},{7,119},{8... | collective-permute-start | bytes 208904 | tf_op jit(solution)/shard_map/ppermute | solution.py:204
  57.8 8.1 %collective-permute-start.24 = (bf16[272,128]{1,0:T(8,128)(2,1)S(1)}, bf16[272,128]{1,0:T(8,128)(2,1)S(1)}, u32[]{:S(2)}, u32[]{:S(2)}) collective-permute-start(bf16[272,128]{1,0:T(8,128)(2,1)S(1)} %get-tuple-element.51.refs_0_), channel_id=1, source_target_pairs={{0,31},{1,18},{2,17},{3,20},{4,19},{5,22},{6,21},{7,24},{8,23},{9,... | collective-permute-start | bytes 208904 | tf_op jit(solution)/shard_map/ppermute | solution.py:204
  60.1 9.2 %collective-permute-start.31 = (bf16[272,128]{1,0:T(8,128)(2,1)S(1)}, bf16[272,128]{1,0:T(8,128)(2,1)S(1)}, u32[]{:S(2)}, u32[]{:S(2)}) collective-permute-start(bf16[272,128]{1,0:T(8,128)(2,1)S(1)} %get-tuple-element.51.refs_0_), channel_id=1, source_target_pairs={{0,127},{1,114},{2,113},{3,116},{4,115},{5,118},{6,117},{7,120},{8... | collective-permute-start | bytes 208904 | tf_op jit(solution)/shard_map/ppermute | solution.py:204
  73.6 10.0 %collective-permute-start.32 = (f32[8,128]{1,0:T(8,128)S(1)}, f32[8,128]{1,0:T(8,128)S(1)}, u32[]{:S(2)}, u32[]{:S(2)}) collective-permute-start(f32[8,128]{1,0:T(8,128)S(1)} %get-tuple-element.55), channel_id=1, source_target_pairs={{0,4},{1,5},{2,6},{3,7},{4,8},{5,9},{6,10},{7,11},{8,12},{9,13},{1... | collective-permute-start | bytes 12296 | tf_op jit(solution)/shard_map/ppermute | solution.py:227
  75.5 8.1 %collective-permute-start.39 = (bf16[256,128]{1,0:T(8,128)(2,1)S(1)}, bf16[256,128]{1,0:T(8,128)(2,1)S(1)}, u32[]{:S(2)}, u32[]{:S(2)}) collective-permute-start(bf16[256,128]{1,0:T(8,128)(2,1)S(1)} %get-tuple-element.56.refs_0_), channel_id=1, source_target_pairs={{0,16},{1,17},{2,18},{3,19},{4,20},{5,21},{6,22},{7,23},{8,24},{9,... | collective-permute-start | bytes 196616 | tf_op jit(solution)/shard_map/ppermute | solution.py:204
  75.5 8.2 %collective-permute-start.38 = (bf16[256,128]{1,0:T(8,128)(2,1)S(1)}, bf16[256,128]{1,0:T(8,128)(2,1)S(1)}, u32[]{:S(2)}, u32[]{:S(2)}) collective-permute-start(bf16[256,128]{1,0:T(8,128)(2,1)S(1)} %get-tuple-element.56.refs_0_), channel_id=1, source_target_pairs={{0,112},{1,113},{2,114},{3,115},{4,116},{5,117},{6,118},{7,119},{8... | collective-permute-start | bytes 196616 | tf_op jit(solution)/shard_map/ppermute | solution.py:204
  77.2 9.2 %collective-permute-start.37 = (bf16[256,128]{1,0:T(8,128)(2,1)S(1)}, bf16[256,128]{1,0:T(8,128)(2,1)S(1)}, u32[]{:S(2)}, u32[]{:S(2)}) collective-permute-start(bf16[256,128]{1,0:T(8,128)(2,1)S(1)} %get-tuple-element.56.refs_0_), channel_id=1, source_target_pairs={{0,127},{1,114},{2,113},{3,116},{4,115},{5,118},{6,117},{7,120},{8... | collective-permute-start | bytes 196616 | tf_op jit(solution)/shard_map/ppermute | solution.py:204
  83.6 12.6 %collective-permute-start.41 = (bf16[256,128]{1,0:T(8,128)(2,1)S(1)}, bf16[256,128]{1,0:T(8,128)(2,1)S(1)}, u32[]{:S(2)}, u32[]{:S(2)}) collective-permute-start(bf16[256,128]{1,0:T(8,128)(2,1)S(1)} %get-tuple-element.56.refs_0_), channel_id=1, source_target_pairs={{0,1},{1,0},{2,3},{3,2},{4,5},{5,4},{6,7},{7,6},{8,9},{9,8},{10,11... | collective-permute-start | bytes 196616 | tf_op jit(solution)/shard_map/ppermute | solution.py:204
  96.7 8.2 %collective-permute-start.46 = (bf16[272,128]{1,0:T(8,128)(2,1)S(1)}, bf16[272,128]{1,0:T(8,128)(2,1)S(1)}, u32[]{:S(2)}, u32[]{:S(2)}) collective-permute-start(bf16[272,128]{1,0:T(8,128)(2,1)S(1)} %shard_map.92.refs_0_), channel_id=1, source_target_pairs={{0,16},{1,17},{2,18},{3,19},{4,20},{5,21},{6,22},{7,23},{8,24},{9,... | collective-permute-start | bytes 208904 | tf_op jit(solution)/shard_map/ppermute | solution.py:204
  96.8 8.1 %collective-permute-start.45 = (bf16[272,128]{1,0:T(8,128)(2,1)S(1)}, bf16[272,128]{1,0:T(8,128)(2,1)S(1)}, u32[]{:S(2)}, u32[]{:S(2)}) collective-permute-start(bf16[272,128]{1,0:T(8,128)(2,1)S(1)} %shard_map.92.refs_0_), channel_id=1, source_target_pairs={{0,112},{1,113},{2,114},{3,115},{4,116},{5,117},{6,118},{7,119},{8... | collective-permute-start | bytes 208904 | tf_op jit(solution)/shard_map/ppermute | solution.py:204
  97.5 10.0 %collective-permute-start.51 = (bf16[272,128]{1,0:T(8,128)(2,1)S(1)}, bf16[272,128]{1,0:T(8,128)(2,1)S(1)}, u32[]{:S(2)}, u32[]{:S(2)}) collective-permute-start(bf16[272,128]{1,0:T(8,128)(2,1)S(1)} %shard_map.92.refs_0_), channel_id=1, source_target_pairs={{0,127},{1,114},{2,113},{3,116},{4,115},{5,118},{6,117},{7,120},{8... | collective-permute-start | bytes 208904 | tf_op jit(solution)/shard_map/ppermute | solution.py:204
  (35 other events, 195.4 us)

commit v6 on v5

--- a/solution.py
+++ b/solution.py
@@ -34,74 +34,55 @@
     return jnp.where(step == 1, 0, jnp.where((step == 2) == (is_odd == 0), 1, 2))
 
 
-def build_kernel(origin_ref, cols_any, count_any, blocks_any, out_ref, blocks_ref, wide_ref, cols_ref, count_ref, sems):
-    copies = [
-        pltpu.make_async_copy(blocks_any, blocks_ref, sems.at[0]),
-        pltpu.make_async_copy(cols_any, cols_ref, sems.at[1]),
-        pltpu.make_async_copy(count_any, count_ref, sems.at[2]),
-    ]
-    for copy in copies:
-        copy.start()
+def spots_of(cols, count):
+    row, col = lax.axis_index("row"), lax.axis_index("col")
+    cell_y = lax.broadcasted_iota(jnp.int32, cols.shape, 0)
+    cell_x = lax.broadcasted_iota(jnp.int32, cols.shape, 1)
+    win_y = (((cols >> LAT_X.bit_length() - 1) - row * SIDE - cell_y + REACH) & (LAT_Y - 1)) + cell_y
+    win_x = (((cols & (LAT_X - 1)) - col * SIDE - cell_x + REACH) & (LAT_X - 1)) + cell_x
+    part = role(win_x >> 1, col & 1) * 3 + role(win_y >> 1, row & 1)
+    live = lax.broadcasted_iota(jnp.int32, cols.shape, 2) < count[:, :, None]
+    return jnp.where(live, part * 2 + (win_y & 1), 2 * PARTS) * 2 + (win_x & 1)
+
+
+def build_kernel(spots_ref, blocks_ref, out_ref, wide_ref):
     out_ref[...] = jnp.zeros_like(out_ref)
-    for copy in copies:
-        copy.wait()
     wide_ref[...] = blocks_ref[...].astype(jnp.float32)
     lane_half = lax.broadcasted_iota(jnp.int32, (HALF, LANES), 1) // BLOCK
-    odd_y = origin_ref[0] % 2
-    odd_x = origin_ref[1] % 2
+    low = (lane_half == 0).astype(jnp.float32).astype(jnp.bfloat16)
+    high = (lane_half == 1).astype(jnp.float32).astype(jnp.bfloat16)
 
     def place(entry, carry):
-        loaded = []
+        stores = []
         for cell in range(CELLS):
             cell_y, cell_x = divmod(cell, SIDE)
-            col_id = cols_ref[cell_y, cell_x, entry]
-            step_y = (lax.div(col_id, LAT_X) - origin_ref[0] * SIDE - cell_y + REACH) & (LAT_Y - 1)
-            step_x = (lax.rem(col_id, LAT_X) - origin_ref[1] * SIDE - cell_x + REACH) & (LAT_X - 1)
-            win_y = step_y + cell_y
-            win_x = step_x + cell_x
-            part = role(win_x >> 1, odd_x) * 3 + role(win_y >> 1, odd_y)
-            tile = jnp.where(entry < count_ref[cell_y, cell_x], part * 2 + (win_y & 1), 2 * PARTS)
-            side = win_x & 1
+            spot = spots_ref[cell_y, cell_x, entry]
+            side = spot & 1
+            lanes = pl.ds(pl.multiple_of((spot >> 1) * LANES, LANES), LANES)
             base = pl.multiple_of((cell_y * ENTRIES + entry) * BLOCK, BLOCK)
             pair = wide_ref[pl.ds(base + cell_x, HALF, stride=2), :]
-            lanes = pl.ds(pl.multiple_of(tile * LANES, LANES), LANES)
-            spots = [(pl.ds(parity * CELLS * HALF + cell * HALF, HALF), lanes) for parity in range(2)]
-            olds = [out_ref[spot].astype(jnp.float32) for spot in spots]
-            loaded.append((side, pair, spots, olds))
-        stores = []
-        for side, pair, spots, olds in loaded:
-            turned = pltpu.roll(pair, BLOCK, 1)
-            here = lane_half == side
-            for parity in range(2):
-                new = jnp.where(side == parity, pair, turned)
-                stores.append((spots[parity], jnp.where(here, new, olds[parity]).astype(jnp.bfloat16)))
-        for spot, value in stores:
-            out_ref[spot] = value
+            mask = jnp.where(side == 0, low, high)
+            for parity, value in ((side, pair), (1 - side, pltpu.roll(pair, BLOCK, 1))):
+                rows = pl.ds(pl.multiple_of(parity * CELLS * HALF + cell * HALF, HALF), HALF)
+                stores.append(((rows, lanes), out_ref[rows, lanes] + value.astype(jnp.bfloat16) * mask))
+        for where, value in stores:
+            out_ref[where] = value
         return carry
 
-    counts = [count_ref[divmod(cell, SIDE)] for cell in range(CELLS)]
-    most = jnp.maximum(jnp.maximum(counts[0], counts[1]), jnp.maximum(counts[2], counts[3]))
-    lax.fori_loop(0, most, place, 0)
-
-
-def build(origin, blocks, cols, count):
+    lax.fori_loop(0, ENTRIES, place, 0, unroll=5)
+
+
+def build(blocks, cols, count):
     rows = blocks.reshape(SIDE, SIDE, ENTRIES, HALF, LANES).transpose(0, 2, 3, 1, 4).reshape(BLOCK_ROWS, LANES)
-    any_space = pl.BlockSpec(memory_space=pltpu.HBM)
     return pl.pallas_call(
         build_kernel,
         out_shape=jax.ShapeDtypeStruct((ROWS, DEPTH + LANES), jnp.bfloat16),
-        in_specs=[smem(), any_space, any_space, any_space],
+        in_specs=[smem(), vmem()],
         out_specs=vmem(),
-        scratch_shapes=[
-            pltpu.VMEM(rows.shape, jnp.bfloat16),
-            pltpu.VMEM(rows.shape, jnp.float32),
-            pltpu.SMEM(cols.shape, jnp.int32),
-            pltpu.SMEM(count.shape, jnp.int32),
-            pltpu.SemaphoreType.DMA((3,)),
-        ],
+        scratch_shapes=[pltpu.VMEM(rows.shape, jnp.float32)],
         compiler_params=pltpu.CompilerParams(vmem_limit_bytes=16 * 2**20),
         cost_estimate=pl.CostEstimate(flops=10_000_000, bytes_accessed=4_000_000, transcendentals=0),
-    )(origin, cols, count, rows)
+    )(spots_of(cols, count), rows)
 
 
 def product(mat_ref, part_refs, turn_ref):
@@ -228,18 +209,17 @@
 
 
 def body(x_slab, h_blocks, h_cols, h_count, z_blocks, z_cols, z_count):
-    origin = jnp.stack([lax.axis_index("row"), lax.axis_index("col")]).astype(jnp.int32)
-    z_mat = build(origin, z_blocks, z_cols, z_count)
-    h_mat = build(origin, h_blocks, h_cols, h_count)
+    z_mat = build(z_blocks, z_cols, z_count)
+    h_mat = build(h_blocks, h_cols, h_count)
     flat = jax.ShapeDtypeStruct((ROWS, SLAB), jnp.bfloat16)
     wide = jax.ShapeDtypeStruct((ROWS, SLAB), jnp.float32)
     sums_shape = jax.ShapeDtypeStruct((8, SLAB), jnp.float32)
     noted = jax.ShapeDtypeStruct((ROWS + NOTE, SLAB), jnp.bfloat16)
     slab = x_slab.reshape(ROWS, SLAB)
 
-    parts, (z_mat,) = surround(slab, late=(z_mat,))
+    parts, _ = surround(slab, whole=False)
     u_one = apply(root_kernel, flat, z_mat, *parts)
-    parts, (h_mat,) = surround(u_one, late=(h_mat,))
+    parts, _ = surround(u_one, whole=False)
     u_two = apply(hamilton_kernel, flat, h_mat, *parts)
     parts, _ = surround(u_two, whole=False)
     power, power_full = apply(power_kernel, (noted, wide), z_mat, slab, *parts)

time: 113 us -> 108 us (0.956)
  waiting for transfers between devices: 36 us -> 32.3 us
  Pallas kernels: 8.88 us -> 6.92 us
  starting transfers between devices: 63.4 us -> 65.3 us
  local copies, waits for them, and re-layouts: 2.53 us -> 1.17 us
    ppermute x48, waiting for transfers between devices: 30.8 us -> 27.7 us  [swap(): return lax.ppermute(value, ('row', 'col'), pairs)]
    pallas_call x2, Pallas kernels: 5.16 us -> 3.22 us  [build(): pl.pallas_call(build_kernel, out_shape=jax.ShapeDtypeStruct((ROWS, DEPTH...]
    unnamed x14 -> x10, local copies, waits for them, and re-layouts: 2.53 us -> 1.17 us
    ppermute x48, starting transfers between devices: 61.4 us -> 62.7 us  [swap(): return lax.ppermute(value, ('row', 'col'), pairs)]
  transfers between devices with their start and end apart: 52 -> 52, of which waited for: 20 -> 16; matrix products, arithmetic and copies ran while one was open for 0% -> 1% of each run, Pallas kernels for 5% -> 3%
where the time goes in v6:
time: 108 us; the launch traced here: 107 us
  starting transfers between devices  65.3 us (60%)
  waiting for transfers between devices  32.3 us (30%)
  Pallas kernels  6.92 us (6%)
  local copies, waits for them, and re-layouts  1.17 us (1%)
    ppermute x48, starting transfers between devices, swap(): return lax.ppermute(value, ('row', 'col'), pairs)  62.7 us
    ppermute x48, waiting for transfers between devices, swap(): return lax.ppermute(value, ('row', 'col'), pairs)  27.7 us
    ppermute x4, waiting for transfers between devices, shifted(): lax.ppermute(sums, axis, [(i, (i + step) % count) for i in range(count)])  4.61 us
    pallas_call x6, Pallas kernels, apply(): pl.pallas_call(kernel, out_shape=outs, in_specs=[vmem()] * len(operands),...  3.7 us
    pallas_call x2, Pallas kernels, build(): pl.pallas_call(build_kernel, out_shape=jax.ShapeDtypeStruct((ROWS, DEPTH...  3.22 us
    ppermute x4, starting transfers between devices, shifted(): lax.ppermute(sums, axis, [(i, (i + step) % count) for i in range(count)])  2.59 us
  transfers between devices with their start and end apart: 52, of which 16 were waited for; matrix products, arithmetic and copies ran while one was open for 1% of the time, Pallas kernels for 3%

profile of v6, /device:TPU:0, one launch (start us, length us, event | category | flops | bytes accessed | tf_op | source)
XLA Modules:
  0.0 107.4 jit_solution(2057352636548679162)
XLA Ops:
  2.4 2.6 %collective-permute-start.1 = (bf16[256,128]{1,0:T(8,128)(2,1)}, bf16[256,128]{1,0:T(8,128)(2,1)S(1)}, u32[]{:S(2)}, u32[]{:S(2)}) collective-permute-start(bf16[256,128]{1,0:T(8,128)(2,1)} %bitcast.16), channel_id=1, source_target_pairs={{0,112},{1,113},{2,114},{3,115},{4,116},{5,117},{6,118},{7,119},{8... | collective-permute-start | bytes 196616 | tf_op jit(solution)/shard_map/ppermute | solution.py:185
  5.0 4.1 %collective-permute-start = (bf16[256,128]{1,0:T(8,128)(2,1)}, bf16[256,128]{1,0:T(8,128)(2,1)S(1)}, u32[]{:S(2)}, u32[]{:S(2)}) collective-permute-start(bf16[256,128]{1,0:T(8,128)(2,1)} %bitcast.17), channel_id=1, source_target_pairs={{0,31},{1,18},{2,17},{3,20},{4,19},{5,22},{6,21},{7,24},{8,23},{9,... | collective-permute-start | bytes 196616 | tf_op jit(solution)/shard_map/ppermute | solution.py:185
  10.3 4.3 %collective-permute-start.6 = (bf16[256,128]{1,0:T(8,128)(2,1)}, bf16[256,128]{1,0:T(8,128)(2,1)S(1)}, u32[]{:S(2)}, u32[]{:S(2)}) collective-permute-start(bf16[256,128]{1,0:T(8,128)(2,1)} %bitcast.19), channel_id=1, source_target_pairs={{0,15},{1,2},{2,1},{3,4},{4,3},{5,6},{6,5},{7,8},{8,7},{9,10},{10,... | collective-permute-start | bytes 196616 | tf_op jit(solution)/shard_map/ppermute | solution.py:185
  22.4 2.9 %collective-permute-start.8 = (bf16[256,128]{1,0:T(8,128)(2,1)S(1)}, bf16[256,128]{1,0:T(8,128)(2,1)S(1)}, u32[]{:S(2)}, u32[]{:S(2)}) collective-permute-start(bf16[256,128]{1,0:T(8,128)(2,1)S(1)} %shard_map.88.refs_0_), channel_id=1, source_target_pairs={{0,31},{1,18},{2,17},{3,20},{4,19},{5,22},{6,21},{7,24},{8,23},{9,... | collective-permute-start | bytes 196616 | tf_op jit(solution)/shard_map/ppermute | solution.py:185
  25.3 2.9 %collective-permute-start.15 = (bf16[256,128]{1,0:T(8,128)(2,1)S(1)}, bf16[256,128]{1,0:T(8,128)(2,1)S(1)}, u32[]{:S(2)}, u32[]{:S(2)}) collective-permute-start(bf16[256,128]{1,0:T(8,128)(2,1)S(1)} %shard_map.88.refs_0_), channel_id=1, source_target_pairs={{0,127},{1,114},{2,113},{3,116},{4,115},{5,118},{6,117},{7,120},{8... | collective-permute-start | bytes 196616 | tf_op jit(solution)/shard_map/ppermute | solution.py:185
  32.1 2.4 %collective-permute-done.15.refs_8_ = bf16[256,128]{1,0:T(8,128)(2,1)S(1)} collective-permute-done((bf16[256,128]{1,0:T(8,128)(2,1)S(1)}, bf16[256,128]{1,0:T(8,128)(2,1)S(1)}, u32[]{:S(2)}, u32[]{:S(2)}) %collective-permute-start.15) | collective-permute-done | bytes 65568 | tf_op jit(solution)/shard_map/ppermute | solution.py:185
  36.1 2.6 %collective-permute-start.17 = (bf16[256,128]{1,0:T(8,128)(2,1)S(1)}, bf16[256,128]{1,0:T(8,128)(2,1)S(1)}, u32[]{:S(2)}, u32[]{:S(2)}) collective-permute-start(bf16[256,128]{1,0:T(8,128)(2,1)S(1)} %shard_map.89.refs_0_), channel_id=1, source_target_pairs={{0,112},{1,113},{2,114},{3,115},{4,116},{5,117},{6,118},{7,119},{8... | collective-permute-start | bytes 196616 | tf_op jit(solution)/shard_map/ppermute | solution.py:185
  38.7 1.9 %collective-permute-start.16 = (bf16[256,128]{1,0:T(8,128)(2,1)S(1)}, bf16[256,128]{1,0:T(8,128)(2,1)S(1)}, u32[]{:S(2)}, u32[]{:S(2)}) collective-permute-start(bf16[256,128]{1,0:T(8,128)(2,1)S(1)} %shard_map.89.refs_0_), channel_id=1, source_target_pairs={{0,31},{1,18},{2,17},{3,20},{4,19},{5,22},{6,21},{7,24},{8,23},{9,... | collective-permute-start | bytes 196616 | tf_op jit(solution)/shard_map/ppermute | solution.py:185
  40.6 3.7 %collective-permute-start.23 = (bf16[256,128]{1,0:T(8,128)(2,1)S(1)}, bf16[256,128]{1,0:T(8,128)(2,1)S(1)}, u32[]{:S(2)}, u32[]{:S(2)}) collective-permute-start(bf16[256,128]{1,0:T(8,128)(2,1)S(1)} %shard_map.89.refs_0_), channel_id=1, source_target_pairs={{0,127},{1,114},{2,113},{3,116},{4,115},{5,118},{6,117},{7,120},{8... | collective-permute-start | bytes 196616 | tf_op jit(solution)/shard_map/ppermute | solution.py:185
  47.6 2.1 %collective-permute-done.23.refs_8_ = bf16[256,128]{1,0:T(8,128)(2,1)S(1)} collective-permute-done((bf16[256,128]{1,0:T(8,128)(2,1)S(1)}, bf16[256,128]{1,0:T(8,128)(2,1)S(1)}, u32[]{:S(2)}, u32[]{:S(2)}) %collective-permute-start.23) | collective-permute-done | bytes 65568 | tf_op jit(solution)/shard_map/ppermute | solution.py:185
  49.7 1.9 %collective-permute-done.22.refs_6_ = bf16[256,128]{1,0:T(8,128)(2,1)S(1)} collective-permute-done((bf16[256,128]{1,0:T(8,128)(2,1)S(1)}, bf16[256,128]{1,0:T(8,128)(2,1)S(1)}, u32[]{:S(2)}, u32[]{:S(2)}) %collective-permute-start.22) | collective-permute-done | bytes 65568 | tf_op jit(solution)/shard_map/ppermute | solution.py:185
  52.3 2.6 %collective-permute-start.25 = (bf16[272,128]{1,0:T(8,128)(2,1)S(1)}, bf16[272,128]{1,0:T(8,128)(2,1)S(1)}, u32[]{:S(2)}, u32[]{:S(2)}) collective-permute-start(bf16[272,128]{1,0:T(8,128)(2,1)S(1)} %get-tuple-element.39.refs_0_), channel_id=1, source_target_pairs={{0,112},{1,113},{2,114},{3,115},{4,116},{5,117},{6,118},{7,119},{8... | collective-permute-start | bytes 208904 | tf_op jit(solution)/shard_map/ppermute | solution.py:185
  56.7 4.0 %collective-permute-start.31 = (bf16[272,128]{1,0:T(8,128)(2,1)S(1)}, bf16[272,128]{1,0:T(8,128)(2,1)S(1)}, u32[]{:S(2)}, u32[]{:S(2)}) collective-permute-start(bf16[272,128]{1,0:T(8,128)(2,1)S(1)} %get-tuple-element.39.refs_0_), channel_id=1, source_target_pairs={{0,127},{1,114},{2,113},{3,116},{4,115},{5,118},{6,117},{7,120},{8... | collective-permute-start | bytes 208904 | tf_op jit(solution)/shard_map/ppermute | solution.py:185
  62.5 3.3 %collective-permute-done.31.refs_8_ = bf16[272,128]{1,0:T(8,128)(2,1)S(1)} collective-permute-done((bf16[272,128]{1,0:T(8,128)(2,1)S(1)}, bf16[272,128]{1,0:T(8,128)(2,1)S(1)}, u32[]{:S(2)}, u32[]{:S(2)}) %collective-permute-start.31) | collective-permute-done | bytes 69664 | tf_op jit(solution)/shard_map/ppermute | solution.py:185
  65.9 2.2 %collective-permute-done.30.refs_6_ = bf16[272,128]{1,0:T(8,128)(2,1)S(1)} collective-permute-done((bf16[272,128]{1,0:T(8,128)(2,1)S(1)}, bf16[272,128]{1,0:T(8,128)(2,1)S(1)}, u32[]{:S(2)}, u32[]{:S(2)}) %collective-permute-start.30) | collective-permute-done | bytes 69664 | tf_op jit(solution)/shard_map/ppermute | solution.py:185
  70.6 2.6 %collective-permute-start.38 = (bf16[256,128]{1,0:T(8,128)(2,1)S(1)}, bf16[256,128]{1,0:T(8,128)(2,1)S(1)}, u32[]{:S(2)}, u32[]{:S(2)}) collective-permute-start(bf16[256,128]{1,0:T(8,128)(2,1)S(1)} %get-tuple-element.44.refs_0_), channel_id=1, source_target_pairs={{0,112},{1,113},{2,114},{3,115},{4,116},{5,117},{6,118},{7,119},{8... | collective-permute-start | bytes 196616 | tf_op jit(solution)/shard_map/ppermute | solution.py:185
  73.2 2.9 %collective-permute-start.37 = (bf16[256,128]{1,0:T(8,128)(2,1)S(1)}, bf16[256,128]{1,0:T(8,128)(2,1)S(1)}, u32[]{:S(2)}, u32[]{:S(2)}) collective-permute-start(bf16[256,128]{1,0:T(8,128)(2,1)S(1)} %get-tuple-element.44.refs_0_), channel_id=1, source_target_pairs={{0,127},{1,114},{2,113},{3,116},{4,115},{5,118},{6,117},{7,120},{8... | collective-permute-start | bytes 196616 | tf_op jit(solution)/shard_map/ppermute | solution.py:185
  76.1 2.6 %collective-permute-start.36 = (bf16[256,128]{1,0:T(8,128)(2,1)S(1)}, bf16[256,128]{1,0:T(8,128)(2,1)S(1)}, u32[]{:S(2)}, u32[]{:S(2)}) collective-permute-start(bf16[256,128]{1,0:T(8,128)(2,1)S(1)} %get-tuple-element.44.refs_0_), channel_id=1, source_target_pairs={{0,15},{1,2},{2,1},{3,4},{4,3},{5,6},{6,5},{7,8},{8,7},{9,10},{10,... | collective-permute-start | bytes 196616 | tf_op jit(solution)/shard_map/ppermute | solution.py:185
  79.2 3.1 %collective-permute-done.37.refs_8_ = bf16[256,128]{1,0:T(8,128)(2,1)S(1)} collective-permute-done((bf16[256,128]{1,0:T(8,128)(2,1)S(1)}, bf16[256,128]{1,0:T(8,128)(2,1)S(1)}, u32[]{:S(2)}, u32[]{:S(2)}) %collective-permute-start.37) | collective-permute-done | bytes 65568 | tf_op jit(solution)/shard_map/ppermute | solution.py:185
  83.4 2.3 %collective-permute-done.35.refs_7_ = bf16[256,128]{1,0:T(8,128)(2,1)S(1)} collective-permute-done((bf16[256,128]{1,0:T(8,128)(2,1)S(1)}, bf16[256,128]{1,0:T(8,128)(2,1)S(1)}, u32[]{:S(2)}, u32[]{:S(2)}) %collective-permute-start.35) | collective-permute-done | bytes 65568 | tf_op jit(solution)/shard_map/ppermute | solution.py:185
  86.7 4.6 %collective-permute-done.40.other_ref = f32[8,128]{1,0:T(8,128)S(1)} collective-permute-done((f32[8,128]{1,0:T(8,128)S(1)}, f32[8,128]{1,0:T(8,128)S(1)}, u32[]{:S(2)}, u32[]{:S(2)}) %collective-permute-start.40) | collective-permute-done | bytes 4128 | tf_op jit(solution)/shard_map/ppermute | solution.py:208
  93.4 5.5 %collective-permute-start.51 = (bf16[272,128]{1,0:T(8,128)(2,1)S(1)}, bf16[272,128]{1,0:T(8,128)(2,1)S(1)}, u32[]{:S(2)}, u32[]{:S(2)}) collective-permute-start(bf16[272,128]{1,0:T(8,128)(2,1)S(1)} %shard_map.92.refs_0_), channel_id=1, source_target_pairs={{0,127},{1,114},{2,113},{3,116},{4,115},{5,118},{6,117},{7,120},{8... | collective-permute-start | bytes 208904 | tf_op jit(solution)/shard_map/ppermute | solution.py:185
  100.9 2.9 %collective-permute-done.51.refs_8_ = bf16[272,128]{1,0:T(8,128)(2,1)S(1)} collective-permute-done((bf16[272,128]{1,0:T(8,128)(2,1)S(1)}, bf16[272,128]{1,0:T(8,128)(2,1)S(1)}, u32[]{:S(2)}, u32[]{:S(2)}) %collective-permute-start.51) | collective-permute-done | bytes 69664 | tf_op jit(solution)/shard_map/ppermute | solution.py:185
  103.8 2.4 %collective-permute-done.50.refs_6_ = bf16[272,128]{1,0:T(8,128)(2,1)S(1)} collective-permute-done((bf16[272,128]{1,0:T(8,128)(2,1)S(1)}, bf16[272,128]{1,0:T(8,128)(2,1)S(1)}, u32[]{:S(2)}, u32[]{:S(2)}) %collective-permute-start.50) | collective-permute-done | bytes 69664 | tf_op jit(solution)/shard_map/ppermute | solution.py:185
  (101 shorter events, 34.1 us)
Async XLA Ops:
  0.6 14.1 %collective-permute-start.2 = (bf16[256,128]{1,0:T(8,128)(2,1)}, bf16[256,128]{1,0:T(8,128)(2,1)S(1)}, u32[]{:S(2)}, u32[]{:S(2)}) collective-permute-start(bf16[256,128]{1,0:T(8,128)(2,1)} %bitcast.15), channel_id=1, source_target_pairs={{0,16},{1,17},{2,18},{3,19},{4,20},{5,21},{6,22},{7,23},{8,24},{9,... | collective-permute-start | bytes 196616 | tf_op jit(solution)/shard_map/ppermute | solution.py:185
  2.4 12.3 %collective-permute-start.1 = (bf16[256,128]{1,0:T(8,128)(2,1)}, bf16[256,128]{1,0:T(8,128)(2,1)S(1)}, u32[]{:S(2)}, u32[]{:S(2)}) collective-permute-start(bf16[256,128]{1,0:T(8,128)(2,1)} %bitcast.16), channel_id=1, source_target_pairs={{0,112},{1,113},{2,114},{3,115},{4,116},{5,117},{6,118},{7,119},{8... | collective-permute-start | bytes 196616 | tf_op jit(solution)/shard_map/ppermute | solution.py:185
  5.0 9.7 %collective-permute-start = (bf16[256,128]{1,0:T(8,128)(2,1)}, bf16[256,128]{1,0:T(8,128)(2,1)S(1)}, u32[]{:S(2)}, u32[]{:S(2)}) collective-permute-start(bf16[256,128]{1,0:T(8,128)(2,1)} %bitcast.17), channel_id=1, source_target_pairs={{0,31},{1,18},{2,17},{3,20},{4,19},{5,22},{6,21},{7,24},{8,23},{9,... | collective-permute-start | bytes 196616 | tf_op jit(solution)/shard_map/ppermute | solution.py:185
  9.1 10.1 %collective-permute-start.7 = (bf16[256,128]{1,0:T(8,128)(2,1)}, bf16[256,128]{1,0:T(8,128)(2,1)S(1)}, u32[]{:S(2)}, u32[]{:S(2)}) collective-permute-start(bf16[256,128]{1,0:T(8,128)(2,1)} %bitcast.18), channel_id=1, source_target_pairs={{0,127},{1,114},{2,113},{3,116},{4,115},{5,118},{6,117},{7,120},{8... | collective-permute-start | bytes 196616 | tf_op jit(solution)/shard_map/ppermute | solution.py:185
  10.3 8.9 %collective-permute-start.6 = (bf16[256,128]{1,0:T(8,128)(2,1)}, bf16[256,128]{1,0:T(8,128)(2,1)S(1)}, u32[]{:S(2)}, u32[]{:S(2)}) collective-permute-start(bf16[256,128]{1,0:T(8,128)(2,1)} %bitcast.19), channel_id=1, source_target_pairs={{0,15},{1,2},{2,1},{3,4},{4,3},{5,6},{6,5},{7,8},{8,7},{9,10},{10,... | collective-permute-start | bytes 196616 | tf_op jit(solution)/shard_map/ppermute | solution.py:185
  19.7 10.0 %collective-permute-start.10 = (bf16[256,128]{1,0:T(8,128)(2,1)S(1)}, bf16[256,128]{1,0:T(8,128)(2,1)S(1)}, u32[]{:S(2)}, u32[]{:S(2)}) collective-permute-start(bf16[256,128]{1,0:T(8,128)(2,1)S(1)} %shard_map.88.refs_0_), channel_id=1, source_target_pairs={{0,16},{1,17},{2,18},{3,19},{4,20},{5,21},{6,22},{7,23},{8,24},{9,... | collective-permute-start | bytes 196616 | tf_op jit(solution)/shard_map/ppermute | solution.py:185
  20.8 9.0 %collective-permute-start.9 = (bf16[256,128]{1,0:T(8,128)(2,1)S(1)}, bf16[256,128]{1,0:T(8,128)(2,1)S(1)}, u32[]{:S(2)}, u32[]{:S(2)}) collective-permute-start(bf16[256,128]{1,0:T(8,128)(2,1)S(1)} %shard_map.88.refs_0_), channel_id=1, source_target_pairs={{0,112},{1,113},{2,114},{3,115},{4,116},{5,117},{6,118},{7,119},{8... | collective-permute-start | bytes 196616 | tf_op jit(solution)/shard_map/ppermute | solution.py:185
  25.3 9.1 %collective-permute-start.15 = (bf16[256,128]{1,0:T(8,128)(2,1)S(1)}, bf16[256,128]{1,0:T(8,128)(2,1)S(1)}, u32[]{:S(2)}, u32[]{:S(2)}) collective-permute-start(bf16[256,128]{1,0:T(8,128)(2,1)S(1)} %shard_map.88.refs_0_), channel_id=1, source_target_pairs={{0,127},{1,114},{2,113},{3,116},{4,115},{5,118},{6,117},{7,120},{8... | collective-permute-start | bytes 196616 | tf_op jit(solution)/shard_map/ppermute | solution.py:185
  36.0 9.8 %collective-permute-start.18 = (bf16[256,128]{1,0:T(8,128)(2,1)S(1)}, bf16[256,128]{1,0:T(8,128)(2,1)S(1)}, u32[]{:S(2)}, u32[]{:S(2)}) collective-permute-start(bf16[256,128]{1,0:T(8,128)(2,1)S(1)} %shard_map.89.refs_0_), channel_id=1, source_target_pairs={{0,16},{1,17},{2,18},{3,19},{4,20},{5,21},{6,22},{7,23},{8,24},{9,... | collective-permute-start | bytes 196616 | tf_op jit(solution)/shard_map/ppermute | solution.py:185
  36.1 9.7 %collective-permute-start.17 = (bf16[256,128]{1,0:T(8,128)(2,1)S(1)}, bf16[256,128]{1,0:T(8,128)(2,1)S(1)}, u32[]{:S(2)}, u32[]{:S(2)}) collective-permute-start(bf16[256,128]{1,0:T(8,128)(2,1)S(1)} %shard_map.89.refs_0_), channel_id=1, source_target_pairs={{0,112},{1,113},{2,114},{3,115},{4,116},{5,117},{6,118},{7,119},{8... | collective-permute-start | bytes 196616 | tf_op jit(solution)/shard_map/ppermute | solution.py:185
  38.7 8.4 %collective-permute-start.16 = (bf16[256,128]{1,0:T(8,128)(2,1)S(1)}, bf16[256,128]{1,0:T(8,128)(2,1)S(1)}, u32[]{:S(2)}, u32[]{:S(2)}) collective-permute-start(bf16[256,128]{1,0:T(8,128)(2,1)S(1)} %shard_map.89.refs_0_), channel_id=1, source_target_pairs={{0,31},{1,18},{2,17},{3,20},{4,19},{5,22},{6,21},{7,24},{8,23},{9,... | collective-permute-start | bytes 196616 | tf_op jit(solution)/shard_map/ppermute | solution.py:185
  40.6 9.1 %collective-permute-start.23 = (bf16[256,128]{1,0:T(8,128)(2,1)S(1)}, bf16[256,128]{1,0:T(8,128)(2,1)S(1)}, u32[]{:S(2)}, u32[]{:S(2)}) collective-permute-start(bf16[256,128]{1,0:T(8,128)(2,1)S(1)} %shard_map.89.refs_0_), channel_id=1, source_target_pairs={{0,127},{1,114},{2,113},{3,116},{4,115},{5,118},{6,117},{7,120},{8... | collective-permute-start | bytes 196616 | tf_op jit(solution)/shard_map/ppermute | solution.py:185
  52.2 8.9 %collective-permute-start.26 = (bf16[272,128]{1,0:T(8,128)(2,1)S(1)}, bf16[272,128]{1,0:T(8,128)(2,1)S(1)}, u32[]{:S(2)}, u32[]{:S(2)}) collective-permute-start(bf16[272,128]{1,0:T(8,128)(2,1)S(1)} %get-tuple-element.39.refs_0_), channel_id=1, source_target_pairs={{0,16},{1,17},{2,18},{3,19},{4,20},{5,21},{6,22},{7,23},{8,24},{9,... | collective-permute-start | bytes 208904 | tf_op jit(solution)/shard_map/ppermute | solution.py:185
  52.3 8.8 %collective-permute-start.25 = (bf16[272,128]{1,0:T(8,128)(2,1)S(1)}, bf16[272,128]{1,0:T(8,128)(2,1)S(1)}, u32[]{:S(2)}, u32[]{:S(2)}) collective-permute-start(bf16[272,128]{1,0:T(8,128)(2,1)S(1)} %get-tuple-element.39.refs_0_), channel_id=1, source_target_pairs={{0,112},{1,113},{2,114},{3,115},{4,116},{5,117},{6,118},{7,119},{8... | collective-permute-start | bytes 208904 | tf_op jit(solution)/shard_map/ppermute | solution.py:185
  56.7 9.2 %collective-permute-start.31 = (bf16[272,128]{1,0:T(8,128)(2,1)S(1)}, bf16[272,128]{1,0:T(8,128)(2,1)S(1)}, u32[]{:S(2)}, u32[]{:S(2)}) collective-permute-start(bf16[272,128]{1,0:T(8,128)(2,1)S(1)} %get-tuple-element.39.refs_0_), channel_id=1, source_target_pairs={{0,127},{1,114},{2,113},{3,116},{4,115},{5,118},{6,117},{7,120},{8... | collective-permute-start | bytes 208904 | tf_op jit(solution)/shard_map/ppermute | solution.py:185
  68.6 7.5 %collective-permute-start.33 = (f32[8,128]{1,0:T(8,128)S(1)}, f32[8,128]{1,0:T(8,128)S(1)}, u32[]{:S(2)}, u32[]{:S(2)}) collective-permute-start(f32[8,128]{1,0:T(8,128)S(1)} %get-tuple-element.43), channel_id=1, source_target_pairs={{0,8},{1,9},{2,10},{3,11},{4,12},{5,13},{6,14},{7,15},{8,0},{9,1},... | collective-permute-start | bytes 12296 | tf_op jit(solution)/shard_map/ppermute | solution.py:208
  68.9 9.8 %collective-permute-start.32 = (f32[8,128]{1,0:T(8,128)S(1)}, f32[8,128]{1,0:T(8,128)S(1)}, u32[]{:S(2)}, u32[]{:S(2)}) collective-permute-start(f32[8,128]{1,0:T(8,128)S(1)} %get-tuple-element.43), channel_id=1, source_target_pairs={{0,4},{1,5},{2,6},{3,7},{4,8},{5,9},{6,10},{7,11},{8,12},{9,13},{1... | collective-permute-start | bytes 12296 | tf_op jit(solution)/shard_map/ppermute | solution.py:208
  70.6 8.5 %collective-permute-start.39 = (bf16[256,128]{1,0:T(8,128)(2,1)S(1)}, bf16[256,128]{1,0:T(8,128)(2,1)S(1)}, u32[]{:S(2)}, u32[]{:S(2)}) collective-permute-start(bf16[256,128]{1,0:T(8,128)(2,1)S(1)} %get-tuple-element.44.refs_0_), channel_id=1, source_target_pairs={{0,16},{1,17},{2,18},{3,19},{4,20},{5,21},{6,22},{7,23},{8,24},{9,... | collective-permute-start | bytes 196616 | tf_op jit(solution)/shard_map/ppermute | solution.py:185
  70.6 8.6 %collective-permute-start.38 = (bf16[256,128]{1,0:T(8,128)(2,1)S(1)}, bf16[256,128]{1,0:T(8,128)(2,1)S(1)}, u32[]{:S(2)}, u32[]{:S(2)}) collective-permute-start(bf16[256,128]{1,0:T(8,128)(2,1)S(1)} %get-tuple-element.44.refs_0_), channel_id=1, source_target_pairs={{0,112},{1,113},{2,114},{3,115},{4,116},{5,117},{6,118},{7,119},{8... | collective-permute-start | bytes 196616 | tf_op jit(solution)/shard_map/ppermute | solution.py:185
  73.2 9.1 %collective-permute-start.37 = (bf16[256,128]{1,0:T(8,128)(2,1)S(1)}, bf16[256,128]{1,0:T(8,128)(2,1)S(1)}, u32[]{:S(2)}, u32[]{:S(2)}) collective-permute-start(bf16[256,128]{1,0:T(8,128)(2,1)S(1)} %get-tuple-element.44.refs_0_), channel_id=1, source_target_pairs={{0,127},{1,114},{2,113},{3,116},{4,115},{5,118},{6,117},{7,120},{8... | collective-permute-start | bytes 196616 | tf_op jit(solution)/shard_map/ppermute | solution.py:185
  79.1 12.2 %collective-permute-start.41 = (bf16[256,128]{1,0:T(8,128)(2,1)S(1)}, bf16[256,128]{1,0:T(8,128)(2,1)S(1)}, u32[]{:S(2)}, u32[]{:S(2)}) collective-permute-start(bf16[256,128]{1,0:T(8,128)(2,1)S(1)} %get-tuple-element.44.refs_0_), channel_id=1, source_target_pairs={{0,1},{1,0},{2,3},{3,2},{4,5},{5,4},{6,7},{7,6},{8,9},{9,8},{10,11... | collective-permute-start | bytes 196616 | tf_op jit(solution)/shard_map/ppermute | solution.py:185
  91.8 8.2 %collective-permute-start.46 = (bf16[272,128]{1,0:T(8,128)(2,1)S(1)}, bf16[272,128]{1,0:T(8,128)(2,1)S(1)}, u32[]{:S(2)}, u32[]{:S(2)}) collective-permute-start(bf16[272,128]{1,0:T(8,128)(2,1)S(1)} %shard_map.92.refs_0_), channel_id=1, source_target_pairs={{0,16},{1,17},{2,18},{3,19},{4,20},{5,21},{6,22},{7,23},{8,24},{9,... | collective-permute-start | bytes 208904 | tf_op jit(solution)/shard_map/ppermute | solution.py:185
  91.9 8.1 %collective-permute-start.45 = (bf16[272,128]{1,0:T(8,128)(2,1)S(1)}, bf16[272,128]{1,0:T(8,128)(2,1)S(1)}, u32[]{:S(2)}, u32[]{:S(2)}) collective-permute-start(bf16[272,128]{1,0:T(8,128)(2,1)S(1)} %shard_map.92.refs_0_), channel_id=1, source_target_pairs={{0,112},{1,113},{2,114},{3,115},{4,116},{5,117},{6,118},{7,119},{8... | collective-permute-start | bytes 208904 | tf_op jit(solution)/shard_map/ppermute | solution.py:185
  93.4 10.4 %collective-permute-start.51 = (bf16[272,128]{1,0:T(8,128)(2,1)S(1)}, bf16[272,128]{1,0:T(8,128)(2,1)S(1)}, u32[]{:S(2)}, u32[]{:S(2)}) collective-permute-start(bf16[272,128]{1,0:T(8,128)(2,1)S(1)} %shard_map.92.refs_0_), channel_id=1, source_target_pairs={{0,127},{1,114},{2,113},{3,116},{4,115},{5,118},{6,117},{7,120},{8... | collective-permute-start | bytes 208904 | tf_op jit(solution)/shard_map/ppermute | solution.py:185
  (33 other events, 205.4 us)

commit v7 on v6

--- a/solution.py
+++ b/solution.py
@@ -185,22 +185,16 @@
     return lax.ppermute(value, ("row", "col"), pairs)
 
 
-def surround(field, late=(), whole=True):
+def surround(field):
+    across_same = swap(field, same, cross)
     near_y = swap(field, near, same)
     far_y = swap(field, cross, same)
-    across_far = swap(field, cross, cross)
-    across_same = swap(field, same, cross)
-    across_near = swap(field, near, cross)
     beside = swap(field, same, near)
-    if whole:
-        *late, across_near, across_same, across_far, far_y, near_y = lax.optimization_barrier(
-            (*late, across_near, across_same, across_far, far_y, near_y)
-        )
-    else:
-        across_near, far_y, near_y = lax.optimization_barrier((across_near, far_y, near_y))
     beside_near = swap(near_y, same, near)
     beside_far = swap(far_y, same, near)
-    return [field, near_y, far_y, beside, beside_near, beside_far, across_same, across_near, across_far], late
+    across_far = swap(across_same, cross, same)
+    across_near = swap(across_same, near, same)
+    return [field, near_y, far_y, beside, beside_near, beside_far, across_same, across_near, across_far]
 
 
 def shifted(sums, axis, step):
@@ -217,21 +211,15 @@
     noted = jax.ShapeDtypeStruct((ROWS + NOTE, SLAB), jnp.bfloat16)
     slab = x_slab.reshape(ROWS, SLAB)
 
-    parts, _ = surround(slab, whole=False)
-    u_one = apply(root_kernel, flat, z_mat, *parts)
-    parts, _ = surround(u_one, whole=False)
-    u_two = apply(hamilton_kernel, flat, h_mat, *parts)
-    parts, _ = surround(u_two, whole=False)
-    power, power_full = apply(power_kernel, (noted, wide), z_mat, slab, *parts)
-
-    parts, _ = surround(power, whole=False)
-    v_one, sums = apply(root_sums_kernel, (flat, sums_shape), z_mat, *parts)
+    u_one = apply(root_kernel, flat, z_mat, *surround(slab))
+    u_two = apply(hamilton_kernel, flat, h_mat, *surround(u_one))
+    power, power_full = apply(power_kernel, (noted, wide), z_mat, slab, *surround(u_two))
+
+    v_one, sums = apply(root_sums_kernel, (flat, sums_shape), z_mat, *surround(power))
     ring = sums + shifted(sums, "col", 4) + shifted(sums, "col", 8) + shifted(sums, "col", 12)
     other = shifted(ring, "row", 4)
-    parts, (ring,) = surround(v_one, late=(ring,))
-    v_two = apply(hamilton_sums_kernel, noted, h_mat, ring, other, *parts)
-    parts, _ = surround(v_two, whole=False)
-    one, two = apply(last_kernel, (flat, flat), z_mat, slab, power_full, *parts)
+    v_two = apply(hamilton_sums_kernel, noted, h_mat, ring, other, *surround(v_one))
+    one, two = apply(last_kernel, (flat, flat), z_mat, slab, power_full, *surround(v_two))
     return one.reshape(x_slab.shape), two.reshape(x_slab.shape)
 
 

time: 108 us -> 100 us (0.926)
  starting transfers between devices: 65.3 us -> 52 us
  waiting for transfers between devices: 32.3 us -> 38 us
    ppermute x48, starting transfers between devices: 62.7 us -> 49 us  [swap(): return lax.ppermute(value, ('row', 'col'), pairs)]
    ppermute x48, waiting for transfers between devices: 27.7 us -> 38 us  [swap(): return lax.ppermute(value, ('row', 'col'), pairs)]
    ppermute x4, waiting for transfers between devices: 4.61 us -> 0.01 us  [shifted(): lax.ppermute(sums, axis, [(i, (i + step) % count) for i in range(count)])]
  transfers between devices with their start and end apart: 52 -> 52, of which waited for: 16 -> 15; matrix products, arithmetic and copies ran while one was open for 1% -> 1% of each run, Pallas kernels for 3% -> 3%
where the time goes in v7:
time: 100 us; the launch traced here: 99.9 us
  starting transfers between devices  52 us (52%)
  waiting for transfers between devices  38 us (38%)
  Pallas kernels  6.92 us (7%)
  local copies, waits for them, and re-layouts  1.17 us (1%)
    ppermute x48, starting transfers between devices, swap(): return lax.ppermute(value, ('row', 'col'), pairs)  49 us
    ppermute x48, waiting for transfers between devices, swap(): return lax.ppermute(value, ('row', 'col'), pairs)  38 us
    pallas_call x6, Pallas kernels, apply(): pl.pallas_call(kernel, out_shape=outs, in_specs=[vmem()] * len(operands),...  3.7 us
    pallas_call x2, Pallas kernels, build(): pl.pallas_call(build_kernel, out_shape=jax.ShapeDtypeStruct((ROWS, DEPTH...  3.22 us
    ppermute x4, starting transfers between devices, shifted(): lax.ppermute(sums, axis, [(i, (i + step) % count) for i in range(count)])  3.03 us
  transfers between devices with their start and end apart: 52, of which 15 were waited for; matrix products, arithmetic and copies ran while one was open for 1% of the time, Pallas kernels for 3%

profile of v7, /device:TPU:0, one launch (start us, length us, event | category | flops | bytes accessed | tf_op | source)
XLA Modules:
  0.0 99.9 jit_solution(5357216595698372130)
XLA Ops:
  0.6 6.3 %collective-permute-start.5 = (bf16[256,128]{1,0:T(8,128)(2,1)}, bf16[256,128]{1,0:T(8,128)(2,1)S(1)}, u32[]{:S(2)}, u32[]{:S(2)}) collective-permute-start(bf16[256,128]{1,0:T(8,128)(2,1)} %bitcast.15), channel_id=1, source_target_pairs={{0,15},{1,2},{2,1},{3,4},{4,3},{5,6},{6,5},{7,8},{8,7},{9,10},{10,... | collective-permute-start | bytes 196616 | tf_op jit(solution)/shard_map/ppermute | solution.py:185
  6.9 2.9 %collective-permute-start.1 = (bf16[256,128]{1,0:T(8,128)(2,1)}, bf16[256,128]{1,0:T(8,128)(2,1)S(1)}, u32[]{:S(2)}, u32[]{:S(2)}) collective-permute-start(bf16[256,128]{1,0:T(8,128)(2,1)} %bitcast.16), channel_id=1, source_target_pairs={{0,112},{1,113},{2,114},{3,115},{4,116},{5,117},{6,118},{7,119},{8... | collective-permute-start | bytes 196616 | tf_op jit(solution)/shard_map/ppermute | solution.py:185
  9.9 2.2 %collective-permute-start.7 = (bf16[256,128]{1,0:T(8,128)(2,1)S(1)}, bf16[256,128]{1,0:T(8,128)(2,1)S(1)}, u32[]{:S(2)}, u32[]{:S(2)}) collective-permute-start(bf16[256,128]{1,0:T(8,128)(2,1)S(1)} %collective-permute-done.5.refs_6_), channel_id=1, source_target_pairs={{0,112},{1,113},{2,114},{3,115},{4,116},{5,117},{6,118},{7,119},{8... | collective-permute-start | bytes 196616 | tf_op jit(solution)/shard_map/ppermute | solution.py:185
  16.2 1.6 %shard_map.86.mat_ref = bf16[256,2432]{1,0:T(8,128)(2,1)S(1)} custom-call(s32[2,2,25]{2,1,0:T(2,128)S(1)} %fusion.1.spots_ref, bf16[3200,128]{1,0:T(8,128)(2,1)S(1)} %bitcast.13), custom_call_target="tpu_custom_call" | custom-call | flops 10000000 | bytes 4000000 | tf_op jit(solution)/shard_map/pallas_call | solution.py:77
  18.4 4.0 %collective-permute-start.13 = (bf16[256,128]{1,0:T(8,128)(2,1)S(1)}, bf16[256,128]{1,0:T(8,128)(2,1)S(1)}, u32[]{:S(2)}, u32[]{:S(2)}) collective-permute-start(bf16[256,128]{1,0:T(8,128)(2,1)S(1)} %shard_map.88.refs_0_), channel_id=1, source_target_pairs={{0,15},{1,2},{2,1},{3,4},{4,3},{5,6},{6,5},{7,8},{8,7},{9,10},{10,... | collective-permute-start | bytes 196616 | tf_op jit(solution)/shard_map/ppermute | solution.py:185
  25.8 3.7 %collective-permute-start.15 = (bf16[256,128]{1,0:T(8,128)(2,1)S(1)}, bf16[256,128]{1,0:T(8,128)(2,1)S(1)}, u32[]{:S(2)}, u32[]{:S(2)}) collective-permute-start(bf16[256,128]{1,0:T(8,128)(2,1)S(1)} %collective-permute-done.13.refs_6_), channel_id=1, source_target_pairs={{0,112},{1,113},{2,114},{3,115},{4,116},{5,117},{6,118},{7,119},{8... | collective-permute-start | bytes 196616 | tf_op jit(solution)/shard_map/ppermute | solution.py:185
  30.0 1.6 %shard_map.87.mat_ref = bf16[256,2432]{1,0:T(8,128)(2,1)S(1)} custom-call(s32[2,2,25]{2,1,0:T(2,128)S(1)} %fusion.7.spots_ref, bf16[3200,128]{1,0:T(8,128)(2,1)S(1)} %bitcast.14), custom_call_target="tpu_custom_call" | custom-call | flops 10000000 | bytes 4000000 | tf_op jit(solution)/shard_map/pallas_call | solution.py:77
  32.1 1.6 %collective-permute-done.14.refs_7_ = bf16[256,128]{1,0:T(8,128)(2,1)S(1)} collective-permute-done((bf16[256,128]{1,0:T(8,128)(2,1)S(1)}, bf16[256,128]{1,0:T(8,128)(2,1)S(1)}, u32[]{:S(2)}, u32[]{:S(2)}) %collective-permute-start.14) | collective-permute-done | bytes 65568 | tf_op jit(solution)/shard_map/ppermute | solution.py:185
  34.2 2.6 %collective-permute-start.21 = (bf16[256,128]{1,0:T(8,128)(2,1)S(1)}, bf16[256,128]{1,0:T(8,128)(2,1)S(1)}, u32[]{:S(2)}, u32[]{:S(2)}) collective-permute-start(bf16[256,128]{1,0:T(8,128)(2,1)S(1)} %shard_map.89.refs_0_), channel_id=1, source_target_pairs={{0,15},{1,2},{2,1},{3,4},{4,3},{5,6},{6,5},{7,8},{8,7},{9,10},{10,... | collective-permute-start | bytes 196616 | tf_op jit(solution)/shard_map/ppermute | solution.py:185
  38.1 3.5 %collective-permute-done.21.refs_6_ = bf16[256,128]{1,0:T(8,128)(2,1)S(1)} collective-permute-done((bf16[256,128]{1,0:T(8,128)(2,1)S(1)}, bf16[256,128]{1,0:T(8,128)(2,1)S(1)}, u32[]{:S(2)}, u32[]{:S(2)}) %collective-permute-start.21) | collective-permute-done | bytes 65568 | tf_op jit(solution)/shard_map/ppermute | solution.py:185
  41.6 2.7 %collective-permute-start.23 = (bf16[256,128]{1,0:T(8,128)(2,1)S(1)}, bf16[256,128]{1,0:T(8,128)(2,1)S(1)}, u32[]{:S(2)}, u32[]{:S(2)}) collective-permute-start(bf16[256,128]{1,0:T(8,128)(2,1)S(1)} %collective-permute-done.21.refs_6_), channel_id=1, source_target_pairs={{0,112},{1,113},{2,114},{3,115},{4,116},{5,117},{6,118},{7,119},{8... | collective-permute-start | bytes 196616 | tf_op jit(solution)/shard_map/ppermute | solution.py:185
  44.9 3.1 %collective-permute-done.23.refs_8_ = bf16[256,128]{1,0:T(8,128)(2,1)S(1)} collective-permute-done((bf16[256,128]{1,0:T(8,128)(2,1)S(1)}, bf16[256,128]{1,0:T(8,128)(2,1)S(1)}, u32[]{:S(2)}, u32[]{:S(2)}) %collective-permute-start.23) | collective-permute-done | bytes 65568 | tf_op jit(solution)/shard_map/ppermute | solution.py:185
  49.3 2.3 %collective-permute-start.29 = (bf16[272,128]{1,0:T(8,128)(2,1)S(1)}, bf16[272,128]{1,0:T(8,128)(2,1)S(1)}, u32[]{:S(2)}, u32[]{:S(2)}) collective-permute-start(bf16[272,128]{1,0:T(8,128)(2,1)S(1)} %get-tuple-element.9.refs_0_), channel_id=1, source_target_pairs={{0,15},{1,2},{2,1},{3,4},{4,3},{5,6},{6,5},{7,8},{8,7},{9,10},{10,... | collective-permute-start | bytes 208904 | tf_op jit(solution)/shard_map/ppermute | solution.py:185
  51.6 1.6 %collective-permute-start.25 = (bf16[272,128]{1,0:T(8,128)(2,1)S(1)}, bf16[272,128]{1,0:T(8,128)(2,1)S(1)}, u32[]{:S(2)}, u32[]{:S(2)}) collective-permute-start(bf16[272,128]{1,0:T(8,128)(2,1)S(1)} %get-tuple-element.9.refs_0_), channel_id=1, source_target_pairs={{0,112},{1,113},{2,114},{3,115},{4,116},{5,117},{6,118},{7,119},{8... | collective-permute-start | bytes 208904 | tf_op jit(solution)/shard_map/ppermute | solution.py:185
  53.2 5.1 %collective-permute-done.29.refs_6_ = bf16[272,128]{1,0:T(8,128)(2,1)S(1)} collective-permute-done((bf16[272,128]{1,0:T(8,128)(2,1)S(1)}, bf16[272,128]{1,0:T(8,128)(2,1)S(1)}, u32[]{:S(2)}, u32[]{:S(2)}) %collective-permute-start.29) | collective-permute-done | bytes 69664 | tf_op jit(solution)/shard_map/ppermute | solution.py:185
  59.4 5.3 %collective-permute-done.31.refs_8_ = bf16[272,128]{1,0:T(8,128)(2,1)S(1)} collective-permute-done((bf16[272,128]{1,0:T(8,128)(2,1)S(1)}, bf16[272,128]{1,0:T(8,128)(2,1)S(1)}, u32[]{:S(2)}, u32[]{:S(2)}) %collective-permute-start.31) | collective-permute-done | bytes 69664 | tf_op jit(solution)/shard_map/ppermute | solution.py:185
  65.5 1.7 %collective-permute-start.32 = (f32[8,128]{1,0:T(8,128)S(1)}, f32[8,128]{1,0:T(8,128)S(1)}, u32[]{:S(2)}, u32[]{:S(2)}) collective-permute-start(f32[8,128]{1,0:T(8,128)S(1)} %get-tuple-element.10), channel_id=1, source_target_pairs={{0,4},{1,5},{2,6},{3,7},{4,8},{5,9},{6,10},{7,11},{8,12},{9,13},{1... | collective-permute-start | bytes 12296 | tf_op jit(solution)/shard_map/ppermute | solution.py:202
  67.3 3.5 %collective-permute-start.41 = (bf16[256,128]{1,0:T(8,128)(2,1)S(1)}, bf16[256,128]{1,0:T(8,128)(2,1)S(1)}, u32[]{:S(2)}, u32[]{:S(2)}) collective-permute-start(bf16[256,128]{1,0:T(8,128)(2,1)S(1)} %get-tuple-element.11.refs_0_), channel_id=1, source_target_pairs={{0,15},{1,2},{2,1},{3,4},{4,3},{5,6},{6,5},{7,8},{8,7},{9,10},{10,... | collective-permute-start | bytes 196616 | tf_op jit(solution)/shard_map/ppermute | solution.py:185
  72.8 3.7 %collective-permute-done.41.refs_6_ = bf16[256,128]{1,0:T(8,128)(2,1)S(1)} collective-permute-done((bf16[256,128]{1,0:T(8,128)(2,1)S(1)}, bf16[256,128]{1,0:T(8,128)(2,1)S(1)}, u32[]{:S(2)}, u32[]{:S(2)}) %collective-permute-start.41) | collective-permute-done | bytes 65568 | tf_op jit(solution)/shard_map/ppermute | solution.py:185
  79.7 3.3 %collective-permute-done.43.refs_8_ = bf16[256,128]{1,0:T(8,128)(2,1)S(1)} collective-permute-done((bf16[256,128]{1,0:T(8,128)(2,1)S(1)}, bf16[256,128]{1,0:T(8,128)(2,1)S(1)}, u32[]{:S(2)}, u32[]{:S(2)}) %collective-permute-start.43) | collective-permute-done | bytes 65568 | tf_op jit(solution)/shard_map/ppermute | solution.py:185
  83.5 3.2 %collective-permute-start.49 = (bf16[272,128]{1,0:T(8,128)(2,1)S(1)}, bf16[272,128]{1,0:T(8,128)(2,1)S(1)}, u32[]{:S(2)}, u32[]{:S(2)}) collective-permute-start(bf16[272,128]{1,0:T(8,128)(2,1)S(1)} %shard_map.92.refs_0_), channel_id=1, source_target_pairs={{0,15},{1,2},{2,1},{3,4},{4,3},{5,6},{6,5},{7,8},{8,7},{9,10},{10,... | collective-permute-start | bytes 208904 | tf_op jit(solution)/shard_map/ppermute | solution.py:185
  87.8 4.0 %collective-permute-done.49.refs_6_ = bf16[272,128]{1,0:T(8,128)(2,1)S(1)} collective-permute-done((bf16[272,128]{1,0:T(8,128)(2,1)S(1)}, bf16[272,128]{1,0:T(8,128)(2,1)S(1)}, u32[]{:S(2)}, u32[]{:S(2)}) %collective-permute-start.49) | collective-permute-done | bytes 69664 | tf_op jit(solution)/shard_map/ppermute | solution.py:185
  91.8 1.8 %collective-permute-start.51 = (bf16[272,128]{1,0:T(8,128)(2,1)S(1)}, bf16[272,128]{1,0:T(8,128)(2,1)S(1)}, u32[]{:S(2)}, u32[]{:S(2)}) collective-permute-start(bf16[272,128]{1,0:T(8,128)(2,1)S(1)} %collective-permute-done.49.refs_6_), channel_id=1, source_target_pairs={{0,112},{1,113},{2,114},{3,115},{4,116},{5,117},{6,118},{7,119},{8... | collective-permute-start | bytes 208904 | tf_op jit(solution)/shard_map/ppermute | solution.py:185
  94.2 4.2 %collective-permute-done.51.refs_8_ = bf16[272,128]{1,0:T(8,128)(2,1)S(1)} collective-permute-done((bf16[272,128]{1,0:T(8,128)(2,1)S(1)}, bf16[272,128]{1,0:T(8,128)(2,1)S(1)}, u32[]{:S(2)}, u32[]{:S(2)}) %collective-permute-start.51) | collective-permute-done | bytes 69664 | tf_op jit(solution)/shard_map/ppermute | solution.py:185
  (101 shorter events, 23.7 us)
Async XLA Ops:
  0.6 9.2 %collective-permute-start.5 = (bf16[256,128]{1,0:T(8,128)(2,1)}, bf16[256,128]{1,0:T(8,128)(2,1)S(1)}, u32[]{:S(2)}, u32[]{:S(2)}) collective-permute-start(bf16[256,128]{1,0:T(8,128)(2,1)} %bitcast.15), channel_id=1, source_target_pairs={{0,15},{1,2},{2,1},{3,4},{4,3},{5,6},{6,5},{7,8},{8,7},{9,10},{10,... | collective-permute-start | bytes 196616 | tf_op jit(solution)/shard_map/ppermute | solution.py:185
  6.9 6.6 %collective-permute-start.1 = (bf16[256,128]{1,0:T(8,128)(2,1)}, bf16[256,128]{1,0:T(8,128)(2,1)S(1)}, u32[]{:S(2)}, u32[]{:S(2)}) collective-permute-start(bf16[256,128]{1,0:T(8,128)(2,1)} %bitcast.16), channel_id=1, source_target_pairs={{0,112},{1,113},{2,114},{3,115},{4,116},{5,117},{6,118},{7,119},{8... | collective-permute-start | bytes 196616 | tf_op jit(solution)/shard_map/ppermute | solution.py:185
  9.9 8.0 %collective-permute-start.2 = (bf16[256,128]{1,0:T(8,128)(2,1)}, bf16[256,128]{1,0:T(8,128)(2,1)S(1)}, u32[]{:S(2)}, u32[]{:S(2)}) collective-permute-start(bf16[256,128]{1,0:T(8,128)(2,1)} %bitcast.18), channel_id=1, source_target_pairs={{0,1},{1,0},{2,3},{3,2},{4,5},{5,4},{6,7},{7,6},{8,9},{9,8},{10,11... | collective-permute-start | bytes 196616 | tf_op jit(solution)/shard_map/ppermute | solution.py:185
  9.9 8.0 %collective-permute-start.7 = (bf16[256,128]{1,0:T(8,128)(2,1)S(1)}, bf16[256,128]{1,0:T(8,128)(2,1)S(1)}, u32[]{:S(2)}, u32[]{:S(2)}) collective-permute-start(bf16[256,128]{1,0:T(8,128)(2,1)S(1)} %collective-permute-done.5.refs_6_), channel_id=1, source_target_pairs={{0,112},{1,113},{2,114},{3,115},{4,116},{5,117},{6,118},{7,119},{8... | collective-permute-start | bytes 196616 | tf_op jit(solution)/shard_map/ppermute | solution.py:185
  18.4 7.4 %collective-permute-start.13 = (bf16[256,128]{1,0:T(8,128)(2,1)S(1)}, bf16[256,128]{1,0:T(8,128)(2,1)S(1)}, u32[]{:S(2)}, u32[]{:S(2)}) collective-permute-start(bf16[256,128]{1,0:T(8,128)(2,1)S(1)} %shard_map.88.refs_0_), channel_id=1, source_target_pairs={{0,15},{1,2},{2,1},{3,4},{4,3},{5,6},{6,5},{7,8},{8,7},{9,10},{10,... | collective-permute-start | bytes 196616 | tf_op jit(solution)/shard_map/ppermute | solution.py:185
  22.3 7.1 %collective-permute-start.9 = (bf16[256,128]{1,0:T(8,128)(2,1)S(1)}, bf16[256,128]{1,0:T(8,128)(2,1)S(1)}, u32[]{:S(2)}, u32[]{:S(2)}) collective-permute-start(bf16[256,128]{1,0:T(8,128)(2,1)S(1)} %shard_map.88.refs_0_), channel_id=1, source_target_pairs={{0,112},{1,113},{2,114},{3,115},{4,116},{5,117},{6,118},{7,119},{8... | collective-permute-start | bytes 196616 | tf_op jit(solution)/shard_map/ppermute | solution.py:185
  24.5 7.2 %collective-permute-start.10 = (bf16[256,128]{1,0:T(8,128)(2,1)S(1)}, bf16[256,128]{1,0:T(8,128)(2,1)S(1)}, u32[]{:S(2)}, u32[]{:S(2)}) collective-permute-start(bf16[256,128]{1,0:T(8,128)(2,1)S(1)} %shard_map.88.refs_0_), channel_id=1, source_target_pairs={{0,1},{1,0},{2,3},{3,2},{4,5},{5,4},{6,7},{7,6},{8,9},{9,8},{10,11... | collective-permute-start | bytes 196616 | tf_op jit(solution)/shard_map/ppermute | solution.py:185
  34.2 7.4 %collective-permute-start.21 = (bf16[256,128]{1,0:T(8,128)(2,1)S(1)}, bf16[256,128]{1,0:T(8,128)(2,1)S(1)}, u32[]{:S(2)}, u32[]{:S(2)}) collective-permute-start(bf16[256,128]{1,0:T(8,128)(2,1)S(1)} %shard_map.89.refs_0_), channel_id=1, source_target_pairs={{0,15},{1,2},{2,1},{3,4},{4,3},{5,6},{6,5},{7,8},{8,7},{9,10},{10,... | collective-permute-start | bytes 196616 | tf_op jit(solution)/shard_map/ppermute | solution.py:185
  36.8 7.6 %collective-permute-start.17 = (bf16[256,128]{1,0:T(8,128)(2,1)S(1)}, bf16[256,128]{1,0:T(8,128)(2,1)S(1)}, u32[]{:S(2)}, u32[]{:S(2)}) collective-permute-start(bf16[256,128]{1,0:T(8,128)(2,1)S(1)} %shard_map.89.refs_0_), channel_id=1, source_target_pairs={{0,112},{1,113},{2,114},{3,115},{4,116},{5,117},{6,118},{7,119},{8... | collective-permute-start | bytes 196616 | tf_op jit(solution)/shard_map/ppermute | solution.py:185
  38.1 6.7 %collective-permute-start.18 = (bf16[256,128]{1,0:T(8,128)(2,1)S(1)}, bf16[256,128]{1,0:T(8,128)(2,1)S(1)}, u32[]{:S(2)}, u32[]{:S(2)}) collective-permute-start(bf16[256,128]{1,0:T(8,128)(2,1)S(1)} %shard_map.89.refs_0_), channel_id=1, source_target_pairs={{0,1},{1,0},{2,3},{3,2},{4,5},{5,4},{6,7},{7,6},{8,9},{9,8},{10,11... | collective-permute-start | bytes 196616 | tf_op jit(solution)/shard_map/ppermute | solution.py:185
  41.6 6.4 %collective-permute-start.23 = (bf16[256,128]{1,0:T(8,128)(2,1)S(1)}, bf16[256,128]{1,0:T(8,128)(2,1)S(1)}, u32[]{:S(2)}, u32[]{:S(2)}) collective-permute-start(bf16[256,128]{1,0:T(8,128)(2,1)S(1)} %collective-permute-done.21.refs_6_), channel_id=1, source_target_pairs={{0,112},{1,113},{2,114},{3,115},{4,116},{5,117},{6,118},{7,119},{8... | collective-permute-start | bytes 196616 | tf_op jit(solution)/shard_map/ppermute | solution.py:185
  49.3 9.0 %collective-permute-start.29 = (bf16[272,128]{1,0:T(8,128)(2,1)S(1)}, bf16[272,128]{1,0:T(8,128)(2,1)S(1)}, u32[]{:S(2)}, u32[]{:S(2)}) collective-permute-start(bf16[272,128]{1,0:T(8,128)(2,1)S(1)} %get-tuple-element.9.refs_0_), channel_id=1, source_target_pairs={{0,15},{1,2},{2,1},{3,4},{4,3},{5,6},{6,5},{7,8},{8,7},{9,10},{10,... | collective-permute-start | bytes 208904 | tf_op jit(solution)/shard_map/ppermute | solution.py:185
  51.6 7.3 %collective-permute-start.25 = (bf16[272,128]{1,0:T(8,128)(2,1)S(1)}, bf16[272,128]{1,0:T(8,128)(2,1)S(1)}, u32[]{:S(2)}, u32[]{:S(2)}) collective-permute-start(bf16[272,128]{1,0:T(8,128)(2,1)S(1)} %get-tuple-element.9.refs_0_), channel_id=1, source_target_pairs={{0,112},{1,113},{2,114},{3,115},{4,116},{5,117},{6,118},{7,119},{8... | collective-permute-start | bytes 208904 | tf_op jit(solution)/shard_map/ppermute | solution.py:185
  58.3 6.4 %collective-permute-start.31 = (bf16[272,128]{1,0:T(8,128)(2,1)S(1)}, bf16[272,128]{1,0:T(8,128)(2,1)S(1)}, u32[]{:S(2)}, u32[]{:S(2)}) collective-permute-start(bf16[272,128]{1,0:T(8,128)(2,1)S(1)} %collective-permute-done.29.refs_6_), channel_id=1, source_target_pairs={{0,112},{1,113},{2,114},{3,115},{4,116},{5,117},{6,118},{7,119},{8... | collective-permute-start | bytes 208904 | tf_op jit(solution)/shard_map/ppermute | solution.py:185
  65.2 6.6 %collective-permute-start.34 = (f32[8,128]{1,0:T(8,128)S(1)}, f32[8,128]{1,0:T(8,128)S(1)}, u32[]{:S(2)}, u32[]{:S(2)}) collective-permute-start(f32[8,128]{1,0:T(8,128)S(1)} %get-tuple-element.10), channel_id=1, source_target_pairs={{0,12},{1,13},{2,14},{3,15},{4,0},{5,1},{6,2},{7,3},{8,4},{9,5},{1... | collective-permute-start | bytes 12296 | tf_op jit(solution)/shard_map/ppermute | solution.py:202
  65.3 6.6 %collective-permute-start.33 = (f32[8,128]{1,0:T(8,128)S(1)}, f32[8,128]{1,0:T(8,128)S(1)}, u32[]{:S(2)}, u32[]{:S(2)}) collective-permute-start(f32[8,128]{1,0:T(8,128)S(1)} %get-tuple-element.10), channel_id=1, source_target_pairs={{0,8},{1,9},{2,10},{3,11},{4,12},{5,13},{6,14},{7,15},{8,0},{9,1},... | collective-permute-start | bytes 12296 | tf_op jit(solution)/shard_map/ppermute | solution.py:202
  67.3 9.2 %collective-permute-start.41 = (bf16[256,128]{1,0:T(8,128)(2,1)S(1)}, bf16[256,128]{1,0:T(8,128)(2,1)S(1)}, u32[]{:S(2)}, u32[]{:S(2)}) collective-permute-start(bf16[256,128]{1,0:T(8,128)(2,1)S(1)} %get-tuple-element.11.refs_0_), channel_id=1, source_target_pairs={{0,15},{1,2},{2,1},{3,4},{4,3},{5,6},{6,5},{7,8},{8,7},{9,10},{10,... | collective-permute-start | bytes 196616 | tf_op jit(solution)/shard_map/ppermute | solution.py:185
  70.7 8.4 %collective-permute-start.37 = (bf16[256,128]{1,0:T(8,128)(2,1)S(1)}, bf16[256,128]{1,0:T(8,128)(2,1)S(1)}, u32[]{:S(2)}, u32[]{:S(2)}) collective-permute-start(bf16[256,128]{1,0:T(8,128)(2,1)S(1)} %get-tuple-element.11.refs_0_), channel_id=1, source_target_pairs={{0,112},{1,113},{2,114},{3,115},{4,116},{5,117},{6,118},{7,119},{8... | collective-permute-start | bytes 196616 | tf_op jit(solution)/shard_map/ppermute | solution.py:185
  71.8 7.3 %collective-permute-start.36 = (bf16[256,128]{1,0:T(8,128)(2,1)S(1)}, bf16[256,128]{1,0:T(8,128)(2,1)S(1)}, u32[]{:S(2)}, u32[]{:S(2)}) collective-permute-start(bf16[256,128]{1,0:T(8,128)(2,1)S(1)} %get-tuple-element.11.refs_0_), channel_id=1, source_target_pairs={{0,16},{1,17},{2,18},{3,19},{4,20},{5,21},{6,22},{7,23},{8,24},{9,... | collective-permute-start | bytes 196616 | tf_op jit(solution)/shard_map/ppermute | solution.py:185
  72.8 6.9 %collective-permute-start.38 = (bf16[256,128]{1,0:T(8,128)(2,1)S(1)}, bf16[256,128]{1,0:T(8,128)(2,1)S(1)}, u32[]{:S(2)}, u32[]{:S(2)}) collective-permute-start(bf16[256,128]{1,0:T(8,128)(2,1)S(1)} %get-tuple-element.11.refs_0_), channel_id=1, source_target_pairs={{0,1},{1,0},{2,3},{3,2},{4,5},{5,4},{6,7},{7,6},{8,9},{9,8},{10,11... | collective-permute-start | bytes 196616 | tf_op jit(solution)/shard_map/ppermute | solution.py:185
  76.5 6.5 %collective-permute-start.43 = (bf16[256,128]{1,0:T(8,128)(2,1)S(1)}, bf16[256,128]{1,0:T(8,128)(2,1)S(1)}, u32[]{:S(2)}, u32[]{:S(2)}) collective-permute-start(bf16[256,128]{1,0:T(8,128)(2,1)S(1)} %collective-permute-done.41.refs_6_), channel_id=1, source_target_pairs={{0,112},{1,113},{2,114},{3,115},{4,116},{5,117},{6,118},{7,119},{8... | collective-permute-start | bytes 196616 | tf_op jit(solution)/shard_map/ppermute | solution.py:185
  83.5 8.3 %collective-permute-start.49 = (bf16[272,128]{1,0:T(8,128)(2,1)S(1)}, bf16[272,128]{1,0:T(8,128)(2,1)S(1)}, u32[]{:S(2)}, u32[]{:S(2)}) collective-permute-start(bf16[272,128]{1,0:T(8,128)(2,1)S(1)} %shard_map.92.refs_0_), channel_id=1, source_target_pairs={{0,15},{1,2},{2,1},{3,4},{4,3},{5,6},{6,5},{7,8},{8,7},{9,10},{10,... | collective-permute-start | bytes 208904 | tf_op jit(solution)/shard_map/ppermute | solution.py:185
  86.7 7.0 %collective-permute-start.45 = (bf16[272,128]{1,0:T(8,128)(2,1)S(1)}, bf16[272,128]{1,0:T(8,128)(2,1)S(1)}, u32[]{:S(2)}, u32[]{:S(2)}) collective-permute-start(bf16[272,128]{1,0:T(8,128)(2,1)S(1)} %shard_map.92.refs_0_), channel_id=1, source_target_pairs={{0,112},{1,113},{2,114},{3,115},{4,116},{5,117},{6,118},{7,119},{8... | collective-permute-start | bytes 208904 | tf_op jit(solution)/shard_map/ppermute | solution.py:185
  91.8 6.5 %collective-permute-start.51 = (bf16[272,128]{1,0:T(8,128)(2,1)S(1)}, bf16[272,128]{1,0:T(8,128)(2,1)S(1)}, u32[]{:S(2)}, u32[]{:S(2)}) collective-permute-start(bf16[272,128]{1,0:T(8,128)(2,1)S(1)} %collective-permute-done.49.refs_6_), channel_id=1, source_target_pairs={{0,112},{1,113},{2,114},{3,115},{4,116},{5,117},{6,118},{7,119},{8... | collective-permute-start | bytes 208904 | tf_op jit(solution)/shard_map/ppermute | solution.py:185
  (33 other events, 183.6 us)

commit v8 on v7

--- a/solution.py
+++ b/solution.py
@@ -192,7 +192,7 @@
     beside = swap(field, same, near)
     beside_near = swap(near_y, same, near)
     beside_far = swap(far_y, same, near)
-    across_far = swap(across_same, cross, same)
+    across_far = swap(field, cross, cross)
     across_near = swap(across_same, near, same)
     return [field, near_y, far_y, beside, beside_near, beside_far, across_same, across_near, across_far]
 

time: 100 us -> 94.8 us (0.948)
  waiting for transfers between devices: 38 us -> 26 us
  starting transfers between devices: 52 us -> 58.8 us
    ppermute x48, waiting for transfers between devices: 38 us -> 25.4 us  [swap(): return lax.ppermute(value, ('row', 'col'), pairs)]
    ppermute x48, starting transfers between devices: 49 us -> 55.3 us  [swap(): return lax.ppermute(value, ('row', 'col'), pairs)]
where the time goes in v8:
time: 94.8 us; the launch traced here: 94.6 us
  starting transfers between devices  58.8 us (62%)
  waiting for transfers between devices  26 us (27%)
  Pallas kernels  6.94 us (7%)
  local copies, waits for them, and re-layouts  1.17 us (1%)
    ppermute x48, starting transfers between devices, swap(): return lax.ppermute(value, ('row', 'col'), pairs)  55.3 us
    ppermute x48, waiting for transfers between devices, swap(): return lax.ppermute(value, ('row', 'col'), pairs)  25.4 us
    pallas_call x6, Pallas kernels, apply(): pl.pallas_call(kernel, out_shape=outs, in_specs=[vmem()] * len(operands),...  3.71 us
    ppermute x4, starting transfers between devices, shifted(): lax.ppermute(sums, axis, [(i, (i + step) % count) for i in range(count)])  3.53 us
    pallas_call x2, Pallas kernels, build(): pl.pallas_call(build_kernel, out_shape=jax.ShapeDtypeStruct((ROWS, DEPTH...  3.22 us
  transfers between devices with their start and end apart: 52, of which 15 were waited for; matrix products, arithmetic and copies ran while one was open for 1% of the time, Pallas kernels for 3%

profile of v8, /device:TPU:0, one launch (start us, length us, event | category | flops | bytes accessed | tf_op | source)
XLA Modules:
  0.0 94.6 jit_solution(8166681918150625603)
XLA Ops:
  0.6 6.3 %collective-permute-start.5 = (bf16[256,128]{1,0:T(8,128)(2,1)}, bf16[256,128]{1,0:T(8,128)(2,1)S(1)}, u32[]{:S(2)}, u32[]{:S(2)}) collective-permute-start(bf16[256,128]{1,0:T(8,128)(2,1)} %bitcast.15), channel_id=1, source_target_pairs={{0,15},{1,2},{2,1},{3,4},{4,3},{5,6},{6,5},{7,8},{8,7},{9,10},{10,... | collective-permute-start | bytes 196616 | tf_op jit(solution)/shard_map/ppermute | solution.py:185
  6.9 2.9 %collective-permute-start.1 = (bf16[256,128]{1,0:T(8,128)(2,1)}, bf16[256,128]{1,0:T(8,128)(2,1)S(1)}, u32[]{:S(2)}, u32[]{:S(2)}) collective-permute-start(bf16[256,128]{1,0:T(8,128)(2,1)} %bitcast.16), channel_id=1, source_target_pairs={{0,112},{1,113},{2,114},{3,115},{4,116},{5,117},{6,118},{7,119},{8... | collective-permute-start | bytes 196616 | tf_op jit(solution)/shard_map/ppermute | solution.py:185
  11.9 1.6 %collective-permute-done.1.refs_2_ = bf16[256,128]{1,0:T(8,128)(2,1)S(1)} collective-permute-done((bf16[256,128]{1,0:T(8,128)(2,1)}, bf16[256,128]{1,0:T(8,128)(2,1)S(1)}, u32[]{:S(2)}, u32[]{:S(2)}) %collective-permute-start.1) | collective-permute-done | bytes 65568 | tf_op jit(solution)/shard_map/ppermute | solution.py:185
  16.6 1.6 %shard_map.86.mat_ref = bf16[256,2432]{1,0:T(8,128)(2,1)S(1)} custom-call(s32[2,2,25]{2,1,0:T(2,128)S(1)} %fusion.1.spots_ref, bf16[3200,128]{1,0:T(8,128)(2,1)S(1)} %bitcast.13), custom_call_target="tpu_custom_call" | custom-call | flops 10000000 | bytes 4000000 | tf_op jit(solution)/shard_map/pallas_call | solution.py:77
  19.7 2.4 %collective-permute-start.13 = (bf16[256,128]{1,0:T(8,128)(2,1)S(1)}, bf16[256,128]{1,0:T(8,128)(2,1)S(1)}, u32[]{:S(2)}, u32[]{:S(2)}) collective-permute-start(bf16[256,128]{1,0:T(8,128)(2,1)S(1)} %shard_map.88.refs_0_), channel_id=1, source_target_pairs={{0,15},{1,2},{2,1},{3,4},{4,3},{5,6},{6,5},{7,8},{8,7},{9,10},{10,... | collective-permute-start | bytes 196616 | tf_op jit(solution)/shard_map/ppermute | solution.py:185
  22.8 2.0 %collective-permute-start.8 = (bf16[256,128]{1,0:T(8,128)(2,1)S(1)}, bf16[256,128]{1,0:T(8,128)(2,1)S(1)}, u32[]{:S(2)}, u32[]{:S(2)}) collective-permute-start(bf16[256,128]{1,0:T(8,128)(2,1)S(1)} %shard_map.88.refs_0_), channel_id=1, source_target_pairs={{0,16},{1,17},{2,18},{3,19},{4,20},{5,21},{6,22},{7,23},{8,24},{9,... | collective-permute-start | bytes 196616 | tf_op jit(solution)/shard_map/ppermute | solution.py:185
  24.8 2.8 %collective-permute-start.15 = (bf16[256,128]{1,0:T(8,128)(2,1)S(1)}, bf16[256,128]{1,0:T(8,128)(2,1)S(1)}, u32[]{:S(2)}, u32[]{:S(2)}) collective-permute-start(bf16[256,128]{1,0:T(8,128)(2,1)S(1)} %shard_map.88.refs_0_), channel_id=1, source_target_pairs={{0,127},{1,114},{2,113},{3,116},{4,115},{5,118},{6,117},{7,120},{8... | collective-permute-start | bytes 196616 | tf_op jit(solution)/shard_map/ppermute | solution.py:185
  29.6 1.6 %shard_map.87.mat_ref = bf16[256,2432]{1,0:T(8,128)(2,1)S(1)} custom-call(s32[2,2,25]{2,1,0:T(2,128)S(1)} %fusion.7.spots_ref, bf16[3200,128]{1,0:T(8,128)(2,1)S(1)} %bitcast.14), custom_call_target="tpu_custom_call" | custom-call | flops 10000000 | bytes 4000000 | tf_op jit(solution)/shard_map/pallas_call | solution.py:77
  31.2 2.7 %collective-permute-done.15.refs_8_ = bf16[256,128]{1,0:T(8,128)(2,1)S(1)} collective-permute-done((bf16[256,128]{1,0:T(8,128)(2,1)S(1)}, bf16[256,128]{1,0:T(8,128)(2,1)S(1)}, u32[]{:S(2)}, u32[]{:S(2)}) %collective-permute-start.15) | collective-permute-done | bytes 65568 | tf_op jit(solution)/shard_map/ppermute | solution.py:185
  35.4 2.7 %collective-permute-start.17 = (bf16[256,128]{1,0:T(8,128)(2,1)S(1)}, bf16[256,128]{1,0:T(8,128)(2,1)S(1)}, u32[]{:S(2)}, u32[]{:S(2)}) collective-permute-start(bf16[256,128]{1,0:T(8,128)(2,1)S(1)} %shard_map.89.refs_0_), channel_id=1, source_target_pairs={{0,112},{1,113},{2,114},{3,115},{4,116},{5,117},{6,118},{7,119},{8... | collective-permute-start | bytes 196616 | tf_op jit(solution)/shard_map/ppermute | solution.py:185
  38.1 4.1 %collective-permute-start.23 = (bf16[256,128]{1,0:T(8,128)(2,1)S(1)}, bf16[256,128]{1,0:T(8,128)(2,1)S(1)}, u32[]{:S(2)}, u32[]{:S(2)}) collective-permute-start(bf16[256,128]{1,0:T(8,128)(2,1)S(1)} %shard_map.89.refs_0_), channel_id=1, source_target_pairs={{0,127},{1,114},{2,113},{3,116},{4,115},{5,118},{6,117},{7,120},{8... | collective-permute-start | bytes 196616 | tf_op jit(solution)/shard_map/ppermute | solution.py:185
  43.0 4.2 %collective-permute-done.23.refs_8_ = bf16[256,128]{1,0:T(8,128)(2,1)S(1)} collective-permute-done((bf16[256,128]{1,0:T(8,128)(2,1)S(1)}, bf16[256,128]{1,0:T(8,128)(2,1)S(1)}, u32[]{:S(2)}, u32[]{:S(2)}) %collective-permute-start.23) | collective-permute-done | bytes 65568 | tf_op jit(solution)/shard_map/ppermute | solution.py:185
  47.9 1.5 %collective-permute-start.29 = (bf16[272,128]{1,0:T(8,128)(2,1)S(1)}, bf16[272,128]{1,0:T(8,128)(2,1)S(1)}, u32[]{:S(2)}, u32[]{:S(2)}) collective-permute-start(bf16[272,128]{1,0:T(8,128)(2,1)S(1)} %get-tuple-element.9.refs_0_), channel_id=1, source_target_pairs={{0,15},{1,2},{2,1},{3,4},{4,3},{5,6},{6,5},{7,8},{8,7},{9,10},{10,... | collective-permute-start | bytes 208904 | tf_op jit(solution)/shard_map/ppermute | solution.py:185
  49.3 3.6 %collective-permute-start.25 = (bf16[272,128]{1,0:T(8,128)(2,1)S(1)}, bf16[272,128]{1,0:T(8,128)(2,1)S(1)}, u32[]{:S(2)}, u32[]{:S(2)}) collective-permute-start(bf16[272,128]{1,0:T(8,128)(2,1)S(1)} %get-tuple-element.9.refs_0_), channel_id=1, source_target_pairs={{0,112},{1,113},{2,114},{3,115},{4,116},{5,117},{6,118},{7,119},{8... | collective-permute-start | bytes 208904 | tf_op jit(solution)/shard_map/ppermute | solution.py:185
  53.0 2.8 %collective-permute-start.31 = (bf16[272,128]{1,0:T(8,128)(2,1)S(1)}, bf16[272,128]{1,0:T(8,128)(2,1)S(1)}, u32[]{:S(2)}, u32[]{:S(2)}) collective-permute-start(bf16[272,128]{1,0:T(8,128)(2,1)S(1)} %get-tuple-element.9.refs_0_), channel_id=1, source_target_pairs={{0,127},{1,114},{2,113},{3,116},{4,115},{5,118},{6,117},{7,120},{8... | collective-permute-start | bytes 208904 | tf_op jit(solution)/shard_map/ppermute | solution.py:185
  57.3 4.9 %collective-permute-done.31.refs_8_ = bf16[272,128]{1,0:T(8,128)(2,1)S(1)} collective-permute-done((bf16[272,128]{1,0:T(8,128)(2,1)S(1)}, bf16[272,128]{1,0:T(8,128)(2,1)S(1)}, u32[]{:S(2)}, u32[]{:S(2)}) %collective-permute-start.31) | collective-permute-done | bytes 69664 | tf_op jit(solution)/shard_map/ppermute | solution.py:185
  63.0 1.7 %collective-permute-start.32 = (f32[8,128]{1,0:T(8,128)S(1)}, f32[8,128]{1,0:T(8,128)S(1)}, u32[]{:S(2)}, u32[]{:S(2)}) collective-permute-start(f32[8,128]{1,0:T(8,128)S(1)} %get-tuple-element.10), channel_id=1, source_target_pairs={{0,4},{1,5},{2,6},{3,7},{4,8},{5,9},{6,10},{7,11},{8,12},{9,13},{1... | collective-permute-start | bytes 12296 | tf_op jit(solution)/shard_map/ppermute | solution.py:202
  65.5 3.6 %collective-permute-start.37 = (bf16[256,128]{1,0:T(8,128)(2,1)S(1)}, bf16[256,128]{1,0:T(8,128)(2,1)S(1)}, u32[]{:S(2)}, u32[]{:S(2)}) collective-permute-start(bf16[256,128]{1,0:T(8,128)(2,1)S(1)} %get-tuple-element.11.refs_0_), channel_id=1, source_target_pairs={{0,112},{1,113},{2,114},{3,115},{4,116},{5,117},{6,118},{7,119},{8... | collective-permute-start | bytes 196616 | tf_op jit(solution)/shard_map/ppermute | solution.py:185
  70.5 3.2 %collective-permute-start.43 = (bf16[256,128]{1,0:T(8,128)(2,1)S(1)}, bf16[256,128]{1,0:T(8,128)(2,1)S(1)}, u32[]{:S(2)}, u32[]{:S(2)}) collective-permute-start(bf16[256,128]{1,0:T(8,128)(2,1)S(1)} %get-tuple-element.11.refs_0_), channel_id=1, source_target_pairs={{0,127},{1,114},{2,113},{3,116},{4,115},{5,118},{6,117},{7,120},{8... | collective-permute-start | bytes 196616 | tf_op jit(solution)/shard_map/ppermute | solution.py:185
  74.3 2.0 %collective-permute-start.42 = (bf16[256,128]{1,0:T(8,128)(2,1)S(1)}, bf16[256,128]{1,0:T(8,128)(2,1)S(1)}, u32[]{:S(2)}, u32[]{:S(2)}) collective-permute-start(bf16[256,128]{1,0:T(8,128)(2,1)S(1)} %collective-permute-done.41.refs_6_), channel_id=1, source_target_pairs={{0,16},{1,17},{2,18},{3,19},{4,20},{5,21},{6,22},{7,23},{8,24},{9,... | collective-permute-start | bytes 196616 | tf_op jit(solution)/shard_map/ppermute | solution.py:185
  76.8 2.8 %collective-permute-done.43.refs_8_ = bf16[256,128]{1,0:T(8,128)(2,1)S(1)} collective-permute-done((bf16[256,128]{1,0:T(8,128)(2,1)S(1)}, bf16[256,128]{1,0:T(8,128)(2,1)S(1)}, u32[]{:S(2)}, u32[]{:S(2)}) %collective-permute-start.43) | collective-permute-done | bytes 65568 | tf_op jit(solution)/shard_map/ppermute | solution.py:185
  80.7 3.6 %collective-permute-start.45 = (bf16[272,128]{1,0:T(8,128)(2,1)S(1)}, bf16[272,128]{1,0:T(8,128)(2,1)S(1)}, u32[]{:S(2)}, u32[]{:S(2)}) collective-permute-start(bf16[272,128]{1,0:T(8,128)(2,1)S(1)} %shard_map.92.refs_0_), channel_id=1, source_target_pairs={{0,112},{1,113},{2,114},{3,115},{4,116},{5,117},{6,118},{7,119},{8... | collective-permute-start | bytes 208904 | tf_op jit(solution)/shard_map/ppermute | solution.py:185
  84.3 3.7 %collective-permute-start.51 = (bf16[272,128]{1,0:T(8,128)(2,1)S(1)}, bf16[272,128]{1,0:T(8,128)(2,1)S(1)}, u32[]{:S(2)}, u32[]{:S(2)}) collective-permute-start(bf16[272,128]{1,0:T(8,128)(2,1)S(1)} %shard_map.92.refs_0_), channel_id=1, source_target_pairs={{0,127},{1,114},{2,113},{3,116},{4,115},{5,118},{6,117},{7,120},{8... | collective-permute-start | bytes 208904 | tf_op jit(solution)/shard_map/ppermute | solution.py:185
  90.5 2.9 %collective-permute-done.51.refs_8_ = bf16[272,128]{1,0:T(8,128)(2,1)S(1)} collective-permute-done((bf16[272,128]{1,0:T(8,128)(2,1)S(1)}, bf16[272,128]{1,0:T(8,128)(2,1)S(1)}, u32[]{:S(2)}, u32[]{:S(2)}) %collective-permute-start.51) | collective-permute-done | bytes 69664 | tf_op jit(solution)/shard_map/ppermute | solution.py:185
  (101 shorter events, 22.6 us)
Async XLA Ops:
  0.6 10.2 %collective-permute-start.5 = (bf16[256,128]{1,0:T(8,128)(2,1)}, bf16[256,128]{1,0:T(8,128)(2,1)S(1)}, u32[]{:S(2)}, u32[]{:S(2)}) collective-permute-start(bf16[256,128]{1,0:T(8,128)(2,1)} %bitcast.15), channel_id=1, source_target_pairs={{0,15},{1,2},{2,1},{3,4},{4,3},{5,6},{6,5},{7,8},{8,7},{9,10},{10,... | collective-permute-start | bytes 196616 | tf_op jit(solution)/shard_map/ppermute | solution.py:185
  6.9 6.6 %collective-permute-start.1 = (bf16[256,128]{1,0:T(8,128)(2,1)}, bf16[256,128]{1,0:T(8,128)(2,1)S(1)}, u32[]{:S(2)}, u32[]{:S(2)}) collective-permute-start(bf16[256,128]{1,0:T(8,128)(2,1)} %bitcast.16), channel_id=1, source_target_pairs={{0,112},{1,113},{2,114},{3,115},{4,116},{5,117},{6,118},{7,119},{8... | collective-permute-start | bytes 196616 | tf_op jit(solution)/shard_map/ppermute | solution.py:185
  9.9 9.3 %collective-permute-start.7 = (bf16[256,128]{1,0:T(8,128)(2,1)}, bf16[256,128]{1,0:T(8,128)(2,1)S(1)}, u32[]{:S(2)}, u32[]{:S(2)}) collective-permute-start(bf16[256,128]{1,0:T(8,128)(2,1)} %bitcast.18), channel_id=1, source_target_pairs={{0,127},{1,114},{2,113},{3,116},{4,115},{5,118},{6,117},{7,120},{8... | collective-permute-start | bytes 196616 | tf_op jit(solution)/shard_map/ppermute | solution.py:185
  10.8 8.4 %collective-permute-start.2 = (bf16[256,128]{1,0:T(8,128)(2,1)}, bf16[256,128]{1,0:T(8,128)(2,1)S(1)}, u32[]{:S(2)}, u32[]{:S(2)}) collective-permute-start(bf16[256,128]{1,0:T(8,128)(2,1)} %bitcast.19), channel_id=1, source_target_pairs={{0,1},{1,0},{2,3},{3,2},{4,5},{5,4},{6,7},{7,6},{8,9},{9,8},{10,11... | collective-permute-start | bytes 196616 | tf_op jit(solution)/shard_map/ppermute | solution.py:185
  10.8 8.4 %collective-permute-start.6 = (bf16[256,128]{1,0:T(8,128)(2,1)S(1)}, bf16[256,128]{1,0:T(8,128)(2,1)S(1)}, u32[]{:S(2)}, u32[]{:S(2)}) collective-permute-start(bf16[256,128]{1,0:T(8,128)(2,1)S(1)} %collective-permute-done.5.refs_6_), channel_id=1, source_target_pairs={{0,16},{1,17},{2,18},{3,19},{4,20},{5,21},{6,22},{7,23},{8,24},{9,... | collective-permute-start | bytes 196616 | tf_op jit(solution)/shard_map/ppermute | solution.py:185
  19.7 9.2 %collective-permute-start.13 = (bf16[256,128]{1,0:T(8,128)(2,1)S(1)}, bf16[256,128]{1,0:T(8,128)(2,1)S(1)}, u32[]{:S(2)}, u32[]{:S(2)}) collective-permute-start(bf16[256,128]{1,0:T(8,128)(2,1)S(1)} %shard_map.88.refs_0_), channel_id=1, source_target_pairs={{0,15},{1,2},{2,1},{3,4},{4,3},{5,6},{6,5},{7,8},{8,7},{9,10},{10,... | collective-permute-start | bytes 196616 | tf_op jit(solution)/shard_map/ppermute | solution.py:185
  22.1 6.9 %collective-permute-start.9 = (bf16[256,128]{1,0:T(8,128)(2,1)S(1)}, bf16[256,128]{1,0:T(8,128)(2,1)S(1)}, u32[]{:S(2)}, u32[]{:S(2)}) collective-permute-start(bf16[256,128]{1,0:T(8,128)(2,1)S(1)} %shard_map.88.refs_0_), channel_id=1, source_target_pairs={{0,112},{1,113},{2,114},{3,115},{4,116},{5,117},{6,118},{7,119},{8... | collective-permute-start | bytes 196616 | tf_op jit(solution)/shard_map/ppermute | solution.py:185
  24.8 9.1 %collective-permute-start.15 = (bf16[256,128]{1,0:T(8,128)(2,1)S(1)}, bf16[256,128]{1,0:T(8,128)(2,1)S(1)}, u32[]{:S(2)}, u32[]{:S(2)}) collective-permute-start(bf16[256,128]{1,0:T(8,128)(2,1)S(1)} %shard_map.88.refs_0_), channel_id=1, source_target_pairs={{0,127},{1,114},{2,113},{3,116},{4,115},{5,118},{6,117},{7,120},{8... | collective-permute-start | bytes 196616 | tf_op jit(solution)/shard_map/ppermute | solution.py:185
  34.4 8.1 %collective-permute-start.21 = (bf16[256,128]{1,0:T(8,128)(2,1)S(1)}, bf16[256,128]{1,0:T(8,128)(2,1)S(1)}, u32[]{:S(2)}, u32[]{:S(2)}) collective-permute-start(bf16[256,128]{1,0:T(8,128)(2,1)S(1)} %shard_map.89.refs_0_), channel_id=1, source_target_pairs={{0,15},{1,2},{2,1},{3,4},{4,3},{5,6},{6,5},{7,8},{8,7},{9,10},{10,... | collective-permute-start | bytes 196616 | tf_op jit(solution)/shard_map/ppermute | solution.py:185
  35.4 7.1 %collective-permute-start.17 = (bf16[256,128]{1,0:T(8,128)(2,1)S(1)}, bf16[256,128]{1,0:T(8,128)(2,1)S(1)}, u32[]{:S(2)}, u32[]{:S(2)}) collective-permute-start(bf16[256,128]{1,0:T(8,128)(2,1)S(1)} %shard_map.89.refs_0_), channel_id=1, source_target_pairs={{0,112},{1,113},{2,114},{3,115},{4,116},{5,117},{6,118},{7,119},{8... | collective-permute-start | bytes 196616 | tf_op jit(solution)/shard_map/ppermute | solution.py:185
  38.1 9.1 %collective-permute-start.23 = (bf16[256,128]{1,0:T(8,128)(2,1)S(1)}, bf16[256,128]{1,0:T(8,128)(2,1)S(1)}, u32[]{:S(2)}, u32[]{:S(2)}) collective-permute-start(bf16[256,128]{1,0:T(8,128)(2,1)S(1)} %shard_map.89.refs_0_), channel_id=1, source_target_pairs={{0,127},{1,114},{2,113},{3,116},{4,115},{5,118},{6,117},{7,120},{8... | collective-permute-start | bytes 196616 | tf_op jit(solution)/shard_map/ppermute | solution.py:185
  47.9 7.8 %collective-permute-start.29 = (bf16[272,128]{1,0:T(8,128)(2,1)S(1)}, bf16[272,128]{1,0:T(8,128)(2,1)S(1)}, u32[]{:S(2)}, u32[]{:S(2)}) collective-permute-start(bf16[272,128]{1,0:T(8,128)(2,1)S(1)} %get-tuple-element.9.refs_0_), channel_id=1, source_target_pairs={{0,15},{1,2},{2,1},{3,4},{4,3},{5,6},{6,5},{7,8},{8,7},{9,10},{10,... | collective-permute-start | bytes 208904 | tf_op jit(solution)/shard_map/ppermute | solution.py:185
  49.3 6.9 %collective-permute-start.25 = (bf16[272,128]{1,0:T(8,128)(2,1)S(1)}, bf16[272,128]{1,0:T(8,128)(2,1)S(1)}, u32[]{:S(2)}, u32[]{:S(2)}) collective-permute-start(bf16[272,128]{1,0:T(8,128)(2,1)S(1)} %get-tuple-element.9.refs_0_), channel_id=1, source_target_pairs={{0,112},{1,113},{2,114},{3,115},{4,116},{5,117},{6,118},{7,119},{8... | collective-permute-start | bytes 208904 | tf_op jit(solution)/shard_map/ppermute | solution.py:185
  53.0 9.2 %collective-permute-start.31 = (bf16[272,128]{1,0:T(8,128)(2,1)S(1)}, bf16[272,128]{1,0:T(8,128)(2,1)S(1)}, u32[]{:S(2)}, u32[]{:S(2)}) collective-permute-start(bf16[272,128]{1,0:T(8,128)(2,1)S(1)} %get-tuple-element.9.refs_0_), channel_id=1, source_target_pairs={{0,127},{1,114},{2,113},{3,116},{4,115},{5,118},{6,117},{7,120},{8... | collective-permute-start | bytes 208904 | tf_op jit(solution)/shard_map/ppermute | solution.py:185
  55.7 6.4 %collective-permute-start.26 = (bf16[272,128]{1,0:T(8,128)(2,1)S(1)}, bf16[272,128]{1,0:T(8,128)(2,1)S(1)}, u32[]{:S(2)}, u32[]{:S(2)}) collective-permute-start(bf16[272,128]{1,0:T(8,128)(2,1)S(1)} %get-tuple-element.9.refs_0_), channel_id=1, source_target_pairs={{0,1},{1,0},{2,3},{3,2},{4,5},{5,4},{6,7},{7,6},{8,9},{9,8},{10,11... | collective-permute-start | bytes 208904 | tf_op jit(solution)/shard_map/ppermute | solution.py:185
  55.7 6.4 %collective-permute-start.30 = (bf16[272,128]{1,0:T(8,128)(2,1)S(1)}, bf16[272,128]{1,0:T(8,128)(2,1)S(1)}, u32[]{:S(2)}, u32[]{:S(2)}) collective-permute-start(bf16[272,128]{1,0:T(8,128)(2,1)S(1)} %collective-permute-done.29.refs_6_), channel_id=1, source_target_pairs={{0,16},{1,17},{2,18},{3,19},{4,20},{5,21},{6,22},{7,23},{8,24},{9,... | collective-permute-start | bytes 208904 | tf_op jit(solution)/shard_map/ppermute | solution.py:185
  62.6 6.4 %collective-permute-start.34 = (f32[8,128]{1,0:T(8,128)S(1)}, f32[8,128]{1,0:T(8,128)S(1)}, u32[]{:S(2)}, u32[]{:S(2)}) collective-permute-start(f32[8,128]{1,0:T(8,128)S(1)} %get-tuple-element.10), channel_id=1, source_target_pairs={{0,12},{1,13},{2,14},{3,15},{4,0},{5,1},{6,2},{7,3},{8,4},{9,5},{1... | collective-permute-start | bytes 12296 | tf_op jit(solution)/shard_map/ppermute | solution.py:202
  64.7 9.5 %collective-permute-start.41 = (bf16[256,128]{1,0:T(8,128)(2,1)S(1)}, bf16[256,128]{1,0:T(8,128)(2,1)S(1)}, u32[]{:S(2)}, u32[]{:S(2)}) collective-permute-start(bf16[256,128]{1,0:T(8,128)(2,1)S(1)} %get-tuple-element.11.refs_0_), channel_id=1, source_target_pairs={{0,15},{1,2},{2,1},{3,4},{4,3},{5,6},{6,5},{7,8},{8,7},{9,10},{10,... | collective-permute-start | bytes 196616 | tf_op jit(solution)/shard_map/ppermute | solution.py:185
  65.5 10.8 %collective-permute-start.37 = (bf16[256,128]{1,0:T(8,128)(2,1)S(1)}, bf16[256,128]{1,0:T(8,128)(2,1)S(1)}, u32[]{:S(2)}, u32[]{:S(2)}) collective-permute-start(bf16[256,128]{1,0:T(8,128)(2,1)S(1)} %get-tuple-element.11.refs_0_), channel_id=1, source_target_pairs={{0,112},{1,113},{2,114},{3,115},{4,116},{5,117},{6,118},{7,119},{8... | collective-permute-start | bytes 196616 | tf_op jit(solution)/shard_map/ppermute | solution.py:185
  69.0 7.5 %collective-permute-start.36 = (bf16[256,128]{1,0:T(8,128)(2,1)S(1)}, bf16[256,128]{1,0:T(8,128)(2,1)S(1)}, u32[]{:S(2)}, u32[]{:S(2)}) collective-permute-start(bf16[256,128]{1,0:T(8,128)(2,1)S(1)} %get-tuple-element.11.refs_0_), channel_id=1, source_target_pairs={{0,16},{1,17},{2,18},{3,19},{4,20},{5,21},{6,22},{7,23},{8,24},{9,... | collective-permute-start | bytes 196616 | tf_op jit(solution)/shard_map/ppermute | solution.py:185
  70.5 9.1 %collective-permute-start.43 = (bf16[256,128]{1,0:T(8,128)(2,1)S(1)}, bf16[256,128]{1,0:T(8,128)(2,1)S(1)}, u32[]{:S(2)}, u32[]{:S(2)}) collective-permute-start(bf16[256,128]{1,0:T(8,128)(2,1)S(1)} %get-tuple-element.11.refs_0_), channel_id=1, source_target_pairs={{0,127},{1,114},{2,113},{3,116},{4,115},{5,118},{6,117},{7,120},{8... | collective-permute-start | bytes 196616 | tf_op jit(solution)/shard_map/ppermute | solution.py:185
  80.1 8.9 %collective-permute-start.49 = (bf16[272,128]{1,0:T(8,128)(2,1)S(1)}, bf16[272,128]{1,0:T(8,128)(2,1)S(1)}, u32[]{:S(2)}, u32[]{:S(2)}) collective-permute-start(bf16[272,128]{1,0:T(8,128)(2,1)S(1)} %shard_map.92.refs_0_), channel_id=1, source_target_pairs={{0,15},{1,2},{2,1},{3,4},{4,3},{5,6},{6,5},{7,8},{8,7},{9,10},{10,... | collective-permute-start | bytes 208904 | tf_op jit(solution)/shard_map/ppermute | solution.py:185
  80.7 9.3 %collective-permute-start.45 = (bf16[272,128]{1,0:T(8,128)(2,1)S(1)}, bf16[272,128]{1,0:T(8,128)(2,1)S(1)}, u32[]{:S(2)}, u32[]{:S(2)}) collective-permute-start(bf16[272,128]{1,0:T(8,128)(2,1)S(1)} %shard_map.92.refs_0_), channel_id=1, source_target_pairs={{0,112},{1,113},{2,114},{3,115},{4,116},{5,117},{6,118},{7,119},{8... | collective-permute-start | bytes 208904 | tf_op jit(solution)/shard_map/ppermute | solution.py:185
  84.3 9.2 %collective-permute-start.51 = (bf16[272,128]{1,0:T(8,128)(2,1)S(1)}, bf16[272,128]{1,0:T(8,128)(2,1)S(1)}, u32[]{:S(2)}, u32[]{:S(2)}) collective-permute-start(bf16[272,128]{1,0:T(8,128)(2,1)S(1)} %shard_map.92.refs_0_), channel_id=1, source_target_pairs={{0,127},{1,114},{2,113},{3,116},{4,115},{5,118},{6,117},{7,120},{8... | collective-permute-start | bytes 208904 | tf_op jit(solution)/shard_map/ppermute | solution.py:185
  (33 other events, 176.3 us)

commit v9 on v8

--- a/solution.py
+++ b/solution.py
@@ -19,6 +19,8 @@
 PARTS = 9
 DEPTH = PARTS * ROWS
 NOTE = 16
+EARLY = (0, 1, 2, 6)
+LATE = (3, 4, 5, 7, 8)
 BLOCK_ROWS = CELLS * ENTRIES * HALF
 
 
@@ -85,11 +87,23 @@
     )(spots_of(cols, count), rows)
 
 
-def product(mat_ref, part_refs, turn_ref):
+def partial(mat_ref, part_refs, indices):
     total = None
-    for index, part_ref in enumerate(part_refs):
-        term = jnp.dot(mat_ref[:, index * ROWS : (index + 1) * ROWS], part_ref[:ROWS], preferred_element_type=jnp.float32)
+    for index in indices:
+        columns = mat_ref[:, index * ROWS : (index + 1) * ROWS]
+        term = jnp.dot(columns, part_refs[index][:ROWS], preferred_element_type=jnp.float32)
         total = term if total is None else total + term
+    return total
+
+
+def early_kernel(mat_ref, *refs):
+    *part_refs, total_ref = refs
+    total_ref[...] = partial(mat_ref, dict(zip(EARLY, part_refs)), EARLY)
+
+
+def product(mats, part_refs, turn_ref):
+    mat_ref, early_ref = mats
+    total = early_ref[...] + partial(mat_ref, part_refs, LATE)
     for cell in range(CELLS):
         for parity in range(2):
             first = parity * CELLS * HALF + cell * HALF
@@ -155,16 +169,27 @@
     two_ref[...] = (2.0 * (image / ratio) / ratio - slab_ref[...].astype(jnp.float32)).astype(jnp.bfloat16)
 
 
-def apply(kernel, outs, *operands):
+def call(kernel, outs, scratch, *operands):
     return pl.pallas_call(
         kernel,
         out_shape=outs,
         in_specs=[vmem()] * len(operands),
         out_specs=jax.tree.map(lambda _: vmem(), outs),
-        scratch_shapes=[pltpu.VMEM((ROWS, SLAB), jnp.float32)],
+        scratch_shapes=scratch,
         compiler_params=pltpu.CompilerParams(vmem_limit_bytes=16 * 2**20),
-        cost_estimate=pl.CostEstimate(flops=2 * ROWS * DEPTH * SLAB, bytes_accessed=2_000_000, transcendentals=0),
+        cost_estimate=pl.CostEstimate(flops=ROWS * DEPTH * SLAB, bytes_accessed=1_000_000, transcendentals=0),
     )(*operands)
+
+
+def apply(kernel, outs, mat, *operands):
+    parts = operands[-PARTS:]
+    wide = jax.ShapeDtypeStruct((ROWS, SLAB), jnp.float32)
+    early = call(early_kernel, wide, [], mat, *(parts[index] for index in EARLY))
+
+    def late_kernel(mat_ref, early_ref, *refs):
+        kernel((mat_ref, early_ref), *refs)
+
+    return call(late_kernel, outs, [pltpu.VMEM((ROWS, SLAB), jnp.float32)], mat, early, *operands)
 
 
 def same(index, count):
@@ -185,11 +210,13 @@
     return lax.ppermute(value, ("row", "col"), pairs)
 
 
-def surround(field):
+def surround(field, together=True):
     across_same = swap(field, same, cross)
     near_y = swap(field, near, same)
     far_y = swap(field, cross, same)
     beside = swap(field, same, near)
+    if together:
+        beside, across_same = lax.optimization_barrier((beside, across_same))
     beside_near = swap(near_y, same, near)
     beside_far = swap(far_y, same, near)
     across_far = swap(field, cross, cross)
@@ -218,7 +245,7 @@
     v_one, sums = apply(root_sums_kernel, (flat, sums_shape), z_mat, *surround(power))
     ring = sums + shifted(sums, "col", 4) + shifted(sums, "col", 8) + shifted(sums, "col", 12)
     other = shifted(ring, "row", 4)
-    v_two = apply(hamilton_sums_kernel, noted, h_mat, ring, other, *surround(v_one))
+    v_two = apply(hamilton_sums_kernel, noted, h_mat, ring, other, *surround(v_one, together=False))
     one, two = apply(last_kernel, (flat, flat), z_mat, slab, power_full, *surround(v_two))
     return one.reshape(x_slab.shape), two.reshape(x_slab.shape)
 

time: 94.8 us -> 94 us (level)
  starting transfers between devices: 58.8 us -> 57.6 us
    ppermute x48, starting transfers between devices: 55.3 us -> 53.3 us  [swap(): return lax.ppermute(value, ('row', 'col'), pairs)]
    pallas_call x6 -> x12, Pallas kernels: 3.71 us -> 4.63 us  [call(): pl.pallas_call(kernel, out_shape=outs, in_specs=[vmem()] * len(operands),...]
  transfers between devices with their start and end apart: 52 -> 52, of which waited for: 15 -> 16; matrix products, arithmetic and copies ran while one was open for 1% -> 1% of each run, Pallas kernels for 3% -> 5%
where the time goes in v9:
time: 94 us; the launch traced here: 93.9 us
  starting transfers between devices  57.6 us (61%)
  waiting for transfers between devices  25.5 us (27%)
  Pallas kernels  7.85 us (8%)
  local copies, waits for them, and re-layouts  1.17 us (1%)
    ppermute x48, starting transfers between devices, swap(): return lax.ppermute(value, ('row', 'col'), pairs)  53.3 us
    ppermute x48, waiting for transfers between devices, swap(): return lax.ppermute(value, ('row', 'col'), pairs)  24.6 us
    pallas_call x12, Pallas kernels, call(): pl.pallas_call(kernel, out_shape=outs, in_specs=[vmem()] * len(operands),...  4.63 us
    ppermute x4, starting transfers between devices, shifted(): lax.ppermute(sums, axis, [(i, (i + step) % count) for i in range(count)])  4.32 us
    pallas_call x2, Pallas kernels, build(): pl.pallas_call(build_kernel, out_shape=jax.ShapeDtypeStruct((ROWS, DEPTH...  3.22 us
  transfers between devices with their start and end apart: 52, of which 16 were waited for; matrix products, arithmetic and copies ran while one was open for 1% of the time, Pallas kernels for 5%

profile of v9, /device:TPU:0, one launch (start us, length us, event | category | flops | bytes accessed | tf_op | source)
XLA Modules:
  0.0 93.9 jit_solution(12152954288469484806)
XLA Ops:
  0.6 6.3 %collective-permute-start.3 = (bf16[256,128]{1,0:T(8,128)(2,1)}, bf16[256,128]{1,0:T(8,128)(2,1)S(1)}, u32[]{:S(2)}, u32[]{:S(2)}) collective-permute-start(bf16[256,128]{1,0:T(8,128)(2,1)} %bitcast.13), channel_id=1, source_target_pairs={{0,15},{1,2},{2,1},{3,4},{4,3},{5,6},{6,5},{7,8},{8,7},{9,10},{10,... | collective-permute-start | bytes 196616 | tf_op jit(solution)/shard_map/ppermute | solution.py:210
  6.9 2.9 %collective-permute-start.1 = (bf16[256,128]{1,0:T(8,128)(2,1)}, bf16[256,128]{1,0:T(8,128)(2,1)S(1)}, u32[]{:S(2)}, u32[]{:S(2)}) collective-permute-start(bf16[256,128]{1,0:T(8,128)(2,1)} %bitcast.15), channel_id=1, source_target_pairs={{0,112},{1,113},{2,114},{3,115},{4,116},{5,117},{6,118},{7,119},{8... | collective-permute-start | bytes 196616 | tf_op jit(solution)/shard_map/ppermute | solution.py:210
  9.9 2.1 %collective-permute-start.7 = (bf16[256,128]{1,0:T(8,128)(2,1)}, bf16[256,128]{1,0:T(8,128)(2,1)S(1)}, u32[]{:S(2)}, u32[]{:S(2)}) collective-permute-start(bf16[256,128]{1,0:T(8,128)(2,1)} %bitcast.17), channel_id=1, source_target_pairs={{0,127},{1,114},{2,113},{3,116},{4,115},{5,118},{6,117},{7,120},{8... | collective-permute-start | bytes 196616 | tf_op jit(solution)/shard_map/ppermute | solution.py:210
  12.0 2.1 %collective-permute-done.1.refs_2_ = bf16[256,128]{1,0:T(8,128)(2,1)S(1)} collective-permute-done((bf16[256,128]{1,0:T(8,128)(2,1)}, bf16[256,128]{1,0:T(8,128)(2,1)S(1)}, u32[]{:S(2)}, u32[]{:S(2)}) %collective-permute-start.1) | collective-permute-done | bytes 65568 | tf_op jit(solution)/shard_map/ppermute | solution.py:210
  19.6 2.4 %collective-permute-start.11 = (bf16[256,128]{1,0:T(8,128)(2,1)S(1)}, bf16[256,128]{1,0:T(8,128)(2,1)S(1)}, u32[]{:S(2)}, u32[]{:S(2)}) collective-permute-start(bf16[256,128]{1,0:T(8,128)(2,1)S(1)} %shard_map.89.refs_0_), channel_id=1, source_target_pairs={{0,15},{1,2},{2,1},{3,4},{4,3},{5,6},{6,5},{7,8},{8,7},{9,10},{10,... | collective-permute-start | bytes 196616 | tf_op jit(solution)/shard_map/ppermute | solution.py:210
  22.9 1.7 %collective-permute-start.8 = (bf16[256,128]{1,0:T(8,128)(2,1)S(1)}, bf16[256,128]{1,0:T(8,128)(2,1)S(1)}, u32[]{:S(2)}, u32[]{:S(2)}) collective-permute-start(bf16[256,128]{1,0:T(8,128)(2,1)S(1)} %shard_map.89.refs_0_), channel_id=1, source_target_pairs={{0,16},{1,17},{2,18},{3,19},{4,20},{5,21},{6,22},{7,23},{8,24},{9,... | collective-permute-start | bytes 196616 | tf_op jit(solution)/shard_map/ppermute | solution.py:210
  24.6 3.1 %collective-permute-start.15 = (bf16[256,128]{1,0:T(8,128)(2,1)S(1)}, bf16[256,128]{1,0:T(8,128)(2,1)S(1)}, u32[]{:S(2)}, u32[]{:S(2)}) collective-permute-start(bf16[256,128]{1,0:T(8,128)(2,1)S(1)} %shard_map.89.refs_0_), channel_id=1, source_target_pairs={{0,127},{1,114},{2,113},{3,116},{4,115},{5,118},{6,117},{7,120},{8... | collective-permute-start | bytes 196616 | tf_op jit(solution)/shard_map/ppermute | solution.py:210
  31.1 2.6 %collective-permute-done.15.refs_8_ = bf16[256,128]{1,0:T(8,128)(2,1)S(1)} collective-permute-done((bf16[256,128]{1,0:T(8,128)(2,1)S(1)}, bf16[256,128]{1,0:T(8,128)(2,1)S(1)}, u32[]{:S(2)}, u32[]{:S(2)}) %collective-permute-start.15) | collective-permute-done | bytes 65568 | tf_op jit(solution)/shard_map/ppermute | solution.py:210
  34.1 1.8 %collective-permute-start.19 = (bf16[256,128]{1,0:T(8,128)(2,1)S(1)}, bf16[256,128]{1,0:T(8,128)(2,1)S(1)}, u32[]{:S(2)}, u32[]{:S(2)}) collective-permute-start(bf16[256,128]{1,0:T(8,128)(2,1)S(1)} %shard_map.91.refs_0_.refs_1_), channel_id=1, source_target_pairs={{0,15},{1,2},{2,1},{3,4},{4,3},{5,6},{6,5},{7,8},{8,7},{9,10},{10,... | collective-permute-start | bytes 196616 | tf_op jit(solution)/shard_map/ppermute | solution.py:210
  35.9 2.2 %collective-permute-start.17 = (bf16[256,128]{1,0:T(8,128)(2,1)S(1)}, bf16[256,128]{1,0:T(8,128)(2,1)S(1)}, u32[]{:S(2)}, u32[]{:S(2)}) collective-permute-start(bf16[256,128]{1,0:T(8,128)(2,1)S(1)} %shard_map.91.refs_0_.refs_1_), channel_id=1, source_target_pairs={{0,112},{1,113},{2,114},{3,115},{4,116},{5,117},{6,118},{7,119},{8... | collective-permute-start | bytes 196616 | tf_op jit(solution)/shard_map/ppermute | solution.py:210
  38.1 3.8 %collective-permute-start.23 = (bf16[256,128]{1,0:T(8,128)(2,1)S(1)}, bf16[256,128]{1,0:T(8,128)(2,1)S(1)}, u32[]{:S(2)}, u32[]{:S(2)}) collective-permute-start(bf16[256,128]{1,0:T(8,128)(2,1)S(1)} %shard_map.91.refs_0_.refs_1_), channel_id=1, source_target_pairs={{0,127},{1,114},{2,113},{3,116},{4,115},{5,118},{6,117},{7,120},{8... | collective-permute-start | bytes 196616 | tf_op jit(solution)/shard_map/ppermute | solution.py:210
  44.3 2.9 %collective-permute-done.23.refs_9_ = bf16[256,128]{1,0:T(8,128)(2,1)S(1)} collective-permute-done((bf16[256,128]{1,0:T(8,128)(2,1)S(1)}, bf16[256,128]{1,0:T(8,128)(2,1)S(1)}, u32[]{:S(2)}, u32[]{:S(2)}) %collective-permute-start.23) | collective-permute-done | bytes 65568 | tf_op jit(solution)/shard_map/ppermute | solution.py:210
  48.8 3.7 %collective-permute-start.25 = (bf16[272,128]{1,0:T(8,128)(2,1)S(1)}, bf16[272,128]{1,0:T(8,128)(2,1)S(1)}, u32[]{:S(2)}, u32[]{:S(2)}) collective-permute-start(bf16[272,128]{1,0:T(8,128)(2,1)S(1)} %get-tuple-element.24.refs_0_), channel_id=1, source_target_pairs={{0,112},{1,113},{2,114},{3,115},{4,116},{5,117},{6,118},{7,119},{8... | collective-permute-start | bytes 208904 | tf_op jit(solution)/shard_map/ppermute | solution.py:210
  52.5 3.1 %collective-permute-start.31 = (bf16[272,128]{1,0:T(8,128)(2,1)S(1)}, bf16[272,128]{1,0:T(8,128)(2,1)S(1)}, u32[]{:S(2)}, u32[]{:S(2)}) collective-permute-start(bf16[272,128]{1,0:T(8,128)(2,1)S(1)} %get-tuple-element.24.refs_0_), channel_id=1, source_target_pairs={{0,127},{1,114},{2,113},{3,116},{4,115},{5,118},{6,117},{7,120},{8... | collective-permute-start | bytes 208904 | tf_op jit(solution)/shard_map/ppermute | solution.py:210
  57.8 3.9 %collective-permute-done.31.refs_8_ = bf16[272,128]{1,0:T(8,128)(2,1)S(1)} collective-permute-done((bf16[272,128]{1,0:T(8,128)(2,1)S(1)}, bf16[272,128]{1,0:T(8,128)(2,1)S(1)}, u32[]{:S(2)}, u32[]{:S(2)}) %collective-permute-start.31) | collective-permute-done | bytes 69664 | tf_op jit(solution)/shard_map/ppermute | solution.py:210
  62.4 1.9 %collective-permute-start.35 = (f32[8,128]{1,0:T(8,128)S(1)}, f32[8,128]{1,0:T(8,128)S(1)}, u32[]{:S(2)}, u32[]{:S(2)}) collective-permute-start(f32[8,128]{1,0:T(8,128)S(1)} %get-tuple-element.28), channel_id=1, source_target_pairs={{0,4},{1,5},{2,6},{3,7},{4,8},{5,9},{6,10},{7,11},{8,12},{9,13},{1... | collective-permute-start | bytes 12296 | tf_op jit(solution)/shard_map/ppermute | solution.py:229
  65.5 3.4 %collective-permute-start.33 = (bf16[256,128]{1,0:T(8,128)(2,1)S(1)}, bf16[256,128]{1,0:T(8,128)(2,1)S(1)}, u32[]{:S(2)}, u32[]{:S(2)}) collective-permute-start(bf16[256,128]{1,0:T(8,128)(2,1)S(1)} %get-tuple-element.27.refs_0_.refs_2_), channel_id=1, source_target_pairs={{0,112},{1,113},{2,114},{3,115},{4,116},{5,117},{6,118},{7,119},{8... | collective-permute-start | bytes 196616 | tf_op jit(solution)/shard_map/ppermute | solution.py:210
  68.9 2.1 %collective-permute-start.38 = (f32[8,128]{1,0:T(8,128)S(1)}, f32[8,128]{1,0:T(8,128)S(1)}, u32[]{:S(2)}, u32[]{:S(2)}) collective-permute-start(f32[8,128]{1,0:T(8,128)S(1)} %add_add_fusion.refs_0_), channel_id=1, source_target_pairs={{0,64},{16,80},{32,96},{48,112},{64,0},{80,16},{96,32},{112,48},{1... | collective-permute-start | bytes 12296 | tf_op jit(solution)/shard_map/ppermute | solution.py:229
  71.0 2.3 %collective-permute-start.43 = (bf16[256,128]{1,0:T(8,128)(2,1)S(1)}, bf16[256,128]{1,0:T(8,128)(2,1)S(1)}, u32[]{:S(2)}, u32[]{:S(2)}) collective-permute-start(bf16[256,128]{1,0:T(8,128)(2,1)S(1)} %get-tuple-element.27.refs_0_.refs_2_), channel_id=1, source_target_pairs={{0,127},{1,114},{2,113},{3,116},{4,115},{5,118},{6,117},{7,120},{8... | collective-permute-start | bytes 196616 | tf_op jit(solution)/shard_map/ppermute | solution.py:210
  74.1 2.1 %collective-permute-start.42 = (bf16[256,128]{1,0:T(8,128)(2,1)S(1)}, bf16[256,128]{1,0:T(8,128)(2,1)S(1)}, u32[]{:S(2)}, u32[]{:S(2)}) collective-permute-start(bf16[256,128]{1,0:T(8,128)(2,1)S(1)} %collective-permute-done.34.refs_3_.refs_8_), channel_id=1, source_target_pairs={{0,16},{1,17},{2,18},{3,19},{4,20},{5,21},{6,22},{7,23},{8,24},{9,... | collective-permute-start | bytes 196616 | tf_op jit(solution)/shard_map/ppermute | solution.py:210
  77.0 3.1 %collective-permute-done.43.refs_10_ = bf16[256,128]{1,0:T(8,128)(2,1)S(1)} collective-permute-done((bf16[256,128]{1,0:T(8,128)(2,1)S(1)}, bf16[256,128]{1,0:T(8,128)(2,1)S(1)}, u32[]{:S(2)}, u32[]{:S(2)}) %collective-permute-start.43) | collective-permute-done | bytes 65568 | tf_op jit(solution)/shard_map/ppermute | solution.py:210
  80.6 3.0 %collective-permute-start.45 = (bf16[272,128]{1,0:T(8,128)(2,1)S(1)}, bf16[272,128]{1,0:T(8,128)(2,1)S(1)}, u32[]{:S(2)}, u32[]{:S(2)}) collective-permute-start(bf16[272,128]{1,0:T(8,128)(2,1)S(1)} %shard_map.97.refs_0_.refs_2_), channel_id=1, source_target_pairs={{0,112},{1,113},{2,114},{3,115},{4,116},{5,117},{6,118},{7,119},{8... | collective-permute-start | bytes 208904 | tf_op jit(solution)/shard_map/ppermute | solution.py:210
  83.7 4.6 %collective-permute-start.51 = (bf16[272,128]{1,0:T(8,128)(2,1)S(1)}, bf16[272,128]{1,0:T(8,128)(2,1)S(1)}, u32[]{:S(2)}, u32[]{:S(2)}) collective-permute-start(bf16[272,128]{1,0:T(8,128)(2,1)S(1)} %shard_map.97.refs_0_.refs_2_), channel_id=1, source_target_pairs={{0,127},{1,114},{2,113},{3,116},{4,115},{5,118},{6,117},{7,120},{8... | collective-permute-start | bytes 208904 | tf_op jit(solution)/shard_map/ppermute | solution.py:210
  89.3 3.5 %collective-permute-done.51.refs_10_ = bf16[272,128]{1,0:T(8,128)(2,1)S(1)} collective-permute-done((bf16[272,128]{1,0:T(8,128)(2,1)S(1)}, bf16[272,128]{1,0:T(8,128)(2,1)S(1)}, u32[]{:S(2)}, u32[]{:S(2)}) %collective-permute-start.51) | collective-permute-done | bytes 69664 | tf_op jit(solution)/shard_map/ppermute | solution.py:210
  (107 shorter events, 22.5 us)
Async XLA Ops:
  0.6 11.4 %collective-permute-start.3 = (bf16[256,128]{1,0:T(8,128)(2,1)}, bf16[256,128]{1,0:T(8,128)(2,1)S(1)}, u32[]{:S(2)}, u32[]{:S(2)}) collective-permute-start(bf16[256,128]{1,0:T(8,128)(2,1)} %bitcast.13), channel_id=1, source_target_pairs={{0,15},{1,2},{2,1},{3,4},{4,3},{5,6},{6,5},{7,8},{8,7},{9,10},{10,... | collective-permute-start | bytes 196616 | tf_op jit(solution)/shard_map/ppermute | solution.py:210
  6.9 7.2 %collective-permute-start.1 = (bf16[256,128]{1,0:T(8,128)(2,1)}, bf16[256,128]{1,0:T(8,128)(2,1)S(1)}, u32[]{:S(2)}, u32[]{:S(2)}) collective-permute-start(bf16[256,128]{1,0:T(8,128)(2,1)} %bitcast.15), channel_id=1, source_target_pairs={{0,112},{1,113},{2,114},{3,115},{4,116},{5,117},{6,118},{7,119},{8... | collective-permute-start | bytes 196616 | tf_op jit(solution)/shard_map/ppermute | solution.py:210
  9.9 9.3 %collective-permute-start.7 = (bf16[256,128]{1,0:T(8,128)(2,1)}, bf16[256,128]{1,0:T(8,128)(2,1)S(1)}, u32[]{:S(2)}, u32[]{:S(2)}) collective-permute-start(bf16[256,128]{1,0:T(8,128)(2,1)} %bitcast.17), channel_id=1, source_target_pairs={{0,127},{1,114},{2,113},{3,116},{4,115},{5,118},{6,117},{7,120},{8... | collective-permute-start | bytes 196616 | tf_op jit(solution)/shard_map/ppermute | solution.py:210
  12.0 7.2 %collective-permute-start.6 = (bf16[256,128]{1,0:T(8,128)(2,1)S(1)}, bf16[256,128]{1,0:T(8,128)(2,1)S(1)}, u32[]{:S(2)}, u32[]{:S(2)}) collective-permute-start(bf16[256,128]{1,0:T(8,128)(2,1)S(1)} %collective-permute-done.3.refs_3_.refs_6_), channel_id=1, source_target_pairs={{0,16},{1,17},{2,18},{3,19},{4,20},{5,21},{6,22},{7,23},{8,24},{9,... | collective-permute-start | bytes 196616 | tf_op jit(solution)/shard_map/ppermute | solution.py:210
  19.6 8.1 %collective-permute-start.11 = (bf16[256,128]{1,0:T(8,128)(2,1)S(1)}, bf16[256,128]{1,0:T(8,128)(2,1)S(1)}, u32[]{:S(2)}, u32[]{:S(2)}) collective-permute-start(bf16[256,128]{1,0:T(8,128)(2,1)S(1)} %shard_map.89.refs_0_), channel_id=1, source_target_pairs={{0,15},{1,2},{2,1},{3,4},{4,3},{5,6},{6,5},{7,8},{8,7},{9,10},{10,... | collective-permute-start | bytes 196616 | tf_op jit(solution)/shard_map/ppermute | solution.py:210
  21.9 6.6 %collective-permute-start.9 = (bf16[256,128]{1,0:T(8,128)(2,1)S(1)}, bf16[256,128]{1,0:T(8,128)(2,1)S(1)}, u32[]{:S(2)}, u32[]{:S(2)}) collective-permute-start(bf16[256,128]{1,0:T(8,128)(2,1)S(1)} %shard_map.89.refs_0_), channel_id=1, source_target_pairs={{0,112},{1,113},{2,114},{3,115},{4,116},{5,117},{6,118},{7,119},{8... | collective-permute-start | bytes 196616 | tf_op jit(solution)/shard_map/ppermute | solution.py:210
  24.6 9.1 %collective-permute-start.15 = (bf16[256,128]{1,0:T(8,128)(2,1)S(1)}, bf16[256,128]{1,0:T(8,128)(2,1)S(1)}, u32[]{:S(2)}, u32[]{:S(2)}) collective-permute-start(bf16[256,128]{1,0:T(8,128)(2,1)S(1)} %shard_map.89.refs_0_), channel_id=1, source_target_pairs={{0,127},{1,114},{2,113},{3,116},{4,115},{5,118},{6,117},{7,120},{8... | collective-permute-start | bytes 196616 | tf_op jit(solution)/shard_map/ppermute | solution.py:210
  34.1 8.6 %collective-permute-start.19 = (bf16[256,128]{1,0:T(8,128)(2,1)S(1)}, bf16[256,128]{1,0:T(8,128)(2,1)S(1)}, u32[]{:S(2)}, u32[]{:S(2)}) collective-permute-start(bf16[256,128]{1,0:T(8,128)(2,1)S(1)} %shard_map.91.refs_0_.refs_1_), channel_id=1, source_target_pairs={{0,15},{1,2},{2,1},{3,4},{4,3},{5,6},{6,5},{7,8},{8,7},{9,10},{10,... | collective-permute-start | bytes 196616 | tf_op jit(solution)/shard_map/ppermute | solution.py:210
  35.9 6.7 %collective-permute-start.18 = (bf16[256,128]{1,0:T(8,128)(2,1)S(1)}, bf16[256,128]{1,0:T(8,128)(2,1)S(1)}, u32[]{:S(2)}, u32[]{:S(2)}) collective-permute-start(bf16[256,128]{1,0:T(8,128)(2,1)S(1)} %shard_map.91.refs_0_.refs_1_), channel_id=1, source_target_pairs={{0,1},{1,0},{2,3},{3,2},{4,5},{5,4},{6,7},{7,6},{8,9},{9,8},{10,11... | collective-permute-start | bytes 196616 | tf_op jit(solution)/shard_map/ppermute | solution.py:210
  35.9 7.0 %collective-permute-start.17 = (bf16[256,128]{1,0:T(8,128)(2,1)S(1)}, bf16[256,128]{1,0:T(8,128)(2,1)S(1)}, u32[]{:S(2)}, u32[]{:S(2)}) collective-permute-start(bf16[256,128]{1,0:T(8,128)(2,1)S(1)} %shard_map.91.refs_0_.refs_1_), channel_id=1, source_target_pairs={{0,112},{1,113},{2,114},{3,115},{4,116},{5,117},{6,118},{7,119},{8... | collective-permute-start | bytes 196616 | tf_op jit(solution)/shard_map/ppermute | solution.py:210
  38.1 9.1 %collective-permute-start.23 = (bf16[256,128]{1,0:T(8,128)(2,1)S(1)}, bf16[256,128]{1,0:T(8,128)(2,1)S(1)}, u32[]{:S(2)}, u32[]{:S(2)}) collective-permute-start(bf16[256,128]{1,0:T(8,128)(2,1)S(1)} %shard_map.91.refs_0_.refs_1_), channel_id=1, source_target_pairs={{0,127},{1,114},{2,113},{3,116},{4,115},{5,118},{6,117},{7,120},{8... | collective-permute-start | bytes 196616 | tf_op jit(solution)/shard_map/ppermute | solution.py:210
  47.7 7.8 %collective-permute-start.27 = (bf16[272,128]{1,0:T(8,128)(2,1)S(1)}, bf16[272,128]{1,0:T(8,128)(2,1)S(1)}, u32[]{:S(2)}, u32[]{:S(2)}) collective-permute-start(bf16[272,128]{1,0:T(8,128)(2,1)S(1)} %get-tuple-element.24.refs_0_), channel_id=1, source_target_pairs={{0,15},{1,2},{2,1},{3,4},{4,3},{5,6},{6,5},{7,8},{8,7},{9,10},{10,... | collective-permute-start | bytes 208904 | tf_op jit(solution)/shard_map/ppermute | solution.py:210
  48.8 6.8 %collective-permute-start.26 = (bf16[272,128]{1,0:T(8,128)(2,1)S(1)}, bf16[272,128]{1,0:T(8,128)(2,1)S(1)}, u32[]{:S(2)}, u32[]{:S(2)}) collective-permute-start(bf16[272,128]{1,0:T(8,128)(2,1)S(1)} %get-tuple-element.24.refs_0_), channel_id=1, source_target_pairs={{0,1},{1,0},{2,3},{3,2},{4,5},{5,4},{6,7},{7,6},{8,9},{9,8},{10,11... | collective-permute-start | bytes 208904 | tf_op jit(solution)/shard_map/ppermute | solution.py:210
  48.8 7.1 %collective-permute-start.25 = (bf16[272,128]{1,0:T(8,128)(2,1)S(1)}, bf16[272,128]{1,0:T(8,128)(2,1)S(1)}, u32[]{:S(2)}, u32[]{:S(2)}) collective-permute-start(bf16[272,128]{1,0:T(8,128)(2,1)S(1)} %get-tuple-element.24.refs_0_), channel_id=1, source_target_pairs={{0,112},{1,113},{2,114},{3,115},{4,116},{5,117},{6,118},{7,119},{8... | collective-permute-start | bytes 208904 | tf_op jit(solution)/shard_map/ppermute | solution.py:210
  52.5 9.2 %collective-permute-start.31 = (bf16[272,128]{1,0:T(8,128)(2,1)S(1)}, bf16[272,128]{1,0:T(8,128)(2,1)S(1)}, u32[]{:S(2)}, u32[]{:S(2)}) collective-permute-start(bf16[272,128]{1,0:T(8,128)(2,1)S(1)} %get-tuple-element.24.refs_0_), channel_id=1, source_target_pairs={{0,127},{1,114},{2,113},{3,116},{4,115},{5,118},{6,117},{7,120},{8... | collective-permute-start | bytes 208904 | tf_op jit(solution)/shard_map/ppermute | solution.py:210
  62.0 6.9 %collective-permute-start.37 = (f32[8,128]{1,0:T(8,128)S(1)}, f32[8,128]{1,0:T(8,128)S(1)}, u32[]{:S(2)}, u32[]{:S(2)}) collective-permute-start(f32[8,128]{1,0:T(8,128)S(1)} %get-tuple-element.28), channel_id=1, source_target_pairs={{0,12},{1,13},{2,14},{3,15},{4,0},{5,1},{6,2},{7,3},{8,4},{9,5},{1... | collective-permute-start | bytes 12296 | tf_op jit(solution)/shard_map/ppermute | solution.py:229
  64.3 9.8 %collective-permute-start.34 = (bf16[256,128]{1,0:T(8,128)(2,1)S(1)}, bf16[256,128]{1,0:T(8,128)(2,1)S(1)}, u32[]{:S(2)}, u32[]{:S(2)}) collective-permute-start(bf16[256,128]{1,0:T(8,128)(2,1)S(1)} %get-tuple-element.27.refs_0_.refs_2_), channel_id=1, source_target_pairs={{0,15},{1,2},{2,1},{3,4},{4,3},{5,6},{6,5},{7,8},{8,7},{9,10},{10,... | collective-permute-start | bytes 196616 | tf_op jit(solution)/shard_map/ppermute | solution.py:210
  65.5 10.7 %collective-permute-start.33 = (bf16[256,128]{1,0:T(8,128)(2,1)S(1)}, bf16[256,128]{1,0:T(8,128)(2,1)S(1)}, u32[]{:S(2)}, u32[]{:S(2)}) collective-permute-start(bf16[256,128]{1,0:T(8,128)(2,1)S(1)} %get-tuple-element.27.refs_0_.refs_2_), channel_id=1, source_target_pairs={{0,112},{1,113},{2,114},{3,115},{4,116},{5,117},{6,118},{7,119},{8... | collective-permute-start | bytes 196616 | tf_op jit(solution)/shard_map/ppermute | solution.py:210
  68.9 7.6 %collective-permute-start.32 = (bf16[256,128]{1,0:T(8,128)(2,1)S(1)}, bf16[256,128]{1,0:T(8,128)(2,1)S(1)}, u32[]{:S(2)}, u32[]{:S(2)}) collective-permute-start(bf16[256,128]{1,0:T(8,128)(2,1)S(1)} %get-tuple-element.27.refs_0_.refs_2_), channel_id=1, source_target_pairs={{0,16},{1,17},{2,18},{3,19},{4,20},{5,21},{6,22},{7,23},{8,24},{9,... | collective-permute-start | bytes 196616 | tf_op jit(solution)/shard_map/ppermute | solution.py:210
  71.0 9.1 %collective-permute-start.43 = (bf16[256,128]{1,0:T(8,128)(2,1)S(1)}, bf16[256,128]{1,0:T(8,128)(2,1)S(1)}, u32[]{:S(2)}, u32[]{:S(2)}) collective-permute-start(bf16[256,128]{1,0:T(8,128)(2,1)S(1)} %get-tuple-element.27.refs_0_.refs_2_), channel_id=1, source_target_pairs={{0,127},{1,114},{2,113},{3,116},{4,115},{5,118},{6,117},{7,120},{8... | collective-permute-start | bytes 196616 | tf_op jit(solution)/shard_map/ppermute | solution.py:210
  80.5 7.8 %collective-permute-start.47 = (bf16[272,128]{1,0:T(8,128)(2,1)S(1)}, bf16[272,128]{1,0:T(8,128)(2,1)S(1)}, u32[]{:S(2)}, u32[]{:S(2)}) collective-permute-start(bf16[272,128]{1,0:T(8,128)(2,1)S(1)} %shard_map.97.refs_0_.refs_2_), channel_id=1, source_target_pairs={{0,15},{1,2},{2,1},{3,4},{4,3},{5,6},{6,5},{7,8},{8,7},{9,10},{10,... | collective-permute-start | bytes 208904 | tf_op jit(solution)/shard_map/ppermute | solution.py:210
  80.5 7.8 %collective-permute-start.46 = (bf16[272,128]{1,0:T(8,128)(2,1)S(1)}, bf16[272,128]{1,0:T(8,128)(2,1)S(1)}, u32[]{:S(2)}, u32[]{:S(2)}) collective-permute-start(bf16[272,128]{1,0:T(8,128)(2,1)S(1)} %shard_map.97.refs_0_.refs_2_), channel_id=1, source_target_pairs={{0,1},{1,0},{2,3},{3,2},{4,5},{5,4},{6,7},{7,6},{8,9},{9,8},{10,11... | collective-permute-start | bytes 208904 | tf_op jit(solution)/shard_map/ppermute | solution.py:210
  80.6 7.9 %collective-permute-start.45 = (bf16[272,128]{1,0:T(8,128)(2,1)S(1)}, bf16[272,128]{1,0:T(8,128)(2,1)S(1)}, u32[]{:S(2)}, u32[]{:S(2)}) collective-permute-start(bf16[272,128]{1,0:T(8,128)(2,1)S(1)} %shard_map.97.refs_0_.refs_2_), channel_id=1, source_target_pairs={{0,112},{1,113},{2,114},{3,115},{4,116},{5,117},{6,118},{7,119},{8... | collective-permute-start | bytes 208904 | tf_op jit(solution)/shard_map/ppermute | solution.py:210
  83.7 9.2 %collective-permute-start.51 = (bf16[272,128]{1,0:T(8,128)(2,1)S(1)}, bf16[272,128]{1,0:T(8,128)(2,1)S(1)}, u32[]{:S(2)}, u32[]{:S(2)}) collective-permute-start(bf16[272,128]{1,0:T(8,128)(2,1)S(1)} %shard_map.97.refs_0_.refs_2_), channel_id=1, source_target_pairs={{0,127},{1,114},{2,113},{3,116},{4,115},{5,118},{6,117},{7,120},{8... | collective-permute-start | bytes 208904 | tf_op jit(solution)/shard_map/ppermute | solution.py:210
  (33 other events, 191.7 us)

commit v10 on v9

--- a/solution.py
+++ b/solution.py
@@ -165,8 +165,9 @@
     sums = read_notes([part_refs[part] for part in (0, 2, 6, 8)])
     ratio = jnp.sqrt(sums[:, :1] / (sums[:, SLAB // 2 : SLAB // 2 + 1] + 1e-06))
     image = part_refs[0][:ROWS].astype(jnp.float32) + product(mat_ref, part_refs, turn_ref)
-    one_ref[...] = (power_ref[...] / ratio).astype(jnp.bfloat16)
-    two_ref[...] = (2.0 * (image / ratio) / ratio - slab_ref[...].astype(jnp.float32)).astype(jnp.bfloat16)
+    inverse = 1.0 / ratio
+    one_ref[...] = (power_ref[...] * inverse).astype(jnp.bfloat16)
+    two_ref[...] = ((image * inverse) * (2.0 * inverse) - slab_ref[...].astype(jnp.float32)).astype(jnp.bfloat16)
 
 
 def call(kernel, outs, scratch, *operands):

time: 94 us -> 94 us (level)
  no operation moved by 1% of the time
where the time goes in v10:
time: 94 us; the launch traced here: 93.9 us
  starting transfers between devices  57.6 us (61%)
  waiting for transfers between devices  25.5 us (27%)
  Pallas kernels  7.85 us (8%)
  local copies, waits for them, and re-layouts  1.17 us (1%)
    ppermute x48, starting transfers between devices, swap(): return lax.ppermute(value, ('row', 'col'), pairs)  53.3 us
    ppermute x48, waiting for transfers between devices, swap(): return lax.ppermute(value, ('row', 'col'), pairs)  24.6 us
    pallas_call x12, Pallas kernels, call(): pl.pallas_call(kernel, out_shape=outs, in_specs=[vmem()] * len(operands),...  4.62 us
    ppermute x4, starting transfers between devices, shifted(): lax.ppermute(sums, axis, [(i, (i + step) % count) for i in range(count)])  4.32 us
    pallas_call x2, Pallas kernels, build(): pl.pallas_call(build_kernel, out_shape=jax.ShapeDtypeStruct((ROWS, DEPTH...  3.22 us
  transfers between devices with their start and end apart: 52, of which 16 were waited for; matrix products, arithmetic and copies ran while one was open for 1% of the time, Pallas kernels for 5%

profile of v10, /device:TPU:0, one launch (start us, length us, event | category | flops | bytes accessed | tf_op | source)
XLA Modules:
  0.0 93.9 jit_solution(10269788279556918671)
XLA Ops:
  0.6 6.3 %collective-permute-start.3 = (bf16[256,128]{1,0:T(8,128)(2,1)}, bf16[256,128]{1,0:T(8,128)(2,1)S(1)}, u32[]{:S(2)}, u32[]{:S(2)}) collective-permute-start(bf16[256,128]{1,0:T(8,128)(2,1)} %bitcast.13), channel_id=1, source_target_pairs={{0,15},{1,2},{2,1},{3,4},{4,3},{5,6},{6,5},{7,8},{8,7},{9,10},{10,... | collective-permute-start | bytes 196616 | tf_op jit(solution)/shard_map/ppermute | solution.py:211
  6.9 2.9 %collective-permute-start.1 = (bf16[256,128]{1,0:T(8,128)(2,1)}, bf16[256,128]{1,0:T(8,128)(2,1)S(1)}, u32[]{:S(2)}, u32[]{:S(2)}) collective-permute-start(bf16[256,128]{1,0:T(8,128)(2,1)} %bitcast.15), channel_id=1, source_target_pairs={{0,112},{1,113},{2,114},{3,115},{4,116},{5,117},{6,118},{7,119},{8... | collective-permute-start | bytes 196616 | tf_op jit(solution)/shard_map/ppermute | solution.py:211
  9.9 2.1 %collective-permute-start.7 = (bf16[256,128]{1,0:T(8,128)(2,1)}, bf16[256,128]{1,0:T(8,128)(2,1)S(1)}, u32[]{:S(2)}, u32[]{:S(2)}) collective-permute-start(bf16[256,128]{1,0:T(8,128)(2,1)} %bitcast.17), channel_id=1, source_target_pairs={{0,127},{1,114},{2,113},{3,116},{4,115},{5,118},{6,117},{7,120},{8... | collective-permute-start | bytes 196616 | tf_op jit(solution)/shard_map/ppermute | solution.py:211
  12.0 2.1 %collective-permute-done.1.refs_2_ = bf16[256,128]{1,0:T(8,128)(2,1)S(1)} collective-permute-done((bf16[256,128]{1,0:T(8,128)(2,1)}, bf16[256,128]{1,0:T(8,128)(2,1)S(1)}, u32[]{:S(2)}, u32[]{:S(2)}) %collective-permute-start.1) | collective-permute-done | bytes 65568 | tf_op jit(solution)/shard_map/ppermute | solution.py:211
  19.6 2.4 %collective-permute-start.11 = (bf16[256,128]{1,0:T(8,128)(2,1)S(1)}, bf16[256,128]{1,0:T(8,128)(2,1)S(1)}, u32[]{:S(2)}, u32[]{:S(2)}) collective-permute-start(bf16[256,128]{1,0:T(8,128)(2,1)S(1)} %shard_map.89.refs_0_), channel_id=1, source_target_pairs={{0,15},{1,2},{2,1},{3,4},{4,3},{5,6},{6,5},{7,8},{8,7},{9,10},{10,... | collective-permute-start | bytes 196616 | tf_op jit(solution)/shard_map/ppermute | solution.py:211
  22.9 1.7 %collective-permute-start.8 = (bf16[256,128]{1,0:T(8,128)(2,1)S(1)}, bf16[256,128]{1,0:T(8,128)(2,1)S(1)}, u32[]{:S(2)}, u32[]{:S(2)}) collective-permute-start(bf16[256,128]{1,0:T(8,128)(2,1)S(1)} %shard_map.89.refs_0_), channel_id=1, source_target_pairs={{0,16},{1,17},{2,18},{3,19},{4,20},{5,21},{6,22},{7,23},{8,24},{9,... | collective-permute-start | bytes 196616 | tf_op jit(solution)/shard_map/ppermute | solution.py:211
  24.6 3.1 %collective-permute-start.15 = (bf16[256,128]{1,0:T(8,128)(2,1)S(1)}, bf16[256,128]{1,0:T(8,128)(2,1)S(1)}, u32[]{:S(2)}, u32[]{:S(2)}) collective-permute-start(bf16[256,128]{1,0:T(8,128)(2,1)S(1)} %shard_map.89.refs_0_), channel_id=1, source_target_pairs={{0,127},{1,114},{2,113},{3,116},{4,115},{5,118},{6,117},{7,120},{8... | collective-permute-start | bytes 196616 | tf_op jit(solution)/shard_map/ppermute | solution.py:211
  31.1 2.6 %collective-permute-done.15.refs_8_ = bf16[256,128]{1,0:T(8,128)(2,1)S(1)} collective-permute-done((bf16[256,128]{1,0:T(8,128)(2,1)S(1)}, bf16[256,128]{1,0:T(8,128)(2,1)S(1)}, u32[]{:S(2)}, u32[]{:S(2)}) %collective-permute-start.15) | collective-permute-done | bytes 65568 | tf_op jit(solution)/shard_map/ppermute | solution.py:211
  34.1 1.8 %collective-permute-start.19 = (bf16[256,128]{1,0:T(8,128)(2,1)S(1)}, bf16[256,128]{1,0:T(8,128)(2,1)S(1)}, u32[]{:S(2)}, u32[]{:S(2)}) collective-permute-start(bf16[256,128]{1,0:T(8,128)(2,1)S(1)} %shard_map.91.refs_0_.refs_1_), channel_id=1, source_target_pairs={{0,15},{1,2},{2,1},{3,4},{4,3},{5,6},{6,5},{7,8},{8,7},{9,10},{10,... | collective-permute-start | bytes 196616 | tf_op jit(solution)/shard_map/ppermute | solution.py:211
  35.9 2.2 %collective-permute-start.17 = (bf16[256,128]{1,0:T(8,128)(2,1)S(1)}, bf16[256,128]{1,0:T(8,128)(2,1)S(1)}, u32[]{:S(2)}, u32[]{:S(2)}) collective-permute-start(bf16[256,128]{1,0:T(8,128)(2,1)S(1)} %shard_map.91.refs_0_.refs_1_), channel_id=1, source_target_pairs={{0,112},{1,113},{2,114},{3,115},{4,116},{5,117},{6,118},{7,119},{8... | collective-permute-start | bytes 196616 | tf_op jit(solution)/shard_map/ppermute | solution.py:211
  38.1 3.8 %collective-permute-start.23 = (bf16[256,128]{1,0:T(8,128)(2,1)S(1)}, bf16[256,128]{1,0:T(8,128)(2,1)S(1)}, u32[]{:S(2)}, u32[]{:S(2)}) collective-permute-start(bf16[256,128]{1,0:T(8,128)(2,1)S(1)} %shard_map.91.refs_0_.refs_1_), channel_id=1, source_target_pairs={{0,127},{1,114},{2,113},{3,116},{4,115},{5,118},{6,117},{7,120},{8... | collective-permute-start | bytes 196616 | tf_op jit(solution)/shard_map/ppermute | solution.py:211
  44.3 2.9 %collective-permute-done.23.refs_9_ = bf16[256,128]{1,0:T(8,128)(2,1)S(1)} collective-permute-done((bf16[256,128]{1,0:T(8,128)(2,1)S(1)}, bf16[256,128]{1,0:T(8,128)(2,1)S(1)}, u32[]{:S(2)}, u32[]{:S(2)}) %collective-permute-start.23) | collective-permute-done | bytes 65568 | tf_op jit(solution)/shard_map/ppermute | solution.py:211
  48.8 3.7 %collective-permute-start.25 = (bf16[272,128]{1,0:T(8,128)(2,1)S(1)}, bf16[272,128]{1,0:T(8,128)(2,1)S(1)}, u32[]{:S(2)}, u32[]{:S(2)}) collective-permute-start(bf16[272,128]{1,0:T(8,128)(2,1)S(1)} %get-tuple-element.24.refs_0_), channel_id=1, source_target_pairs={{0,112},{1,113},{2,114},{3,115},{4,116},{5,117},{6,118},{7,119},{8... | collective-permute-start | bytes 208904 | tf_op jit(solution)/shard_map/ppermute | solution.py:211
  52.5 3.1 %collective-permute-start.31 = (bf16[272,128]{1,0:T(8,128)(2,1)S(1)}, bf16[272,128]{1,0:T(8,128)(2,1)S(1)}, u32[]{:S(2)}, u32[]{:S(2)}) collective-permute-start(bf16[272,128]{1,0:T(8,128)(2,1)S(1)} %get-tuple-element.24.refs_0_), channel_id=1, source_target_pairs={{0,127},{1,114},{2,113},{3,116},{4,115},{5,118},{6,117},{7,120},{8... | collective-permute-start | bytes 208904 | tf_op jit(solution)/shard_map/ppermute | solution.py:211
  57.8 3.9 %collective-permute-done.31.refs_8_ = bf16[272,128]{1,0:T(8,128)(2,1)S(1)} collective-permute-done((bf16[272,128]{1,0:T(8,128)(2,1)S(1)}, bf16[272,128]{1,0:T(8,128)(2,1)S(1)}, u32[]{:S(2)}, u32[]{:S(2)}) %collective-permute-start.31) | collective-permute-done | bytes 69664 | tf_op jit(solution)/shard_map/ppermute | solution.py:211
  62.4 1.9 %collective-permute-start.35 = (f32[8,128]{1,0:T(8,128)S(1)}, f32[8,128]{1,0:T(8,128)S(1)}, u32[]{:S(2)}, u32[]{:S(2)}) collective-permute-start(f32[8,128]{1,0:T(8,128)S(1)} %get-tuple-element.28), channel_id=1, source_target_pairs={{0,4},{1,5},{2,6},{3,7},{4,8},{5,9},{6,10},{7,11},{8,12},{9,13},{1... | collective-permute-start | bytes 12296 | tf_op jit(solution)/shard_map/ppermute | solution.py:230
  65.5 3.4 %collective-permute-start.33 = (bf16[256,128]{1,0:T(8,128)(2,1)S(1)}, bf16[256,128]{1,0:T(8,128)(2,1)S(1)}, u32[]{:S(2)}, u32[]{:S(2)}) collective-permute-start(bf16[256,128]{1,0:T(8,128)(2,1)S(1)} %get-tuple-element.27.refs_0_.refs_2_), channel_id=1, source_target_pairs={{0,112},{1,113},{2,114},{3,115},{4,116},{5,117},{6,118},{7,119},{8... | collective-permute-start | bytes 196616 | tf_op jit(solution)/shard_map/ppermute | solution.py:211
  68.9 2.1 %collective-permute-start.38 = (f32[8,128]{1,0:T(8,128)S(1)}, f32[8,128]{1,0:T(8,128)S(1)}, u32[]{:S(2)}, u32[]{:S(2)}) collective-permute-start(f32[8,128]{1,0:T(8,128)S(1)} %add_add_fusion.refs_0_), channel_id=1, source_target_pairs={{0,64},{16,80},{32,96},{48,112},{64,0},{80,16},{96,32},{112,48},{1... | collective-permute-start | bytes 12296 | tf_op jit(solution)/shard_map/ppermute | solution.py:230
  71.0 2.3 %collective-permute-start.43 = (bf16[256,128]{1,0:T(8,128)(2,1)S(1)}, bf16[256,128]{1,0:T(8,128)(2,1)S(1)}, u32[]{:S(2)}, u32[]{:S(2)}) collective-permute-start(bf16[256,128]{1,0:T(8,128)(2,1)S(1)} %get-tuple-element.27.refs_0_.refs_2_), channel_id=1, source_target_pairs={{0,127},{1,114},{2,113},{3,116},{4,115},{5,118},{6,117},{7,120},{8... | collective-permute-start | bytes 196616 | tf_op jit(solution)/shard_map/ppermute | solution.py:211
  74.1 2.1 %collective-permute-start.42 = (bf16[256,128]{1,0:T(8,128)(2,1)S(1)}, bf16[256,128]{1,0:T(8,128)(2,1)S(1)}, u32[]{:S(2)}, u32[]{:S(2)}) collective-permute-start(bf16[256,128]{1,0:T(8,128)(2,1)S(1)} %collective-permute-done.34.refs_3_.refs_8_), channel_id=1, source_target_pairs={{0,16},{1,17},{2,18},{3,19},{4,20},{5,21},{6,22},{7,23},{8,24},{9,... | collective-permute-start | bytes 196616 | tf_op jit(solution)/shard_map/ppermute | solution.py:211
  77.0 3.1 %collective-permute-done.43.refs_10_ = bf16[256,128]{1,0:T(8,128)(2,1)S(1)} collective-permute-done((bf16[256,128]{1,0:T(8,128)(2,1)S(1)}, bf16[256,128]{1,0:T(8,128)(2,1)S(1)}, u32[]{:S(2)}, u32[]{:S(2)}) %collective-permute-start.43) | collective-permute-done | bytes 65568 | tf_op jit(solution)/shard_map/ppermute | solution.py:211
  80.6 3.0 %collective-permute-start.45 = (bf16[272,128]{1,0:T(8,128)(2,1)S(1)}, bf16[272,128]{1,0:T(8,128)(2,1)S(1)}, u32[]{:S(2)}, u32[]{:S(2)}) collective-permute-start(bf16[272,128]{1,0:T(8,128)(2,1)S(1)} %shard_map.97.refs_0_.refs_2_), channel_id=1, source_target_pairs={{0,112},{1,113},{2,114},{3,115},{4,116},{5,117},{6,118},{7,119},{8... | collective-permute-start | bytes 208904 | tf_op jit(solution)/shard_map/ppermute | solution.py:211
  83.7 4.6 %collective-permute-start.51 = (bf16[272,128]{1,0:T(8,128)(2,1)S(1)}, bf16[272,128]{1,0:T(8,128)(2,1)S(1)}, u32[]{:S(2)}, u32[]{:S(2)}) collective-permute-start(bf16[272,128]{1,0:T(8,128)(2,1)S(1)} %shard_map.97.refs_0_.refs_2_), channel_id=1, source_target_pairs={{0,127},{1,114},{2,113},{3,116},{4,115},{5,118},{6,117},{7,120},{8... | collective-permute-start | bytes 208904 | tf_op jit(solution)/shard_map/ppermute | solution.py:211
  89.3 3.5 %collective-permute-done.51.refs_10_ = bf16[272,128]{1,0:T(8,128)(2,1)S(1)} collective-permute-done((bf16[272,128]{1,0:T(8,128)(2,1)S(1)}, bf16[272,128]{1,0:T(8,128)(2,1)S(1)}, u32[]{:S(2)}, u32[]{:S(2)}) %collective-permute-start.51) | collective-permute-done | bytes 69664 | tf_op jit(solution)/shard_map/ppermute | solution.py:211
  (107 shorter events, 22.5 us)
Async XLA Ops:
  0.6 11.4 %collective-permute-start.3 = (bf16[256,128]{1,0:T(8,128)(2,1)}, bf16[256,128]{1,0:T(8,128)(2,1)S(1)}, u32[]{:S(2)}, u32[]{:S(2)}) collective-permute-start(bf16[256,128]{1,0:T(8,128)(2,1)} %bitcast.13), channel_id=1, source_target_pairs={{0,15},{1,2},{2,1},{3,4},{4,3},{5,6},{6,5},{7,8},{8,7},{9,10},{10,... | collective-permute-start | bytes 196616 | tf_op jit(solution)/shard_map/ppermute | solution.py:211
  6.9 7.2 %collective-permute-start.1 = (bf16[256,128]{1,0:T(8,128)(2,1)}, bf16[256,128]{1,0:T(8,128)(2,1)S(1)}, u32[]{:S(2)}, u32[]{:S(2)}) collective-permute-start(bf16[256,128]{1,0:T(8,128)(2,1)} %bitcast.15), channel_id=1, source_target_pairs={{0,112},{1,113},{2,114},{3,115},{4,116},{5,117},{6,118},{7,119},{8... | collective-permute-start | bytes 196616 | tf_op jit(solution)/shard_map/ppermute | solution.py:211
  9.9 9.3 %collective-permute-start.7 = (bf16[256,128]{1,0:T(8,128)(2,1)}, bf16[256,128]{1,0:T(8,128)(2,1)S(1)}, u32[]{:S(2)}, u32[]{:S(2)}) collective-permute-start(bf16[256,128]{1,0:T(8,128)(2,1)} %bitcast.17), channel_id=1, source_target_pairs={{0,127},{1,114},{2,113},{3,116},{4,115},{5,118},{6,117},{7,120},{8... | collective-permute-start | bytes 196616 | tf_op jit(solution)/shard_map/ppermute | solution.py:211
  12.0 7.2 %collective-permute-start.6 = (bf16[256,128]{1,0:T(8,128)(2,1)S(1)}, bf16[256,128]{1,0:T(8,128)(2,1)S(1)}, u32[]{:S(2)}, u32[]{:S(2)}) collective-permute-start(bf16[256,128]{1,0:T(8,128)(2,1)S(1)} %collective-permute-done.3.refs_3_.refs_6_), channel_id=1, source_target_pairs={{0,16},{1,17},{2,18},{3,19},{4,20},{5,21},{6,22},{7,23},{8,24},{9,... | collective-permute-start | bytes 196616 | tf_op jit(solution)/shard_map/ppermute | solution.py:211
  19.6 8.1 %collective-permute-start.11 = (bf16[256,128]{1,0:T(8,128)(2,1)S(1)}, bf16[256,128]{1,0:T(8,128)(2,1)S(1)}, u32[]{:S(2)}, u32[]{:S(2)}) collective-permute-start(bf16[256,128]{1,0:T(8,128)(2,1)S(1)} %shard_map.89.refs_0_), channel_id=1, source_target_pairs={{0,15},{1,2},{2,1},{3,4},{4,3},{5,6},{6,5},{7,8},{8,7},{9,10},{10,... | collective-permute-start | bytes 196616 | tf_op jit(solution)/shard_map/ppermute | solution.py:211
  21.9 6.6 %collective-permute-start.9 = (bf16[256,128]{1,0:T(8,128)(2,1)S(1)}, bf16[256,128]{1,0:T(8,128)(2,1)S(1)}, u32[]{:S(2)}, u32[]{:S(2)}) collective-permute-start(bf16[256,128]{1,0:T(8,128)(2,1)S(1)} %shard_map.89.refs_0_), channel_id=1, source_target_pairs={{0,112},{1,113},{2,114},{3,115},{4,116},{5,117},{6,118},{7,119},{8... | collective-permute-start | bytes 196616 | tf_op jit(solution)/shard_map/ppermute | solution.py:211
  24.6 9.1 %collective-permute-start.15 = (bf16[256,128]{1,0:T(8,128)(2,1)S(1)}, bf16[256,128]{1,0:T(8,128)(2,1)S(1)}, u32[]{:S(2)}, u32[]{:S(2)}) collective-permute-start(bf16[256,128]{1,0:T(8,128)(2,1)S(1)} %shard_map.89.refs_0_), channel_id=1, source_target_pairs={{0,127},{1,114},{2,113},{3,116},{4,115},{5,118},{6,117},{7,120},{8... | collective-permute-start | bytes 196616 | tf_op jit(solution)/shard_map/ppermute | solution.py:211
  34.1 8.6 %collective-permute-start.19 = (bf16[256,128]{1,0:T(8,128)(2,1)S(1)}, bf16[256,128]{1,0:T(8,128)(2,1)S(1)}, u32[]{:S(2)}, u32[]{:S(2)}) collective-permute-start(bf16[256,128]{1,0:T(8,128)(2,1)S(1)} %shard_map.91.refs_0_.refs_1_), channel_id=1, source_target_pairs={{0,15},{1,2},{2,1},{3,4},{4,3},{5,6},{6,5},{7,8},{8,7},{9,10},{10,... | collective-permute-start | bytes 196616 | tf_op jit(solution)/shard_map/ppermute | solution.py:211
  35.9 6.7 %collective-permute-start.18 = (bf16[256,128]{1,0:T(8,128)(2,1)S(1)}, bf16[256,128]{1,0:T(8,128)(2,1)S(1)}, u32[]{:S(2)}, u32[]{:S(2)}) collective-permute-start(bf16[256,128]{1,0:T(8,128)(2,1)S(1)} %shard_map.91.refs_0_.refs_1_), channel_id=1, source_target_pairs={{0,1},{1,0},{2,3},{3,2},{4,5},{5,4},{6,7},{7,6},{8,9},{9,8},{10,11... | collective-permute-start | bytes 196616 | tf_op jit(solution)/shard_map/ppermute | solution.py:211
  35.9 7.0 %collective-permute-start.17 = (bf16[256,128]{1,0:T(8,128)(2,1)S(1)}, bf16[256,128]{1,0:T(8,128)(2,1)S(1)}, u32[]{:S(2)}, u32[]{:S(2)}) collective-permute-start(bf16[256,128]{1,0:T(8,128)(2,1)S(1)} %shard_map.91.refs_0_.refs_1_), channel_id=1, source_target_pairs={{0,112},{1,113},{2,114},{3,115},{4,116},{5,117},{6,118},{7,119},{8... | collective-permute-start | bytes 196616 | tf_op jit(solution)/shard_map/ppermute | solution.py:211
  38.1 9.1 %collective-permute-start.23 = (bf16[256,128]{1,0:T(8,128)(2,1)S(1)}, bf16[256,128]{1,0:T(8,128)(2,1)S(1)}, u32[]{:S(2)}, u32[]{:S(2)}) collective-permute-start(bf16[256,128]{1,0:T(8,128)(2,1)S(1)} %shard_map.91.refs_0_.refs_1_), channel_id=1, source_target_pairs={{0,127},{1,114},{2,113},{3,116},{4,115},{5,118},{6,117},{7,120},{8... | collective-permute-start | bytes 196616 | tf_op jit(solution)/shard_map/ppermute | solution.py:211
  47.7 7.8 %collective-permute-start.27 = (bf16[272,128]{1,0:T(8,128)(2,1)S(1)}, bf16[272,128]{1,0:T(8,128)(2,1)S(1)}, u32[]{:S(2)}, u32[]{:S(2)}) collective-permute-start(bf16[272,128]{1,0:T(8,128)(2,1)S(1)} %get-tuple-element.24.refs_0_), channel_id=1, source_target_pairs={{0,15},{1,2},{2,1},{3,4},{4,3},{5,6},{6,5},{7,8},{8,7},{9,10},{10,... | collective-permute-start | bytes 208904 | tf_op jit(solution)/shard_map/ppermute | solution.py:211
  48.8 6.8 %collective-permute-start.26 = (bf16[272,128]{1,0:T(8,128)(2,1)S(1)}, bf16[272,128]{1,0:T(8,128)(2,1)S(1)}, u32[]{:S(2)}, u32[]{:S(2)}) collective-permute-start(bf16[272,128]{1,0:T(8,128)(2,1)S(1)} %get-tuple-element.24.refs_0_), channel_id=1, source_target_pairs={{0,1},{1,0},{2,3},{3,2},{4,5},{5,4},{6,7},{7,6},{8,9},{9,8},{10,11... | collective-permute-start | bytes 208904 | tf_op jit(solution)/shard_map/ppermute | solution.py:211
  48.8 7.1 %collective-permute-start.25 = (bf16[272,128]{1,0:T(8,128)(2,1)S(1)}, bf16[272,128]{1,0:T(8,128)(2,1)S(1)}, u32[]{:S(2)}, u32[]{:S(2)}) collective-permute-start(bf16[272,128]{1,0:T(8,128)(2,1)S(1)} %get-tuple-element.24.refs_0_), channel_id=1, source_target_pairs={{0,112},{1,113},{2,114},{3,115},{4,116},{5,117},{6,118},{7,119},{8... | collective-permute-start | bytes 208904 | tf_op jit(solution)/shard_map/ppermute | solution.py:211
  52.5 9.2 %collective-permute-start.31 = (bf16[272,128]{1,0:T(8,128)(2,1)S(1)}, bf16[272,128]{1,0:T(8,128)(2,1)S(1)}, u32[]{:S(2)}, u32[]{:S(2)}) collective-permute-start(bf16[272,128]{1,0:T(8,128)(2,1)S(1)} %get-tuple-element.24.refs_0_), channel_id=1, source_target_pairs={{0,127},{1,114},{2,113},{3,116},{4,115},{5,118},{6,117},{7,120},{8... | collective-permute-start | bytes 208904 | tf_op jit(solution)/shard_map/ppermute | solution.py:211
  62.0 6.9 %collective-permute-start.37 = (f32[8,128]{1,0:T(8,128)S(1)}, f32[8,128]{1,0:T(8,128)S(1)}, u32[]{:S(2)}, u32[]{:S(2)}) collective-permute-start(f32[8,128]{1,0:T(8,128)S(1)} %get-tuple-element.28), channel_id=1, source_target_pairs={{0,12},{1,13},{2,14},{3,15},{4,0},{5,1},{6,2},{7,3},{8,4},{9,5},{1... | collective-permute-start | bytes 12296 | tf_op jit(solution)/shard_map/ppermute | solution.py:230
  64.3 9.8 %collective-permute-start.34 = (bf16[256,128]{1,0:T(8,128)(2,1)S(1)}, bf16[256,128]{1,0:T(8,128)(2,1)S(1)}, u32[]{:S(2)}, u32[]{:S(2)}) collective-permute-start(bf16[256,128]{1,0:T(8,128)(2,1)S(1)} %get-tuple-element.27.refs_0_.refs_2_), channel_id=1, source_target_pairs={{0,15},{1,2},{2,1},{3,4},{4,3},{5,6},{6,5},{7,8},{8,7},{9,10},{10,... | collective-permute-start | bytes 196616 | tf_op jit(solution)/shard_map/ppermute | solution.py:211
  65.5 10.7 %collective-permute-start.33 = (bf16[256,128]{1,0:T(8,128)(2,1)S(1)}, bf16[256,128]{1,0:T(8,128)(2,1)S(1)}, u32[]{:S(2)}, u32[]{:S(2)}) collective-permute-start(bf16[256,128]{1,0:T(8,128)(2,1)S(1)} %get-tuple-element.27.refs_0_.refs_2_), channel_id=1, source_target_pairs={{0,112},{1,113},{2,114},{3,115},{4,116},{5,117},{6,118},{7,119},{8... | collective-permute-start | bytes 196616 | tf_op jit(solution)/shard_map/ppermute | solution.py:211
  68.9 7.6 %collective-permute-start.32 = (bf16[256,128]{1,0:T(8,128)(2,1)S(1)}, bf16[256,128]{1,0:T(8,128)(2,1)S(1)}, u32[]{:S(2)}, u32[]{:S(2)}) collective-permute-start(bf16[256,128]{1,0:T(8,128)(2,1)S(1)} %get-tuple-element.27.refs_0_.refs_2_), channel_id=1, source_target_pairs={{0,16},{1,17},{2,18},{3,19},{4,20},{5,21},{6,22},{7,23},{8,24},{9,... | collective-permute-start | bytes 196616 | tf_op jit(solution)/shard_map/ppermute | solution.py:211
  71.0 9.1 %collective-permute-start.43 = (bf16[256,128]{1,0:T(8,128)(2,1)S(1)}, bf16[256,128]{1,0:T(8,128)(2,1)S(1)}, u32[]{:S(2)}, u32[]{:S(2)}) collective-permute-start(bf16[256,128]{1,0:T(8,128)(2,1)S(1)} %get-tuple-element.27.refs_0_.refs_2_), channel_id=1, source_target_pairs={{0,127},{1,114},{2,113},{3,116},{4,115},{5,118},{6,117},{7,120},{8... | collective-permute-start | bytes 196616 | tf_op jit(solution)/shard_map/ppermute | solution.py:211
  80.5 7.8 %collective-permute-start.47 = (bf16[272,128]{1,0:T(8,128)(2,1)S(1)}, bf16[272,128]{1,0:T(8,128)(2,1)S(1)}, u32[]{:S(2)}, u32[]{:S(2)}) collective-permute-start(bf16[272,128]{1,0:T(8,128)(2,1)S(1)} %shard_map.97.refs_0_.refs_2_), channel_id=1, source_target_pairs={{0,15},{1,2},{2,1},{3,4},{4,3},{5,6},{6,5},{7,8},{8,7},{9,10},{10,... | collective-permute-start | bytes 208904 | tf_op jit(solution)/shard_map/ppermute | solution.py:211
  80.5 7.8 %collective-permute-start.46 = (bf16[272,128]{1,0:T(8,128)(2,1)S(1)}, bf16[272,128]{1,0:T(8,128)(2,1)S(1)}, u32[]{:S(2)}, u32[]{:S(2)}) collective-permute-start(bf16[272,128]{1,0:T(8,128)(2,1)S(1)} %shard_map.97.refs_0_.refs_2_), channel_id=1, source_target_pairs={{0,1},{1,0},{2,3},{3,2},{4,5},{5,4},{6,7},{7,6},{8,9},{9,8},{10,11... | collective-permute-start | bytes 208904 | tf_op jit(solution)/shard_map/ppermute | solution.py:211
  80.6 7.9 %collective-permute-start.45 = (bf16[272,128]{1,0:T(8,128)(2,1)S(1)}, bf16[272,128]{1,0:T(8,128)(2,1)S(1)}, u32[]{:S(2)}, u32[]{:S(2)}) collective-permute-start(bf16[272,128]{1,0:T(8,128)(2,1)S(1)} %shard_map.97.refs_0_.refs_2_), channel_id=1, source_target_pairs={{0,112},{1,113},{2,114},{3,115},{4,116},{5,117},{6,118},{7,119},{8... | collective-permute-start | bytes 208904 | tf_op jit(solution)/shard_map/ppermute | solution.py:211
  83.7 9.2 %collective-permute-start.51 = (bf16[272,128]{1,0:T(8,128)(2,1)S(1)}, bf16[272,128]{1,0:T(8,128)(2,1)S(1)}, u32[]{:S(2)}, u32[]{:S(2)}) collective-permute-start(bf16[272,128]{1,0:T(8,128)(2,1)S(1)} %shard_map.97.refs_0_.refs_2_), channel_id=1, source_target_pairs={{0,127},{1,114},{2,113},{3,116},{4,115},{5,118},{6,117},{7,120},{8... | collective-permute-start | bytes 208904 | tf_op jit(solution)/shard_map/ppermute | solution.py:211
  (33 other events, 191.7 us)
